TPU v7x, 128 devices: a whole 4x4x4 slice. The times are simulated.
128 devices in a mesh: dp: 16 (over y_lo, x, core), tensor: 8 (over z, y_hi).
Axes of the slice: x: 4, y: 4 (y_hi: 2, y_lo: 2; y = y_hi * 2 + y_lo), z: 4, core: 2. Of those that a mesh axis runs over, the one named last changes fastest.
Arguments:
- attn: bfloat16 [16, 1024, 6144], P('dp', None, 'tensor'), may hold values from -1.796875 to 1.796875
- w_out: bfloat16 [8192, 6144], P('dp', 'tensor'), may hold values from -0.09375 to 0.09375
- counts: int32 [8], replicated, may hold values from 1 to 6, 32 in all
- grad_out: bfloat16 [16, 1024, 8192], P('dp', 'tensor'), may hold values from -1.796875 to 1.796875
Outputs:
- projected: bfloat16 [16, 1024, 8192], P('dp', 'tensor')
- grad_attn: bfloat16 [16, 1024, 6144], P('dp', None, 'tensor')
- grad_w: float32 [8192, 6144], P('dp', 'tensor')
Inputs may be any that keep to these rules, and one draw needn't show every extreme that they name: counts[r] is the number of live head slots of tensor rank r, its first ones; they sum to 32, and the largest is 6.
All inputs are finite; a program needn't handle non-finite values.
Results may differ from a plain program's by a relative error of at most 0.02.
Values may be sent and summed in bfloat16 or wider, within the bound.
No kernel may reach another device: no remote copies, remote signals or barrier semaphores. Data moves between devices by JAX's collectives and lax.ppermute only.
A program may use at most 256 MiB of HBM per device.

v0:
```python
import jax
import jax.numpy as jnp
from jax import lax
from jax.sharding import PartitionSpec as P

HD = 128


def per_device(attn, w_out, counts, grad_out):
    rank = lax.axis_index("tensor")
    width = attn.shape[2]
    own = jnp.sum(jnp.where(jnp.arange(counts.shape[0], dtype=jnp.int32) == rank, counts, 0))
    live = (jnp.arange(width, dtype=jnp.int32) // HD < own).astype(jnp.float32)
    masked = attn[0] * live.astype(jnp.bfloat16)
    w_full = lax.all_gather(w_out, "dp", axis=0, tiled=True)
    projected = lax.psum_scatter(
        lax.dot_general(
            masked, w_full, (((1,), (1,)), ((), ())), preferred_element_type=jnp.float32
        ).astype(jnp.bfloat16),
        "tensor",
        scatter_dimension=0,
        tiled=True,
    )
    cot_full = lax.all_gather(grad_out[0], "tensor", axis=0, tiled=True)
    grad_rows = (jnp.dot(cot_full, w_full, preferred_element_type=jnp.float32) * live).astype(
        jnp.bfloat16
    )
    grad_w = lax.psum_scatter(
        lax.dot_general(
            cot_full, masked, (((0,), (0,)), ((), ())), preferred_element_type=jnp.float32
        ).astype(jnp.bfloat16),
        "dp",
        scatter_dimension=0,
        tiled=True,
    ).astype(jnp.float32)
    return (projected[None], grad_rows[None], grad_w)


def solution(mesh):
    placed = (P("dp", None, "tensor"), P("dp", "tensor"), P(), P("dp", "tensor", None))
    return jax.shard_map(
        per_device,
        mesh=mesh,
        in_specs=placed,
        out_specs=(P("dp", "tensor", None), P("dp", None, "tensor"), P("dp", "tensor")),
        check_vma=False,
    )
```

profile of v0, /device:TPU:0, one launch (start us, length us, event | category | flops | bytes accessed | tf_op | source)
XLA Modules:
  0.0 556.1 jit_solution(7206613942591138797)
XLA Ops:
  7.2 0.0 all-gather.6.cloned.1.call-start
  7.2 0.7 all-gather.6.cloned.1.call-update
  7.9 0.0 all-gather.4.cloned.1.call-start
  7.9 0.7 all-gather.4.cloned.1.call-update
  8.6 0.0 reduce-scatter.5.cloned.1.call-start
  8.7 1.3 fusion.23
  10.0 0.6 fusion.22
  10.6 185.1 %all-gather.6.cloned.1.call-done = bf16[1,1024,8192]{2,1,0:T(8,128)(2,1)} async-done(((bf16[1,128,8192]{2,1,0:T(8,128)(2,1)}), bf16[1,1024,8192]{2,1,0:T(8,128)(2,1)}) %all-gather.6.cloned.1.call-update) | async-done | bytes 16777232 | tf_op jit(solution)/shard_map/all_gather | solution.py:24
  195.8 22.2 %fusion.7 = bf16[8192,768]{0,1:T(8,128)(2,1)} fusion(bf16[1,1024,8192]{2,1,0:T(8,128)(2,1)} %all-gather.6.cloned.1.call-done, bf16[1,1024,768]{2,1,0:T(8,128)(2,1)} %param.4, bf16[768]{0:T(1024)(128)(2,1)S(1)} %fusion.22), kind=kOutput, calls=%fused_computation.6 | convolution fusion | flops 12891979776 | bytes 30934528 | tf_op jit(solution)/shard_map/dot_general | solution.py:29
  218.0 0.0 copy-start
  218.0 0.0 reduce-scatter.5.cloned.1.call-update
  218.1 0.2 reduce-scatter.3.cloned.1.call-start
  218.3 48.8 %all-gather.4.cloned.1.call-done = bf16[8192,768]{1,0:T(8,128)(2,1)} async-done(((bf16[512,768]{1,0:T(8,128)(2,1)}), bf16[8192,768]{1,0:T(8,128)(2,1)}) %all-gather.4.cloned.1.call-update) | async-done | bytes 12582928 | tf_op jit(solution)/shard_map/all_gather | solution.py:15
  267.1 0.0 copy-done
  267.1 20.4 %convolution_convert_fusion = bf16[1024,8192]{1,0:T(8,128)(2,1)} fusion(bf16[8192,768]{1,0:T(8,128)(2,1)} %all-gather.4.cloned.1.call-done, bf16[1,1024,768]{2,1,0:T(8,128)(2,1)S(1)} %copy-done, bf16[768]{0:T(1024)(128)(2,1)S(1)} %fusion.22), kind=kOutput, calls=%fused_computation.4 | convolution fusion | flops 12894076928 | bytes 30934528 | tf_op jit(solution)/shard_map/dot_general | solution.py:17
  287.5 0.0 reduce-scatter.3.cloned.1.call-update
  287.5 0.7 fusion.21
  288.2 20.2 %fusion.12 = bf16[1,1024,768]{2,1,0:T(8,128)(2,1)} fusion(f32[768]{0:T(1024)S(1)} %fusion.21, bf16[8192,768]{1,0:T(8,128)(2,1)} %all-gather.4.cloned.1.call-done, bf16[1,1024,8192]{2,1,0:T(8,128)(2,1)} %all-gather.6.cloned.1.call-done), kind=kOutput, calls=%fused_computation.9 | convolution fusion | flops 12886474752 | bytes 30936064 | tf_op jit(solution)/shard_map/dot_general | solution.py:25
  308.3 44.6 %reduce-scatter.5.cloned.1.call-done = bf16[512,768]{0,1:T(8,128)(2,1)} async-done(((bf16[8192,768]{0,1:T(8,128)(2,1)}), bf16[512,768]{0,1:T(8,128)(2,1)}) %reduce-scatter.5.cloned.1.call-update) | async-done | bytes 786448 | tf_op jit(solution)/shard_map/reduce_scatter | solution.py:28
  352.9 2.5 copy.7
  355.4 194.2 %reduce-scatter.3.cloned.1.call-done = bf16[128,8192]{1,0:T(8,128)(2,1)} async-done(((bf16[1024,8192]{1,0:T(8,128)(2,1)}), bf16[128,8192]{1,0:T(8,128)(2,1)}) %reduce-scatter.3.cloned.1.call-update) | async-done | bytes 2097168 | tf_op jit(solution)/shard_map/reduce_scatter | solution.py:16
Async XLA Ops:
  7.2 188.6 %all-gather.6.cloned.1.call-start = ((), (), s32[]{:S(2)}) async-start(), calls=%async_computation.5 | async-start | bytes 18874368 | tf_op jit(solution)/shard_map/all_gather | solution.py:24
  7.9 259.2 %all-gather.4.cloned.1.call-start = ((), (), s32[]{:S(2)}) async-start(), calls=%async_computation.2 | async-start | bytes 13369344 | tf_op jit(solution)/shard_map/all_gather | solution.py:15
  8.6 344.2 %reduce-scatter.5.cloned.1.call-start = ((), (), s32[]{:S(2)}) async-start(), calls=%async_computation.4 | async-start | bytes 13369344 | tf_op jit(solution)/shard_map/reduce_scatter | solution.py:28
  218.0 49.0 %copy-start = (bf16[1,1024,768]{2,1,0:T(8,128)(2,1)S(1)}, bf16[1,1024,768]{2,1,0:T(8,128)(2,1)}, u32[]{:S(2)}) copy-start(bf16[1,1024,768]{2,1,0:T(8,128)(2,1)} %param.4) | copy-start | bytes 4718596
  218.1 331.5 %reduce-scatter.3.cloned.1.call-start = ((), (), s32[]{:S(2)}) async-start(), calls=%async_computation.3 | async-start | bytes 18874368 | tf_op jit(solution)/shard_map/reduce_scatter | solution.py:16
Sparse Core Ops, SparseCore 0:
  10.3 185.3 all-gather.5
  197.5 69.5 all-gather.3
  269.5 83.3 reduce-scatter.4
  357.3 192.2 reduce-scatter.2
where the time goes:
time: 556 us
  waiting for transfers between devices  474 us (85%)
  matrix products  62.8 us (11%)
  between operations  13.8 us (2%)
    reduce_scatter x1, waiting for transfers between devices, per_device(): lax.psum_scatter(lax.dot_general(masked, w_full, (((1,), (1,)), ((), ()))...  194 us
    all_gather x1, waiting for transfers between devices, per_device(): cot_full = lax.all_gather(grad_out[0], 'tensor', axis=0, tiled=True)  185 us
    all_gather x1, waiting for transfers between devices, per_device(): w_full = lax.all_gather(w_out, 'dp', axis=0, tiled=True)  48.8 us
    reduce_scatter x1, waiting for transfers between devices, per_device(): lax.psum_scatter(lax.dot_general(cot_full, masked, (((0,), (0,)), ((), ()...  44.6 us
    dot_general x1, matrix products, per_device(): lax.dot_general(cot_full, masked, (((0,), (0,)), ((), ())), preferred_ele...  22.2 us
    dot_general x1, matrix products, per_device(): lax.dot_general(masked, w_full, (((1,), (1,)), ((), ())), preferred_eleme...  20.4 us
    dot_general x1, matrix products, per_device(): jnp.dot(cot_full, w_full, preferred_element_type=jnp.float32) * live  20.2 us
  transfers between devices with their start and end apart: 4, of which 4 were waited for; matrix products, arithmetic and copies ran while one was open for 12% of the time, Pallas kernels for 0%

commit v1 on v0

v1 whole, which is shorter than its diff:
```python
import jax
import jax.numpy as jnp
from jax import lax
from jax.sharding import PartitionSpec as P

HD = 128
NZ = 4
NH = 2


def ring(step):
    return [
        (z * NH + h, ((z + step) % NZ) * NH + h) for z in range(NZ) for h in range(NH)
    ]


SWAP = [(t, t ^ 1) for t in range(NZ * NH)]


def shift(value, step):
    return lax.ppermute(value, "tensor", ring(step))


def swap(value):
    return lax.ppermute(value, "tensor", SWAP)


def pick(blocks, index):
    return lax.dynamic_index_in_dim(blocks, index % NZ, 0, keepdims=False)


def per_device(attn, w_out, counts, grad_out):
    rank = lax.axis_index("tensor")
    z, h = rank // NH, rank % NH
    s, width = attn.shape[1:]
    own_rows, d = grad_out.shape[1:]
    n_dp = d // w_out.shape[0]
    piece = w_out.shape[0] // NZ
    feats = n_dp * piece
    half = s // 2

    own = jnp.sum(
        jnp.where(jnp.arange(counts.shape[0], dtype=jnp.int32) == rank, counts, 0)
    )
    live = (jnp.arange(width, dtype=jnp.int32) // HD < own).astype(jnp.float32)

    w_blocks = w_out.reshape(NZ, piece, width)
    w_near = [pick(w_blocks, z)] + [shift(pick(w_blocks, z + k), k) for k in range(1, NZ)]
    w_all = lax.all_gather(jnp.concatenate(w_near, axis=1), "dp", axis=0, tiled=True)

    g_blocks = grad_out[0].reshape(own_rows, n_dp, NZ, piece).transpose(2, 0, 1, 3)
    g_blocks = g_blocks.reshape(NZ, own_rows, feats)
    g_near = [pick(g_blocks, z)] + [shift(pick(g_blocks, z + k), k) for k in range(1, NZ)]
    g_far = [swap(block) for block in g_near]

    def in_order(pieces):
        stacked = jnp.stack(pieces)
        return [pick(stacked, z - a) for a in range(NZ)]

    cot = jnp.concatenate(in_order(g_far) + in_order(g_near), axis=0)

    rows = attn[0].reshape(NZ, NH, own_rows, width)
    other = lax.dynamic_index_in_dim(rows, 1 - h, 1, keepdims=False)
    same = lax.dynamic_index_in_dim(rows, h, 1, keepdims=False)
    masked = jnp.concatenate([other, same], axis=0).reshape(s, width) * live.astype(
        jnp.bfloat16
    )
    left = shift(masked, 1)
    right = shift(masked, -1)
    across = jnp.concatenate([shift(left[:half], 1), shift(right[half:], -1)], axis=0)
    act = jnp.concatenate([masked, left, across, right], axis=1)

    term = lax.dot_general(
        cot, act, (((0,), (0,)), ((), ())), preferred_element_type=jnp.float32
    ).astype(jnp.bfloat16)
    term = lax.psum_scatter(term, "dp", scatter_dimension=0, tiled=True)
    parts = [term[:, k * width : (k + 1) * width] for k in range(NZ)]
    parts = [parts[0]] + [shift(parts[k], -k) for k in range(1, NZ)]
    stacked = jnp.stack(parts)
    grad_w = jnp.concatenate([pick(stacked, a - z) for a in range(NZ)], axis=0).astype(
        jnp.float32
    )

    def rows_term(k):
        return jnp.dot(
            cot, w_all[:, k * width : (k + 1) * width], preferred_element_type=jnp.float32
        )

    far = rows_term(2).astype(jnp.bfloat16)
    up = shift(far[:half], 1)
    down = shift(far[half:], -1)
    to_right = rows_term(3)
    to_right = jnp.concatenate(
        [to_right[:half] + up.astype(jnp.float32), to_right[half:]], axis=0
    ).astype(jnp.bfloat16)
    to_left = rows_term(1)
    to_left = jnp.concatenate(
        [to_left[:half], to_left[half:] + down.astype(jnp.float32)], axis=0
    ).astype(jnp.bfloat16)
    total = (
        rows_term(0)
        + shift(to_right, 1).astype(jnp.float32)
        + shift(to_left, -1).astype(jnp.float32)
    )
    total = (total * live).astype(jnp.bfloat16).reshape(NH, NZ, own_rows, width)
    even = lax.dynamic_index_in_dim(total, 1 - h, 0, keepdims=False)
    odd = lax.dynamic_index_in_dim(total, h, 0, keepdims=False)
    grad_rows = jnp.stack([even, odd], axis=1).reshape(s, width)

    def project(x):
        return lax.dot_general(
            x, w_all, (((1,), (1,)), ((), ())), preferred_element_type=jnp.float32
        )

    sent = swap(project(act[:half]).astype(jnp.bfloat16))
    summed = (project(act[half:]) + sent.astype(jnp.float32)).astype(jnp.bfloat16)
    blocks = summed.reshape(NZ, own_rows, feats)
    quarters = [pick(blocks, z)] + [shift(pick(blocks, z + k), k) for k in range(1, NZ)]
    projected = jnp.stack(
        [q.reshape(own_rows, n_dp, piece) for q in in_order(quarters)], axis=2
    ).reshape(own_rows, d)
    return (projected[None], grad_rows[None], grad_w)


def solution(mesh):
    placed = (P("dp", None, "tensor"), P("dp", "tensor"), P(), P("dp", "tensor", None))
    return jax.shard_map(
        per_device,
        mesh=mesh,
        in_specs=placed,
        out_specs=(P("dp", "tensor", None), P("dp", None, "tensor"), P("dp", "tensor")),
        check_vma=False,
    )
```

time: 556 us -> 371 us (0.67); the launches traced: 556 us -> 364 us
  waiting for transfers between devices: 474 us -> 189 us
  starting transfers between devices: 0.34 us -> 48.4 us
  local copies, waits for them, and re-layouts: 2.55 us -> 22.3 us
  other arithmetic: 2.59 us -> 22.2 us
    reduce_scatter x2 -> x1, waiting for transfers between devices: 239 us -> 0.02 us  [per_device(): term = lax.psum_scatter(term, 'dp', scatter_dimension=0, tiled=True)]
    all_gather x2 -> x1, waiting for transfers between devices: 234 us -> 0.01 us  [per_device(): lax.all_gather(jnp.concatenate(w_near, axis=1), 'dp', axis=0, tiled=True)]
    ppermute x0 -> x25, waiting for transfers between devices: none -> 189 us  [the longest x5 136 us: swap(): return lax.ppermute(value, 'tensor', SWAP)]
    ppermute x0 -> x25, starting transfers between devices: none -> 48.4 us  [the longest x20 34.4 us: shift(): return lax.ppermute(value, 'tensor', ring(step))]
    concatenate x0 -> x5, other arithmetic: none -> 10.8 us  [the longest x1 7.18 us: per_device(): act = jnp.concatenate([masked, left, across, right], axis=1)]
    unnamed x3 -> x16, local copies, waits for them, and re-layouts: 2.55 us -> 12.5 us
    another operation x0 -> x8, other arithmetic: none -> 8.03 us  [the longest x3 5.01 us: in_order(): stacked = jnp.stack(pieces)]
    dot_general x3 -> x7, matrix products: 62.8 us -> 67.8 us  [the longest x4 28 us: rows_term(): jnp.dot(cot, w_all[:, k * width:(k + 1) * width], preferred_element_type=...]
  transfers between devices with their start and end apart: 4 -> 27, of which waited for: 4 -> 15; matrix products, arithmetic and copies ran while one was open for 12% -> 29% of each run, Pallas kernels for 0% -> 0%
where the time goes in v1:
time: 371 us; the launch traced here: 364 us
  waiting for transfers between devices  189 us (51%)
  matrix products  67.8 us (18%)
  starting transfers between devices  48.4 us (13%)
  local copies, waits for them, and re-layouts  22.3 us (6%)
  other arithmetic  22.2 us (6%)
  between operations  14.9 us (4%)
    ppermute x5, waiting for transfers between devices, swap(): return lax.ppermute(value, 'tensor', SWAP)  136 us
    ppermute x20, waiting for transfers between devices, shift(): return lax.ppermute(value, 'tensor', ring(step))  52.2 us
    ppermute x20, starting transfers between devices, shift(): return lax.ppermute(value, 'tensor', ring(step))  34.4 us
    dot_general x4, matrix products, rows_term(): jnp.dot(cot, w_all[:, k * width:(k + 1) * width], preferred_element_type=...  28 us
    dot_general x2, matrix products, project(): lax.dot_general(x, w_all, (((1,), (1,)), ((), ())), preferred_element_typ...  20.8 us
    dot_general x1, matrix products, per_device(): lax.dot_general(cot, act, (((0,), (0,)), ((), ())), preferred_element_typ...  19.1 us
    ppermute x5, starting transfers between devices, swap(): return lax.ppermute(value, 'tensor', SWAP)  14 us
    unnamed x16, local copies, waits for them, and re-layouts  12.5 us
  transfers between devices with their start and end apart: 27, of which 15 were waited for; matrix products, arithmetic and copies ran while one was open for 29% of the time, Pallas kernels for 0%

profile of v1, /device:TPU:0, one launch (start us, length us, event | category | flops | bytes accessed | tf_op | source)
XLA Modules:
  0.0 364.3 jit_solution(3036665269979593826)
XLA Ops:
  7.3 1.3 dynamic-slice_bitcast_fusion.14
  8.6 2.1 collective-permute-start.4
  10.7 3.6 collective-permute-start.5
  15.2 2.4 collective-permute-done.4
  17.7 5.4 %collective-permute-done.5 = bf16[128,768]{1,0:T(8,128)(2,1)S(1)} collective-permute-done((bf16[128,768]{1,0:T(8,128)(2,1)S(1)}, bf16[128,768]{1,0:T(8,128)(2,1)S(1)}, u32[]{:S(2)}, u32[]{:S(2)}) %collective-permute-start.5) | collective-permute-done | bytes 196640 | tf_op jit(solution)/shard_map/ppermute | solution.py:21
  24.1 3.2 copy.16
  29.7 2.4 collective-permute-start.14
  33.3 3.2 collective-permute-start.11
  38.1 4.7 %collective-permute-done.12 = bf16[128,2048]{0,1:T(8,128)(2,1)} collective-permute-done((bf16[128,2048]{0,1:T(8,128)(2,1)S(1)}, bf16[128,2048]{0,1:T(8,128)(2,1)}, u32[]{:S(2)}, u32[]{:S(2)}) %collective-permute-start.12) | collective-permute-done | bytes 524320 | tf_op jit(solution)/shard_map/ppermute | solution.py:21
  42.8 3.2 collective-permute-start.13
  46.0 9.2 %collective-permute-done.14 = bf16[128,2048]{0,1:T(8,128)(2,1)} collective-permute-done((bf16[128,2048]{0,1:T(8,128)(2,1)S(1)}, bf16[128,2048]{0,1:T(8,128)(2,1)}, u32[]{:S(2)}, u32[]{:S(2)}) %collective-permute-start.14) | collective-permute-done | bytes 524320 | tf_op jit(solution)/shard_map/ppermute | solution.py:21
  55.2 3.2 collective-permute-start.15
  59.4 1.3 collective-permute-done.11
  60.8 1.5 collective-permute-start.2
  62.3 1.8 pad_maximum_fusion.4
  64.1 19.2 %collective-permute-done.13 = bf16[128,2048]{0,1:T(8,128)(2,1)} collective-permute-done((bf16[128,2048]{0,1:T(8,128)(2,1)}, bf16[128,2048]{0,1:T(8,128)(2,1)}, u32[]{:S(2)}, u32[]{:S(2)}) %collective-permute-start.13) | collective-permute-done | bytes 524320 | tf_op jit(solution)/shard_map/ppermute | solution.py:25
  83.2 22.5 %collective-permute-done.15 = bf16[128,2048]{0,1:T(8,128)(2,1)} collective-permute-done((bf16[128,2048]{0,1:T(8,128)(2,1)}, bf16[128,2048]{0,1:T(8,128)(2,1)}, u32[]{:S(2)}, u32[]{:S(2)}) %collective-permute-start.15) | collective-permute-done | bytes 524320 | tf_op jit(solution)/shard_map/ppermute | solution.py:25
  105.7 21.0 %collective-permute-done.17 = bf16[128,2048]{0,1:T(8,128)(2,1)} collective-permute-done((bf16[128,2048]{0,1:T(8,128)(2,1)}, bf16[128,2048]{0,1:T(8,128)(2,1)}, u32[]{:S(2)}, u32[]{:S(2)}) %collective-permute-start.17) | collective-permute-done | bytes 524320 | tf_op jit(solution)/shard_map/ppermute | solution.py:25
  126.8 1.8 pad_maximum_fusion.3
  134.5 2.4 collective-permute-start.3
  140.4 9.8 %collective-permute-done.1 = bf16[512,768]{1,0:T(8,128)(2,1)} collective-permute-done((bf16[512,768]{1,0:T(8,128)(2,1)S(1)}, bf16[512,768]{1,0:T(8,128)(2,1)}, u32[]{:S(2)}, u32[]{:S(2)}) %collective-permute-start.1) | collective-permute-done | bytes 786464 | tf_op jit(solution)/shard_map/ppermute | solution.py:21
  150.2 2.0 collective-permute-done.3
  152.2 19.1 %convolution_convert_fusion = bf16[2048,3072]{1,0:T(8,128)(2,1)} fusion(bf16[1024,2048]{0,1:T(8,128)(2,1)} %bitcast_dynamic-update-slice_fusion, bf16[1024,768]{1,0:T(8,128)(2,1)} %collective-permute-done.2, bf16[512,768]{1,0:T(8,128)(2,1)} %collective-permute-done.3, bf16[512,768]{1,0:T(8,128)(2,1)} %collective-permute-done.1, ...), kind=kOutput, calls=%fused_computation | convolution fusion | flops 12922650624 | bytes 23068672 | tf_op jit(solution)/shard_map/dot_general | solution.py:73
  172.0 7.2 %pad_maximum_fusion = bf16[1024,3072]{1,0:T(8,128)(2,1)} fusion(bf16[1024,768]{1,0:T(8,128)(2,1)} %collective-permute-done.2, bf16[512,768]{1,0:T(8,128)(2,1)} %collective-permute-done.3, bf16[512,768]{1,0:T(8,128)(2,1)} %collective-permute-done.1, bf16[1024,768]{1,0:T(8,128)(2,1)S(1)} %collective-permute-done, bf16[1024,768]{1,0:T(8,128)(2,1)S(1)} %bitcast_multiply_fusion), kind=kLoop, calls=%fused_computation.1 | loop fusion | flops 31457280 | bytes 12582912 | tf_op jit(solution)/shard_map/concatenate | solution.py:71
  179.2 7.4 %fusion.19 = bf16[1024,768]{1,0:T(8,128)(2,1)S(1)} fusion(bf16[1024,2048]{0,1:T(8,128)(2,1)} %bitcast_dynamic-update-slice_fusion, bf16[2048,3072]{1,0:T(8,128)(2,1)} %all-gather.2.cloned.1.call-done), kind=kOutput, calls=%fused_computation.21 | convolution fusion | flops 3222011904 | bytes 8912896 | tf_op jit(solution)/shard_map/dot_general | solution.py:85
  187.0 3.2 collective-permute-start.20
  190.2 9.8 %fusion.12 = bf16[512,2048]{1,0:T(8,128)(2,1)S(1)} fusion(bf16[2048,3072]{1,0:T(8,128)(2,1)} %all-gather.2.cloned.1.call-done, bf16[1024,3072]{1,0:T(8,128)(2,1)S(1)} %copy-done), kind=kOutput, calls=%fused_computation.16 | convolution fusion | flops 6443499520 | bytes 17825792 | tf_op jit(solution)/shard_map/dot_general | solution.py:111
  200.1 4.1 %collective-permute-start.7 = (bf16[512,2048]{1,0:T(8,128)(2,1)S(1)}, bf16[512,2048]{1,0:T(8,128)(2,1)}, u32[]{:S(2)}, u32[]{:S(2)}) collective-permute-start(bf16[512,2048]{1,0:T(8,128)(2,1)S(1)} %fusion.12), channel_id=1, source_target_pairs={{0,1},{1,0},{2,3},{3,2},{4,5},{5,4},{6,7},{7,6},{8,9},{9,8},{10,11... | collective-permute-start | bytes 6291464 | tf_op jit(solution)/shard_map/ppermute | solution.py:25
  204.1 6.5 %fusion.4 = f32[1024,768]{1,0:T(8,128)S(1)} fusion(bf16[1024,2048]{0,1:T(8,128)(2,1)} %bitcast_dynamic-update-slice_fusion, bf16[2048,3072]{1,0:T(8,128)(2,1)} %all-gather.2.cloned.1.call-done), kind=kOutput, calls=%fused_computation.7 | convolution fusion | flops 3221225472 | bytes 10485760 | tf_op jit(solution)/shard_map/dot_general | solution.py:85
  210.6 6.4 %fusion = f32[1024,768]{1,0:T(8,128)S(1)} fusion(bf16[1024,2048]{0,1:T(8,128)(2,1)} %bitcast_dynamic-update-slice_fusion, bf16[2048,3072]{1,0:T(8,128)(2,1)} %all-gather.2.cloned.1.call-done), kind=kOutput, calls=%fused_computation.3 | convolution fusion | flops 3221225472 | bytes 10485760 | tf_op jit(solution)/shard_map/dot_general | solution.py:85
  220.1 3.2 collective-permute-start.21
  223.3 72.4 %collective-permute-done.7 = bf16[512,2048]{1,0:T(8,128)(2,1)} collective-permute-done((bf16[512,2048]{1,0:T(8,128)(2,1)S(1)}, bf16[512,2048]{1,0:T(8,128)(2,1)}, u32[]{:S(2)}, u32[]{:S(2)}) %collective-permute-start.7) | collective-permute-done | bytes 2097184 | tf_op jit(solution)/shard_map/ppermute | solution.py:25
  295.7 10.9 %add_convert_fusion = bf16[512,2048]{1,0:T(8,128)(2,1)} fusion(bf16[512,2048]{1,0:T(8,128)(2,1)} %collective-permute-done.7, bf16[2048,3072]{1,0:T(8,128)(2,1)} %all-gather.2.cloned.1.call-done, bf16[1024,3072]{1,0:T(8,128)(2,1)S(1)} %copy-done), kind=kOutput, calls=%fused_computation.2 | convolution fusion | flops 6445596672 | bytes 19922944 | tf_op jit(solution)/shard_map/dot_general | solution.py:111
  306.7 1.7 constant_dynamic-slice_fusion.8
  308.6 1.9 collective-permute-start.8
  310.8 2.9 collective-permute-start.9
  313.9 1.5 collective-permute-start.10
  315.7 7.7 %multiply_convert_fusion = bf16[1024,768]{1,0:T(8,128)(2,1)S(1)} fusion(bf16[1024,768]{1,0:T(8,128)(2,1)} %collective-permute-done.21, bf16[1024,768]{1,0:T(8,128)(2,1)} %collective-permute-done.19, bf16[1024,2048]{0,1:T(8,128)(2,1)} %bitcast_dynamic-update-slice_fusion, bf16[2048,3072]{1,0:T(8,128)(2,1)} %all-gather.2.cloned.1.call-done, f32[768]{0:T(1024)S(1)} %fusion.28), kind=kOutput, calls=%fused_computation.15 | convolution fusion | flops 3225944064 | bytes 12061696 | tf_op jit(solution)/shard_map/dot_general | solution.py:85
  323.5 1.3 pad_maximum_fusion.8
  324.8 11.6 %collective-permute-done.9 = bf16[128,2048]{0,1:T(8,128)(2,1)} collective-permute-done((bf16[128,2048]{0,1:T(8,128)(2,1)S(1)}, bf16[128,2048]{0,1:T(8,128)(2,1)}, u32[]{:S(2)}, u32[]{:S(2)}) %collective-permute-start.9) | collective-permute-done | bytes 524320 | tf_op jit(solution)/shard_map/ppermute | solution.py:21
  336.5 1.5 pad_maximum_fusion.1
  338.0 2.0 slice_bitcast_fusion
  339.9 2.4 collective-permute-start.22
  342.3 1.5 collective-permute-start.23
  344.9 2.9 copy.18
  347.7 3.5 collective-permute-done.22
  351.7 3.0 collective-permute-done.24
  355.8 1.3 maximum_convert_fusion
  (68 shorter events, 25.6 us)
Async XLA Ops:
  7.2 172.0 %all-gather.2.cloned.1.call-start = ((), (), s32[]{:S(2)}) async-start(), calls=%async_computation.1 | async-start | bytes 13369344 | tf_op jit(solution)/shard_map/all_gather | solution.py:49
  8.6 9.1 %collective-permute-start.4 = (bf16[128,768]{1,0:T(8,128)(2,1)S(1)}, bf16[128,768]{1,0:T(8,128)(2,1)S(1)}, u32[]{:S(2)}, u32[]{:S(2)}) collective-permute-start(bf16[128,768]{1,0:T(8,128)(2,1)S(1)} %get-tuple-element.35), channel_id=1, source_target_pairs={{0,2},{1,3},{2,4},{3,5},{4,6},{5,7},{6,0},{7,1},{8,10},{9,11},{10,... | collective-permute-start | bytes 589832 | tf_op jit(solution)/shard_map/ppermute | solution.py:21
  10.7 12.4 %collective-permute-start.5 = (bf16[128,768]{1,0:T(8,128)(2,1)S(1)}, bf16[128,768]{1,0:T(8,128)(2,1)S(1)}, u32[]{:S(2)}, u32[]{:S(2)}) collective-permute-start(bf16[128,768]{1,0:T(8,128)(2,1)S(1)} %get-tuple-element.34), channel_id=1, source_target_pairs={{0,4},{1,5},{2,6},{3,7},{4,0},{5,1},{6,2},{7,3},{8,12},{9,13},{10,... | collective-permute-start | bytes 589832 | tf_op jit(solution)/shard_map/ppermute | solution.py:21
  14.2 8.8 %collective-permute-start.6 = (bf16[128,768]{1,0:T(8,128)(2,1)S(1)}, bf16[128,768]{1,0:T(8,128)(2,1)S(1)}, u32[]{:S(2)}, u32[]{:S(2)}) collective-permute-start(bf16[128,768]{1,0:T(8,128)(2,1)S(1)} %get-tuple-element.33), channel_id=1, source_target_pairs={{0,6},{1,7},{2,0},{3,1},{4,2},{5,3},{6,4},{7,5},{8,14},{9,15},{10,... | collective-permute-start | bytes 589832 | tf_op jit(solution)/shard_map/ppermute | solution.py:21
  24.1 313.9 %reduce-scatter.2.cloned.1.call-start = ((), (), s32[]{:S(2)}) async-start(), calls=%async_computation.2 | async-start | bytes 13369344 | tf_op jit(solution)/shard_map/reduce_scatter | solution.py:76
  27.5 9.0 %copy-start.2 = (s32[8]{0:T(128)S(1)}, s32[8]{0:T(128)}, u32[]{:S(2)}) copy-start(s32[8]{0:T(128)} %param.6) | copy-start | bytes 100
  27.5 9.7 %copy-start.1 = (bf16[1,1024,768]{2,1,0:T(8,128)(2,1)S(1)}, bf16[1,1024,768]{2,1,0:T(8,128)(2,1)}, u32[]{:S(2)}) copy-start(bf16[1,1024,768]{2,1,0:T(8,128)(2,1)} %param.4) | copy-start | bytes 4718596
  28.5 14.4 %collective-permute-start.12 = (bf16[128,2048]{0,1:T(8,128)(2,1)S(1)}, bf16[128,2048]{0,1:T(8,128)(2,1)}, u32[]{:S(2)}, u32[]{:S(2)}) collective-permute-start(bf16[128,2048]{0,1:T(8,128)(2,1)S(1)} %get-tuple-element.9), channel_id=1, source_target_pairs={{0,2},{1,3},{2,4},{3,5},{4,6},{5,7},{6,0},{7,1},{8,10},{9,11},{10,... | collective-permute-start | bytes 1572872 | tf_op jit(solution)/shard_map/ppermute | solution.py:21
  29.7 25.5 %collective-permute-start.14 = (bf16[128,2048]{0,1:T(8,128)(2,1)S(1)}, bf16[128,2048]{0,1:T(8,128)(2,1)}, u32[]{:S(2)}, u32[]{:S(2)}) collective-permute-start(bf16[128,2048]{0,1:T(8,128)(2,1)S(1)} %get-tuple-element.8), channel_id=1, source_target_pairs={{0,4},{1,5},{2,6},{3,7},{4,0},{5,1},{6,2},{7,3},{8,12},{9,13},{10,... | collective-permute-start | bytes 1572872 | tf_op jit(solution)/shard_map/ppermute | solution.py:21
  32.1 26.4 %collective-permute-start.16 = (bf16[128,2048]{0,1:T(8,128)(2,1)S(1)}, bf16[128,2048]{0,1:T(8,128)(2,1)}, u32[]{:S(2)}, u32[]{:S(2)}) collective-permute-start(bf16[128,2048]{0,1:T(8,128)(2,1)S(1)} %get-tuple-element.7), channel_id=1, source_target_pairs={{0,6},{1,7},{2,0},{3,1},{4,2},{5,3},{6,4},{7,5},{8,14},{9,15},{10,... | collective-permute-start | bytes 1572872 | tf_op jit(solution)/shard_map/ppermute | solution.py:21
  33.3 27.5 %collective-permute-start.11 = (bf16[128,2048]{0,1:T(8,128)(2,1)}, bf16[128,2048]{0,1:T(8,128)(2,1)}, u32[]{:S(2)}, u32[]{:S(2)}) collective-permute-start(bf16[128,2048]{0,1:T(8,128)(2,1)} %bitcast.24), channel_id=1, source_target_pairs={{0,1},{1,0},{2,3},{3,2},{4,5},{5,4},{6,7},{7,6},{8,9},{9,8},{10,11... | collective-permute-start | bytes 1572872 | tf_op jit(solution)/shard_map/ppermute | solution.py:25
  42.8 40.4 %collective-permute-start.13 = (bf16[128,2048]{0,1:T(8,128)(2,1)}, bf16[128,2048]{0,1:T(8,128)(2,1)}, u32[]{:S(2)}, u32[]{:S(2)}) collective-permute-start(bf16[128,2048]{0,1:T(8,128)(2,1)} %collective-permute-done.12), channel_id=1, source_target_pairs={{0,1},{1,0},{2,3},{3,2},{4,5},{5,4},{6,7},{7,6},{8,9},{9,8},{10,11... | collective-permute-start | bytes 1572872 | tf_op jit(solution)/shard_map/ppermute | solution.py:25
  55.2 50.5 %collective-permute-start.15 = (bf16[128,2048]{0,1:T(8,128)(2,1)}, bf16[128,2048]{0,1:T(8,128)(2,1)}, u32[]{:S(2)}, u32[]{:S(2)}) collective-permute-start(bf16[128,2048]{0,1:T(8,128)(2,1)} %collective-permute-done.14), channel_id=1, source_target_pairs={{0,1},{1,0},{2,3},{3,2},{4,5},{5,4},{6,7},{7,6},{8,9},{9,8},{10,11... | collective-permute-start | bytes 1572872 | tf_op jit(solution)/shard_map/ppermute | solution.py:25
  58.4 68.3 %collective-permute-start.17 = (bf16[128,2048]{0,1:T(8,128)(2,1)}, bf16[128,2048]{0,1:T(8,128)(2,1)}, u32[]{:S(2)}, u32[]{:S(2)}) collective-permute-start(bf16[128,2048]{0,1:T(8,128)(2,1)} %collective-permute-done.16), channel_id=1, source_target_pairs={{0,1},{1,0},{2,3},{3,2},{4,5},{5,4},{6,7},{7,6},{8,9},{9,8},{10,11... | collective-permute-start | bytes 1572872 | tf_op jit(solution)/shard_map/ppermute | solution.py:25
  59.0 73.1 %collective-permute-start = (bf16[1024,768]{1,0:T(8,128)(2,1)S(1)}, bf16[1024,768]{1,0:T(8,128)(2,1)S(1)}, u32[]{:S(2)}, u32[]{:S(2)}) collective-permute-start(bf16[1024,768]{1,0:T(8,128)(2,1)S(1)} %bitcast_multiply_fusion), channel_id=1, source_target_pairs={{0,2},{1,3},{2,4},{3,5},{4,6},{5,7},{6,0},{7,1},{8,10},{9,11},{10,... | collective-permute-start | bytes 4718600 | tf_op jit(solution)/shard_map/ppermute | solution.py:21
  60.8 72.5 %collective-permute-start.2 = (bf16[1024,768]{1,0:T(8,128)(2,1)S(1)}, bf16[1024,768]{1,0:T(8,128)(2,1)}, u32[]{:S(2)}, u32[]{:S(2)}) collective-permute-start(bf16[1024,768]{1,0:T(8,128)(2,1)S(1)} %bitcast_multiply_fusion), channel_id=1, source_target_pairs={{0,6},{1,7},{2,0},{3,1},{4,2},{5,3},{6,4},{7,5},{8,14},{9,15},{10,... | collective-permute-start | bytes 4718600 | tf_op jit(solution)/shard_map/ppermute | solution.py:21
  132.1 18.0 %collective-permute-start.1 = (bf16[512,768]{1,0:T(8,128)(2,1)S(1)}, bf16[512,768]{1,0:T(8,128)(2,1)}, u32[]{:S(2)}, u32[]{:S(2)}) collective-permute-start(bf16[512,768]{1,0:T(8,128)(2,1)S(1)} %slice.74), channel_id=1, source_target_pairs={{0,2},{1,3},{2,4},{3,5},{4,6},{5,7},{6,0},{7,1},{8,10},{9,11},{10,... | collective-permute-start | bytes 2359304 | tf_op jit(solution)/shard_map/ppermute | solution.py:21
  134.5 17.6 %collective-permute-start.3 = (bf16[512,768]{1,0:T(8,128)(2,1)S(1)}, bf16[512,768]{1,0:T(8,128)(2,1)}, u32[]{:S(2)}, u32[]{:S(2)}) collective-permute-start(bf16[512,768]{1,0:T(8,128)(2,1)S(1)} %slice.75), channel_id=1, source_target_pairs={{0,6},{1,7},{2,0},{3,1},{4,2},{5,3},{6,4},{7,5},{8,14},{9,15},{10,... | collective-permute-start | bytes 2359304 | tf_op jit(solution)/shard_map/ppermute | solution.py:21
  179.2 11.1 %copy-start = (bf16[1024,3072]{1,0:T(8,128)(2,1)S(1)}, bf16[1024,3072]{1,0:T(8,128)(2,1)}, u32[]{:S(2)}) copy-start(bf16[1024,3072]{1,0:T(8,128)(2,1)} %pad_maximum_fusion) | copy-start | bytes 18874372
  186.7 30.5 %collective-permute-start.18 = (bf16[512,768]{1,0:T(8,128)(2,1)S(1)}, bf16[512,768]{1,0:T(8,128)(2,1)S(1)}, u32[]{:S(2)}, u32[]{:S(2)}) collective-permute-start(bf16[512,768]{1,0:T(8,128)(2,1)S(1)} %get-tuple-element.20), channel_id=1, source_target_pairs={{0,2},{1,3},{2,4},{3,5},{4,6},{5,7},{6,0},{7,1},{8,10},{9,11},{10,... | collective-permute-start | bytes 2359304 | tf_op jit(solution)/shard_map/ppermute | solution.py:21
  187.0 31.7 %collective-permute-start.20 = (bf16[512,768]{1,0:T(8,128)(2,1)S(1)}, bf16[512,768]{1,0:T(8,128)(2,1)S(1)}, u32[]{:S(2)}, u32[]{:S(2)}) collective-permute-start(bf16[512,768]{1,0:T(8,128)(2,1)S(1)} %get-tuple-element.21), channel_id=1, source_target_pairs={{0,6},{1,7},{2,0},{3,1},{4,2},{5,3},{6,4},{7,5},{8,14},{9,15},{10,... | collective-permute-start | bytes 2359304 | tf_op jit(solution)/shard_map/ppermute | solution.py:21
  200.1 95.7 %collective-permute-start.7 = (bf16[512,2048]{1,0:T(8,128)(2,1)S(1)}, bf16[512,2048]{1,0:T(8,128)(2,1)}, u32[]{:S(2)}, u32[]{:S(2)}) collective-permute-start(bf16[512,2048]{1,0:T(8,128)(2,1)S(1)} %fusion.12), channel_id=1, source_target_pairs={{0,1},{1,0},{2,3},{3,2},{4,5},{5,4},{6,7},{7,6},{8,9},{9,8},{10,11... | collective-permute-start | bytes 6291464 | tf_op jit(solution)/shard_map/ppermute | solution.py:25
  218.6 97.0 %collective-permute-start.19 = (bf16[1024,768]{1,0:T(8,128)(2,1)}, bf16[1024,768]{1,0:T(8,128)(2,1)}, u32[]{:S(2)}, u32[]{:S(2)}) collective-permute-start(bf16[1024,768]{1,0:T(8,128)(2,1)} %pad_maximum_fusion.6), channel_id=1, source_target_pairs={{0,2},{1,3},{2,4},{3,5},{4,6},{5,7},{6,0},{7,1},{8,10},{9,11},{10,... | collective-permute-start | bytes 4718600 | tf_op jit(solution)/shard_map/ppermute | solution.py:21
  220.1 95.6 %collective-permute-start.21 = (bf16[1024,768]{1,0:T(8,128)(2,1)}, bf16[1024,768]{1,0:T(8,128)(2,1)}, u32[]{:S(2)}, u32[]{:S(2)}) collective-permute-start(bf16[1024,768]{1,0:T(8,128)(2,1)} %pad_maximum_fusion.7), channel_id=1, source_target_pairs={{0,6},{1,7},{2,0},{3,1},{4,2},{5,3},{6,4},{7,5},{8,14},{9,15},{10,... | collective-permute-start | bytes 4718600 | tf_op jit(solution)/shard_map/ppermute | solution.py:21
  308.6 16.2 %collective-permute-start.8 = (bf16[128,2048]{0,1:T(8,128)(2,1)S(1)}, bf16[128,2048]{0,1:T(8,128)(2,1)S(1)}, u32[]{:S(2)}, u32[]{:S(2)}) collective-permute-start(bf16[128,2048]{0,1:T(8,128)(2,1)S(1)} %bitcast.100), channel_id=1, source_target_pairs={{0,2},{1,3},{2,4},{3,5},{4,6},{5,7},{6,0},{7,1},{8,10},{9,11},{10,... | collective-permute-start | bytes 1572872 | tf_op jit(solution)/shard_map/ppermute | solution.py:21
  310.8 25.7 %collective-permute-start.9 = (bf16[128,2048]{0,1:T(8,128)(2,1)S(1)}, bf16[128,2048]{0,1:T(8,128)(2,1)}, u32[]{:S(2)}, u32[]{:S(2)}) collective-permute-start(bf16[128,2048]{0,1:T(8,128)(2,1)S(1)} %bitcast.101), channel_id=1, source_target_pairs={{0,4},{1,5},{2,6},{3,7},{4,0},{5,1},{6,2},{7,3},{8,12},{9,13},{10,... | collective-permute-start | bytes 1572872 | tf_op jit(solution)/shard_map/ppermute | solution.py:21
  313.9 22.5 %collective-permute-start.10 = (bf16[128,2048]{0,1:T(8,128)(2,1)S(1)}, bf16[128,2048]{0,1:T(8,128)(2,1)}, u32[]{:S(2)}, u32[]{:S(2)}) collective-permute-start(bf16[128,2048]{0,1:T(8,128)(2,1)S(1)} %bitcast.102), channel_id=1, source_target_pairs={{0,6},{1,7},{2,0},{3,1},{4,2},{5,3},{6,4},{7,5},{8,14},{9,15},{10,... | collective-permute-start | bytes 1572872 | tf_op jit(solution)/shard_map/ppermute | solution.py:21
  339.9 11.3 %collective-permute-start.22 = (bf16[128,768]{1,0:T(8,128)(2,1)}, bf16[128,768]{1,0:T(8,128)(2,1)S(1)}, u32[]{:S(2)}, u32[]{:S(2)}) collective-permute-start(bf16[128,768]{1,0:T(8,128)(2,1)} %get-tuple-element.31), channel_id=1, source_target_pairs={{0,6},{1,7},{2,0},{3,1},{4,2},{5,3},{6,4},{7,5},{8,14},{9,15},{10,... | collective-permute-start | bytes 589832 | tf_op jit(solution)/shard_map/ppermute | solution.py:21
  342.3 9.4 %collective-permute-start.23 = (bf16[128,768]{1,0:T(8,128)(2,1)S(1)}, bf16[128,768]{1,0:T(8,128)(2,1)S(1)}, u32[]{:S(2)}, u32[]{:S(2)}) collective-permute-start(bf16[128,768]{1,0:T(8,128)(2,1)S(1)} %get-tuple-element.30), channel_id=1, source_target_pairs={{0,4},{1,5},{2,6},{3,7},{4,0},{5,1},{6,2},{7,3},{8,12},{9,13},{10,... | collective-permute-start | bytes 589832 | tf_op jit(solution)/shard_map/ppermute | solution.py:21
  343.8 10.9 %collective-permute-start.24 = (bf16[128,768]{1,0:T(8,128)(2,1)S(1)}, bf16[128,768]{1,0:T(8,128)(2,1)}, u32[]{:S(2)}, u32[]{:S(2)}) collective-permute-start(bf16[128,768]{1,0:T(8,128)(2,1)S(1)} %get-tuple-element.29), channel_id=1, source_target_pairs={{0,2},{1,3},{2,4},{3,5},{4,6},{5,7},{6,0},{7,1},{8,10},{9,11},{10,... | collective-permute-start | bytes 589832 | tf_op jit(solution)/shard_map/ppermute | solution.py:21
Sparse Core Ops, SparseCore 0:
  24.2 117.3 all-gather.1
  171.4 83.7 reduce-scatter.1

commit v2 on v0

v2 whole, which is shorter than its diff:
```python
import jax
import jax.numpy as jnp
from jax import lax
from jax.experimental import pallas as pl
from jax.experimental.pallas import tpu as pltpu
from jax.sharding import PartitionSpec as P

HD = 128
NZ = 4
NH = 2
SWAP = [(t, t ^ 1) for t in range(NZ * NH)]
ANY = pl.BlockSpec(memory_space=pl.ANY)
SMEM = pl.BlockSpec(memory_space=pltpu.SMEM)
VMEM = pl.BlockSpec(memory_space=pltpu.VMEM)
LIMIT = 56 << 20


def ring(step):
    return [
        (z * NH + h, ((z + step) % NZ) * NH + h) for z in range(NZ) for h in range(NH)
    ]


def shift(value, step):
    return lax.ppermute(value, "tensor", ring(step))


def swap(value):
    return lax.ppermute(value, "tensor", SWAP)


def dot(a, b, dims):
    return lax.dot_general(a, b, (dims, ((), ())), preferred_element_type=jnp.float32)


def of(shape, dtype=jnp.bfloat16):
    return jax.ShapeDtypeStruct(shape, dtype)


def run(body, out, args, specs, after=(), grid=(), out_specs=VMEM, name=None, scratch=()):
    n, m = len(args), len(after)

    def kernel(*refs):
        body(*refs[:n], *refs[n + m :])

    return pl.pallas_call(
        kernel,
        out_shape=out,
        grid=grid,
        in_specs=list(specs) + [ANY] * m,
        out_specs=out_specs,
        scratch_shapes=list(scratch),
        name=name,
        cost_estimate=pl.CostEstimate(flops=1000, bytes_accessed=1000, transcendentals=0),
        compiler_params=pltpu.CompilerParams(vmem_limit_bytes=LIMIT),
    )(*args, *after)


def block(rows, start=0):
    return pl.ds(pl.multiple_of(start * rows, rows), rows)


def per_device(attn, w_out, counts, grad_out):
    rank = lax.axis_index("tensor")
    z, h = rank // NH, rank % NH
    s, width = attn.shape[1:]
    own_rows, d = grad_out.shape[1:]
    n_dp = d // w_out.shape[0]
    n_x = n_dp // 2
    piece = w_out.shape[0] // NZ
    feats = n_x * piece
    half = s // 2
    lanes = NZ * width
    y = lax.axis_index("dp") // n_x
    groups = [list(range(n_x)), list(range(n_x, n_dp))]
    pair = [(i, (i + n_x) % n_dp) for i in range(n_dp)]
    own = jnp.sum(
        jnp.where(jnp.arange(counts.shape[0], dtype=jnp.int32) == rank, counts, 0)
    )
    place = jnp.stack([z, h, y, own]).astype(jnp.int32)

    def split_w(place_ref, w_ref, *outs):
        for k in range(NZ):
            outs[k][...] = w_ref[block(piece, (place_ref[0] + k) % NZ), :]

    w_out4 = run(
        split_w, [of((piece, width))] * NZ, (place, w_out), [SMEM, VMEM],
        out_specs=[VMEM] * NZ, name="w_split",
    )
    w_near = [w_out4[0]] + [shift(w_out4[k], k) for k in range(1, NZ)]

    def split_g(place_ref, g_ref, *outs):
        for k in range(NZ):
            zk = (place_ref[0] + k) % NZ
            for i in range(2):
                first = ((place_ref[2] + i) % 2) * n_x
                for x in range(n_x):
                    outs[k][:, (i * n_x + x) * piece : (i * n_x + x + 1) * piece] = g_ref[
                        :, block(piece, (first + x) * NZ + zk)
                    ]

    g_out4 = run(
        split_g, [of((own_rows, 2 * feats))] * NZ, (place, grad_out[0]), [SMEM, VMEM],
        after=(w_out4[0],), out_specs=[VMEM] * NZ, name="g_split",
    )
    g_near = [g_out4[0]] + [shift(g_out4[k], k) for k in range(1, NZ)]

    def mask_body(place_ref, a_ref, *outs):
        slot = lax.broadcasted_iota(jnp.int32, (1, width), 1) // HD
        live = (slot < place_ref[3]).astype(jnp.float32).astype(jnp.bfloat16)
        for q in range(2):
            parity = (place_ref[1] + 1 + q) % NH
            for a in range(NZ):
                outs[q][a * own_rows : (a + 1) * own_rows, :] = (
                    a_ref[block(own_rows, a * NH + parity), :] * live
                )

    act = run(
        mask_body, [of((half, width))] * 2, (place, attn[0]), [SMEM, VMEM],
        after=(g_out4[0],), out_specs=[VMEM] * 2, name="mask",
    )
    left = [shift(act[0], 1), None]
    right = [None, shift(act[1], -1)]
    g_far = [swap(g) for g in g_near]

    def join_w(a, b, c, e, out_ref):
        for k, ref in enumerate((a, b, c, e)):
            out_ref[:, k * width : (k + 1) * width] = ref[...]

    w_own = run(
        join_w, of((piece, lanes)), w_near, [VMEM] * NZ, after=(act[0],), name="w_join"
    )

    def move(a_ref, out_ref):
        out_ref[...] = a_ref[...]

    w_pair = run(
        move, of((piece, lanes)), (lax.ppermute(w_own, "dp", pair),), [VMEM],
        after=(left[0], right[1], *g_near[1:], *g_far[:2]), name="w_move",
    )

    def gather(x):
        return lax.all_gather(x, "dp", axis=0, tiled=True, axis_index_groups=groups)

    w_all = [gather(w_own), gather(w_pair)]

    left[1] = shift(act[1], 1)
    right[0] = shift(act[0], -1)
    across = [shift(left[0], 1), shift(right[1], -1)]
    acts = [*act, *left, *across, *right]

    def join_g(place_ref, *refs):
        out_ref, sem = refs[2 * NZ], refs[2 * NZ + 1]
        copies = []
        for q in range(2):
            for k in range(NZ):
                row = q * NZ + (place_ref[0] + NZ - k) % NZ
                copies.append(
                    pltpu.make_async_copy(
                        refs[q * NZ + k], out_ref.at[block(own_rows, row), :], sem.at[q * NZ + k]
                    )
                )
        for copy in copies:
            copy.start()
        for copy in copies:
            copy.wait()

    cot = run(
        join_g, of((s, 2 * feats)), (place, *g_far, *g_near), [SMEM] + [ANY] * (2 * NZ),
        out_specs=ANY, name="g_join", scratch=[pltpu.SemaphoreType.DMA((2 * NZ,))],
    )

    tile = min(256, feats)
    steps = feats // tile

    def term_of(i, after):
        def body(g_ref, *refs):
            top, bottom, out_ref = g_ref[:half, :], g_ref[half:, :], refs[-1]
            for k in range(NZ):
                out_ref[:, k * width : (k + 1) * width] = (
                    dot(top, refs[2 * k][...], ((0,), (0,)))
                    + dot(bottom, refs[2 * k + 1][...], ((0,), (0,)))
                ).astype(jnp.bfloat16)

        return run(
            body, of((feats, lanes)), (cot, *acts),
            [pl.BlockSpec((s, tile), lambda j: (0, i * steps + j))] + [VMEM] * 8,
            after=after, grid=(steps,), out_specs=pl.BlockSpec((tile, lanes), lambda j: (j, 0)),
            name="term",
        )

    def project(i, after):
        def body(w_ref, *refs):
            for q in range(2):
                total = 0.0
                for k in range(NZ):
                    w = w_ref[:, k * width : (k + 1) * width]
                    total += dot(refs[2 * k + q][...], w, ((1,), (1,)))
                refs[8 + q][...] = total.astype(refs[8 + q].dtype)

        return run(
            body, [of((half, feats)), of((half, feats), jnp.float32)], (w_all[i], *acts),
            [pl.BlockSpec((tile, lanes), lambda j: (j, 0))] + [VMEM] * 8,
            after=after, grid=(steps,), out_specs=[pl.BlockSpec((half, tile), lambda j: (0, j))] * 2,
            name="project",
        )

    cols = width // 3 if width % 384 == 0 else width

    def rows_term(k, dtype, after, more=None, q=None):
        def body(g_ref, w_ref, v_ref, *refs):
            total = dot(g_ref[:, :feats], w_ref[...], ((1,), (0,)))
            total += dot(g_ref[:, feats:], v_ref[...], ((1,), (0,)))
            parts = [total[:half], total[half:]]
            if more is not None:
                parts[q] = parts[q] + refs[0][...].astype(jnp.float32)
            if len(outs) == 2:
                refs[-2][...] = parts[0].astype(dtype)
                refs[-1][...] = parts[1].astype(dtype)
            else:
                refs[-1][:half, :] = parts[0].astype(dtype)
                refs[-1][half:, :] = parts[1].astype(dtype)

        n = width // cols
        outs = [of((half, width), dtype)] * 2 if k else [of((s, width), dtype)]
        args = [cot, w_all[0], w_all[1]]
        column = pl.BlockSpec((feats, cols), lambda j: (0, k * n + j))
        specs = [VMEM, column, column]
        if more is not None:
            args.append(more)
            specs.append(pl.BlockSpec((half, cols), lambda j: (0, j)))
        got = run(
            body, outs, args, specs, after=after, grid=(n,),
            out_specs=[pl.BlockSpec((o.shape[0], cols), lambda j: (0, j)) for o in outs],
            name="rows_term",
        )
        return got if k else got[0]

    def scatter(x):
        return lax.psum_scatter(
            x, "dp", scatter_dimension=0, tiled=True, axis_index_groups=groups
        )

    term_pair = term_of(1, ())
    term_own = term_of(0, (term_pair,))
    far = rows_term(2, jnp.bfloat16, (term_own,))
    up = shift(far[0], 1)
    down = shift(far[1], -1)
    sent0, kept0 = project(0, (far[0],))
    got0 = swap(sent0)
    sent1, kept1 = project(1, (kept0,))
    got1 = swap(sent1)
    to_right = rows_term(3, jnp.bfloat16, (kept1,), up, 0)
    to_left = rows_term(1, jnp.bfloat16, (to_right[0],), down, 1)
    from_left = [shift(x, 1) for x in (to_right[1], to_right[0])][::-1]
    from_right = [shift(x, -1) for x in to_left]
    stay = rows_term(0, jnp.float32, (to_left[0],))
    term_pair = scatter(term_pair)
    term_own = scatter(term_own)

    def settle(place_ref, kept_ref, got_ref, *outs):
        for k in range(NZ):
            row = block(own_rows, (place_ref[0] + k) % NZ)
            outs[k][...] = (kept_ref[row, :] + got_ref[row, :].astype(jnp.float32)).astype(
                jnp.bfloat16
            )

    def spread(kept, got, after):
        outs = run(
            settle, [of((own_rows, feats))] * NZ, (place, kept, got), [SMEM, VMEM, VMEM],
            after=after, out_specs=[VMEM] * NZ, name="settle",
        )
        return [outs[0]] + [shift(outs[k], k) for k in range(1, NZ)], outs[0]

    quarters0, last = spread(kept0, got0, (stay, term_pair))
    term_pair = lax.ppermute(term_pair, "dp", pair)
    quarters1, last = spread(kept1, got1, (term_pair, last))

    def add_rows(place_ref, stay_ref, *refs):
        slot = lax.broadcasted_iota(jnp.int32, (1, width), 1) // HD
        live = (slot < place_ref[3]).astype(jnp.float32)
        for q in range(2):
            parity = (place_ref[1] + 1 + q) % NH
            for a in range(NZ):
                rows = slice(a * own_rows, (a + 1) * own_rows)
                total = (
                    stay_ref[q * half + a * own_rows : q * half + (a + 1) * own_rows, :]
                    + refs[q][rows, :].astype(jnp.float32)
                    + refs[2 + q][rows, :].astype(jnp.float32)
                )
                refs[4][block(own_rows, a * NH + parity), :] = (total * live).astype(
                    jnp.bfloat16
                )

    grad_rows = run(
        add_rows, of((s, width)), (place, stay, *from_left, *from_right), [SMEM] + [VMEM] * 5,
        after=(last,), name="add_rows",
    )

    def join_out(place_ref, *refs):
        out_ref = refs[-1]
        for i in range(2):
            first = ((place_ref[2] + i) % 2) * n_x
            for k in range(NZ):
                zk = (place_ref[0] + NZ - k) % NZ
                for x in range(n_x):
                    out_ref[:, block(piece, (first + x) * NZ + zk)] = refs[i * NZ + k][
                        :, x * piece : (x + 1) * piece
                    ]

    projected = run(
        join_out, of((own_rows, d)), (place, *quarters0, *quarters1),
        [SMEM] + [VMEM] * (2 * NZ), name="join_out",
    )

    def add_terms(a_ref, b_ref, *outs):
        for k in range(NZ):
            cols = slice(k * width, (k + 1) * width)
            outs[k][...] = (
                a_ref[:, cols].astype(jnp.float32) + b_ref[:, cols].astype(jnp.float32)
            ).astype(jnp.bfloat16)

    parts = run(
        add_terms, [of((piece, width))] * NZ, (term_own, term_pair), [VMEM] * 2,
        out_specs=[VMEM] * NZ, name="add_terms",
    )
    parts = [parts[0]] + [shift(parts[k], -k) for k in range(1, NZ)]

    def join_term(place_ref, *refs):
        for k in range(NZ):
            refs[-1][block(piece, (place_ref[0] + k) % NZ), :] = refs[k][...].astype(
                jnp.float32
            )

    grad_w = run(
        join_term, of((NZ * piece, width), jnp.float32), (place, *parts),
        [SMEM] + [VMEM] * NZ, name="join_term",
    )
    return (projected[None], grad_rows[None], grad_w)


def solution(mesh):
    placed = (P("dp", None, "tensor"), P("dp", "tensor"), P(), P("dp", "tensor", None))
    return jax.shard_map(
        per_device,
        mesh=mesh,
        in_specs=placed,
        out_specs=(P("dp", "tensor", None), P("dp", None, "tensor"), P("dp", "tensor")),
        check_vma=False,
    )
```

time: 556 us -> 410 us (0.74)
  waiting for transfers between devices: 474 us -> 90.1 us
  Pallas kernels: 0 us -> 237 us
  matrix products: 62.8 us -> 0 us
  starting transfers between devices: 0.34 us -> 59 us
    reduce_scatter x2, waiting for transfers between devices: 239 us -> 0.01 us  [scatter(): lax.psum_scatter(x, 'dp', scatter_dimension=0, tiled=True, axis_index_gro...]
    pallas_call x0 -> x20, Pallas kernels: none -> 237 us  [run(): pl.pallas_call(kernel, out_shape=out, grid=grid, in_specs=list(specs) + [...]
    all_gather x2, waiting for transfers between devices: 234 us -> 0.04 us  [gather(): return lax.all_gather(x, 'dp', axis=0, tiled=True, axis_index_groups=groups)]
    ppermute x0 -> x35, waiting for transfers between devices: none -> 90 us  [the longest x6 45.7 us: swap(): return lax.ppermute(value, 'tensor', SWAP)]
    dot_general x3 -> x0, matrix products: 62.8 us -> none  [the longest x1 22.2 us: per_device(): lax.dot_general(cot_full, masked, (((0,), (0,)), ((), ())), preferred_ele...]
    ppermute x0 -> x35, starting transfers between devices: none -> 58.7 us  [the longest x27 42 us: shift(): return lax.ppermute(value, 'tensor', ring(step))]
  transfers between devices with their start and end apart: 4 -> 39, of which waited for: 4 -> 11; matrix products, arithmetic and copies ran while one was open for 12% -> 0% of each run, Pallas kernels for 0% -> 56%
where the time goes in v2:
time: 410 us; the launch traced here: 409 us
  Pallas kernels  237 us (58%)
  waiting for transfers between devices  90.1 us (22%)
  starting transfers between devices  59 us (14%)
  between operations  14.1 us (3%)
  local copies, waits for them, and re-layouts  6.71 us (2%)
    pallas_call x20, Pallas kernels, run(): pl.pallas_call(kernel, out_shape=out, grid=grid, in_specs=list(specs) + [...  237 us
    ppermute x6, waiting for transfers between devices, swap(): return lax.ppermute(value, 'tensor', SWAP)  45.7 us
    ppermute x27, waiting for transfers between devices, shift(): return lax.ppermute(value, 'tensor', ring(step))  44.2 us
    ppermute x27, starting transfers between devices, shift(): return lax.ppermute(value, 'tensor', ring(step))  42 us
    ppermute x6, starting transfers between devices, swap(): return lax.ppermute(value, 'tensor', SWAP)  13.6 us
  transfers between devices with their start and end apart: 39, of which 11 were waited for; matrix products, arithmetic and copies ran while one was open for 0% of the time, Pallas kernels for 56%

profile of v2, /device:TPU:0, one launch (start us, length us, event | category | flops | bytes accessed | tf_op | source)
XLA Modules:
  0.0 409.2 jit_solution(172793871692360215)
XLA Ops:
  9.8 2.1 w_split.1
  11.9 2.0 collective-permute-start
  13.9 3.6 collective-permute-start.1
  18.5 3.5 g_split.1
  22.0 2.7 mask.1
  24.7 1.8 collective-permute-done.1.refs_2_
  27.3 2.1 w_join.1
  30.6 2.4 collective-permute-start.12
  35.1 2.5 collective-permute-start.6
  37.6 19.1 %collective-permute-done.10.refs_6_.refs_3_ = bf16[128,2048]{1,0:T(8,128)(2,1)S(1)} collective-permute-done((bf16[128,2048]{1,0:T(8,128)(2,1)S(1)}, bf16[128,2048]{1,0:T(8,128)(2,1)S(1)}, u32[]{:S(2)}, u32[]{:S(2)}) %collective-permute-start.10) | collective-permute-done | bytes 524320 | tf_op jit(solution)/shard_map/ppermute | solution.py:25
  56.7 1.6 collective-permute-start.16
  58.3 3.0 collective-permute-start.9
  61.9 22.7 %collective-permute-done.9.refs_1_.refs_6_ = bf16[128,2048]{1,0:T(8,128)(2,1)S(1)} collective-permute-done((bf16[128,2048]{1,0:T(8,128)(2,1)S(1)}, bf16[128,2048]{1,0:T(8,128)(2,1)S(1)}, u32[]{:S(2)}, u32[]{:S(2)}) %collective-permute-start.9) | collective-permute-done | bytes 524320 | tf_op jit(solution)/shard_map/ppermute | solution.py:29
  84.7 7.5 %collective-permute-done.11.refs_2_.refs_7_ = bf16[128,2048]{1,0:T(8,128)(2,1)S(1)} collective-permute-done((bf16[128,2048]{1,0:T(8,128)(2,1)S(1)}, bf16[128,2048]{1,0:T(8,128)(2,1)S(1)}, u32[]{:S(2)}, u32[]{:S(2)}) %collective-permute-start.11) | collective-permute-done | bytes 524320 | tf_op jit(solution)/shard_map/ppermute | solution.py:29
  93.0 2.1 w_move.1
  95.2 3.2 collective-permute-start.13
  98.4 3.2 collective-permute-start.8
  101.6 3.2 collective-permute-start.7
  104.9 6.4 %collective-permute-done.13.refs_3_ = bf16[128,2048]{1,0:T(8,128)(2,1)S(1)} collective-permute-done((bf16[128,2048]{1,0:T(8,128)(2,1)}, bf16[128,2048]{1,0:T(8,128)(2,1)S(1)}, u32[]{:S(2)}, u32[]{:S(2)}) %collective-permute-start.13) | collective-permute-done | bytes 524320 | tf_op jit(solution)/shard_map/ppermute | solution.py:29
  111.2 3.2 collective-permute-start.15
  114.4 7.7 %collective-permute-done.15.refs_4_ = bf16[128,2048]{1,0:T(8,128)(2,1)S(1)} collective-permute-done((bf16[128,2048]{1,0:T(8,128)(2,1)}, bf16[128,2048]{1,0:T(8,128)(2,1)S(1)}, u32[]{:S(2)}, u32[]{:S(2)}) %collective-permute-start.15) | collective-permute-done | bytes 524320 | tf_op jit(solution)/shard_map/ppermute | solution.py:29
  123.0 128.9 %g_join.1.refs_0_ = bf16[1024,2048]{1,0:T(8,128)(2,1)} custom-call(s32[4]{0:T(128)} %pad_add_fusion.refs_0_, bf16[128,2048]{1,0:T(8,128)(2,1)} %copy-done.13, bf16[128,2048]{1,0:T(8,128)(2,1)} %copy-done.14, bf16[128,2048]{1,0:T(8,128)(2,1)} %copy-done.18, bf16[128,2048]{1,0:T(8,128)(2,1)} %copy-done.19, ...), custom_call_target="tpu_custom_call" | custom-call | flops 1000 | bytes 1000 | tf_op jit(solution)/shard_map/g_join/pallas_call | solution.py:46
  254.2 11.6 %term.2.refs_9_ = bf16[1024,3072]{1,0:T(8,128)(2,1)} custom-call(bf16[1024,2048]{1,0:T(8,128)(2,1)} %g_join.1.refs_0_, bf16[512,768]{1,0:T(8,128)(2,1)} %get-tuple-element.40.refs_4_.refs_1_, bf16[512,768]{1,0:T(8,128)(2,1)} %get-tuple-element.41.refs_2_, bf16[512,768]{1,0:T(8,128)(2,1)} %copy-done.1, bf16[512,768]{1,0:T(8,128)(2,1)} %copy-done.4, ...), custom_call_target="tpu_custom_call" | custom-call | flops 1000 | bytes 1000 | tf_op jit(solution)/shard_map/term/pallas_call | solution.py:46
  266.1 11.5 %term.3.refs_3_ = bf16[1024,3072]{1,0:T(8,128)(2,1)} custom-call(bf16[1024,2048]{1,0:T(8,128)(2,1)} %g_join.1.refs_0_, bf16[512,768]{1,0:T(8,128)(2,1)} %get-tuple-element.40.refs_4_.refs_1_, bf16[512,768]{1,0:T(8,128)(2,1)} %get-tuple-element.41.refs_2_, bf16[512,768]{1,0:T(8,128)(2,1)} %copy-done.1, bf16[512,768]{1,0:T(8,128)(2,1)} %copy-done.4, ...), custom_call_target="tpu_custom_call" | custom-call | flops 1000 | bytes 1000 | tf_op jit(solution)/shard_map/term/pallas_call | solution.py:46
  277.7 7.2 %rows_term.4 = (bf16[512,768]{1,0:T(8,128)(2,1)}, bf16[512,768]{1,0:T(8,128)(2,1)}) custom-call(bf16[1024,2048]{1,0:T(8,128)(2,1)} %g_join.1.refs_0_, bf16[1024,3072]{1,0:T(8,128)(2,1)} %all-gather.3.cloned.1.call-done.refs_1_.refs_0_, bf16[1024,3072]{1,0:T(8,128)(2,1)} %all-gather.5.cloned.1.call-done.refs_2_.refs_0_, bf16[1024,3072]{1,0:T(8,128)(2,1)} %term.3.refs_3_), custom_call_target="tpu_custom_call" | custom-call | flops 1000 | bytes 1000 | tf_op jit(solution)/shard_map/rows_term/pallas_call | solution.py:46
  284.9 11.7 %project.2 = (bf16[512,1024]{1,0:T(8,128)(2,1)}, f32[512,1024]{1,0:T(8,128)}) custom-call(bf16[1024,3072]{1,0:T(8,128)(2,1)} %all-gather.3.cloned.1.call-done.refs_1_.refs_0_, bf16[512,768]{1,0:T(8,128)(2,1)} %get-tuple-element.40.refs_4_.refs_1_, bf16[512,768]{1,0:T(8,128)(2,1)} %get-tuple-element.41.refs_2_, bf16[512,768]{1,0:T(8,128)(2,1)} %copy-done.1, ...), custom_call_target="tpu_custom_call" | custom-call | flops 1000 | bytes 1000 | tf_op jit(solution)/shard_map/project/pallas_call | solution.py:46
  296.6 3.2 collective-permute-start.17
  299.8 11.7 %project.3 = (bf16[512,1024]{1,0:T(8,128)(2,1)}, f32[512,1024]{1,0:T(8,128)}) custom-call(bf16[1024,3072]{1,0:T(8,128)(2,1)} %all-gather.5.cloned.1.call-done.refs_2_.refs_0_, bf16[512,768]{1,0:T(8,128)(2,1)} %get-tuple-element.40.refs_4_.refs_1_, bf16[512,768]{1,0:T(8,128)(2,1)} %get-tuple-element.41.refs_2_, bf16[512,768]{1,0:T(8,128)(2,1)} %copy-done.1, ...), custom_call_target="tpu_custom_call" | custom-call | flops 1000 | bytes 1000 | tf_op jit(solution)/shard_map/project/pallas_call | solution.py:46
  311.8 3.2 collective-permute-start.18
  315.1 1.5 collective-permute-start.24
  316.6 8.7 %collective-permute-done.19.refs_3_ = bf16[512,768]{1,0:T(8,128)(2,1)} collective-permute-done((bf16[512,768]{1,0:T(8,128)(2,1)}, bf16[512,768]{1,0:T(8,128)(2,1)}, u32[]{:S(2)}, u32[]{:S(2)}) %collective-permute-start.19) | collective-permute-done | bytes 786464 | tf_op jit(solution)/shard_map/ppermute | solution.py:25
  325.3 7.6 %rows_term.5 = (bf16[512,768]{1,0:T(8,128)(2,1)}, bf16[512,768]{1,0:T(8,128)(2,1)}) custom-call(bf16[1024,2048]{1,0:T(8,128)(2,1)} %g_join.1.refs_0_, bf16[1024,3072]{1,0:T(8,128)(2,1)} %all-gather.3.cloned.1.call-done.refs_1_.refs_0_, bf16[1024,3072]{1,0:T(8,128)(2,1)} %all-gather.5.cloned.1.call-done.refs_2_.refs_0_, ...), custom_call_target="tpu_custom_call" | custom-call | flops 1000 | bytes 1000 | tf_op jit(solution)/shard_map/rows_term/pallas_call | solution.py:46
  332.9 7.6 %rows_term.6 = (bf16[512,768]{1,0:T(8,128)(2,1)}, bf16[512,768]{1,0:T(8,128)(2,1)}) custom-call(bf16[1024,2048]{1,0:T(8,128)(2,1)} %g_join.1.refs_0_, bf16[1024,3072]{1,0:T(8,128)(2,1)} %all-gather.3.cloned.1.call-done.refs_1_.refs_0_, bf16[1024,3072]{1,0:T(8,128)(2,1)} %all-gather.5.cloned.1.call-done.refs_2_.refs_0_, ...), custom_call_target="tpu_custom_call" | custom-call | flops 1000 | bytes 1000 | tf_op jit(solution)/shard_map/rows_term/pallas_call | solution.py:46
  340.6 2.0 collective-permute-start.28
  344.6 7.8 %rows_term.7.refs_3_.refs_1_ = f32[1024,768]{1,0:T(8,128)} custom-call(bf16[1024,2048]{1,0:T(8,128)(2,1)} %g_join.1.refs_0_, bf16[1024,3072]{1,0:T(8,128)(2,1)} %all-gather.3.cloned.1.call-done.refs_1_.refs_0_, bf16[1024,3072]{1,0:T(8,128)(2,1)} %all-gather.5.cloned.1.call-done.refs_2_.refs_0_, bf16[512,768]{1,0:T(8,128)(2,1)} %get-tuple-element.51.refs_3_), custom_call_target="tpu_custom_call" | custom-call | flops 1000 | bytes 1000 | tf_op jit(solution)/shard_map/rows_term/pallas_call | solution.py:46
  352.4 3.0 settle.2
  356.3 2.3 add_terms.1
  358.6 2.7 collective-permute-start.32
  361.3 10.6 %collective-permute-done.31.refs_5_ = bf16[512,768]{1,0:T(8,128)(2,1)} collective-permute-done((bf16[512,768]{1,0:T(8,128)(2,1)}, bf16[512,768]{1,0:T(8,128)(2,1)}, u32[]{:S(2)}, u32[]{:S(2)}) %collective-permute-start.31) | collective-permute-done | bytes 786464 | tf_op jit(solution)/shard_map/ppermute | solution.py:25
  371.9 3.4 collective-permute-start.34
  375.3 3.0 settle.3
  378.3 2.0 collective-permute-start.21
  381.5 1.5 collective-permute-start.22
  383.5 2.8 collective-permute-done.33.refs_3_
  386.3 3.7 collective-permute-start.26
  390.7 4.5 %add_rows.1 = bf16[1024,768]{1,0:T(8,128)(2,1)} custom-call(s32[4]{0:T(128)} %pad_add_fusion.refs_0_, f32[1024,768]{1,0:T(8,128)} %rows_term.7.refs_3_.refs_1_, bf16[512,768]{1,0:T(8,128)(2,1)} %collective-permute-done.28.refs_2_, bf16[512,768]{1,0:T(8,128)(2,1)} %collective-permute-done.29.refs_3_, bf16[512,768]{1,0:T(8,128)(2,1)} %collective-permute-done.30.refs_4_, ...), custom_call_target="tpu_custom_call" | custom-call | flops 1000 | bytes 1000 | tf_op jit(solution)/shard_map/add_rows/pallas_call | solution.py:46
  395.2 2.5 join_term.1
  399.4 3.3 join_out.1
  (128 shorter events, 19.9 us)
Async XLA Ops:
  7.2 270.5 %all-gather.3.cloned.1.call-start = ((), (), s32[]{:S(2)}) async-start(), calls=%async_computation.2 | async-start | bytes 7077888 | tf_op jit(solution)/shard_map/all_gather | solution.py:143
  11.9 12.8 %collective-permute-start = (bf16[128,768]{1,0:T(8,128)(2,1)}, bf16[128,768]{1,0:T(8,128)(2,1)S(1)}, u32[]{:S(2)}, u32[]{:S(2)}) collective-permute-start(bf16[128,768]{1,0:T(8,128)(2,1)} %get-tuple-element.36), channel_id=1, source_target_pairs={{0,2},{1,3},{2,4},{3,5},{4,6},{5,7},{6,0},{7,1},{8,10},{9,11},{10,... | collective-permute-start | bytes 589832 | tf_op jit(solution)/shard_map/ppermute | solution.py:25
  13.9 12.6 %collective-permute-start.1 = (bf16[128,768]{1,0:T(8,128)(2,1)}, bf16[128,768]{1,0:T(8,128)(2,1)S(1)}, u32[]{:S(2)}, u32[]{:S(2)}) collective-permute-start(bf16[128,768]{1,0:T(8,128)(2,1)} %get-tuple-element.37), channel_id=1, source_target_pairs={{0,4},{1,5},{2,6},{3,7},{4,0},{5,1},{6,2},{7,3},{8,12},{9,13},{10,... | collective-permute-start | bytes 589832 | tf_op jit(solution)/shard_map/ppermute | solution.py:25
  17.5 9.0 %collective-permute-start.2 = (bf16[128,768]{1,0:T(8,128)(2,1)}, bf16[128,768]{1,0:T(8,128)(2,1)S(1)}, u32[]{:S(2)}, u32[]{:S(2)}) collective-permute-start(bf16[128,768]{1,0:T(8,128)(2,1)} %get-tuple-element.38), channel_id=1, source_target_pairs={{0,6},{1,7},{2,0},{3,1},{4,2},{5,3},{6,4},{7,5},{8,14},{9,15},{10,... | collective-permute-start | bytes 589832 | tf_op jit(solution)/shard_map/ppermute | solution.py:25
  24.6 10.4 %copy-start.3 = (bf16[512,768]{1,0:T(8,128)(2,1)S(1)}, bf16[512,768]{1,0:T(8,128)(2,1)}, u32[]{:S(2)}) copy-start(bf16[512,768]{1,0:T(8,128)(2,1)} %get-tuple-element.41.refs_2_) | copy-start | bytes 2359300
  24.7 33.6 %copy-start.9 = (bf16[128,2048]{1,0:T(8,128)(2,1)S(1)}, bf16[128,2048]{1,0:T(8,128)(2,1)}, u32[]{:S(2)}) copy-start(bf16[128,2048]{1,0:T(8,128)(2,1)} %get-tuple-element.39.refs_2_.refs_5_) | copy-start | bytes 1572868
  29.5 248.2 %all-gather.5.cloned.1.call-start = ((), (), s32[]{:S(2)}) async-start(), calls=%async_computation.3 | async-start | bytes 7077888 | tf_op jit(solution)/shard_map/all_gather | solution.py:143
  29.5 27.2 %collective-permute-start.10 = (bf16[128,2048]{1,0:T(8,128)(2,1)S(1)}, bf16[128,2048]{1,0:T(8,128)(2,1)S(1)}, u32[]{:S(2)}, u32[]{:S(2)}) collective-permute-start(bf16[128,2048]{1,0:T(8,128)(2,1)S(1)} %copy-done.33), channel_id=1, source_target_pairs={{0,2},{1,3},{2,4},{3,5},{4,6},{5,7},{6,0},{7,1},{8,10},{9,11},{10,... | collective-permute-start | bytes 1572872 | tf_op jit(solution)/shard_map/ppermute | solution.py:25
  30.6 27.6 %collective-permute-start.12 = (bf16[128,2048]{1,0:T(8,128)(2,1)}, bf16[128,2048]{1,0:T(8,128)(2,1)S(1)}, u32[]{:S(2)}, u32[]{:S(2)}) collective-permute-start(bf16[128,2048]{1,0:T(8,128)(2,1)} %get-tuple-element.43), channel_id=1, source_target_pairs={{0,4},{1,5},{2,6},{3,7},{4,0},{5,1},{6,2},{7,3},{8,12},{9,13},{10,... | collective-permute-start | bytes 1572872 | tf_op jit(solution)/shard_map/ppermute | solution.py:25
  33.0 28.2 %collective-permute-start.14 = (bf16[128,2048]{1,0:T(8,128)(2,1)S(1)}, bf16[128,2048]{1,0:T(8,128)(2,1)S(1)}, u32[]{:S(2)}, u32[]{:S(2)}) collective-permute-start(bf16[128,2048]{1,0:T(8,128)(2,1)S(1)} %copy-done.32), channel_id=1, source_target_pairs={{0,6},{1,7},{2,0},{3,1},{4,2},{5,3},{6,4},{7,5},{8,14},{9,15},{10,... | collective-permute-start | bytes 1572872 | tf_op jit(solution)/shard_map/ppermute | solution.py:25
  34.4 50.3 %collective-permute-start.3 = (bf16[512,768]{1,0:T(8,128)(2,1)S(1)}, bf16[512,768]{1,0:T(8,128)(2,1)S(1)}, u32[]{:S(2)}, u32[]{:S(2)}) collective-permute-start(bf16[512,768]{1,0:T(8,128)(2,1)S(1)} %copy-done), channel_id=1, source_target_pairs={{0,2},{1,3},{2,4},{3,5},{4,6},{5,7},{6,0},{7,1},{8,10},{9,11},{10,... | collective-permute-start | bytes 2359304 | tf_op jit(solution)/shard_map/ppermute | solution.py:25
  35.1 49.6 %collective-permute-start.6 = (bf16[512,768]{1,0:T(8,128)(2,1)S(1)}, bf16[512,768]{1,0:T(8,128)(2,1)S(1)}, u32[]{:S(2)}, u32[]{:S(2)}) collective-permute-start(bf16[512,768]{1,0:T(8,128)(2,1)S(1)} %copy-done.3), channel_id=1, source_target_pairs={{0,6},{1,7},{2,0},{3,1},{4,2},{5,3},{6,4},{7,5},{8,14},{9,15},{10,... | collective-permute-start | bytes 2359304 | tf_op jit(solution)/shard_map/ppermute | solution.py:25
  56.7 35.5 %copy-start.10 = (bf16[128,2048]{1,0:T(8,128)(2,1)}, bf16[128,2048]{1,0:T(8,128)(2,1)S(1)}, u32[]{:S(2)}) copy-start(bf16[128,2048]{1,0:T(8,128)(2,1)S(1)} %collective-permute-done.10.refs_6_.refs_3_) | copy-start | bytes 1572868
  56.7 27.9 %collective-permute-start.16 = (bf16[128,3072]{1,0:T(8,128)(2,1)}, bf16[128,3072]{1,0:T(8,128)(2,1)S(1)}, u32[]{:S(2)}, u32[]{:S(2)}) collective-permute-start(bf16[128,3072]{1,0:T(8,128)(2,1)} %w_join.1), channel_id=1, source_target_pairs={{0,64},{8,72},{16,80},{24,88},{32,96},{40,104},{48,112},{56,120},{... | collective-permute-start | bytes 2359304 | tf_op jit(solution)/shard_map/ppermute | solution.py:138
  58.3 33.9 %copy-start.11 = (bf16[128,2048]{1,0:T(8,128)(2,1)}, bf16[128,2048]{1,0:T(8,128)(2,1)S(1)}, u32[]{:S(2)}) copy-start(bf16[128,2048]{1,0:T(8,128)(2,1)S(1)} %collective-permute-done.12.refs_7_.refs_4_) | copy-start | bytes 1572868
  58.3 26.3 %collective-permute-start.9 = (bf16[128,2048]{1,0:T(8,128)(2,1)S(1)}, bf16[128,2048]{1,0:T(8,128)(2,1)S(1)}, u32[]{:S(2)}, u32[]{:S(2)}) collective-permute-start(bf16[128,2048]{1,0:T(8,128)(2,1)S(1)} %copy-done.9), channel_id=1, source_target_pairs={{0,1},{1,0},{2,3},{3,2},{4,5},{5,4},{6,7},{7,6},{8,9},{9,8},{10,11... | collective-permute-start | bytes 1572872 | tf_op jit(solution)/shard_map/ppermute | solution.py:29
  61.3 30.9 %copy-start.12 = (bf16[128,2048]{1,0:T(8,128)(2,1)}, bf16[128,2048]{1,0:T(8,128)(2,1)S(1)}, u32[]{:S(2)}) copy-start(bf16[128,2048]{1,0:T(8,128)(2,1)S(1)} %collective-permute-done.14.refs_8_.refs_5_) | copy-start | bytes 1572868
  61.3 30.9 %collective-permute-start.11 = (bf16[128,2048]{1,0:T(8,128)(2,1)S(1)}, bf16[128,2048]{1,0:T(8,128)(2,1)S(1)}, u32[]{:S(2)}, u32[]{:S(2)}) collective-permute-start(bf16[128,2048]{1,0:T(8,128)(2,1)S(1)} %collective-permute-done.10.refs_6_.refs_3_), channel_id=1, source_target_pairs={{0,1},{1,0},{2,3},{3,2},{4,5},{5,4},{6,7},{7,6},{8,9},{9,8},{10,11... | collective-permute-start | bytes 1572872 | tf_op jit(solution)/shard_map/ppermute | solution.py:29
  95.1 219.9 %reduce-scatter.3.cloned.1.call-start = ((), (), s32[]{:S(2)}) async-start(), calls=%async_computation.4 | async-start | bytes 7077888 | tf_op jit(solution)/shard_map/reduce_scatter | solution.py:240
  95.2 16.1 %collective-permute-start.13 = (bf16[128,2048]{1,0:T(8,128)(2,1)}, bf16[128,2048]{1,0:T(8,128)(2,1)S(1)}, u32[]{:S(2)}, u32[]{:S(2)}) collective-permute-start(bf16[128,2048]{1,0:T(8,128)(2,1)} %copy-done.11), channel_id=1, source_target_pairs={{0,1},{1,0},{2,3},{3,2},{4,5},{5,4},{6,7},{7,6},{8,9},{9,8},{10,11... | collective-permute-start | bytes 1572872 | tf_op jit(solution)/shard_map/ppermute | solution.py:29
  98.4 153.5 %collective-permute-start.4 = (bf16[512,768]{1,0:T(8,128)(2,1)S(1)}, bf16[512,768]{1,0:T(8,128)(2,1)S(1)}, u32[]{:S(2)}, u32[]{:S(2)}) collective-permute-start(bf16[512,768]{1,0:T(8,128)(2,1)S(1)} %copy-done.3), channel_id=1, source_target_pairs={{0,2},{1,3},{2,4},{3,5},{4,6},{5,7},{6,0},{7,1},{8,10},{9,11},{10,... | collective-permute-start | bytes 2359304 | tf_op jit(solution)/shard_map/ppermute | solution.py:25
  98.4 153.5 %collective-permute-start.8 = (bf16[512,768]{1,0:T(8,128)(2,1)S(1)}, bf16[512,768]{1,0:T(8,128)(2,1)S(1)}, u32[]{:S(2)}, u32[]{:S(2)}) collective-permute-start(bf16[512,768]{1,0:T(8,128)(2,1)S(1)} %copy-done), channel_id=1, source_target_pairs={{0,6},{1,7},{2,0},{3,1},{4,2},{5,3},{6,4},{7,5},{8,14},{9,15},{10,... | collective-permute-start | bytes 2359304 | tf_op jit(solution)/shard_map/ppermute | solution.py:25
  101.6 150.3 %collective-permute-start.5 = (bf16[512,768]{1,0:T(8,128)(2,1)}, bf16[512,768]{1,0:T(8,128)(2,1)S(1)}, u32[]{:S(2)}, u32[]{:S(2)}) collective-permute-start(bf16[512,768]{1,0:T(8,128)(2,1)} %copy-done.1), channel_id=1, source_target_pairs={{0,2},{1,3},{2,4},{3,5},{4,6},{5,7},{6,0},{7,1},{8,10},{9,11},{10,... | collective-permute-start | bytes 2359304 | tf_op jit(solution)/shard_map/ppermute | solution.py:25
  101.6 150.3 %collective-permute-start.7 = (bf16[512,768]{1,0:T(8,128)(2,1)}, bf16[512,768]{1,0:T(8,128)(2,1)S(1)}, u32[]{:S(2)}, u32[]{:S(2)}) collective-permute-start(bf16[512,768]{1,0:T(8,128)(2,1)} %copy-done.2), channel_id=1, source_target_pairs={{0,6},{1,7},{2,0},{3,1},{4,2},{5,3},{6,4},{7,5},{8,14},{9,15},{10,... | collective-permute-start | bytes 2359304 | tf_op jit(solution)/shard_map/ppermute | solution.py:25
  111.2 10.9 %copy-start.18 = (bf16[128,2048]{1,0:T(8,128)(2,1)}, bf16[128,2048]{1,0:T(8,128)(2,1)S(1)}, u32[]{:S(2)}) copy-start(bf16[128,2048]{1,0:T(8,128)(2,1)S(1)} %collective-permute-done.13.refs_3_) | copy-start | bytes 1572868
  111.2 10.9 %collective-permute-start.15 = (bf16[128,2048]{1,0:T(8,128)(2,1)}, bf16[128,2048]{1,0:T(8,128)(2,1)S(1)}, u32[]{:S(2)}, u32[]{:S(2)}) collective-permute-start(bf16[128,2048]{1,0:T(8,128)(2,1)} %copy-done.12), channel_id=1, source_target_pairs={{0,1},{1,0},{2,3},{3,2},{4,5},{5,4},{6,7},{7,6},{8,9},{9,8},{10,11... | collective-permute-start | bytes 1572872 | tf_op jit(solution)/shard_map/ppermute | solution.py:29
  265.8 90.1 %reduce-scatter.5.cloned.1.call-start = ((), (), s32[]{:S(2)}) async-start(), calls=%async_computation.5 | async-start | bytes 7077888 | tf_op jit(solution)/shard_map/reduce_scatter | solution.py:240
  296.6 44.0 %collective-permute-start.17 = (bf16[512,1024]{1,0:T(8,128)(2,1)}, bf16[512,1024]{1,0:T(8,128)(2,1)S(1)}, u32[]{:S(2)}, u32[]{:S(2)}) collective-permute-start(bf16[512,1024]{1,0:T(8,128)(2,1)} %get-tuple-element.47), channel_id=1, source_target_pairs={{0,1},{1,0},{2,3},{3,2},{4,5},{5,4},{6,7},{7,6},{8,9},{9,8},{10,11... | collective-permute-start | bytes 3145736 | tf_op jit(solution)/shard_map/ppermute | solution.py:29
  311.4 32.6 %collective-permute-start.23 = (bf16[512,1024]{1,0:T(8,128)(2,1)}, bf16[512,1024]{1,0:T(8,128)(2,1)S(1)}, u32[]{:S(2)}, u32[]{:S(2)}) collective-permute-start(bf16[512,1024]{1,0:T(8,128)(2,1)} %get-tuple-element.56), channel_id=1, source_target_pairs={{0,1},{1,0},{2,3},{3,2},{4,5},{5,4},{6,7},{7,6},{8,9},{9,8},{10,11... | collective-permute-start | bytes 3145736 | tf_op jit(solution)/shard_map/ppermute | solution.py:29
  311.8 13.5 %collective-permute-start.19 = (bf16[512,768]{1,0:T(8,128)(2,1)}, bf16[512,768]{1,0:T(8,128)(2,1)}, u32[]{:S(2)}, u32[]{:S(2)}) collective-permute-start(bf16[512,768]{1,0:T(8,128)(2,1)} %get-tuple-element.45.refs_9_), channel_id=1, source_target_pairs={{0,2},{1,3},{2,4},{3,5},{4,6},{5,7},{6,0},{7,1},{8,10},{9,11},{10,... | collective-permute-start | bytes 2359304 | tf_op jit(solution)/shard_map/ppermute | solution.py:25
  311.8 21.1 %collective-permute-start.18 = (bf16[512,768]{1,0:T(8,128)(2,1)}, bf16[512,768]{1,0:T(8,128)(2,1)}, u32[]{:S(2)}, u32[]{:S(2)}) collective-permute-start(bf16[512,768]{1,0:T(8,128)(2,1)} %get-tuple-element.48), channel_id=1, source_target_pairs={{0,6},{1,7},{2,0},{3,1},{4,2},{5,3},{6,4},{7,5},{8,14},{9,15},{10,... | collective-permute-start | bytes 2359304 | tf_op jit(solution)/shard_map/ppermute | solution.py:25
  315.1 40.4 %collective-permute-start.24 = (bf16[128,3072]{1,0:T(8,128)(2,1)}, bf16[128,3072]{1,0:T(8,128)(2,1)S(1)}, u32[]{:S(2)}, u32[]{:S(2)}) collective-permute-start(bf16[128,3072]{1,0:T(8,128)(2,1)} %reduce-scatter.3.cloned.1.call-done.refs_4_), channel_id=1, source_target_pairs={{0,64},{8,72},{16,80},{24,88},{32,96},{40,104},{48,112},{56,120},{... | collective-permute-start | bytes 2359304 | tf_op jit(solution)/shard_map/ppermute | solution.py:276
  340.5 18.1 %collective-permute-start.30 = (bf16[512,768]{1,0:T(8,128)(2,1)}, bf16[512,768]{1,0:T(8,128)(2,1)}, u32[]{:S(2)}, u32[]{:S(2)}) collective-permute-start(bf16[512,768]{1,0:T(8,128)(2,1)} %get-tuple-element.51.refs_3_), channel_id=1, source_target_pairs={{0,6},{1,7},{2,0},{3,1},{4,2},{5,3},{6,4},{7,5},{8,14},{9,15},{10,... | collective-permute-start | bytes 2359304 | tf_op jit(solution)/shard_map/ppermute | solution.py:25
  340.5 31.3 %collective-permute-start.31 = (bf16[512,768]{1,0:T(8,128)(2,1)}, bf16[512,768]{1,0:T(8,128)(2,1)}, u32[]{:S(2)}, u32[]{:S(2)}) collective-permute-start(bf16[512,768]{1,0:T(8,128)(2,1)} %get-tuple-element.62), channel_id=1, source_target_pairs={{0,6},{1,7},{2,0},{3,1},{4,2},{5,3},{6,4},{7,5},{8,14},{9,15},{10,... | collective-permute-start | bytes 2359304 | tf_op jit(solution)/shard_map/ppermute | solution.py:25
  340.6 11.8 %copy-start.16 = (bf16[512,1024]{1,0:T(8,128)(2,1)}, bf16[512,1024]{1,0:T(8,128)(2,1)S(1)}, u32[]{:S(2)}) copy-start(bf16[512,1024]{1,0:T(8,128)(2,1)S(1)} %collective-permute-done.17.refs_2_) | copy-start | bytes 3145732
  340.6 31.3 %collective-permute-start.28 = (bf16[512,768]{1,0:T(8,128)(2,1)}, bf16[512,768]{1,0:T(8,128)(2,1)}, u32[]{:S(2)}, u32[]{:S(2)}) collective-permute-start(bf16[512,768]{1,0:T(8,128)(2,1)} %get-tuple-element.50.refs_4_), channel_id=1, source_target_pairs={{0,2},{1,3},{2,4},{3,5},{4,6},{5,7},{6,0},{7,1},{8,10},{9,11},{10,... | collective-permute-start | bytes 2359304 | tf_op jit(solution)/shard_map/ppermute | solution.py:25
  344.0 34.3 %collective-permute-start.29 = (bf16[512,768]{1,0:T(8,128)(2,1)}, bf16[512,768]{1,0:T(8,128)(2,1)}, u32[]{:S(2)}, u32[]{:S(2)}) collective-permute-start(bf16[512,768]{1,0:T(8,128)(2,1)} %get-tuple-element.61), channel_id=1, source_target_pairs={{0,2},{1,3},{2,4},{3,5},{4,6},{5,7},{6,0},{7,1},{8,10},{9,11},{10,... | collective-permute-start | bytes 2359304 | tf_op jit(solution)/shard_map/ppermute | solution.py:25
  355.4 26.1 %collective-permute-start.20 = (bf16[128,1024]{1,0:T(8,128)(2,1)}, bf16[128,1024]{1,0:T(8,128)(2,1)S(1)}, u32[]{:S(2)}, u32[]{:S(2)}) collective-permute-start(bf16[128,1024]{1,0:T(8,128)(2,1)} %get-tuple-element.53), channel_id=1, source_target_pairs={{0,2},{1,3},{2,4},{3,5},{4,6},{5,7},{6,0},{7,1},{8,10},{9,11},{10,... | collective-permute-start | bytes 786440 | tf_op jit(solution)/shard_map/ppermute | solution.py:25
  358.6 24.4 %collective-permute-start.32 = (bf16[128,768]{1,0:T(8,128)(2,1)}, bf16[128,768]{1,0:T(8,128)(2,1)S(1)}, u32[]{:S(2)}, u32[]{:S(2)}) collective-permute-start(bf16[128,768]{1,0:T(8,128)(2,1)} %get-tuple-element.64), channel_id=1, source_target_pairs={{0,6},{1,7},{2,0},{3,1},{4,2},{5,3},{6,4},{7,5},{8,14},{9,15},{10,... | collective-permute-start | bytes 589832 | tf_op jit(solution)/shard_map/ppermute | solution.py:25
  371.9 14.5 %collective-permute-start.33 = (bf16[128,768]{1,0:T(8,128)(2,1)}, bf16[128,768]{1,0:T(8,128)(2,1)S(1)}, u32[]{:S(2)}, u32[]{:S(2)}) collective-permute-start(bf16[128,768]{1,0:T(8,128)(2,1)} %get-tuple-element.65), channel_id=1, source_target_pairs={{0,4},{1,5},{2,6},{3,7},{4,0},{5,1},{6,2},{7,3},{8,12},{9,13},{10,... | collective-permute-start | bytes 589832 | tf_op jit(solution)/shard_map/ppermute | solution.py:25
  371.9 18.1 %collective-permute-start.34 = (bf16[128,768]{1,0:T(8,128)(2,1)}, bf16[128,768]{1,0:T(8,128)(2,1)S(1)}, u32[]{:S(2)}, u32[]{:S(2)}) collective-permute-start(bf16[128,768]{1,0:T(8,128)(2,1)} %get-tuple-element.66), channel_id=1, source_target_pairs={{0,2},{1,3},{2,4},{3,5},{4,6},{5,7},{6,0},{7,1},{8,10},{9,11},{10,... | collective-permute-start | bytes 589832 | tf_op jit(solution)/shard_map/ppermute | solution.py:25
  378.3 19.4 %collective-permute-start.21 = (bf16[128,1024]{1,0:T(8,128)(2,1)S(1)}, bf16[128,1024]{1,0:T(8,128)(2,1)S(1)}, u32[]{:S(2)}, u32[]{:S(2)}) collective-permute-start(bf16[128,1024]{1,0:T(8,128)(2,1)S(1)} %copy-done.35), channel_id=1, source_target_pairs={{0,4},{1,5},{2,6},{3,7},{4,0},{5,1},{6,2},{7,3},{8,12},{9,13},{10,... | collective-permute-start | bytes 786440 | tf_op jit(solution)/shard_map/ppermute | solution.py:25
  381.5 13.7 %copy-start.20 = (bf16[128,1024]{1,0:T(8,128)(2,1)}, bf16[128,1024]{1,0:T(8,128)(2,1)S(1)}, u32[]{:S(2)}) copy-start(bf16[128,1024]{1,0:T(8,128)(2,1)S(1)} %collective-permute-done.20.refs_2_) | copy-start | bytes 786436
  381.5 16.2 %collective-permute-start.22 = (bf16[128,1024]{1,0:T(8,128)(2,1)S(1)}, bf16[128,1024]{1,0:T(8,128)(2,1)S(1)}, u32[]{:S(2)}, u32[]{:S(2)}) collective-permute-start(bf16[128,1024]{1,0:T(8,128)(2,1)S(1)} %copy-done.34), channel_id=1, source_target_pairs={{0,6},{1,7},{2,0},{3,1},{4,2},{5,3},{6,4},{7,5},{8,14},{9,15},{10,... | collective-permute-start | bytes 786440 | tf_op jit(solution)/shard_map/ppermute | solution.py:25
  383.0 12.2 %copy-start.26 = (bf16[128,768]{1,0:T(8,128)(2,1)}, bf16[128,768]{1,0:T(8,128)(2,1)S(1)}, u32[]{:S(2)}) copy-start(bf16[128,768]{1,0:T(8,128)(2,1)S(1)} %collective-permute-done.32.refs_2_) | copy-start | bytes 589828
  383.0 14.7 %collective-permute-start.25 = (bf16[128,1024]{1,0:T(8,128)(2,1)}, bf16[128,1024]{1,0:T(8,128)(2,1)S(1)}, u32[]{:S(2)}, u32[]{:S(2)}) collective-permute-start(bf16[128,1024]{1,0:T(8,128)(2,1)} %get-tuple-element.58), channel_id=1, source_target_pairs={{0,2},{1,3},{2,4},{3,5},{4,6},{5,7},{6,0},{7,1},{8,10},{9,11},{10,... | collective-permute-start | bytes 786440 | tf_op jit(solution)/shard_map/ppermute | solution.py:25
  386.3 11.4 %collective-permute-start.26 = (bf16[128,1024]{1,0:T(8,128)(2,1)}, bf16[128,1024]{1,0:T(8,128)(2,1)S(1)}, u32[]{:S(2)}, u32[]{:S(2)}) collective-permute-start(bf16[128,1024]{1,0:T(8,128)(2,1)} %get-tuple-element.59), channel_id=1, source_target_pairs={{0,4},{1,5},{2,6},{3,7},{4,0},{5,1},{6,2},{7,3},{8,12},{9,13},{10,... | collective-permute-start | bytes 786440 | tf_op jit(solution)/shard_map/ppermute | solution.py:25
  390.0 7.8 %collective-permute-start.27 = (bf16[128,1024]{1,0:T(8,128)(2,1)}, bf16[128,1024]{1,0:T(8,128)(2,1)S(1)}, u32[]{:S(2)}, u32[]{:S(2)}) collective-permute-start(bf16[128,1024]{1,0:T(8,128)(2,1)} %get-tuple-element.60), channel_id=1, source_target_pairs={{0,6},{1,7},{2,0},{3,1},{4,2},{5,3},{6,4},{7,5},{8,14},{9,15},{10,... | collective-permute-start | bytes 786440 | tf_op jit(solution)/shard_map/ppermute | solution.py:25
  (27 other events, 99.2 us)
Sparse Core Ops, SparseCore 0:
  29.6 41.3 all-gather.2
  95.3 39.8 all-gather.4
  266.0 41.3 reduce-scatter.2
  309.6 42.4 reduce-scatter.4

commit v3 on v2

--- a/solution.py
+++ b/solution.py
@@ -12,7 +12,8 @@
 ANY = pl.BlockSpec(memory_space=pl.ANY)
 SMEM = pl.BlockSpec(memory_space=pltpu.SMEM)
 VMEM = pl.BlockSpec(memory_space=pltpu.VMEM)
-LIMIT = 56 << 20
+BIG = 48 << 20
+SMALL = 32 << 20
 
 
 def ring(step):
@@ -37,7 +38,7 @@
     return jax.ShapeDtypeStruct(shape, dtype)
 
 
-def run(body, out, args, specs, after=(), grid=(), out_specs=VMEM, name=None, scratch=()):
+def run(body, out, args, specs, after=(), grid=(), out_specs=VMEM, name=None, limit=SMALL):
     n, m = len(args), len(after)
 
     def kernel(*refs):
@@ -49,10 +50,9 @@
         grid=grid,
         in_specs=list(specs) + [ANY] * m,
         out_specs=out_specs,
-        scratch_shapes=list(scratch),
         name=name,
         cost_estimate=pl.CostEstimate(flops=1000, bytes_accessed=1000, transcendentals=0),
-        compiler_params=pltpu.CompilerParams(vmem_limit_bytes=LIMIT),
+        compiler_params=pltpu.CompilerParams(vmem_limit_bytes=limit),
     )(*args, *after)
 
 
@@ -74,10 +74,7 @@
     y = lax.axis_index("dp") // n_x
     groups = [list(range(n_x)), list(range(n_x, n_dp))]
     pair = [(i, (i + n_x) % n_dp) for i in range(n_dp)]
-    own = jnp.sum(
-        jnp.where(jnp.arange(counts.shape[0], dtype=jnp.int32) == rank, counts, 0)
-    )
-    place = jnp.stack([z, h, y, own]).astype(jnp.int32)
+    place = jnp.stack([z, h, y, rank]).astype(jnp.int32)
 
     def split_w(place_ref, w_ref, *outs):
         for k in range(NZ):
@@ -105,9 +102,9 @@
     )
     g_near = [g_out4[0]] + [shift(g_out4[k], k) for k in range(1, NZ)]
 
-    def mask_body(place_ref, a_ref, *outs):
+    def mask_body(place_ref, counts_ref, a_ref, *outs):
         slot = lax.broadcasted_iota(jnp.int32, (1, width), 1) // HD
-        live = (slot < place_ref[3]).astype(jnp.float32).astype(jnp.bfloat16)
+        live = (slot < counts_ref[place_ref[3]]).astype(jnp.float32).astype(jnp.bfloat16)
         for q in range(2):
             parity = (place_ref[1] + 1 + q) % NH
             for a in range(NZ):
@@ -116,7 +113,7 @@
                 )
 
     act = run(
-        mask_body, [of((half, width))] * 2, (place, attn[0]), [SMEM, VMEM],
+        mask_body, [of((half, width))] * 2, (place, counts, attn[0]), [SMEM, SMEM, VMEM],
         after=(g_out4[0],), out_specs=[VMEM] * 2, name="mask",
     )
     left = [shift(act[0], 1), None]
@@ -136,7 +133,7 @@
 
     w_pair = run(
         move, of((piece, lanes)), (lax.ppermute(w_own, "dp", pair),), [VMEM],
-        after=(left[0], right[1], *g_near[1:], *g_far[:2]), name="w_move",
+        after=(left[0], right[1], *g_near[1:], g_far[0]), name="w_move",
     )
 
     def gather(x):
@@ -150,24 +147,14 @@
     acts = [*act, *left, *across, *right]
 
     def join_g(place_ref, *refs):
-        out_ref, sem = refs[2 * NZ], refs[2 * NZ + 1]
-        copies = []
         for q in range(2):
             for k in range(NZ):
                 row = q * NZ + (place_ref[0] + NZ - k) % NZ
-                copies.append(
-                    pltpu.make_async_copy(
-                        refs[q * NZ + k], out_ref.at[block(own_rows, row), :], sem.at[q * NZ + k]
-                    )
-                )
-        for copy in copies:
-            copy.start()
-        for copy in copies:
-            copy.wait()
+                refs[-1][block(own_rows, row), :] = refs[q * NZ + k][...]
 
     cot = run(
-        join_g, of((s, 2 * feats)), (place, *g_far, *g_near), [SMEM] + [ANY] * (2 * NZ),
-        out_specs=ANY, name="g_join", scratch=[pltpu.SemaphoreType.DMA((2 * NZ,))],
+        join_g, of((s, 2 * feats)), (place, *g_far, *g_near), [SMEM] + [VMEM] * (2 * NZ),
+        name="g_join",
     )
 
     tile = min(256, feats)
@@ -186,7 +173,7 @@
             body, of((feats, lanes)), (cot, *acts),
             [pl.BlockSpec((s, tile), lambda j: (0, i * steps + j))] + [VMEM] * 8,
             after=after, grid=(steps,), out_specs=pl.BlockSpec((tile, lanes), lambda j: (j, 0)),
-            name="term",
+            name="term", limit=BIG,
         )
 
     def project(i, after):
@@ -202,7 +189,7 @@
             body, [of((half, feats)), of((half, feats), jnp.float32)], (w_all[i], *acts),
             [pl.BlockSpec((tile, lanes), lambda j: (j, 0))] + [VMEM] * 8,
             after=after, grid=(steps,), out_specs=[pl.BlockSpec((half, tile), lambda j: (0, j))] * 2,
-            name="project",
+            name="project", limit=BIG,
         )
 
     cols = width // 3 if width % 384 == 0 else width
@@ -232,7 +219,7 @@
         got = run(
             body, outs, args, specs, after=after, grid=(n,),
             out_specs=[pl.BlockSpec((o.shape[0], cols), lambda j: (0, j)) for o in outs],
-            name="rows_term",
+            name="rows_term", limit=BIG,
         )
         return got if k else got[0]
 
@@ -248,13 +235,13 @@
     down = shift(far[1], -1)
     sent0, kept0 = project(0, (far[0],))
     got0 = swap(sent0)
-    sent1, kept1 = project(1, (kept0,))
+    stay = rows_term(0, jnp.float32, (kept0,))
+    sent1, kept1 = project(1, (stay, up, down))
     got1 = swap(sent1)
     to_right = rows_term(3, jnp.bfloat16, (kept1,), up, 0)
     to_left = rows_term(1, jnp.bfloat16, (to_right[0],), down, 1)
     from_left = [shift(x, 1) for x in (to_right[1], to_right[0])][::-1]
     from_right = [shift(x, -1) for x in to_left]
-    stay = rows_term(0, jnp.float32, (to_left[0],))
     term_pair = scatter(term_pair)
     term_own = scatter(term_own)
 
@@ -272,13 +259,13 @@
         )
         return [outs[0]] + [shift(outs[k], k) for k in range(1, NZ)], outs[0]
 
-    quarters0, last = spread(kept0, got0, (stay, term_pair))
+    quarters0, last = spread(kept0, got0, (to_left[0], term_pair))
     term_pair = lax.ppermute(term_pair, "dp", pair)
     quarters1, last = spread(kept1, got1, (term_pair, last))
 
-    def add_rows(place_ref, stay_ref, *refs):
+    def add_rows(place_ref, counts_ref, stay_ref, *refs):
         slot = lax.broadcasted_iota(jnp.int32, (1, width), 1) // HD
-        live = (slot < place_ref[3]).astype(jnp.float32)
+        live = (slot < counts_ref[place_ref[3]]).astype(jnp.float32)
         for q in range(2):
             parity = (place_ref[1] + 1 + q) % NH
             for a in range(NZ):
@@ -293,7 +280,7 @@
                 )
 
     grad_rows = run(
-        add_rows, of((s, width)), (place, stay, *from_left, *from_right), [SMEM] + [VMEM] * 5,
+        add_rows, of((s, width)), (place, counts, stay, *from_left, *from_right), [SMEM] * 2 + [VMEM] * 5,
         after=(last,), name="add_rows",
     )
 

time: 410 us -> 299 us (0.73)
  Pallas kernels: 237 us -> 82.4 us
  local copies, waits for them, and re-layouts: 6.71 us -> 39.4 us
  waiting for transfers between devices: 90.1 us -> 104 us
    pallas_call x20, Pallas kernels: 237 us -> 82.4 us  [run(): pl.pallas_call(kernel, out_shape=out, grid=grid, in_specs=list(specs) + [...]
    unnamed x72 -> x98, local copies, waits for them, and re-layouts: 6.71 us -> 39.4 us
    ppermute x6, waiting for transfers between devices: 45.7 us -> 26.9 us  [swap(): return lax.ppermute(value, 'tensor', SWAP)]
    ppermute x27, waiting for transfers between devices: 44.2 us -> 62.5 us  [shift(): return lax.ppermute(value, 'tensor', ring(step))]
    ppermute x1, waiting for transfers between devices: 0.01 us -> 14.6 us  [per_device(): term_pair = lax.ppermute(term_pair, 'dp', pair)]
  transfers between devices with their start and end apart: 39 -> 39, of which waited for: 11 -> 14; matrix products, arithmetic and copies ran while one was open for 0% -> 0% of each run, Pallas kernels for 56% -> 26%
where the time goes in v3:
time: 299 us; the launch traced here: 297 us
  waiting for transfers between devices  104 us (35%)
  Pallas kernels  82.4 us (28%)
  starting transfers between devices  57.4 us (19%)
  local copies, waits for them, and re-layouts  39.4 us (13%)
  between operations  14.1 us (5%)
    pallas_call x20, Pallas kernels, run(): pl.pallas_call(kernel, out_shape=out, grid=grid, in_specs=list(specs) + [...  82.4 us
    ppermute x27, waiting for transfers between devices, shift(): return lax.ppermute(value, 'tensor', ring(step))  62.5 us
    ppermute x27, starting transfers between devices, shift(): return lax.ppermute(value, 'tensor', ring(step))  40.5 us
    unnamed x98, local copies, waits for them, and re-layouts  39.4 us
    ppermute x6, waiting for transfers between devices, swap(): return lax.ppermute(value, 'tensor', SWAP)  26.9 us
    ppermute x1, waiting for transfers between devices, per_device(): term_pair = lax.ppermute(term_pair, 'dp', pair)  14.6 us
    ppermute x6, starting transfers between devices, swap(): return lax.ppermute(value, 'tensor', SWAP)  13.3 us
  transfers between devices with their start and end apart: 39, of which 14 were waited for; matrix products, arithmetic and copies ran while one was open for 0% of the time, Pallas kernels for 26%

profile of v3, /device:TPU:0, one launch (start us, length us, event | category | flops | bytes accessed | tf_op | source)
XLA Modules:
  0.0 297.5 jit_solution(6055055641095558051)
XLA Ops:
  9.1 2.1 collective-permute-start
  11.1 3.6 %collective-permute-start.1 = (bf16[128,768]{1,0:T(8,128)(2,1)S(1)}, bf16[128,768]{1,0:T(8,128)(2,1)S(1)}, u32[]{:S(2)}, u32[]{:S(2)}) collective-permute-start(bf16[128,768]{1,0:T(8,128)(2,1)S(1)} %get-tuple-element.37), channel_id=1, source_target_pairs={{0,4},{1,5},{2,6},{3,7},{4,0},{5,1},{6,2},{7,3},{8,12},{9,13},{10,... | collective-permute-start | bytes 589832 | tf_op jit(solution)/shard_map/ppermute | solution.py:26
  15.7 1.6 copy-done.33
  17.3 2.1 g_split.1
  20.9 2.6 collective-permute-done.1.refs_2_
  25.9 2.4 collective-permute-start.12
  30.3 1.6 collective-permute-start.16
  31.9 19.9 %collective-permute-done.10.refs_6_.refs_3_ = bf16[128,2048]{1,0:T(8,128)(2,1)S(1)} collective-permute-done((bf16[128,2048]{1,0:T(8,128)(2,1)}, bf16[128,2048]{1,0:T(8,128)(2,1)S(1)}, u32[]{:S(2)}, u32[]{:S(2)}) %collective-permute-start.10) | collective-permute-done | bytes 524320 | tf_op jit(solution)/shard_map/ppermute | solution.py:26
  52.5 3.2 %collective-permute-start.9 = (bf16[128,2048]{1,0:T(8,128)(2,1)}, bf16[128,2048]{1,0:T(8,128)(2,1)S(1)}, u32[]{:S(2)}, u32[]{:S(2)}) collective-permute-start(bf16[128,2048]{1,0:T(8,128)(2,1)} %copy-done.34), channel_id=1, source_target_pairs={{0,1},{1,0},{2,3},{3,2},{4,5},{5,4},{6,7},{7,6},{8,9},{9,8},{10,11... | collective-permute-start | bytes 1572872 | tf_op jit(solution)/shard_map/ppermute | solution.py:30
  55.7 12.2 %collective-permute-done.14.refs_8_.refs_5_ = bf16[128,2048]{1,0:T(8,128)(2,1)S(1)} collective-permute-done((bf16[128,2048]{1,0:T(8,128)(2,1)}, bf16[128,2048]{1,0:T(8,128)(2,1)S(1)}, u32[]{:S(2)}, u32[]{:S(2)}) %collective-permute-start.14) | collective-permute-done | bytes 524320 | tf_op jit(solution)/shard_map/ppermute | solution.py:26
  72.3 3.3 %collective-permute-start.11 = (bf16[128,2048]{1,0:T(8,128)(2,1)}, bf16[128,2048]{1,0:T(8,128)(2,1)S(1)}, u32[]{:S(2)}, u32[]{:S(2)}) collective-permute-start(bf16[128,2048]{1,0:T(8,128)(2,1)} %copy-done.25), channel_id=1, source_target_pairs={{0,1},{1,0},{2,3},{3,2},{4,5},{5,4},{6,7},{7,6},{8,9},{9,8},{10,11... | collective-permute-start | bytes 1572872 | tf_op jit(solution)/shard_map/ppermute | solution.py:30
  77.2 1.9 collective-permute-start.8
  80.6 8.4 %collective-permute-done.11.refs_2_ = bf16[128,2048]{1,0:T(8,128)(2,1)S(1)} collective-permute-done((bf16[128,2048]{1,0:T(8,128)(2,1)}, bf16[128,2048]{1,0:T(8,128)(2,1)S(1)}, u32[]{:S(2)}, u32[]{:S(2)}) %collective-permute-start.11) | collective-permute-done | bytes 524320 | tf_op jit(solution)/shard_map/ppermute | solution.py:30
  90.2 8.0 %collective-permute-done.13.refs_3_ = bf16[128,2048]{1,0:T(8,128)(2,1)S(1)} collective-permute-done((bf16[128,2048]{1,0:T(8,128)(2,1)}, bf16[128,2048]{1,0:T(8,128)(2,1)S(1)}, u32[]{:S(2)}, u32[]{:S(2)}) %collective-permute-start.13) | collective-permute-done | bytes 524320 | tf_op jit(solution)/shard_map/ppermute | solution.py:30
  98.2 3.2 %collective-permute-start.15 = (bf16[128,2048]{1,0:T(8,128)(2,1)}, bf16[128,2048]{1,0:T(8,128)(2,1)S(1)}, u32[]{:S(2)}, u32[]{:S(2)}) collective-permute-start(bf16[128,2048]{1,0:T(8,128)(2,1)} %copy-done.29), channel_id=1, source_target_pairs={{0,1},{1,0},{2,3},{3,2},{4,5},{5,4},{6,7},{7,6},{8,9},{9,8},{10,11... | collective-permute-start | bytes 1572872 | tf_op jit(solution)/shard_map/ppermute | solution.py:30
  101.4 10.5 %collective-permute-done.15.refs_4_ = bf16[128,2048]{1,0:T(8,128)(2,1)S(1)} collective-permute-done((bf16[128,2048]{1,0:T(8,128)(2,1)}, bf16[128,2048]{1,0:T(8,128)(2,1)S(1)}, u32[]{:S(2)}, u32[]{:S(2)}) %collective-permute-start.15) | collective-permute-done | bytes 524320 | tf_op jit(solution)/shard_map/ppermute | solution.py:30
  118.0 2.1 copy-done
  120.1 9.9 %term.2.refs_9_ = bf16[1024,3072]{1,0:T(8,128)(2,1)} custom-call(bf16[1024,2048]{1,0:T(8,128)(2,1)} %copy-done, bf16[512,768]{1,0:T(8,128)(2,1)S(1)} %get-tuple-element.40.refs_4_.refs_1_, bf16[512,768]{1,0:T(8,128)(2,1)S(1)} %get-tuple-element.41.refs_2_, bf16[512,768]{1,0:T(8,128)(2,1)S(1)} %collective-permute-done.3.refs_1_.refs_3_, ...), custom_call_target="tpu_custom_call" | custom-call | flops 1000 | bytes 1000 | tf_op jit(solution)/shard_map/term/pallas_call | solution.py:47
  138.2 9.9 %term.3.refs_3_ = bf16[1024,3072]{1,0:T(8,128)(2,1)} custom-call(bf16[1024,2048]{1,0:T(8,128)(2,1)} %copy-done, bf16[512,768]{1,0:T(8,128)(2,1)S(1)} %get-tuple-element.40.refs_4_.refs_1_, bf16[512,768]{1,0:T(8,128)(2,1)S(1)} %get-tuple-element.41.refs_2_, bf16[512,768]{1,0:T(8,128)(2,1)S(1)} %collective-permute-done.3.refs_1_.refs_3_, ...), custom_call_target="tpu_custom_call" | custom-call | flops 1000 | bytes 1000 | tf_op jit(solution)/shard_map/term/pallas_call | solution.py:47
  148.1 2.2 copy-done.1
  150.3 5.3 %rows_term.4 = (bf16[512,768]{1,0:T(8,128)(2,1)S(1)}, bf16[512,768]{1,0:T(8,128)(2,1)S(1)}) custom-call(bf16[1024,2048]{1,0:T(8,128)(2,1)S(1)} %copy-done.1, bf16[1024,3072]{1,0:T(8,128)(2,1)} %all-gather.3.cloned.1.call-done.refs_1_.refs_0_, bf16[1024,3072]{1,0:T(8,128)(2,1)} %all-gather.5.cloned.1.call-done.refs_2_.refs_0_, bf16[1024,3072]{1,0:T(8,128)(2,1)} %term.3.refs_3_), custom_call_target="tpu_custom_call" | custom-call | flops 1000 | bytes 1000 | tf_op jit(solution)/shard_map/rows_term/pallas_call | solution.py:47
  155.6 4.8 %collective-permute-start.18 = (bf16[512,768]{1,0:T(8,128)(2,1)S(1)}, bf16[512,768]{1,0:T(8,128)(2,1)S(1)}, u32[]{:S(2)}, u32[]{:S(2)}) collective-permute-start(bf16[512,768]{1,0:T(8,128)(2,1)S(1)} %get-tuple-element.48), channel_id=1, source_target_pairs={{0,6},{1,7},{2,0},{3,1},{4,2},{5,3},{6,4},{7,5},{8,14},{9,15},{10,... | collective-permute-start | bytes 2359304 | tf_op jit(solution)/shard_map/ppermute | solution.py:26
  160.4 9.9 %project.2 = (bf16[512,1024]{1,0:T(8,128)(2,1)}, f32[512,1024]{1,0:T(8,128)}) custom-call(bf16[1024,3072]{1,0:T(8,128)(2,1)} %all-gather.3.cloned.1.call-done.refs_1_.refs_0_, bf16[512,768]{1,0:T(8,128)(2,1)S(1)} %get-tuple-element.40.refs_4_.refs_1_, bf16[512,768]{1,0:T(8,128)(2,1)S(1)} %get-tuple-element.41.refs_2_, ...), custom_call_target="tpu_custom_call" | custom-call | flops 1000 | bytes 1000 | tf_op jit(solution)/shard_map/project/pallas_call | solution.py:47
  170.3 3.3 %collective-permute-start.17 = (bf16[512,1024]{1,0:T(8,128)(2,1)}, bf16[512,1024]{1,0:T(8,128)(2,1)}, u32[]{:S(2)}, u32[]{:S(2)}) collective-permute-start(bf16[512,1024]{1,0:T(8,128)(2,1)} %get-tuple-element.47), channel_id=1, source_target_pairs={{0,1},{1,0},{2,3},{3,2},{4,5},{5,4},{6,7},{7,6},{8,9},{9,8},{10,11... | collective-permute-start | bytes 3145736 | tf_op jit(solution)/shard_map/ppermute | solution.py:30
  173.6 1.6 copy-done.18
  175.2 6.6 %rows_term.5.refs_9_.refs_2_ = f32[1024,768]{1,0:T(8,128)S(1)} custom-call(bf16[1024,2048]{1,0:T(8,128)(2,1)} %copy-done, bf16[1024,3072]{1,0:T(8,128)(2,1)} %all-gather.3.cloned.1.call-done.refs_1_.refs_0_, bf16[1024,3072]{1,0:T(8,128)(2,1)} %all-gather.5.cloned.1.call-done.refs_2_.refs_0_, f32[512,1024]{1,0:T(8,128)S(1)} %copy-done.18), custom_call_target="tpu_custom_call" | custom-call | flops 1000 | bytes 1000 | tf_op jit(solution)/shard_map/rows_term/pallas_call | solution.py:47
  181.9 1.6 copy-done.2
  185.3 10.0 %project.3 = (bf16[512,1024]{1,0:T(8,128)(2,1)}, f32[512,1024]{1,0:T(8,128)}) custom-call(bf16[1024,3072]{1,0:T(8,128)(2,1)} %all-gather.5.cloned.1.call-done.refs_2_.refs_0_, bf16[512,768]{1,0:T(8,128)(2,1)S(1)} %get-tuple-element.40.refs_4_.refs_1_, bf16[512,768]{1,0:T(8,128)(2,1)S(1)} %get-tuple-element.41.refs_2_, ...), custom_call_target="tpu_custom_call" | custom-call | flops 1000 | bytes 1000 | tf_op jit(solution)/shard_map/project/pallas_call | solution.py:47
  195.3 1.6 copy-done.16
  198.1 6.6 %rows_term.6 = (bf16[512,768]{1,0:T(8,128)(2,1)S(1)}, bf16[512,768]{1,0:T(8,128)(2,1)S(1)}) custom-call(bf16[1024,2048]{1,0:T(8,128)(2,1)} %copy-done, bf16[1024,3072]{1,0:T(8,128)(2,1)} %all-gather.3.cloned.1.call-done.refs_1_.refs_0_, bf16[1024,3072]{1,0:T(8,128)(2,1)} %all-gather.5.cloned.1.call-done.refs_2_.refs_0_, bf16[512,768]{1,0:T(8,128)(2,1)S(1)} %copy-done.23, ...), custom_call_target="tpu_custom_call" | custom-call | flops 1000 | bytes 1000 | tf_op jit(solution)/shard_map/rows_term/pallas_call | solution.py:47
  205.6 7.5 %rows_term.7 = (bf16[512,768]{1,0:T(8,128)(2,1)}, bf16[512,768]{1,0:T(8,128)(2,1)}) custom-call(bf16[1024,2048]{1,0:T(8,128)(2,1)} %copy-done, bf16[1024,3072]{1,0:T(8,128)(2,1)} %all-gather.3.cloned.1.call-done.refs_1_.refs_0_, bf16[1024,3072]{1,0:T(8,128)(2,1)} %all-gather.5.cloned.1.call-done.refs_2_.refs_0_, bf16[512,768]{1,0:T(8,128)(2,1)S(1)} %copy-done.21, ...), custom_call_target="tpu_custom_call" | custom-call | flops 1000 | bytes 1000 | tf_op jit(solution)/shard_map/rows_term/pallas_call | solution.py:47
  213.1 3.2 %collective-permute-start.31 = (bf16[512,768]{1,0:T(8,128)(2,1)}, bf16[512,768]{1,0:T(8,128)(2,1)}, u32[]{:S(2)}, u32[]{:S(2)}) collective-permute-start(bf16[512,768]{1,0:T(8,128)(2,1)} %get-tuple-element.62), channel_id=1, source_target_pairs={{0,6},{1,7},{2,0},{3,1},{4,2},{5,3},{6,4},{7,5},{8,14},{9,15},{10,... | collective-permute-start | bytes 2359304 | tf_op jit(solution)/shard_map/ppermute | solution.py:26
  216.4 1.8 collective-permute-start.24
  218.3 1.9 collective-permute-start.29
  220.2 14.4 %collective-permute-done.31.refs_6_ = bf16[512,768]{1,0:T(8,128)(2,1)} collective-permute-done((bf16[512,768]{1,0:T(8,128)(2,1)}, bf16[512,768]{1,0:T(8,128)(2,1)}, u32[]{:S(2)}, u32[]{:S(2)}) %collective-permute-start.31) | collective-permute-done | bytes 786464 | tf_op jit(solution)/shard_map/ppermute | solution.py:26
  234.7 1.6 copy-done.19
  237.4 2.1 settle.2
  240.9 14.6 %collective-permute-done.24.refs_3_.refs_1_ = bf16[128,3072]{1,0:T(8,128)(2,1)S(1)} collective-permute-done((bf16[128,3072]{1,0:T(8,128)(2,1)}, bf16[128,3072]{1,0:T(8,128)(2,1)S(1)}, u32[]{:S(2)}, u32[]{:S(2)}) %collective-permute-start.24) | collective-permute-done | bytes 786464 | tf_op jit(solution)/shard_map/ppermute | solution.py:263
  256.8 3.3 %collective-permute-start.32 = (bf16[128,768]{1,0:T(8,128)(2,1)S(1)}, bf16[128,768]{1,0:T(8,128)(2,1)S(1)}, u32[]{:S(2)}, u32[]{:S(2)}) collective-permute-start(bf16[128,768]{1,0:T(8,128)(2,1)S(1)} %get-tuple-element.64), channel_id=1, source_target_pairs={{0,6},{1,7},{2,0},{3,1},{4,2},{5,3},{6,4},{7,5},{8,14},{9,15},{10,... | collective-permute-start | bytes 589832 | tf_op jit(solution)/shard_map/ppermute | solution.py:26
  261.1 1.6 settle.3
  262.7 2.7 collective-permute-start.21
  265.3 7.2 %collective-permute-done.20.refs_2_ = bf16[128,1024]{1,0:T(8,128)(2,1)S(1)} collective-permute-done((bf16[128,1024]{1,0:T(8,128)(2,1)}, bf16[128,1024]{1,0:T(8,128)(2,1)S(1)}, u32[]{:S(2)}, u32[]{:S(2)}) %collective-permute-start.20) | collective-permute-done | bytes 262176 | tf_op jit(solution)/shard_map/ppermute | solution.py:26
  272.6 2.6 collective-permute-done.32.refs_2_
  275.2 5.3 %collective-permute-start.26 = (bf16[128,1024]{1,0:T(8,128)(2,1)S(1)}, bf16[128,1024]{1,0:T(8,128)(2,1)S(1)}, u32[]{:S(2)}, u32[]{:S(2)}) collective-permute-start(bf16[128,1024]{1,0:T(8,128)(2,1)S(1)} %get-tuple-element.59), channel_id=1, source_target_pairs={{0,4},{1,5},{2,6},{3,7},{4,0},{5,1},{6,2},{7,3},{8,12},{9,13},{10,... | collective-permute-start | bytes 786440 | tf_op jit(solution)/shard_map/ppermute | solution.py:26
  280.5 1.7 collective-permute-done.34.refs_4_
  282.2 3.6 %add_rows.1 = bf16[1024,768]{1,0:T(8,128)(2,1)} custom-call(s32[4]{0:T(128)S(1)} %pad_add_fusion.refs_0_, s32[8]{0:T(128)S(1)} %copy-done.42, f32[1024,768]{1,0:T(8,128)S(1)} %copy-done.3, bf16[512,768]{1,0:T(8,128)(2,1)} %collective-permute-done.28.refs_3_, bf16[512,768]{1,0:T(8,128)(2,1)} %collective-permute-done.29.refs_4_, ...), custom_call_target="tpu_custom_call" | custom-call | flops 1000 | bytes 1000 | tf_op jit(solution)/shard_map/add_rows/pallas_call | solution.py:47
  285.8 1.8 join_term.1
  288.6 2.3 join_out.1
  (153 shorter events, 42.1 us)
Async XLA Ops:
  7.2 12.2 %copy-start.42 = (s32[8]{0:T(128)S(1)}, s32[8]{0:T(128)}, u32[]{:S(2)}) copy-start(s32[8]{0:T(128)} %refs_1_.5) | copy-start | bytes 100
  7.2 140.9 %all-gather.3.cloned.1.call-start = ((), (), s32[]{:S(2)}) async-start(), calls=%async_computation.2 | async-start | bytes 7077888 | tf_op jit(solution)/shard_map/all_gather | solution.py:140
  9.1 11.9 %collective-permute-start = (bf16[128,768]{1,0:T(8,128)(2,1)S(1)}, bf16[128,768]{1,0:T(8,128)(2,1)S(1)}, u32[]{:S(2)}, u32[]{:S(2)}) collective-permute-start(bf16[128,768]{1,0:T(8,128)(2,1)S(1)} %get-tuple-element.36), channel_id=1, source_target_pairs={{0,2},{1,3},{2,4},{3,5},{4,6},{5,7},{6,0},{7,1},{8,10},{9,11},{10,... | collective-permute-start | bytes 589832 | tf_op jit(solution)/shard_map/ppermute | solution.py:26
  11.1 12.4 %collective-permute-start.1 = (bf16[128,768]{1,0:T(8,128)(2,1)S(1)}, bf16[128,768]{1,0:T(8,128)(2,1)S(1)}, u32[]{:S(2)}, u32[]{:S(2)}) collective-permute-start(bf16[128,768]{1,0:T(8,128)(2,1)S(1)} %get-tuple-element.37), channel_id=1, source_target_pairs={{0,4},{1,5},{2,6},{3,7},{4,0},{5,1},{6,2},{7,3},{8,12},{9,13},{10,... | collective-permute-start | bytes 589832 | tf_op jit(solution)/shard_map/ppermute | solution.py:26
  14.7 8.8 %collective-permute-start.2 = (bf16[128,768]{1,0:T(8,128)(2,1)S(1)}, bf16[128,768]{1,0:T(8,128)(2,1)S(1)}, u32[]{:S(2)}, u32[]{:S(2)}) collective-permute-start(bf16[128,768]{1,0:T(8,128)(2,1)S(1)} %get-tuple-element.38), channel_id=1, source_target_pairs={{0,6},{1,7},{2,0},{3,1},{4,2},{5,3},{6,4},{7,5},{8,14},{9,15},{10,... | collective-permute-start | bytes 589832 | tf_op jit(solution)/shard_map/ppermute | solution.py:26
  24.5 123.6 %all-gather.5.cloned.1.call-start = ((), (), s32[]{:S(2)}) async-start(), calls=%async_computation.3 | async-start | bytes 7077888 | tf_op jit(solution)/shard_map/all_gather | solution.py:140
  24.6 27.2 %collective-permute-start.10 = (bf16[128,2048]{1,0:T(8,128)(2,1)}, bf16[128,2048]{1,0:T(8,128)(2,1)S(1)}, u32[]{:S(2)}, u32[]{:S(2)}) collective-permute-start(bf16[128,2048]{1,0:T(8,128)(2,1)} %get-tuple-element.42), channel_id=1, source_target_pairs={{0,2},{1,3},{2,4},{3,5},{4,6},{5,7},{6,0},{7,1},{8,10},{9,11},{10,... | collective-permute-start | bytes 1572872 | tf_op jit(solution)/shard_map/ppermute | solution.py:26
  25.9 26.6 %collective-permute-start.12 = (bf16[128,2048]{1,0:T(8,128)(2,1)}, bf16[128,2048]{1,0:T(8,128)(2,1)S(1)}, u32[]{:S(2)}, u32[]{:S(2)}) collective-permute-start(bf16[128,2048]{1,0:T(8,128)(2,1)} %get-tuple-element.43), channel_id=1, source_target_pairs={{0,4},{1,5},{2,6},{3,7},{4,0},{5,1},{6,2},{7,3},{8,12},{9,13},{10,... | collective-permute-start | bytes 1572872 | tf_op jit(solution)/shard_map/ppermute | solution.py:26
  28.3 39.6 %collective-permute-start.6 = (bf16[512,768]{1,0:T(8,128)(2,1)S(1)}, bf16[512,768]{1,0:T(8,128)(2,1)S(1)}, u32[]{:S(2)}, u32[]{:S(2)}) collective-permute-start(bf16[512,768]{1,0:T(8,128)(2,1)S(1)} %get-tuple-element.41.refs_2_), channel_id=1, source_target_pairs={{0,6},{1,7},{2,0},{3,1},{4,2},{5,3},{6,4},{7,5},{8,14},{9,15},{10,... | collective-permute-start | bytes 2359304 | tf_op jit(solution)/shard_map/ppermute | solution.py:26
  29.5 38.4 %collective-permute-start.3 = (bf16[512,768]{1,0:T(8,128)(2,1)S(1)}, bf16[512,768]{1,0:T(8,128)(2,1)S(1)}, u32[]{:S(2)}, u32[]{:S(2)}) collective-permute-start(bf16[512,768]{1,0:T(8,128)(2,1)S(1)} %get-tuple-element.40.refs_4_.refs_1_), channel_id=1, source_target_pairs={{0,2},{1,3},{2,4},{3,5},{4,6},{5,7},{6,0},{7,1},{8,10},{9,11},{10,... | collective-permute-start | bytes 2359304 | tf_op jit(solution)/shard_map/ppermute | solution.py:26
  30.3 37.6 %collective-permute-start.16 = (bf16[128,3072]{1,0:T(8,128)(2,1)}, bf16[128,3072]{1,0:T(8,128)(2,1)S(1)}, u32[]{:S(2)}, u32[]{:S(2)}) collective-permute-start(bf16[128,3072]{1,0:T(8,128)(2,1)} %w_join.1), channel_id=1, source_target_pairs={{0,64},{8,72},{16,80},{24,88},{32,96},{40,104},{48,112},{56,120},{... | collective-permute-start | bytes 2359304 | tf_op jit(solution)/shard_map/ppermute | solution.py:135
  51.8 16.1 %collective-permute-start.14 = (bf16[128,2048]{1,0:T(8,128)(2,1)}, bf16[128,2048]{1,0:T(8,128)(2,1)S(1)}, u32[]{:S(2)}, u32[]{:S(2)}) collective-permute-start(bf16[128,2048]{1,0:T(8,128)(2,1)} %copy-done.44), channel_id=1, source_target_pairs={{0,6},{1,7},{2,0},{3,1},{4,2},{5,3},{6,4},{7,5},{8,14},{9,15},{10,... | collective-permute-start | bytes 1572872 | tf_op jit(solution)/shard_map/ppermute | solution.py:26
  52.5 15.4 %collective-permute-start.9 = (bf16[128,2048]{1,0:T(8,128)(2,1)}, bf16[128,2048]{1,0:T(8,128)(2,1)S(1)}, u32[]{:S(2)}, u32[]{:S(2)}) collective-permute-start(bf16[128,2048]{1,0:T(8,128)(2,1)} %copy-done.34), channel_id=1, source_target_pairs={{0,1},{1,0},{2,3},{3,2},{4,5},{5,4},{6,7},{7,6},{8,9},{9,8},{10,11... | collective-permute-start | bytes 1572872 | tf_op jit(solution)/shard_map/ppermute | solution.py:30
  67.9 11.3 %copy-start.4 = (bf16[512,768]{1,0:T(8,128)(2,1)}, bf16[512,768]{1,0:T(8,128)(2,1)S(1)}, u32[]{:S(2)}) copy-start(bf16[512,768]{1,0:T(8,128)(2,1)S(1)} %collective-permute-done.6.refs_2_.refs_8_) | copy-start | bytes 2359300
  72.3 144.1 %reduce-scatter.3.cloned.1.call-start = ((), (), s32[]{:S(2)}) async-start(), calls=%async_computation.4 | async-start | bytes 7077888 | tf_op jit(solution)/shard_map/reduce_scatter | solution.py:227
  72.3 16.7 %collective-permute-start.11 = (bf16[128,2048]{1,0:T(8,128)(2,1)}, bf16[128,2048]{1,0:T(8,128)(2,1)S(1)}, u32[]{:S(2)}, u32[]{:S(2)}) collective-permute-start(bf16[128,2048]{1,0:T(8,128)(2,1)} %copy-done.25), channel_id=1, source_target_pairs={{0,1},{1,0},{2,3},{3,2},{4,5},{5,4},{6,7},{7,6},{8,9},{9,8},{10,11... | collective-permute-start | bytes 1572872 | tf_op jit(solution)/shard_map/ppermute | solution.py:30
  75.6 22.6 %collective-permute-start.13 = (bf16[128,2048]{1,0:T(8,128)(2,1)}, bf16[128,2048]{1,0:T(8,128)(2,1)S(1)}, u32[]{:S(2)}, u32[]{:S(2)}) collective-permute-start(bf16[128,2048]{1,0:T(8,128)(2,1)} %copy-done.27), channel_id=1, source_target_pairs={{0,1},{1,0},{2,3},{3,2},{4,5},{5,4},{6,7},{7,6},{8,9},{9,8},{10,11... | collective-permute-start | bytes 1572872 | tf_op jit(solution)/shard_map/ppermute | solution.py:30
  76.0 44.2 %collective-permute-start.4 = (bf16[512,768]{1,0:T(8,128)(2,1)S(1)}, bf16[512,768]{1,0:T(8,128)(2,1)S(1)}, u32[]{:S(2)}, u32[]{:S(2)}) collective-permute-start(bf16[512,768]{1,0:T(8,128)(2,1)S(1)} %get-tuple-element.41.refs_2_), channel_id=1, source_target_pairs={{0,2},{1,3},{2,4},{3,5},{4,6},{5,7},{6,0},{7,1},{8,10},{9,11},{10,... | collective-permute-start | bytes 2359304 | tf_op jit(solution)/shard_map/ppermute | solution.py:26
  77.2 42.9 %collective-permute-start.8 = (bf16[512,768]{1,0:T(8,128)(2,1)S(1)}, bf16[512,768]{1,0:T(8,128)(2,1)S(1)}, u32[]{:S(2)}, u32[]{:S(2)}) collective-permute-start(bf16[512,768]{1,0:T(8,128)(2,1)S(1)} %get-tuple-element.40.refs_4_.refs_1_), channel_id=1, source_target_pairs={{0,6},{1,7},{2,0},{3,1},{4,2},{5,3},{6,4},{7,5},{8,14},{9,15},{10,... | collective-permute-start | bytes 2359304 | tf_op jit(solution)/shard_map/ppermute | solution.py:26
  79.2 40.9 %collective-permute-start.7 = (bf16[512,768]{1,0:T(8,128)(2,1)S(1)}, bf16[512,768]{1,0:T(8,128)(2,1)S(1)}, u32[]{:S(2)}, u32[]{:S(2)}) collective-permute-start(bf16[512,768]{1,0:T(8,128)(2,1)S(1)} %collective-permute-done.6.refs_2_.refs_8_), channel_id=1, source_target_pairs={{0,6},{1,7},{2,0},{3,1},{4,2},{5,3},{6,4},{7,5},{8,14},{9,15},{10,... | collective-permute-start | bytes 2359304 | tf_op jit(solution)/shard_map/ppermute | solution.py:26
  89.0 31.1 %collective-permute-start.5 = (bf16[512,768]{1,0:T(8,128)(2,1)S(1)}, bf16[512,768]{1,0:T(8,128)(2,1)S(1)}, u32[]{:S(2)}, u32[]{:S(2)}) collective-permute-start(bf16[512,768]{1,0:T(8,128)(2,1)S(1)} %collective-permute-done.3.refs_1_.refs_3_), channel_id=1, source_target_pairs={{0,2},{1,3},{2,4},{3,5},{4,6},{5,7},{6,0},{7,1},{8,10},{9,11},{10,... | collective-permute-start | bytes 2359304 | tf_op jit(solution)/shard_map/ppermute | solution.py:26
  98.2 13.7 %collective-permute-start.15 = (bf16[128,2048]{1,0:T(8,128)(2,1)}, bf16[128,2048]{1,0:T(8,128)(2,1)S(1)}, u32[]{:S(2)}, u32[]{:S(2)}) collective-permute-start(bf16[128,2048]{1,0:T(8,128)(2,1)} %copy-done.29), channel_id=1, source_target_pairs={{0,1},{1,0},{2,3},{3,2},{4,5},{5,4},{6,7},{7,6},{8,9},{9,8},{10,11... | collective-permute-start | bytes 1572872 | tf_op jit(solution)/shard_map/ppermute | solution.py:30
  133.7 121.8 %reduce-scatter.5.cloned.1.call-start = ((), (), s32[]{:S(2)}) async-start(), calls=%async_computation.5 | async-start | bytes 7077888 | tf_op jit(solution)/shard_map/reduce_scatter | solution.py:227
  150.3 10.1 %copy-start.9 = (bf16[512,768]{1,0:T(8,128)(2,1)S(1)}, bf16[512,768]{1,0:T(8,128)(2,1)}, u32[]{:S(2)}) copy-start(bf16[512,768]{1,0:T(8,128)(2,1)} %copy-done.7) | copy-start | bytes 2359300
  150.3 10.1 %copy-start.12 = (bf16[512,768]{1,0:T(8,128)(2,1)S(1)}, bf16[512,768]{1,0:T(8,128)(2,1)}, u32[]{:S(2)}) copy-start(bf16[512,768]{1,0:T(8,128)(2,1)} %copy-done.10) | copy-start | bytes 2359300
  150.3 10.1 %copy-start.15 = (bf16[512,768]{1,0:T(8,128)(2,1)S(1)}, bf16[512,768]{1,0:T(8,128)(2,1)}, u32[]{:S(2)}) copy-start(bf16[512,768]{1,0:T(8,128)(2,1)} %copy-done.13) | copy-start | bytes 2359300
  155.6 27.9 %collective-permute-start.18 = (bf16[512,768]{1,0:T(8,128)(2,1)S(1)}, bf16[512,768]{1,0:T(8,128)(2,1)S(1)}, u32[]{:S(2)}, u32[]{:S(2)}) collective-permute-start(bf16[512,768]{1,0:T(8,128)(2,1)S(1)} %get-tuple-element.48), channel_id=1, source_target_pairs={{0,6},{1,7},{2,0},{3,1},{4,2},{5,3},{6,4},{7,5},{8,14},{9,15},{10,... | collective-permute-start | bytes 2359304 | tf_op jit(solution)/shard_map/ppermute | solution.py:26
  160.4 23.1 %collective-permute-start.19 = (bf16[512,768]{1,0:T(8,128)(2,1)S(1)}, bf16[512,768]{1,0:T(8,128)(2,1)S(1)}, u32[]{:S(2)}, u32[]{:S(2)}) collective-permute-start(bf16[512,768]{1,0:T(8,128)(2,1)S(1)} %get-tuple-element.45.refs_9_), channel_id=1, source_target_pairs={{0,2},{1,3},{2,4},{3,5},{4,6},{5,7},{6,0},{7,1},{8,10},{9,11},{10,... | collective-permute-start | bytes 2359304 | tf_op jit(solution)/shard_map/ppermute | solution.py:26
  170.3 47.9 %collective-permute-start.17 = (bf16[512,1024]{1,0:T(8,128)(2,1)}, bf16[512,1024]{1,0:T(8,128)(2,1)}, u32[]{:S(2)}, u32[]{:S(2)}) collective-permute-start(bf16[512,1024]{1,0:T(8,128)(2,1)} %get-tuple-element.47), channel_id=1, source_target_pairs={{0,1},{1,0},{2,3},{3,2},{4,5},{5,4},{6,7},{7,6},{8,9},{9,8},{10,11... | collective-permute-start | bytes 3145736 | tf_op jit(solution)/shard_map/ppermute | solution.py:30
  198.1 7.5 %copy-start.21 = (bf16[512,768]{1,0:T(8,128)(2,1)S(1)}, bf16[512,768]{1,0:T(8,128)(2,1)}, u32[]{:S(2)}) copy-start(bf16[512,768]{1,0:T(8,128)(2,1)} %copy-done.20) | copy-start | bytes 2359300
  213.1 21.5 %collective-permute-start.31 = (bf16[512,768]{1,0:T(8,128)(2,1)}, bf16[512,768]{1,0:T(8,128)(2,1)}, u32[]{:S(2)}, u32[]{:S(2)}) collective-permute-start(bf16[512,768]{1,0:T(8,128)(2,1)} %get-tuple-element.62), channel_id=1, source_target_pairs={{0,6},{1,7},{2,0},{3,1},{4,2},{5,3},{6,4},{7,5},{8,14},{9,15},{10,... | collective-permute-start | bytes 2359304 | tf_op jit(solution)/shard_map/ppermute | solution.py:26
  216.4 43.7 %collective-permute-start.23 = (bf16[512,1024]{1,0:T(8,128)(2,1)}, bf16[512,1024]{1,0:T(8,128)(2,1)}, u32[]{:S(2)}, u32[]{:S(2)}) collective-permute-start(bf16[512,1024]{1,0:T(8,128)(2,1)} %get-tuple-element.56), channel_id=1, source_target_pairs={{0,1},{1,0},{2,3},{3,2},{4,5},{5,4},{6,7},{7,6},{8,9},{9,8},{10,11... | collective-permute-start | bytes 3145736 | tf_op jit(solution)/shard_map/ppermute | solution.py:30
  216.4 39.1 %collective-permute-start.24 = (bf16[128,3072]{1,0:T(8,128)(2,1)}, bf16[128,3072]{1,0:T(8,128)(2,1)S(1)}, u32[]{:S(2)}, u32[]{:S(2)}) collective-permute-start(bf16[128,3072]{1,0:T(8,128)(2,1)} %reduce-scatter.3.cloned.1.call-done.refs_4_), channel_id=1, source_target_pairs={{0,64},{8,72},{16,80},{24,88},{32,96},{40,104},{48,112},{56,120},{... | collective-permute-start | bytes 2359304 | tf_op jit(solution)/shard_map/ppermute | solution.py:263
  218.2 38.6 %collective-permute-start.30 = (bf16[512,768]{1,0:T(8,128)(2,1)}, bf16[512,768]{1,0:T(8,128)(2,1)}, u32[]{:S(2)}, u32[]{:S(2)}) collective-permute-start(bf16[512,768]{1,0:T(8,128)(2,1)} %get-tuple-element.51.refs_3_), channel_id=1, source_target_pairs={{0,6},{1,7},{2,0},{3,1},{4,2},{5,3},{6,4},{7,5},{8,14},{9,15},{10,... | collective-permute-start | bytes 2359304 | tf_op jit(solution)/shard_map/ppermute | solution.py:26
  218.3 42.8 %copy-start.17 = (f32[512,1024]{1,0:T(8,128)S(1)}, f32[512,1024]{1,0:T(8,128)}, u32[]{:S(2)}) copy-start(f32[512,1024]{1,0:T(8,128)} %get-tuple-element.49.refs_4_.refs_1_) | copy-start | bytes 6291460
  218.3 41.8 %collective-permute-start.29 = (bf16[512,768]{1,0:T(8,128)(2,1)}, bf16[512,768]{1,0:T(8,128)(2,1)}, u32[]{:S(2)}, u32[]{:S(2)}) collective-permute-start(bf16[512,768]{1,0:T(8,128)(2,1)} %copy-done.43), channel_id=1, source_target_pairs={{0,2},{1,3},{2,4},{3,5},{4,6},{5,7},{6,0},{7,1},{8,10},{9,11},{10,... | collective-permute-start | bytes 2359304 | tf_op jit(solution)/shard_map/ppermute | solution.py:26
  234.7 28.0 %collective-permute-start.28 = (bf16[512,768]{1,0:T(8,128)(2,1)}, bf16[512,768]{1,0:T(8,128)(2,1)}, u32[]{:S(2)}, u32[]{:S(2)}) collective-permute-start(bf16[512,768]{1,0:T(8,128)(2,1)} %copy-done.37), channel_id=1, source_target_pairs={{0,2},{1,3},{2,4},{3,5},{4,6},{5,7},{6,0},{7,1},{8,10},{9,11},{10,... | collective-permute-start | bytes 2359304 | tf_op jit(solution)/shard_map/ppermute | solution.py:26
  255.5 17.1 %collective-permute-start.20 = (bf16[128,1024]{1,0:T(8,128)(2,1)}, bf16[128,1024]{1,0:T(8,128)(2,1)S(1)}, u32[]{:S(2)}, u32[]{:S(2)}) collective-permute-start(bf16[128,1024]{1,0:T(8,128)(2,1)} %get-tuple-element.53), channel_id=1, source_target_pairs={{0,2},{1,3},{2,4},{3,5},{4,6},{5,7},{6,0},{7,1},{8,10},{9,11},{10,... | collective-permute-start | bytes 786440 | tf_op jit(solution)/shard_map/ppermute | solution.py:26
  256.8 18.4 %collective-permute-start.32 = (bf16[128,768]{1,0:T(8,128)(2,1)S(1)}, bf16[128,768]{1,0:T(8,128)(2,1)S(1)}, u32[]{:S(2)}, u32[]{:S(2)}) collective-permute-start(bf16[128,768]{1,0:T(8,128)(2,1)S(1)} %get-tuple-element.64), channel_id=1, source_target_pairs={{0,6},{1,7},{2,0},{3,1},{4,2},{5,3},{6,4},{7,5},{8,14},{9,15},{10,... | collective-permute-start | bytes 589832 | tf_op jit(solution)/shard_map/ppermute | solution.py:26
  260.1 15.1 %collective-permute-start.33 = (bf16[128,768]{1,0:T(8,128)(2,1)S(1)}, bf16[128,768]{1,0:T(8,128)(2,1)S(1)}, u32[]{:S(2)}, u32[]{:S(2)}) collective-permute-start(bf16[128,768]{1,0:T(8,128)(2,1)S(1)} %get-tuple-element.65), channel_id=1, source_target_pairs={{0,4},{1,5},{2,6},{3,7},{4,0},{5,1},{6,2},{7,3},{8,12},{9,13},{10,... | collective-permute-start | bytes 589832 | tf_op jit(solution)/shard_map/ppermute | solution.py:26
  260.1 22.1 %collective-permute-start.34 = (bf16[128,768]{1,0:T(8,128)(2,1)S(1)}, bf16[128,768]{1,0:T(8,128)(2,1)S(1)}, u32[]{:S(2)}, u32[]{:S(2)}) collective-permute-start(bf16[128,768]{1,0:T(8,128)(2,1)S(1)} %get-tuple-element.66), channel_id=1, source_target_pairs={{0,2},{1,3},{2,4},{3,5},{4,6},{5,7},{6,0},{7,1},{8,10},{9,11},{10,... | collective-permute-start | bytes 589832 | tf_op jit(solution)/shard_map/ppermute | solution.py:26
  261.1 11.5 %copy-start.46 = (bf16[128,1024]{1,0:T(8,128)(2,1)S(1)}, bf16[128,1024]{1,0:T(8,128)(2,1)}, u32[]{:S(2)}) copy-start(bf16[128,1024]{1,0:T(8,128)(2,1)} %copy-done.45) | copy-start | bytes 786436
  261.1 21.2 %copy-start.3 = (f32[1024,768]{1,0:T(8,128)S(1)}, f32[1024,768]{1,0:T(8,128)}, u32[]{:S(2)}) copy-start(f32[1024,768]{1,0:T(8,128)} %copy-done.2) | copy-start | bytes 9437188
  262.7 24.9 %collective-permute-start.21 = (bf16[128,1024]{1,0:T(8,128)(2,1)S(1)}, bf16[128,1024]{1,0:T(8,128)(2,1)S(1)}, u32[]{:S(2)}, u32[]{:S(2)}) collective-permute-start(bf16[128,1024]{1,0:T(8,128)(2,1)S(1)} %copy-done.48), channel_id=1, source_target_pairs={{0,4},{1,5},{2,6},{3,7},{4,0},{5,1},{6,2},{7,3},{8,12},{9,13},{10,... | collective-permute-start | bytes 786440 | tf_op jit(solution)/shard_map/ppermute | solution.py:26
  272.6 15.0 %collective-permute-start.22 = (bf16[128,1024]{1,0:T(8,128)(2,1)S(1)}, bf16[128,1024]{1,0:T(8,128)(2,1)S(1)}, u32[]{:S(2)}, u32[]{:S(2)}) collective-permute-start(bf16[128,1024]{1,0:T(8,128)(2,1)S(1)} %copy-done.46), channel_id=1, source_target_pairs={{0,6},{1,7},{2,0},{3,1},{4,2},{5,3},{6,4},{7,5},{8,14},{9,15},{10,... | collective-permute-start | bytes 786440 | tf_op jit(solution)/shard_map/ppermute | solution.py:26
  275.2 12.7 %collective-permute-start.25 = (bf16[128,1024]{1,0:T(8,128)(2,1)S(1)}, bf16[128,1024]{1,0:T(8,128)(2,1)S(1)}, u32[]{:S(2)}, u32[]{:S(2)}) collective-permute-start(bf16[128,1024]{1,0:T(8,128)(2,1)S(1)} %get-tuple-element.58), channel_id=1, source_target_pairs={{0,2},{1,3},{2,4},{3,5},{4,6},{5,7},{6,0},{7,1},{8,10},{9,11},{10,... | collective-permute-start | bytes 786440 | tf_op jit(solution)/shard_map/ppermute | solution.py:26
  275.2 12.7 %collective-permute-start.26 = (bf16[128,1024]{1,0:T(8,128)(2,1)S(1)}, bf16[128,1024]{1,0:T(8,128)(2,1)S(1)}, u32[]{:S(2)}, u32[]{:S(2)}) collective-permute-start(bf16[128,1024]{1,0:T(8,128)(2,1)S(1)} %get-tuple-element.59), channel_id=1, source_target_pairs={{0,4},{1,5},{2,6},{3,7},{4,0},{5,1},{6,2},{7,3},{8,12},{9,13},{10,... | collective-permute-start | bytes 786440 | tf_op jit(solution)/shard_map/ppermute | solution.py:26
  282.2 6.4 %collective-permute-start.27 = (bf16[128,1024]{1,0:T(8,128)(2,1)S(1)}, bf16[128,1024]{1,0:T(8,128)(2,1)S(1)}, u32[]{:S(2)}, u32[]{:S(2)}) collective-permute-start(bf16[128,1024]{1,0:T(8,128)(2,1)S(1)} %get-tuple-element.60), channel_id=1, source_target_pairs={{0,6},{1,7},{2,0},{3,1},{4,2},{5,3},{6,4},{7,5},{8,14},{9,15},{10,... | collective-permute-start | bytes 786440 | tf_op jit(solution)/shard_map/ppermute | solution.py:26
  (40 other events, 59.6 us)
Sparse Core Ops, SparseCore 0:
  24.6 41.4 all-gather.2
  72.4 41.8 all-gather.4
  133.8 45.4 reduce-scatter.2
  181.5 42.2 reduce-scatter.4

commit v4 on v3

--- a/solution.py
+++ b/solution.py
@@ -12,8 +12,8 @@
 ANY = pl.BlockSpec(memory_space=pl.ANY)
 SMEM = pl.BlockSpec(memory_space=pltpu.SMEM)
 VMEM = pl.BlockSpec(memory_space=pltpu.VMEM)
-BIG = 48 << 20
-SMALL = 32 << 20
+BIG = 56 << 20
+SMALL = 56 << 20
 
 
 def ring(step):
@@ -194,34 +194,24 @@
 
     cols = width // 3 if width % 384 == 0 else width
 
-    def rows_term(k, dtype, after, more=None, q=None):
+    def rows_term(k, dtypes, after):
         def body(g_ref, w_ref, v_ref, *refs):
             total = dot(g_ref[:, :feats], w_ref[...], ((1,), (0,)))
             total += dot(g_ref[:, feats:], v_ref[...], ((1,), (0,)))
-            parts = [total[:half], total[half:]]
-            if more is not None:
-                parts[q] = parts[q] + refs[0][...].astype(jnp.float32)
-            if len(outs) == 2:
-                refs[-2][...] = parts[0].astype(dtype)
-                refs[-1][...] = parts[1].astype(dtype)
+            if len(dtypes) == 2:
+                refs[0][...] = total[:half].astype(dtypes[0])
+                refs[1][...] = total[half:].astype(dtypes[1])
             else:
-                refs[-1][:half, :] = parts[0].astype(dtype)
-                refs[-1][half:, :] = parts[1].astype(dtype)
+                refs[0][...] = total.astype(dtypes[0])
 
         n = width // cols
-        outs = [of((half, width), dtype)] * 2 if k else [of((s, width), dtype)]
-        args = [cot, w_all[0], w_all[1]]
+        outs = [of((s // len(dtypes), width), dtype) for dtype in dtypes]
         column = pl.BlockSpec((feats, cols), lambda j: (0, k * n + j))
-        specs = [VMEM, column, column]
-        if more is not None:
-            args.append(more)
-            specs.append(pl.BlockSpec((half, cols), lambda j: (0, j)))
-        got = run(
-            body, outs, args, specs, after=after, grid=(n,),
+        return run(
+            body, outs, [cot, w_all[0], w_all[1]], [VMEM, column, column], after=after, grid=(n,),
             out_specs=[pl.BlockSpec((o.shape[0], cols), lambda j: (0, j)) for o in outs],
             name="rows_term", limit=BIG,
         )
-        return got if k else got[0]
 
     def scatter(x):
         return lax.psum_scatter(
@@ -230,18 +220,30 @@
 
     term_pair = term_of(1, ())
     term_own = term_of(0, (term_pair,))
-    far = rows_term(2, jnp.bfloat16, (term_own,))
+    sent0, kept0 = project(0, (term_own,))
+    got0 = swap(sent0)
+    bf16, f32 = jnp.bfloat16, jnp.float32
+    far = rows_term(2, (bf16, bf16), (sent0,))
     up = shift(far[0], 1)
     down = shift(far[1], -1)
-    sent0, kept0 = project(0, (far[0],))
-    got0 = swap(sent0)
-    stay = rows_term(0, jnp.float32, (kept0,))
-    sent1, kept1 = project(1, (stay, up, down))
+    right_top, right_bottom = rows_term(3, (f32, bf16), (far[0],))
+    left_top, left_bottom = rows_term(1, (bf16, f32), (right_bottom,))
+    from_left_bottom = shift(right_bottom, 1)
+    from_right_top = shift(left_top, -1)
+
+    def add_far(a_ref, up_ref, b_ref, down_ref, *outs):
+        outs[0][...] = (a_ref[...] + up_ref[...].astype(jnp.float32)).astype(jnp.bfloat16)
+        outs[1][...] = (b_ref[...] + down_ref[...].astype(jnp.float32)).astype(jnp.bfloat16)
+
+    right_top, left_bottom = run(
+        add_far, [of((half, width))] * 2, (right_top, up, left_bottom, down), [VMEM] * 4,
+        after=(left_top,), out_specs=[VMEM] * 2, name="add_far",
+    )
+    from_left = [shift(right_top, 1), from_left_bottom]
+    from_right = [from_right_top, shift(left_bottom, -1)]
+    sent1, kept1 = project(1, (right_top,))
     got1 = swap(sent1)
-    to_right = rows_term(3, jnp.bfloat16, (kept1,), up, 0)
-    to_left = rows_term(1, jnp.bfloat16, (to_right[0],), down, 1)
-    from_left = [shift(x, 1) for x in (to_right[1], to_right[0])][::-1]
-    from_right = [shift(x, -1) for x in to_left]
+    stay = rows_term(0, (f32,), (kept1,))[0]
     term_pair = scatter(term_pair)
     term_own = scatter(term_own)
 
@@ -259,9 +261,9 @@
         )
         return [outs[0]] + [shift(outs[k], k) for k in range(1, NZ)], outs[0]
 
-    quarters0, last = spread(kept0, got0, (to_left[0], term_pair))
+    quarters0, last = spread(kept0, got0, (stay, term_pair, from_left_bottom, from_right_top))
     term_pair = lax.ppermute(term_pair, "dp", pair)
-    quarters1, last = spread(kept1, got1, (term_pair, last))
+    quarters1, last = spread(kept1, got1, (term_pair, *quarters0[1:]))
 
     def add_rows(place_ref, counts_ref, stay_ref, *refs):
         slot = lax.broadcasted_iota(jnp.int32, (1, width), 1) // HD
@@ -309,7 +311,7 @@
 
     parts = run(
         add_terms, [of((piece, width))] * NZ, (term_own, term_pair), [VMEM] * 2,
-        out_specs=[VMEM] * NZ, name="add_terms",
+        after=(last,), out_specs=[VMEM] * NZ, name="add_terms",
     )
     parts = [parts[0]] + [shift(parts[k], -k) for k in range(1, NZ)]
 

time: 299 us -> 288 us (0.963)
  Pallas kernels: 82.4 us -> 116 us
  local copies, waits for them, and re-layouts: 39.4 us -> 10.3 us
  waiting for transfers between devices: 104 us -> 89.9 us
    pallas_call x20 -> x21, Pallas kernels: 82.4 us -> 116 us  [run(): pl.pallas_call(kernel, out_shape=out, grid=grid, in_specs=list(specs) + [...]
    unnamed x98 -> x76, local copies, waits for them, and re-layouts: 39.4 us -> 10.3 us
    ppermute x1, waiting for transfers between devices: 14.6 us -> 1.15 us  [per_device(): term_pair = lax.ppermute(term_pair, 'dp', pair)]
    ppermute x27, waiting for transfers between devices: 62.5 us -> 51.8 us  [shift(): return lax.ppermute(value, 'tensor', ring(step))]
    ppermute x6, waiting for transfers between devices: 26.9 us -> 36.8 us  [swap(): return lax.ppermute(value, 'tensor', SWAP)]
    ppermute x6, starting transfers between devices: 13.3 us -> 16.5 us  [swap(): return lax.ppermute(value, 'tensor', SWAP)]
  transfers between devices with their start and end apart: 39 -> 39, of which waited for: 14 -> 16; matrix products, arithmetic and copies ran while one was open for 0% -> 0% of each run, Pallas kernels for 26% -> 38%
where the time goes in v4:
time: 288 us
  Pallas kernels  116 us (40%)
  waiting for transfers between devices  89.9 us (31%)
  starting transfers between devices  57.4 us (20%)
  between operations  14.1 us (5%)
  local copies, waits for them, and re-layouts  10.3 us (4%)
    pallas_call x21, Pallas kernels, run(): pl.pallas_call(kernel, out_shape=out, grid=grid, in_specs=list(specs) + [...  116 us
    ppermute x27, waiting for transfers between devices, shift(): return lax.ppermute(value, 'tensor', ring(step))  51.8 us
    ppermute x27, starting transfers between devices, shift(): return lax.ppermute(value, 'tensor', ring(step))  38.4 us
    ppermute x6, waiting for transfers between devices, swap(): return lax.ppermute(value, 'tensor', SWAP)  36.8 us
    ppermute x6, starting transfers between devices, swap(): return lax.ppermute(value, 'tensor', SWAP)  16.5 us
    unnamed x76, local copies, waits for them, and re-layouts  10.3 us
  transfers between devices with their start and end apart: 39, of which 16 were waited for; matrix products, arithmetic and copies ran while one was open for 0% of the time, Pallas kernels for 38%

profile of v4, /device:TPU:0, one launch (start us, length us, event | category | flops | bytes accessed | tf_op | source)
XLA Modules:
  0.0 287.9 jit_solution(5184244936786385926)
XLA Ops:
  7.9 2.1 w_split.1
  9.9 2.0 collective-permute-start
  11.9 3.6 %collective-permute-start.1 = (bf16[128,768]{1,0:T(8,128)(2,1)}, bf16[128,768]{1,0:T(8,128)(2,1)S(1)}, u32[]{:S(2)}, u32[]{:S(2)}) collective-permute-start(bf16[128,768]{1,0:T(8,128)(2,1)} %get-tuple-element.39), channel_id=1, source_target_pairs={{0,4},{1,5},{2,6},{3,7},{4,0},{5,1},{6,2},{7,3},{8,12},{9,13},{10,... | collective-permute-start | bytes 589832 | tf_op jit(solution)/shard_map/ppermute | solution.py:26
  16.5 3.5 %g_split.1 = (bf16[128,2048]{1,0:T(8,128)(2,1)}, bf16[128,2048]{1,0:T(8,128)(2,1)}, bf16[128,2048]{1,0:T(8,128)(2,1)}, bf16[128,2048]{1,0:T(8,128)(2,1)}) custom-call(s32[4]{0:T(128)} %pad_add_fusion.refs_0_, bf16[128,8192]{1,0:T(8,128)(2,1)} %bitcast.8, bf16[128,768]{1,0:T(8,128)(2,1)} %get-tuple-element.37.refs_2_.refs_0_), custom_call_target="tpu_custom_call" | custom-call | flops 1000 | bytes 1000 | tf_op jit(solution)/shard_map/g_split/pallas_call | solution.py:47
  20.0 2.7 mask.1
  22.8 1.8 collective-permute-done.1.refs_2_
  25.3 2.1 w_join.1
  28.6 2.4 collective-permute-start.12
  34.6 20.3 %collective-permute-done.10.refs_6_.refs_3_ = bf16[128,2048]{1,0:T(8,128)(2,1)S(1)} collective-permute-done((bf16[128,2048]{1,0:T(8,128)(2,1)}, bf16[128,2048]{1,0:T(8,128)(2,1)S(1)}, u32[]{:S(2)}, u32[]{:S(2)}) %collective-permute-start.10) | collective-permute-done | bytes 524320 | tf_op jit(solution)/shard_map/ppermute | solution.py:26
  55.3 3.2 %collective-permute-start.9 = (bf16[128,2048]{1,0:T(8,128)(2,1)S(1)}, bf16[128,2048]{1,0:T(8,128)(2,1)S(1)}, u32[]{:S(2)}, u32[]{:S(2)}) collective-permute-start(bf16[128,2048]{1,0:T(8,128)(2,1)S(1)} %copy-done.15), channel_id=1, source_target_pairs={{0,1},{1,0},{2,3},{3,2},{4,5},{5,4},{6,7},{7,6},{8,9},{9,8},{10,11... | collective-permute-start | bytes 1572872 | tf_op jit(solution)/shard_map/ppermute | solution.py:30
  58.5 12.0 %collective-permute-done.14.refs_8_.refs_5_ = bf16[128,2048]{1,0:T(8,128)(2,1)S(1)} collective-permute-done((bf16[128,2048]{1,0:T(8,128)(2,1)S(1)}, bf16[128,2048]{1,0:T(8,128)(2,1)S(1)}, u32[]{:S(2)}, u32[]{:S(2)}) %collective-permute-start.14) | collective-permute-done | bytes 524320 | tf_op jit(solution)/shard_map/ppermute | solution.py:26
  72.8 2.1 w_move.1
  74.9 3.3 %collective-permute-start.11 = (bf16[128,2048]{1,0:T(8,128)(2,1)}, bf16[128,2048]{1,0:T(8,128)(2,1)S(1)}, u32[]{:S(2)}, u32[]{:S(2)}) collective-permute-start(bf16[128,2048]{1,0:T(8,128)(2,1)} %copy-done.11), channel_id=1, source_target_pairs={{0,1},{1,0},{2,3},{3,2},{4,5},{5,4},{6,7},{7,6},{8,9},{9,8},{10,11... | collective-permute-start | bytes 1572872 | tf_op jit(solution)/shard_map/ppermute | solution.py:30
  79.8 2.0 collective-permute-start.8
  83.2 8.4 %collective-permute-done.11.refs_2_ = bf16[128,2048]{1,0:T(8,128)(2,1)S(1)} collective-permute-done((bf16[128,2048]{1,0:T(8,128)(2,1)}, bf16[128,2048]{1,0:T(8,128)(2,1)S(1)}, u32[]{:S(2)}, u32[]{:S(2)}) %collective-permute-start.11) | collective-permute-done | bytes 524320 | tf_op jit(solution)/shard_map/ppermute | solution.py:30
  92.7 8.0 %collective-permute-done.13.refs_3_ = bf16[128,2048]{1,0:T(8,128)(2,1)S(1)} collective-permute-done((bf16[128,2048]{1,0:T(8,128)(2,1)}, bf16[128,2048]{1,0:T(8,128)(2,1)S(1)}, u32[]{:S(2)}, u32[]{:S(2)}) %collective-permute-start.13) | collective-permute-done | bytes 524320 | tf_op jit(solution)/shard_map/ppermute | solution.py:30
  100.7 3.2 %collective-permute-start.15 = (bf16[128,2048]{1,0:T(8,128)(2,1)}, bf16[128,2048]{1,0:T(8,128)(2,1)S(1)}, u32[]{:S(2)}, u32[]{:S(2)}) collective-permute-start(bf16[128,2048]{1,0:T(8,128)(2,1)} %copy-done.13), channel_id=1, source_target_pairs={{0,1},{1,0},{2,3},{3,2},{4,5},{5,4},{6,7},{7,6},{8,9},{9,8},{10,11... | collective-permute-start | bytes 1572872 | tf_op jit(solution)/shard_map/ppermute | solution.py:30
  103.9 10.4 %collective-permute-done.15.refs_4_ = bf16[128,2048]{1,0:T(8,128)(2,1)S(1)} collective-permute-done((bf16[128,2048]{1,0:T(8,128)(2,1)}, bf16[128,2048]{1,0:T(8,128)(2,1)S(1)}, u32[]{:S(2)}, u32[]{:S(2)}) %collective-permute-start.15) | collective-permute-done | bytes 524320 | tf_op jit(solution)/shard_map/ppermute | solution.py:30
  115.2 4.6 %g_join.1.refs_0_ = bf16[1024,2048]{1,0:T(8,128)(2,1)} custom-call(s32[4]{0:T(128)} %pad_add_fusion.refs_0_, bf16[128,2048]{1,0:T(8,128)(2,1)} %copy-done.14, bf16[128,2048]{1,0:T(8,128)(2,1)} %copy-done.24, bf16[128,2048]{1,0:T(8,128)(2,1)} %copy-done.25, bf16[128,2048]{1,0:T(8,128)(2,1)} %copy-done.26, ...), custom_call_target="tpu_custom_call" | custom-call | flops 1000 | bytes 1000 | tf_op jit(solution)/shard_map/g_join/pallas_call | solution.py:47
  122.1 11.6 %term.2.refs_9_ = bf16[1024,3072]{1,0:T(8,128)(2,1)} custom-call(bf16[1024,2048]{1,0:T(8,128)(2,1)} %g_join.1.refs_0_, bf16[512,768]{1,0:T(8,128)(2,1)} %get-tuple-element.42.refs_4_.refs_1_, bf16[512,768]{1,0:T(8,128)(2,1)} %get-tuple-element.43.refs_2_, bf16[512,768]{1,0:T(8,128)(2,1)} %copy-done.1, bf16[512,768]{1,0:T(8,128)(2,1)} %copy-done.4, ...), custom_call_target="tpu_custom_call" | custom-call | flops 1000 | bytes 1000 | tf_op jit(solution)/shard_map/term/pallas_call | solution.py:47
  134.0 11.6 %term.3.refs_9_ = bf16[1024,3072]{1,0:T(8,128)(2,1)} custom-call(bf16[1024,2048]{1,0:T(8,128)(2,1)} %g_join.1.refs_0_, bf16[512,768]{1,0:T(8,128)(2,1)} %get-tuple-element.42.refs_4_.refs_1_, bf16[512,768]{1,0:T(8,128)(2,1)} %get-tuple-element.43.refs_2_, bf16[512,768]{1,0:T(8,128)(2,1)} %copy-done.1, bf16[512,768]{1,0:T(8,128)(2,1)} %copy-done.4, ...), custom_call_target="tpu_custom_call" | custom-call | flops 1000 | bytes 1000 | tf_op jit(solution)/shard_map/term/pallas_call | solution.py:47
  145.7 11.7 %project.2 = (bf16[512,1024]{1,0:T(8,128)(2,1)}, f32[512,1024]{1,0:T(8,128)}) custom-call(bf16[1024,3072]{1,0:T(8,128)(2,1)} %all-gather.3.cloned.1.call-done.refs_0_.refs_1_, bf16[512,768]{1,0:T(8,128)(2,1)} %get-tuple-element.42.refs_4_.refs_1_, bf16[512,768]{1,0:T(8,128)(2,1)} %get-tuple-element.43.refs_2_, bf16[512,768]{1,0:T(8,128)(2,1)} %copy-done.1, ...), custom_call_target="tpu_custom_call" | custom-call | flops 1000 | bytes 1000 | tf_op jit(solution)/shard_map/project/pallas_call | solution.py:47
  157.3 7.2 %rows_term.4 = (bf16[512,768]{1,0:T(8,128)(2,1)}, bf16[512,768]{1,0:T(8,128)(2,1)}) custom-call(bf16[1024,2048]{1,0:T(8,128)(2,1)} %g_join.1.refs_0_, bf16[1024,3072]{1,0:T(8,128)(2,1)} %all-gather.3.cloned.1.call-done.refs_0_.refs_1_, bf16[1024,3072]{1,0:T(8,128)(2,1)} %all-gather.5.cloned.1.call-done.refs_2_.refs_0_, ...), custom_call_target="tpu_custom_call" | custom-call | flops 1000 | bytes 1000 | tf_op jit(solution)/shard_map/rows_term/pallas_call | solution.py:47
  164.6 4.7 %collective-permute-start.19 = (bf16[512,768]{1,0:T(8,128)(2,1)}, bf16[512,768]{1,0:T(8,128)(2,1)S(1)}, u32[]{:S(2)}, u32[]{:S(2)}) collective-permute-start(bf16[512,768]{1,0:T(8,128)(2,1)} %get-tuple-element.53), channel_id=1, source_target_pairs={{0,6},{1,7},{2,0},{3,1},{4,2},{5,3},{6,4},{7,5},{8,14},{9,15},{10,... | collective-permute-start | bytes 2359304 | tf_op jit(solution)/shard_map/ppermute | solution.py:26
  169.2 3.2 %collective-permute-start.16 = (bf16[512,1024]{1,0:T(8,128)(2,1)}, bf16[512,1024]{1,0:T(8,128)(2,1)S(1)}, u32[]{:S(2)}, u32[]{:S(2)}) collective-permute-start(bf16[512,1024]{1,0:T(8,128)(2,1)} %get-tuple-element.48.refs_3_), channel_id=1, source_target_pairs={{0,1},{1,0},{2,3},{3,2},{4,5},{5,4},{6,7},{7,6},{8,9},{9,8},{10,11... | collective-permute-start | bytes 3145736 | tf_op jit(solution)/shard_map/ppermute | solution.py:30
  172.5 7.3 %rows_term.5 = (f32[512,768]{1,0:T(8,128)}, bf16[512,768]{1,0:T(8,128)(2,1)}) custom-call(bf16[1024,2048]{1,0:T(8,128)(2,1)} %g_join.1.refs_0_, bf16[1024,3072]{1,0:T(8,128)(2,1)} %all-gather.3.cloned.1.call-done.refs_0_.refs_1_, bf16[1024,3072]{1,0:T(8,128)(2,1)} %all-gather.5.cloned.1.call-done.refs_2_.refs_0_, bf16[512,768]{1,0:T(8,128)(2,1)} %get-tuple-element.49.refs_3_), custom_call_target="tpu_custom_call" | custom-call | flops 1000 | bytes 1000 | tf_op jit(solution)/shard_map/rows_term/pallas_call | solution.py:47
  180.4 7.2 %rows_term.6 = (bf16[512,768]{1,0:T(8,128)(2,1)}, f32[512,768]{1,0:T(8,128)}) custom-call(bf16[1024,2048]{1,0:T(8,128)(2,1)} %g_join.1.refs_0_, bf16[1024,3072]{1,0:T(8,128)(2,1)} %all-gather.3.cloned.1.call-done.refs_0_.refs_1_, bf16[1024,3072]{1,0:T(8,128)(2,1)} %all-gather.5.cloned.1.call-done.refs_2_.refs_0_, bf16[512,768]{1,0:T(8,128)(2,1)} %get-tuple-element.51.refs_3_), custom_call_target="tpu_custom_call" | custom-call | flops 1000 | bytes 1000 | tf_op jit(solution)/shard_map/rows_term/pallas_call | solution.py:47
  187.7 2.6 collective-permute-start.21
  192.0 3.6 %add_far.1 = (bf16[512,768]{1,0:T(8,128)(2,1)}, bf16[512,768]{1,0:T(8,128)(2,1)}) custom-call(f32[512,768]{1,0:T(8,128)} %get-tuple-element.50.refs_0_, bf16[512,768]{1,0:T(8,128)(2,1)} %copy-done.23, f32[512,768]{1,0:T(8,128)} %get-tuple-element.52.refs_2_, bf16[512,768]{1,0:T(8,128)(2,1)} %copy-done.22, bf16[512,768]{1,0:T(8,128)(2,1)} %get-tuple-element.54.refs_4_), custom_call_target="tpu_custom_call" | custom-call | flops 1000 | bytes 1000 | tf_op jit(solution)/shard_map/add_far/pallas_call | solution.py:47
  195.6 11.7 %project.3 = (bf16[512,1024]{1,0:T(8,128)(2,1)}, f32[512,1024]{1,0:T(8,128)}) custom-call(bf16[1024,3072]{1,0:T(8,128)(2,1)} %all-gather.5.cloned.1.call-done.refs_2_.refs_0_, bf16[512,768]{1,0:T(8,128)(2,1)} %get-tuple-element.42.refs_4_.refs_1_, bf16[512,768]{1,0:T(8,128)(2,1)} %get-tuple-element.43.refs_2_, bf16[512,768]{1,0:T(8,128)(2,1)} %copy-done.1, ...), custom_call_target="tpu_custom_call" | custom-call | flops 1000 | bytes 1000 | tf_op jit(solution)/shard_map/project/pallas_call | solution.py:47
  207.3 3.3 %collective-permute-start.25 = (bf16[512,1024]{1,0:T(8,128)(2,1)}, bf16[512,1024]{1,0:T(8,128)(2,1)}, u32[]{:S(2)}, u32[]{:S(2)}) collective-permute-start(bf16[512,1024]{1,0:T(8,128)(2,1)} %get-tuple-element.61), channel_id=1, source_target_pairs={{0,1},{1,0},{2,3},{3,2},{4,5},{5,4},{6,7},{7,6},{8,9},{9,8},{10,11... | collective-permute-start | bytes 3145736 | tf_op jit(solution)/shard_map/ppermute | solution.py:30
  211.3 2.0 collective-permute-start.30
  213.3 7.8 %rows_term.7.refs_3_.refs_2_ = f32[1024,768]{1,0:T(8,128)} custom-call(bf16[1024,2048]{1,0:T(8,128)(2,1)} %g_join.1.refs_0_, bf16[1024,3072]{1,0:T(8,128)(2,1)} %all-gather.3.cloned.1.call-done.refs_0_.refs_1_, bf16[1024,3072]{1,0:T(8,128)(2,1)} %all-gather.5.cloned.1.call-done.refs_2_.refs_0_, f32[512,1024]{1,0:T(8,128)} %get-tuple-element.56.refs_3_.refs_1_), custom_call_target="tpu_custom_call" | custom-call | flops 1000 | bytes 1000 | tf_op jit(solution)/shard_map/rows_term/pallas_call | solution.py:47
  222.0 3.0 %settle.2 = (bf16[128,1024]{1,0:T(8,128)(2,1)}, bf16[128,1024]{1,0:T(8,128)(2,1)}, bf16[128,1024]{1,0:T(8,128)(2,1)}, bf16[128,1024]{1,0:T(8,128)(2,1)}) custom-call(s32[4]{0:T(128)} %pad_add_fusion.refs_0_, f32[512,1024]{1,0:T(8,128)} %get-tuple-element.47.refs_1_, bf16[512,1024]{1,0:T(8,128)(2,1)} %copy-done.16, f32[1024,768]{1,0:T(8,128)} %rows_term.7.refs_3_.refs_2_, ...), custom_call_target="tpu_custom_call" | custom-call | flops 1000 | bytes 1000 | tf_op jit(solution)/shard_map/settle/pallas_call | solution.py:47
  225.3 10.0 %collective-permute-done.25.refs_2_ = bf16[512,1024]{1,0:T(8,128)(2,1)} collective-permute-done((bf16[512,1024]{1,0:T(8,128)(2,1)}, bf16[512,1024]{1,0:T(8,128)(2,1)}, u32[]{:S(2)}, u32[]{:S(2)}) %collective-permute-start.25) | collective-permute-done | bytes 1048608 | tf_op jit(solution)/shard_map/ppermute | solution.py:30
  237.3 6.0 %collective-permute-done.23.refs_5_.refs_3_ = bf16[128,1024]{1,0:T(8,128)(2,1)S(1)} collective-permute-done((bf16[128,1024]{1,0:T(8,128)(2,1)}, bf16[128,1024]{1,0:T(8,128)(2,1)S(1)}, u32[]{:S(2)}, u32[]{:S(2)}) %collective-permute-start.23) | collective-permute-done | bytes 262176 | tf_op jit(solution)/shard_map/ppermute | solution.py:26
  243.3 1.7 collective-permute-done.24.refs_6_.refs_4_
  247.0 3.0 %settle.3 = (bf16[128,1024]{1,0:T(8,128)(2,1)}, bf16[128,1024]{1,0:T(8,128)(2,1)}, bf16[128,1024]{1,0:T(8,128)(2,1)}, bf16[128,1024]{1,0:T(8,128)(2,1)}) custom-call(s32[4]{0:T(128)} %pad_add_fusion.refs_0_, f32[512,1024]{1,0:T(8,128)} %get-tuple-element.56.refs_3_.refs_1_, bf16[512,1024]{1,0:T(8,128)(2,1)} %collective-permute-done.25.refs_2_, ...), custom_call_target="tpu_custom_call" | custom-call | flops 1000 | bytes 1000 | tf_op jit(solution)/shard_map/settle/pallas_call | solution.py:47
  250.0 2.3 add_terms.1
  252.3 2.2 collective-permute-start.32
  254.5 1.8 collective-permute-start.28
  257.8 2.9 %collective-permute-start.33 = (bf16[128,768]{1,0:T(8,128)(2,1)}, bf16[128,768]{1,0:T(8,128)(2,1)S(1)}, u32[]{:S(2)}, u32[]{:S(2)}) collective-permute-start(bf16[128,768]{1,0:T(8,128)(2,1)} %get-tuple-element.69), channel_id=1, source_target_pairs={{0,4},{1,5},{2,6},{3,7},{4,0},{5,1},{6,2},{7,3},{8,12},{9,13},{10,... | collective-permute-start | bytes 589832 | tf_op jit(solution)/shard_map/ppermute | solution.py:26
  260.7 2.5 collective-permute-done.32.refs_2_
  263.2 4.6 %add_rows.1 = bf16[1024,768]{1,0:T(8,128)(2,1)} custom-call(s32[4]{0:T(128)} %pad_add_fusion.refs_0_, s32[8]{0:T(128)} %refs_1_.5, f32[1024,768]{1,0:T(8,128)} %rows_term.7.refs_3_.refs_2_, bf16[512,768]{1,0:T(8,128)(2,1)} %collective-permute-done.30.refs_3_, bf16[512,768]{1,0:T(8,128)(2,1)} %copy-done.8, bf16[512,768]{1,0:T(8,128)(2,1)} %copy-done.9, ...), custom_call_target="tpu_custom_call" | custom-call | flops 1000 | bytes 1000 | tf_op jit(solution)/shard_map/add_rows/pallas_call | solution.py:47
  267.8 2.9 %collective-permute-done.33.refs_3_ = bf16[128,768]{1,0:T(8,128)(2,1)S(1)} collective-permute-done((bf16[128,768]{1,0:T(8,128)(2,1)}, bf16[128,768]{1,0:T(8,128)(2,1)S(1)}, u32[]{:S(2)}, u32[]{:S(2)}) %collective-permute-start.33) | collective-permute-done | bytes 196640 | tf_op jit(solution)/shard_map/ppermute | solution.py:26
  270.7 3.3 %collective-permute-done.34.refs_4_ = bf16[128,768]{1,0:T(8,128)(2,1)S(1)} collective-permute-done((bf16[128,768]{1,0:T(8,128)(2,1)}, bf16[128,768]{1,0:T(8,128)(2,1)S(1)}, u32[]{:S(2)}, u32[]{:S(2)}) %collective-permute-start.34) | collective-permute-done | bytes 196640 | tf_op jit(solution)/shard_map/ppermute | solution.py:26
  274.7 2.5 join_term.1
  278.0 3.3 %join_out.1 = bf16[128,8192]{1,0:T(8,128)(2,1)} custom-call(s32[4]{0:T(128)} %pad_add_fusion.refs_0_, bf16[128,1024]{1,0:T(8,128)(2,1)} %get-tuple-element.57.refs_1_, bf16[128,1024]{1,0:T(8,128)(2,1)} %copy-done.17, bf16[128,1024]{1,0:T(8,128)(2,1)} %copy-done.18, bf16[128,1024]{1,0:T(8,128)(2,1)} %copy-done.19, ...), custom_call_target="tpu_custom_call" | custom-call | flops 1000 | bytes 1000 | tf_op jit(solution)/shard_map/join_out/pallas_call | solution.py:47
  (132 shorter events, 28.6 us)
Async XLA Ops:
  7.2 138.5 %all-gather.3.cloned.1.call-start = ((), (), s32[]{:S(2)}) async-start(), calls=%async_computation.2 | async-start | bytes 7077888 | tf_op jit(solution)/shard_map/all_gather | solution.py:140
  9.9 12.8 %collective-permute-start = (bf16[128,768]{1,0:T(8,128)(2,1)}, bf16[128,768]{1,0:T(8,128)(2,1)S(1)}, u32[]{:S(2)}, u32[]{:S(2)}) collective-permute-start(bf16[128,768]{1,0:T(8,128)(2,1)} %get-tuple-element.38), channel_id=1, source_target_pairs={{0,2},{1,3},{2,4},{3,5},{4,6},{5,7},{6,0},{7,1},{8,10},{9,11},{10,... | collective-permute-start | bytes 589832 | tf_op jit(solution)/shard_map/ppermute | solution.py:26
  11.9 12.6 %collective-permute-start.1 = (bf16[128,768]{1,0:T(8,128)(2,1)}, bf16[128,768]{1,0:T(8,128)(2,1)S(1)}, u32[]{:S(2)}, u32[]{:S(2)}) collective-permute-start(bf16[128,768]{1,0:T(8,128)(2,1)} %get-tuple-element.39), channel_id=1, source_target_pairs={{0,4},{1,5},{2,6},{3,7},{4,0},{5,1},{6,2},{7,3},{8,12},{9,13},{10,... | collective-permute-start | bytes 589832 | tf_op jit(solution)/shard_map/ppermute | solution.py:26
  15.5 9.0 %collective-permute-start.2 = (bf16[128,768]{1,0:T(8,128)(2,1)}, bf16[128,768]{1,0:T(8,128)(2,1)S(1)}, u32[]{:S(2)}, u32[]{:S(2)}) collective-permute-start(bf16[128,768]{1,0:T(8,128)(2,1)} %get-tuple-element.40), channel_id=1, source_target_pairs={{0,6},{1,7},{2,0},{3,1},{4,2},{5,3},{6,4},{7,5},{8,14},{9,15},{10,... | collective-permute-start | bytes 589832 | tf_op jit(solution)/shard_map/ppermute | solution.py:26
  22.7 32.2 %copy-start.36 = (bf16[128,2048]{1,0:T(8,128)(2,1)S(1)}, bf16[128,2048]{1,0:T(8,128)(2,1)}, u32[]{:S(2)}) copy-start(bf16[128,2048]{1,0:T(8,128)(2,1)} %get-tuple-element.46) | copy-start | bytes 1572868
  22.7 32.5 %copy-start.15 = (bf16[128,2048]{1,0:T(8,128)(2,1)S(1)}, bf16[128,2048]{1,0:T(8,128)(2,1)}, u32[]{:S(2)}) copy-start(bf16[128,2048]{1,0:T(8,128)(2,1)} %get-tuple-element.41.refs_3_.refs_5_) | copy-start | bytes 1572868
  27.5 129.9 %all-gather.5.cloned.1.call-start = ((), (), s32[]{:S(2)}) async-start(), calls=%async_computation.3 | async-start | bytes 7077888 | tf_op jit(solution)/shard_map/all_gather | solution.py:140
  27.5 27.4 %collective-permute-start.10 = (bf16[128,2048]{1,0:T(8,128)(2,1)}, bf16[128,2048]{1,0:T(8,128)(2,1)S(1)}, u32[]{:S(2)}, u32[]{:S(2)}) collective-permute-start(bf16[128,2048]{1,0:T(8,128)(2,1)} %get-tuple-element.44), channel_id=1, source_target_pairs={{0,2},{1,3},{2,4},{3,5},{4,6},{5,7},{6,0},{7,1},{8,10},{9,11},{10,... | collective-permute-start | bytes 1572872 | tf_op jit(solution)/shard_map/ppermute | solution.py:26
  28.6 26.6 %collective-permute-start.12 = (bf16[128,2048]{1,0:T(8,128)(2,1)S(1)}, bf16[128,2048]{1,0:T(8,128)(2,1)S(1)}, u32[]{:S(2)}, u32[]{:S(2)}) collective-permute-start(bf16[128,2048]{1,0:T(8,128)(2,1)S(1)} %copy-done.37), channel_id=1, source_target_pairs={{0,4},{1,5},{2,6},{3,7},{4,0},{5,1},{6,2},{7,3},{8,12},{9,13},{10,... | collective-permute-start | bytes 1572872 | tf_op jit(solution)/shard_map/ppermute | solution.py:26
  31.0 39.4 %collective-permute-start.6 = (bf16[512,768]{1,0:T(8,128)(2,1)S(1)}, bf16[512,768]{1,0:T(8,128)(2,1)S(1)}, u32[]{:S(2)}, u32[]{:S(2)}) collective-permute-start(bf16[512,768]{1,0:T(8,128)(2,1)S(1)} %copy-done.3), channel_id=1, source_target_pairs={{0,6},{1,7},{2,0},{3,1},{4,2},{5,3},{6,4},{7,5},{8,14},{9,15},{10,... | collective-permute-start | bytes 2359304 | tf_op jit(solution)/shard_map/ppermute | solution.py:26
  32.4 38.1 %collective-permute-start.3 = (bf16[512,768]{1,0:T(8,128)(2,1)S(1)}, bf16[512,768]{1,0:T(8,128)(2,1)S(1)}, u32[]{:S(2)}, u32[]{:S(2)}) collective-permute-start(bf16[512,768]{1,0:T(8,128)(2,1)S(1)} %copy-done.2), channel_id=1, source_target_pairs={{0,2},{1,3},{2,4},{3,5},{4,6},{5,7},{6,0},{7,1},{8,10},{9,11},{10,... | collective-permute-start | bytes 2359304 | tf_op jit(solution)/shard_map/ppermute | solution.py:26
  33.1 37.4 %collective-permute-start.17 = (bf16[128,3072]{1,0:T(8,128)(2,1)}, bf16[128,3072]{1,0:T(8,128)(2,1)S(1)}, u32[]{:S(2)}, u32[]{:S(2)}) collective-permute-start(bf16[128,3072]{1,0:T(8,128)(2,1)} %w_join.1), channel_id=1, source_target_pairs={{0,64},{8,72},{16,80},{24,88},{32,96},{40,104},{48,112},{56,120},{... | collective-permute-start | bytes 2359304 | tf_op jit(solution)/shard_map/ppermute | solution.py:135
  54.9 15.6 %copy-start.11 = (bf16[128,2048]{1,0:T(8,128)(2,1)}, bf16[128,2048]{1,0:T(8,128)(2,1)S(1)}, u32[]{:S(2)}) copy-start(bf16[128,2048]{1,0:T(8,128)(2,1)S(1)} %collective-permute-done.10.refs_6_.refs_3_) | copy-start | bytes 1572868
  54.9 15.6 %collective-permute-start.14 = (bf16[128,2048]{1,0:T(8,128)(2,1)S(1)}, bf16[128,2048]{1,0:T(8,128)(2,1)S(1)}, u32[]{:S(2)}, u32[]{:S(2)}) collective-permute-start(bf16[128,2048]{1,0:T(8,128)(2,1)S(1)} %copy-done.36), channel_id=1, source_target_pairs={{0,6},{1,7},{2,0},{3,1},{4,2},{5,3},{6,4},{7,5},{8,14},{9,15},{10,... | collective-permute-start | bytes 1572872 | tf_op jit(solution)/shard_map/ppermute | solution.py:26
  55.3 15.2 %copy-start.12 = (bf16[128,2048]{1,0:T(8,128)(2,1)}, bf16[128,2048]{1,0:T(8,128)(2,1)S(1)}, u32[]{:S(2)}) copy-start(bf16[128,2048]{1,0:T(8,128)(2,1)S(1)} %collective-permute-done.12.refs_7_.refs_4_) | copy-start | bytes 1572868
  55.3 15.2 %collective-permute-start.9 = (bf16[128,2048]{1,0:T(8,128)(2,1)S(1)}, bf16[128,2048]{1,0:T(8,128)(2,1)S(1)}, u32[]{:S(2)}, u32[]{:S(2)}) collective-permute-start(bf16[128,2048]{1,0:T(8,128)(2,1)S(1)} %copy-done.15), channel_id=1, source_target_pairs={{0,1},{1,0},{2,3},{3,2},{4,5},{5,4},{6,7},{7,6},{8,9},{9,8},{10,11... | collective-permute-start | bytes 1572872 | tf_op jit(solution)/shard_map/ppermute | solution.py:30
  74.9 135.7 %reduce-scatter.3.cloned.1.call-start = ((), (), s32[]{:S(2)}) async-start(), calls=%async_computation.4 | async-start | bytes 7077888 | tf_op jit(solution)/shard_map/reduce_scatter | solution.py:217
  74.9 16.7 %collective-permute-start.11 = (bf16[128,2048]{1,0:T(8,128)(2,1)}, bf16[128,2048]{1,0:T(8,128)(2,1)S(1)}, u32[]{:S(2)}, u32[]{:S(2)}) collective-permute-start(bf16[128,2048]{1,0:T(8,128)(2,1)} %copy-done.11), channel_id=1, source_target_pairs={{0,1},{1,0},{2,3},{3,2},{4,5},{5,4},{6,7},{7,6},{8,9},{9,8},{10,11... | collective-permute-start | bytes 1572872 | tf_op jit(solution)/shard_map/ppermute | solution.py:30
  78.2 22.5 %collective-permute-start.13 = (bf16[128,2048]{1,0:T(8,128)(2,1)}, bf16[128,2048]{1,0:T(8,128)(2,1)S(1)}, u32[]{:S(2)}, u32[]{:S(2)}) collective-permute-start(bf16[128,2048]{1,0:T(8,128)(2,1)} %copy-done.12), channel_id=1, source_target_pairs={{0,1},{1,0},{2,3},{3,2},{4,5},{5,4},{6,7},{7,6},{8,9},{9,8},{10,11... | collective-permute-start | bytes 1572872 | tf_op jit(solution)/shard_map/ppermute | solution.py:30
  78.5 41.3 %collective-permute-start.4 = (bf16[512,768]{1,0:T(8,128)(2,1)S(1)}, bf16[512,768]{1,0:T(8,128)(2,1)S(1)}, u32[]{:S(2)}, u32[]{:S(2)}) collective-permute-start(bf16[512,768]{1,0:T(8,128)(2,1)S(1)} %copy-done.3), channel_id=1, source_target_pairs={{0,2},{1,3},{2,4},{3,5},{4,6},{5,7},{6,0},{7,1},{8,10},{9,11},{10,... | collective-permute-start | bytes 2359304 | tf_op jit(solution)/shard_map/ppermute | solution.py:26
  79.8 40.0 %collective-permute-start.8 = (bf16[512,768]{1,0:T(8,128)(2,1)S(1)}, bf16[512,768]{1,0:T(8,128)(2,1)S(1)}, u32[]{:S(2)}, u32[]{:S(2)}) collective-permute-start(bf16[512,768]{1,0:T(8,128)(2,1)S(1)} %copy-done.2), channel_id=1, source_target_pairs={{0,6},{1,7},{2,0},{3,1},{4,2},{5,3},{6,4},{7,5},{8,14},{9,15},{10,... | collective-permute-start | bytes 2359304 | tf_op jit(solution)/shard_map/ppermute | solution.py:26
  81.8 38.0 %collective-permute-start.7 = (bf16[512,768]{1,0:T(8,128)(2,1)}, bf16[512,768]{1,0:T(8,128)(2,1)S(1)}, u32[]{:S(2)}, u32[]{:S(2)}) collective-permute-start(bf16[512,768]{1,0:T(8,128)(2,1)} %copy-done), channel_id=1, source_target_pairs={{0,6},{1,7},{2,0},{3,1},{4,2},{5,3},{6,4},{7,5},{8,14},{9,15},{10,... | collective-permute-start | bytes 2359304 | tf_op jit(solution)/shard_map/ppermute | solution.py:26
  91.6 22.8 %copy-start.24 = (bf16[128,2048]{1,0:T(8,128)(2,1)}, bf16[128,2048]{1,0:T(8,128)(2,1)S(1)}, u32[]{:S(2)}) copy-start(bf16[128,2048]{1,0:T(8,128)(2,1)S(1)} %collective-permute-done.11.refs_2_) | copy-start | bytes 1572868
  91.6 28.3 %collective-permute-start.5 = (bf16[512,768]{1,0:T(8,128)(2,1)}, bf16[512,768]{1,0:T(8,128)(2,1)S(1)}, u32[]{:S(2)}, u32[]{:S(2)}) collective-permute-start(bf16[512,768]{1,0:T(8,128)(2,1)} %copy-done.1), channel_id=1, source_target_pairs={{0,2},{1,3},{2,4},{3,5},{4,6},{5,7},{6,0},{7,1},{8,10},{9,11},{10,... | collective-permute-start | bytes 2359304 | tf_op jit(solution)/shard_map/ppermute | solution.py:26
  100.7 13.6 %copy-start.25 = (bf16[128,2048]{1,0:T(8,128)(2,1)}, bf16[128,2048]{1,0:T(8,128)(2,1)S(1)}, u32[]{:S(2)}) copy-start(bf16[128,2048]{1,0:T(8,128)(2,1)S(1)} %collective-permute-done.13.refs_3_) | copy-start | bytes 1572868
  100.7 13.6 %collective-permute-start.15 = (bf16[128,2048]{1,0:T(8,128)(2,1)}, bf16[128,2048]{1,0:T(8,128)(2,1)S(1)}, u32[]{:S(2)}, u32[]{:S(2)}) collective-permute-start(bf16[128,2048]{1,0:T(8,128)(2,1)} %copy-done.13), channel_id=1, source_target_pairs={{0,1},{1,0},{2,3},{3,2},{4,5},{5,4},{6,7},{7,6},{8,9},{9,8},{10,11... | collective-permute-start | bytes 1572872 | tf_op jit(solution)/shard_map/ppermute | solution.py:30
  133.8 116.3 %reduce-scatter.5.cloned.1.call-start = ((), (), s32[]{:S(2)}) async-start(), calls=%async_computation.5 | async-start | bytes 7077888 | tf_op jit(solution)/shard_map/reduce_scatter | solution.py:217
  164.6 25.7 %collective-permute-start.19 = (bf16[512,768]{1,0:T(8,128)(2,1)}, bf16[512,768]{1,0:T(8,128)(2,1)S(1)}, u32[]{:S(2)}, u32[]{:S(2)}) collective-permute-start(bf16[512,768]{1,0:T(8,128)(2,1)} %get-tuple-element.53), channel_id=1, source_target_pairs={{0,6},{1,7},{2,0},{3,1},{4,2},{5,3},{6,4},{7,5},{8,14},{9,15},{10,... | collective-permute-start | bytes 2359304 | tf_op jit(solution)/shard_map/ppermute | solution.py:26
  169.2 21.9 %collective-permute-start.18 = (bf16[512,768]{1,0:T(8,128)(2,1)}, bf16[512,768]{1,0:T(8,128)(2,1)S(1)}, u32[]{:S(2)}, u32[]{:S(2)}) collective-permute-start(bf16[512,768]{1,0:T(8,128)(2,1)} %get-tuple-element.49.refs_3_), channel_id=1, source_target_pairs={{0,2},{1,3},{2,4},{3,5},{4,6},{5,7},{6,0},{7,1},{8,10},{9,11},{10,... | collective-permute-start | bytes 2359304 | tf_op jit(solution)/shard_map/ppermute | solution.py:26
  169.2 41.9 %collective-permute-start.16 = (bf16[512,1024]{1,0:T(8,128)(2,1)}, bf16[512,1024]{1,0:T(8,128)(2,1)S(1)}, u32[]{:S(2)}, u32[]{:S(2)}) collective-permute-start(bf16[512,1024]{1,0:T(8,128)(2,1)} %get-tuple-element.48.refs_3_), channel_id=1, source_target_pairs={{0,1},{1,0},{2,3},{3,2},{4,5},{5,4},{6,7},{7,6},{8,9},{9,8},{10,11... | collective-permute-start | bytes 3145736 | tf_op jit(solution)/shard_map/ppermute | solution.py:30
  179.8 31.5 %collective-permute-start.20 = (bf16[512,768]{1,0:T(8,128)(2,1)}, bf16[512,768]{1,0:T(8,128)(2,1)S(1)}, u32[]{:S(2)}, u32[]{:S(2)}) collective-permute-start(bf16[512,768]{1,0:T(8,128)(2,1)} %get-tuple-element.51.refs_3_), channel_id=1, source_target_pairs={{0,2},{1,3},{2,4},{3,5},{4,6},{5,7},{6,0},{7,1},{8,10},{9,11},{10,... | collective-permute-start | bytes 2359304 | tf_op jit(solution)/shard_map/ppermute | solution.py:26
  187.7 33.4 %collective-permute-start.21 = (bf16[512,768]{1,0:T(8,128)(2,1)}, bf16[512,768]{1,0:T(8,128)(2,1)S(1)}, u32[]{:S(2)}, u32[]{:S(2)}) collective-permute-start(bf16[512,768]{1,0:T(8,128)(2,1)} %get-tuple-element.54.refs_4_), channel_id=1, source_target_pairs={{0,6},{1,7},{2,0},{3,1},{4,2},{5,3},{6,4},{7,5},{8,14},{9,15},{10,... | collective-permute-start | bytes 2359304 | tf_op jit(solution)/shard_map/ppermute | solution.py:26
  195.6 15.7 %copy-start.20 = (bf16[512,768]{1,0:T(8,128)(2,1)S(1)}, bf16[512,768]{1,0:T(8,128)(2,1)}, u32[]{:S(2)}) copy-start(bf16[512,768]{1,0:T(8,128)(2,1)} %get-tuple-element.55.refs_9_) | copy-start | bytes 2359300
  207.3 27.9 %collective-permute-start.25 = (bf16[512,1024]{1,0:T(8,128)(2,1)}, bf16[512,1024]{1,0:T(8,128)(2,1)}, u32[]{:S(2)}, u32[]{:S(2)}) collective-permute-start(bf16[512,1024]{1,0:T(8,128)(2,1)} %get-tuple-element.61), channel_id=1, source_target_pairs={{0,1},{1,0},{2,3},{3,2},{4,5},{5,4},{6,7},{7,6},{8,9},{9,8},{10,11... | collective-permute-start | bytes 3145736 | tf_op jit(solution)/shard_map/ppermute | solution.py:30
  210.6 35.6 %collective-permute-start.26 = (bf16[128,3072]{1,0:T(8,128)(2,1)}, bf16[128,3072]{1,0:T(8,128)(2,1)S(1)}, u32[]{:S(2)}, u32[]{:S(2)}) collective-permute-start(bf16[128,3072]{1,0:T(8,128)(2,1)} %reduce-scatter.3.cloned.1.call-done.refs_4_), channel_id=1, source_target_pairs={{0,64},{8,72},{16,80},{24,88},{32,96},{40,104},{48,112},{56,120},{... | collective-permute-start | bytes 2359304 | tf_op jit(solution)/shard_map/ppermute | solution.py:265
  211.2 9.9 %copy-start.16 = (bf16[512,1024]{1,0:T(8,128)(2,1)}, bf16[512,1024]{1,0:T(8,128)(2,1)S(1)}, u32[]{:S(2)}) copy-start(bf16[512,1024]{1,0:T(8,128)(2,1)S(1)} %collective-permute-done.16.refs_2_) | copy-start | bytes 3145732
  211.2 45.2 %collective-permute-start.31 = (bf16[512,768]{1,0:T(8,128)(2,1)}, bf16[512,768]{1,0:T(8,128)(2,1)}, u32[]{:S(2)}, u32[]{:S(2)}) collective-permute-start(bf16[512,768]{1,0:T(8,128)(2,1)} %get-tuple-element.66), channel_id=1, source_target_pairs={{0,6},{1,7},{2,0},{3,1},{4,2},{5,3},{6,4},{7,5},{8,14},{9,15},{10,... | collective-permute-start | bytes 2359304 | tf_op jit(solution)/shard_map/ppermute | solution.py:26
  211.3 9.8 %copy-start.8 = (bf16[512,768]{1,0:T(8,128)(2,1)}, bf16[512,768]{1,0:T(8,128)(2,1)S(1)}, u32[]{:S(2)}) copy-start(bf16[512,768]{1,0:T(8,128)(2,1)S(1)} %collective-permute-done.20.refs_5_.refs_4_) | copy-start | bytes 2359300
  211.3 46.5 %collective-permute-start.30 = (bf16[512,768]{1,0:T(8,128)(2,1)S(1)}, bf16[512,768]{1,0:T(8,128)(2,1)}, u32[]{:S(2)}, u32[]{:S(2)}) collective-permute-start(bf16[512,768]{1,0:T(8,128)(2,1)S(1)} %copy-done.20), channel_id=1, source_target_pairs={{0,2},{1,3},{2,4},{3,5},{4,6},{5,7},{6,0},{7,1},{8,10},{9,11},{10,... | collective-permute-start | bytes 2359304 | tf_op jit(solution)/shard_map/ppermute | solution.py:26
  225.0 11.6 %collective-permute-start.22 = (bf16[128,1024]{1,0:T(8,128)(2,1)}, bf16[128,1024]{1,0:T(8,128)(2,1)S(1)}, u32[]{:S(2)}, u32[]{:S(2)}) collective-permute-start(bf16[128,1024]{1,0:T(8,128)(2,1)} %get-tuple-element.58), channel_id=1, source_target_pairs={{0,2},{1,3},{2,4},{3,5},{4,6},{5,7},{6,0},{7,1},{8,10},{9,11},{10,... | collective-permute-start | bytes 786440 | tf_op jit(solution)/shard_map/ppermute | solution.py:26
  235.3 8.1 %collective-permute-start.23 = (bf16[128,1024]{1,0:T(8,128)(2,1)}, bf16[128,1024]{1,0:T(8,128)(2,1)S(1)}, u32[]{:S(2)}, u32[]{:S(2)}) collective-permute-start(bf16[128,1024]{1,0:T(8,128)(2,1)} %get-tuple-element.59), channel_id=1, source_target_pairs={{0,4},{1,5},{2,6},{3,7},{4,0},{5,1},{6,2},{7,3},{8,12},{9,13},{10,... | collective-permute-start | bytes 786440 | tf_op jit(solution)/shard_map/ppermute | solution.py:26
  236.6 8.4 %collective-permute-start.24 = (bf16[128,1024]{1,0:T(8,128)(2,1)}, bf16[128,1024]{1,0:T(8,128)(2,1)S(1)}, u32[]{:S(2)}, u32[]{:S(2)}) collective-permute-start(bf16[128,1024]{1,0:T(8,128)(2,1)} %get-tuple-element.60), channel_id=1, source_target_pairs={{0,6},{1,7},{2,0},{3,1},{4,2},{5,3},{6,4},{7,5},{8,14},{9,15},{10,... | collective-permute-start | bytes 786440 | tf_op jit(solution)/shard_map/ppermute | solution.py:26
  252.3 10.9 %collective-permute-start.32 = (bf16[128,768]{1,0:T(8,128)(2,1)}, bf16[128,768]{1,0:T(8,128)(2,1)S(1)}, u32[]{:S(2)}, u32[]{:S(2)}) collective-permute-start(bf16[128,768]{1,0:T(8,128)(2,1)} %get-tuple-element.68), channel_id=1, source_target_pairs={{0,6},{1,7},{2,0},{3,1},{4,2},{5,3},{6,4},{7,5},{8,14},{9,15},{10,... | collective-permute-start | bytes 589832 | tf_op jit(solution)/shard_map/ppermute | solution.py:26
  254.5 22.6 %collective-permute-start.27 = (bf16[128,1024]{1,0:T(8,128)(2,1)}, bf16[128,1024]{1,0:T(8,128)(2,1)S(1)}, u32[]{:S(2)}, u32[]{:S(2)}) collective-permute-start(bf16[128,1024]{1,0:T(8,128)(2,1)} %get-tuple-element.63), channel_id=1, source_target_pairs={{0,2},{1,3},{2,4},{3,5},{4,6},{5,7},{6,0},{7,1},{8,10},{9,11},{10,... | collective-permute-start | bytes 786440 | tf_op jit(solution)/shard_map/ppermute | solution.py:26
  254.5 22.6 %collective-permute-start.28 = (bf16[128,1024]{1,0:T(8,128)(2,1)}, bf16[128,1024]{1,0:T(8,128)(2,1)S(1)}, u32[]{:S(2)}, u32[]{:S(2)}) collective-permute-start(bf16[128,1024]{1,0:T(8,128)(2,1)} %get-tuple-element.64), channel_id=1, source_target_pairs={{0,4},{1,5},{2,6},{3,7},{4,0},{5,1},{6,2},{7,3},{8,12},{9,13},{10,... | collective-permute-start | bytes 786440 | tf_op jit(solution)/shard_map/ppermute | solution.py:26
  256.4 20.8 %collective-permute-start.29 = (bf16[128,1024]{1,0:T(8,128)(2,1)}, bf16[128,1024]{1,0:T(8,128)(2,1)S(1)}, u32[]{:S(2)}, u32[]{:S(2)}) collective-permute-start(bf16[128,1024]{1,0:T(8,128)(2,1)} %get-tuple-element.65), channel_id=1, source_target_pairs={{0,6},{1,7},{2,0},{3,1},{4,2},{5,3},{6,4},{7,5},{8,14},{9,15},{10,... | collective-permute-start | bytes 786440 | tf_op jit(solution)/shard_map/ppermute | solution.py:26
  257.8 12.9 %collective-permute-start.33 = (bf16[128,768]{1,0:T(8,128)(2,1)}, bf16[128,768]{1,0:T(8,128)(2,1)S(1)}, u32[]{:S(2)}, u32[]{:S(2)}) collective-permute-start(bf16[128,768]{1,0:T(8,128)(2,1)} %get-tuple-element.69), channel_id=1, source_target_pairs={{0,4},{1,5},{2,6},{3,7},{4,0},{5,1},{6,2},{7,3},{8,12},{9,13},{10,... | collective-permute-start | bytes 589832 | tf_op jit(solution)/shard_map/ppermute | solution.py:26
  263.2 10.8 %collective-permute-start.34 = (bf16[128,768]{1,0:T(8,128)(2,1)}, bf16[128,768]{1,0:T(8,128)(2,1)S(1)}, u32[]{:S(2)}, u32[]{:S(2)}) collective-permute-start(bf16[128,768]{1,0:T(8,128)(2,1)} %get-tuple-element.70), channel_id=1, source_target_pairs={{0,2},{1,3},{2,4},{3,5},{4,6},{5,7},{6,0},{7,1},{8,10},{9,11},{10,... | collective-permute-start | bytes 589832 | tf_op jit(solution)/shard_map/ppermute | solution.py:26
  (29 other events, 65.4 us)
Sparse Core Ops, SparseCore 0:
  27.6 41.3 all-gather.2
  75.0 41.8 all-gather.4
  133.9 45.4 reduce-scatter.2
  181.7 42.4 reduce-scatter.4

commit v5 on v4

--- a/solution.py
+++ b/solution.py
@@ -76,31 +76,23 @@
     pair = [(i, (i + n_x) % n_dp) for i in range(n_dp)]
     place = jnp.stack([z, h, y, rank]).astype(jnp.int32)
 
-    def split_w(place_ref, w_ref, *outs):
-        for k in range(NZ):
-            outs[k][...] = w_ref[block(piece, (place_ref[0] + k) % NZ), :]
-
-    w_out4 = run(
-        split_w, [of((piece, width))] * NZ, (place, w_out), [SMEM, VMEM],
-        out_specs=[VMEM] * NZ, name="w_split",
-    )
-    w_near = [w_out4[0]] + [shift(w_out4[k], k) for k in range(1, NZ)]
-
-    def split_g(place_ref, g_ref, *outs):
+    def split(place_ref, w_ref, g_ref, w0_ref, g0_ref, *outs):
         for k in range(NZ):
             zk = (place_ref[0] + k) % NZ
+            w_to, g_to, at = (outs[k - 1], outs[k - 1], width) if k else (w0_ref, g0_ref, 0)
+            w_to[:, :width] = w_ref[block(piece, zk), :]
             for i in range(2):
                 first = ((place_ref[2] + i) % 2) * n_x
                 for x in range(n_x):
-                    outs[k][:, (i * n_x + x) * piece : (i * n_x + x + 1) * piece] = g_ref[
-                        :, block(piece, (first + x) * NZ + zk)
-                    ]
-
-    g_out4 = run(
-        split_g, [of((own_rows, 2 * feats))] * NZ, (place, grad_out[0]), [SMEM, VMEM],
-        after=(w_out4[0],), out_specs=[VMEM] * NZ, name="g_split",
-    )
-    g_near = [g_out4[0]] + [shift(g_out4[k], k) for k in range(1, NZ)]
+                    col = at + (i * n_x + x) * piece
+                    g_to[:, col : col + piece] = g_ref[:, block(piece, (first + x) * NZ + zk)]
+
+    w_own, g_own, *packs = run(
+        split,
+        [of((piece, width)), of((piece, 2 * feats))] + [of((piece, width + 2 * feats))] * 3,
+        (place, w_out, grad_out[0]), [SMEM, VMEM, VMEM], out_specs=[VMEM] * 5, name="split",
+    )
+    packs = [shift(packs[k - 1], k) for k in range(1, NZ)]
 
     def mask_body(place_ref, counts_ref, a_ref, *outs):
         slot = lax.broadcasted_iota(jnp.int32, (1, width), 1) // HD
@@ -114,26 +106,32 @@
 
     act = run(
         mask_body, [of((half, width))] * 2, (place, counts, attn[0]), [SMEM, SMEM, VMEM],
-        after=(g_out4[0],), out_specs=[VMEM] * 2, name="mask",
+        after=(w_own,), out_specs=[VMEM] * 2, name="mask",
     )
     left = [shift(act[0], 1), None]
     right = [None, shift(act[1], -1)]
-    g_far = [swap(g) for g in g_near]
-
-    def join_w(a, b, c, e, out_ref):
-        for k, ref in enumerate((a, b, c, e)):
-            out_ref[:, k * width : (k + 1) * width] = ref[...]
-
-    w_own = run(
-        join_w, of((piece, lanes)), w_near, [VMEM] * NZ, after=(act[0],), name="w_join"
-    )
+    g_far = [swap(g_own)]
+
+    def unpack(w0_ref, *refs):
+        packed, outs = refs[: NZ - 1], refs[NZ - 1 :]
+        outs[0][:, :width] = w0_ref[...]
+        for k in range(1, NZ):
+            outs[0][:, k * width : (k + 1) * width] = packed[k - 1][:, :width]
+            outs[k][...] = packed[k - 1][:, width:]
+
+    w_own, *g_near = run(
+        unpack, [of((piece, lanes))] + [of((piece, 2 * feats))] * 3, (w_own, *packs),
+        [VMEM] * NZ, after=(act[0], g_far[0]), out_specs=[VMEM] * NZ, name="unpack",
+    )
+    g_far += [swap(g) for g in g_near]
+    g_near = [g_own, *g_near]
 
     def move(a_ref, out_ref):
         out_ref[...] = a_ref[...]
 
     w_pair = run(
         move, of((piece, lanes)), (lax.ppermute(w_own, "dp", pair),), [VMEM],
-        after=(left[0], right[1], *g_near[1:], g_far[0]), name="w_move",
+        after=(left[0], right[1], g_far[1], g_far[3]), name="w_move",
     )
 
     def gather(x):
@@ -218,16 +216,31 @@
             x, "dp", scatter_dimension=0, tiled=True, axis_index_groups=groups
         )
 
-    term_pair = term_of(1, ())
+    def settle(place_ref, kept_ref, got_ref, *outs):
+        for k in range(NZ):
+            row = block(own_rows, (place_ref[0] + k) % NZ)
+            outs[k][...] = (kept_ref[row, :] + got_ref[row, :].astype(jnp.float32)).astype(
+                jnp.bfloat16
+            )
+
+    def spread(kept, got, after):
+        outs = run(
+            settle, [of((own_rows, feats))] * NZ, (place, kept, got), [SMEM, VMEM, VMEM],
+            after=after, out_specs=[VMEM] * NZ, name="settle",
+        )
+        return [outs[0]] + [shift(outs[k], k) for k in range(1, NZ)], outs[0]
+
+    sent0, kept0 = project(0, ())
+    got0 = swap(sent0)
+    term_pair = term_of(1, (sent0,))
     term_own = term_of(0, (term_pair,))
-    sent0, kept0 = project(0, (term_own,))
-    got0 = swap(sent0)
+    quarters0, last = spread(kept0, got0, (term_own,))
     bf16, f32 = jnp.bfloat16, jnp.float32
-    far = rows_term(2, (bf16, bf16), (sent0,))
+    far = rows_term(2, (bf16, bf16), (last,))
     up = shift(far[0], 1)
     down = shift(far[1], -1)
     right_top, right_bottom = rows_term(3, (f32, bf16), (far[0],))
-    left_top, left_bottom = rows_term(1, (bf16, f32), (right_bottom,))
+    left_top, left_bottom = rows_term(1, (bf16, f32), (right_bottom, *quarters0[1:]))
     from_left_bottom = shift(right_bottom, 1)
     from_right_top = shift(left_top, -1)
 
@@ -247,23 +260,8 @@
     term_pair = scatter(term_pair)
     term_own = scatter(term_own)
 
-    def settle(place_ref, kept_ref, got_ref, *outs):
-        for k in range(NZ):
-            row = block(own_rows, (place_ref[0] + k) % NZ)
-            outs[k][...] = (kept_ref[row, :] + got_ref[row, :].astype(jnp.float32)).astype(
-                jnp.bfloat16
-            )
-
-    def spread(kept, got, after):
-        outs = run(
-            settle, [of((own_rows, feats))] * NZ, (place, kept, got), [SMEM, VMEM, VMEM],
-            after=after, out_specs=[VMEM] * NZ, name="settle",
-        )
-        return [outs[0]] + [shift(outs[k], k) for k in range(1, NZ)], outs[0]
-
-    quarters0, last = spread(kept0, got0, (stay, term_pair, from_left_bottom, from_right_top))
     term_pair = lax.ppermute(term_pair, "dp", pair)
-    quarters1, last = spread(kept1, got1, (term_pair, *quarters0[1:]))
+    quarters1, last = spread(kept1, got1, (stay, term_pair, from_left_bottom, from_right_top))
 
     def add_rows(place_ref, counts_ref, stay_ref, *refs):
         slot = lax.broadcasted_iota(jnp.int32, (1, width), 1) // HD

time: 288 us -> 360 us (1.25)
  waiting for transfers between devices: 89.9 us -> 176 us
  starting transfers between devices: 57.4 us -> 41.3 us
    ppermute x27 -> x24, waiting for transfers between devices: 51.8 us -> 92.7 us  [shift(): return lax.ppermute(value, 'tensor', ring(step))]
    ppermute x6, waiting for transfers between devices: 36.8 us -> 75.1 us  [swap(): return lax.ppermute(value, 'tensor', SWAP)]
    ppermute x6, starting transfers between devices: 16.5 us -> 8.61 us  [swap(): return lax.ppermute(value, 'tensor', SWAP)]
    ppermute x27 -> x24, starting transfers between devices: 38.4 us -> 30.7 us  [shift(): return lax.ppermute(value, 'tensor', ring(step))]
    ppermute x1, waiting for transfers between devices: 1.15 us -> 8.38 us  [per_device(): term_pair = lax.ppermute(term_pair, 'dp', pair)]
    unnamed x76 -> x70, local copies, waits for them, and re-layouts: 10.3 us -> 11.3 us
    pallas_call x21 -> x20, Pallas kernels: 116 us -> 115 us  [run(): pl.pallas_call(kernel, out_shape=out, grid=grid, in_specs=list(specs) + [...]
  transfers between devices with their start and end apart: 39 -> 36, of which waited for: 16 -> 18; matrix products, arithmetic and copies ran while one was open for 0% -> 0% of each run, Pallas kernels for 38% -> 29%
where the time goes in v5:
time: 360 us; the launch traced here: 359 us
  waiting for transfers between devices  176 us (49%)
  Pallas kernels  115 us (32%)
  starting transfers between devices  41.3 us (11%)
  between operations  14 us (4%)
  local copies, waits for them, and re-layouts  11.3 us (3%)
    pallas_call x20, Pallas kernels, run(): pl.pallas_call(kernel, out_shape=out, grid=grid, in_specs=list(specs) + [...  115 us
    ppermute x24, waiting for transfers between devices, shift(): return lax.ppermute(value, 'tensor', ring(step))  92.7 us
    ppermute x6, waiting for transfers between devices, swap(): return lax.ppermute(value, 'tensor', SWAP)  75.1 us
    ppermute x24, starting transfers between devices, shift(): return lax.ppermute(value, 'tensor', ring(step))  30.7 us
    unnamed x70, local copies, waits for them, and re-layouts  11.3 us
    ppermute x6, starting transfers between devices, swap(): return lax.ppermute(value, 'tensor', SWAP)  8.61 us
    ppermute x1, waiting for transfers between devices, per_device(): term_pair = lax.ppermute(term_pair, 'dp', pair)  8.38 us
  transfers between devices with their start and end apart: 36, of which 18 were waited for; matrix products, arithmetic and copies ran while one was open for 0% of the time, Pallas kernels for 29%

profile of v5, /device:TPU:0, one launch (start us, length us, event | category | flops | bytes accessed | tf_op | source)
XLA Modules:
  0.0 358.8 jit_solution(13571691263045846779)
XLA Ops:
  7.9 4.0 %split.1 = (bf16[128,768]{1,0:T(8,128)(2,1)}, bf16[128,2048]{1,0:T(8,128)(2,1)}, bf16[128,2816]{1,0:T(8,128)(2,1)}, bf16[128,2816]{1,0:T(8,128)(2,1)}, bf16[128,2816]{1,0:T(8,128)(2,1)}) custom-call(s32[4]{0:T(128)} %pad_add_fusion.refs_0_, bf16[512,768]{1,0:T(8,128)(2,1)} %refs_1_.3, bf16[128,8192]{1,0:T(8,128)(2,1)} %bitcast.8), custom_call_target="tpu_custom_call" | custom-call | flops 1000 | bytes 1000 | tf_op jit(solution)/shard_map/split/pallas_call | solution.py:47
  11.9 2.0 collective-permute-start
  13.9 3.6 collective-permute-start.1
  18.5 3.2 collective-permute-start.3
  21.7 2.7 mask.1
  24.4 8.7 %collective-permute-done.3.refs_5_.refs_1_ = bf16[128,2048]{1,0:T(8,128)(2,1)S(1)} collective-permute-done((bf16[128,2048]{1,0:T(8,128)(2,1)}, bf16[128,2048]{1,0:T(8,128)(2,1)S(1)}, u32[]{:S(2)}, u32[]{:S(2)}) %collective-permute-start.3) | collective-permute-done | bytes 524320 | tf_op jit(solution)/shard_map/ppermute | solution.py:30
  33.0 16.0 %collective-permute-done.1.refs_2_ = bf16[128,2816]{1,0:T(8,128)(2,1)S(1)} collective-permute-done((bf16[128,2816]{1,0:T(8,128)(2,1)}, bf16[128,2816]{1,0:T(8,128)(2,1)S(1)}, u32[]{:S(2)}, u32[]{:S(2)}) %collective-permute-start.1) | collective-permute-done | bytes 720928 | tf_op jit(solution)/shard_map/ppermute | solution.py:26
  50.1 3.2 unpack.1
  53.4 1.9 collective-permute-start.7
  57.0 2.9 collective-permute-start.11
  60.6 11.7 %collective-permute-done.7.refs_8_.refs_2_ = bf16[512,768]{1,0:T(8,128)(2,1)S(1)} collective-permute-done((bf16[512,768]{1,0:T(8,128)(2,1)S(1)}, bf16[512,768]{1,0:T(8,128)(2,1)S(1)}, u32[]{:S(2)}, u32[]{:S(2)}) %collective-permute-start.7) | collective-permute-done | bytes 786464 | tf_op jit(solution)/shard_map/ppermute | solution.py:26
  72.2 3.4 collective-permute-done.4.refs_3_.refs_1_
  75.7 14.2 %collective-permute-done.11.refs_2_.refs_3_ = bf16[128,2048]{1,0:T(8,128)(2,1)S(1)} collective-permute-done((bf16[128,2048]{1,0:T(8,128)(2,1)}, bf16[128,2048]{1,0:T(8,128)(2,1)S(1)}, u32[]{:S(2)}, u32[]{:S(2)}) %collective-permute-start.11) | collective-permute-done | bytes 524320 | tf_op jit(solution)/shard_map/ppermute | solution.py:30
  89.8 9.8 %collective-permute-done.13.refs_4_ = bf16[128,2048]{1,0:T(8,128)(2,1)S(1)} collective-permute-done((bf16[128,2048]{1,0:T(8,128)(2,1)}, bf16[128,2048]{1,0:T(8,128)(2,1)S(1)}, u32[]{:S(2)}, u32[]{:S(2)}) %collective-permute-start.13) | collective-permute-done | bytes 524320 | tf_op jit(solution)/shard_map/ppermute | solution.py:30
  101.3 2.1 w_move.1
  103.8 2.9 collective-permute-start.9
  109.4 12.4 %collective-permute-done.12.refs_3_ = bf16[128,2048]{1,0:T(8,128)(2,1)S(1)} collective-permute-done((bf16[128,2048]{1,0:T(8,128)(2,1)}, bf16[128,2048]{1,0:T(8,128)(2,1)S(1)}, u32[]{:S(2)}, u32[]{:S(2)}) %collective-permute-start.12) | collective-permute-done | bytes 524320 | tf_op jit(solution)/shard_map/ppermute | solution.py:30
  122.6 4.7 %g_join.1.refs_0_ = bf16[1024,2048]{1,0:T(8,128)(2,1)} custom-call(s32[4]{0:T(128)} %pad_add_fusion.refs_0_, bf16[128,2048]{1,0:T(8,128)(2,1)} %copy-done.9, bf16[128,2048]{1,0:T(8,128)(2,1)} %copy-done.10, bf16[128,2048]{1,0:T(8,128)(2,1)} %copy-done.25, bf16[128,2048]{1,0:T(8,128)(2,1)} %copy-done.11, bf16[128,2048]{1,0:T(8,128)(2,1)} %get-tuple-element.43.refs_5_, ...), custom_call_target="tpu_custom_call" | custom-call | flops 1000 | bytes 1000 | tf_op jit(solution)/shard_map/g_join/pallas_call | solution.py:47
  127.3 11.7 %collective-permute-done.8.refs_6_ = bf16[512,768]{1,0:T(8,128)(2,1)} collective-permute-done((bf16[512,768]{1,0:T(8,128)(2,1)}, bf16[512,768]{1,0:T(8,128)(2,1)}, u32[]{:S(2)}, u32[]{:S(2)}) %collective-permute-start.8) | collective-permute-done | bytes 786464 | tf_op jit(solution)/shard_map/ppermute | solution.py:26
  139.8 11.7 %project.2 = (bf16[512,1024]{1,0:T(8,128)(2,1)}, f32[512,1024]{1,0:T(8,128)}) custom-call(bf16[1024,3072]{1,0:T(8,128)(2,1)} %all-gather.3.cloned.1.call-done.refs_0_.refs_1_, bf16[512,768]{1,0:T(8,128)(2,1)} %get-tuple-element.42.refs_4_.refs_1_, bf16[512,768]{1,0:T(8,128)(2,1)} %get-tuple-element.45.refs_2_, bf16[512,768]{1,0:T(8,128)(2,1)} %copy-done.2, ...), custom_call_target="tpu_custom_call" | custom-call | flops 1000 | bytes 1000 | tf_op jit(solution)/shard_map/project/pallas_call | solution.py:47
  151.4 11.7 %term.2.refs_9_ = bf16[1024,3072]{1,0:T(8,128)(2,1)} custom-call(bf16[1024,2048]{1,0:T(8,128)(2,1)} %g_join.1.refs_0_, bf16[512,768]{1,0:T(8,128)(2,1)} %get-tuple-element.42.refs_4_.refs_1_, bf16[512,768]{1,0:T(8,128)(2,1)} %get-tuple-element.45.refs_2_, bf16[512,768]{1,0:T(8,128)(2,1)} %copy-done.2, bf16[512,768]{1,0:T(8,128)(2,1)} %copy-done.4, ...), custom_call_target="tpu_custom_call" | custom-call | flops 1000 | bytes 1000 | tf_op jit(solution)/shard_map/term/pallas_call | solution.py:47
  163.2 11.5 %term.3.refs_3_ = bf16[1024,3072]{1,0:T(8,128)(2,1)} custom-call(bf16[1024,2048]{1,0:T(8,128)(2,1)} %g_join.1.refs_0_, bf16[512,768]{1,0:T(8,128)(2,1)} %get-tuple-element.42.refs_4_.refs_1_, bf16[512,768]{1,0:T(8,128)(2,1)} %get-tuple-element.45.refs_2_, bf16[512,768]{1,0:T(8,128)(2,1)} %copy-done.2, bf16[512,768]{1,0:T(8,128)(2,1)} %copy-done.4, ...), custom_call_target="tpu_custom_call" | custom-call | flops 1000 | bytes 1000 | tf_op jit(solution)/shard_map/term/pallas_call | solution.py:47
  176.5 23.7 %collective-permute-done.10.refs_2_ = bf16[512,1024]{1,0:T(8,128)(2,1)S(1)} collective-permute-done((bf16[512,1024]{1,0:T(8,128)(2,1)S(1)}, bf16[512,1024]{1,0:T(8,128)(2,1)S(1)}, u32[]{:S(2)}, u32[]{:S(2)}) %collective-permute-start.10) | collective-permute-done | bytes 1048608 | tf_op jit(solution)/shard_map/ppermute | solution.py:30
  201.1 3.0 settle.2
  204.2 7.2 %rows_term.4 = (bf16[512,768]{1,0:T(8,128)(2,1)}, bf16[512,768]{1,0:T(8,128)(2,1)}) custom-call(bf16[1024,2048]{1,0:T(8,128)(2,1)} %g_join.1.refs_0_, bf16[1024,3072]{1,0:T(8,128)(2,1)} %all-gather.3.cloned.1.call-done.refs_0_.refs_1_, bf16[1024,3072]{1,0:T(8,128)(2,1)} %all-gather.5.cloned.1.call-done.refs_2_.refs_0_, ...), custom_call_target="tpu_custom_call" | custom-call | flops 1000 | bytes 1000 | tf_op jit(solution)/shard_map/rows_term/pallas_call | solution.py:47
  211.3 2.7 collective-permute-start.19
  214.3 7.7 %rows_term.5 = (f32[512,768]{1,0:T(8,128)}, bf16[512,768]{1,0:T(8,128)(2,1)}) custom-call(bf16[1024,2048]{1,0:T(8,128)(2,1)} %g_join.1.refs_0_, bf16[1024,3072]{1,0:T(8,128)(2,1)} %all-gather.3.cloned.1.call-done.refs_0_.refs_1_, bf16[1024,3072]{1,0:T(8,128)(2,1)} %all-gather.5.cloned.1.call-done.refs_2_.refs_0_, bf16[512,768]{1,0:T(8,128)(2,1)} %get-tuple-element.55.refs_3_), custom_call_target="tpu_custom_call" | custom-call | flops 1000 | bytes 1000 | tf_op jit(solution)/shard_map/rows_term/pallas_call | solution.py:47
  223.5 3.0 collective-permute-start.15
  226.6 15.0 %collective-permute-done.14.refs_4_.refs_2_ = bf16[128,1024]{1,0:T(8,128)(2,1)S(1)} collective-permute-done((bf16[128,1024]{1,0:T(8,128)(2,1)S(1)}, bf16[128,1024]{1,0:T(8,128)(2,1)S(1)}, u32[]{:S(2)}, u32[]{:S(2)}) %collective-permute-start.14) | collective-permute-done | bytes 262176 | tf_op jit(solution)/shard_map/ppermute | solution.py:26
  241.6 16.4 %collective-permute-done.15.refs_5_.refs_3_ = bf16[128,1024]{1,0:T(8,128)(2,1)S(1)} collective-permute-done((bf16[128,1024]{1,0:T(8,128)(2,1)S(1)}, bf16[128,1024]{1,0:T(8,128)(2,1)S(1)}, u32[]{:S(2)}, u32[]{:S(2)}) %collective-permute-start.15) | collective-permute-done | bytes 262176 | tf_op jit(solution)/shard_map/ppermute | solution.py:26
  259.4 7.2 %rows_term.6 = (bf16[512,768]{1,0:T(8,128)(2,1)}, f32[512,768]{1,0:T(8,128)}) custom-call(bf16[1024,2048]{1,0:T(8,128)(2,1)} %g_join.1.refs_0_, bf16[1024,3072]{1,0:T(8,128)(2,1)} %all-gather.3.cloned.1.call-done.refs_0_.refs_1_, bf16[1024,3072]{1,0:T(8,128)(2,1)} %all-gather.5.cloned.1.call-done.refs_2_.refs_0_, ...), custom_call_target="tpu_custom_call" | custom-call | flops 1000 | bytes 1000 | tf_op jit(solution)/shard_map/rows_term/pallas_call | solution.py:47
  267.8 3.6 %add_far.1 = (bf16[512,768]{1,0:T(8,128)(2,1)}, bf16[512,768]{1,0:T(8,128)(2,1)}) custom-call(f32[512,768]{1,0:T(8,128)} %get-tuple-element.56.refs_0_, bf16[512,768]{1,0:T(8,128)(2,1)} %copy-done.21, f32[512,768]{1,0:T(8,128)} %get-tuple-element.58.refs_2_, bf16[512,768]{1,0:T(8,128)(2,1)} %copy-done.20, bf16[512,768]{1,0:T(8,128)(2,1)} %get-tuple-element.60.refs_4_), custom_call_target="tpu_custom_call" | custom-call | flops 1000 | bytes 1000 | tf_op jit(solution)/shard_map/add_far/pallas_call | solution.py:47
  271.4 11.6 %project.3 = (bf16[512,1024]{1,0:T(8,128)(2,1)}, f32[512,1024]{1,0:T(8,128)}) custom-call(bf16[1024,3072]{1,0:T(8,128)(2,1)} %all-gather.5.cloned.1.call-done.refs_2_.refs_0_, bf16[512,768]{1,0:T(8,128)(2,1)} %get-tuple-element.42.refs_4_.refs_1_, bf16[512,768]{1,0:T(8,128)(2,1)} %get-tuple-element.45.refs_2_, bf16[512,768]{1,0:T(8,128)(2,1)} %copy-done.2, ...), custom_call_target="tpu_custom_call" | custom-call | flops 1000 | bytes 1000 | tf_op jit(solution)/shard_map/project/pallas_call | solution.py:47
  284.0 2.4 collective-permute-start.28
  286.5 7.9 %rows_term.7.refs_3_.refs_2_ = f32[1024,768]{1,0:T(8,128)} custom-call(bf16[1024,2048]{1,0:T(8,128)(2,1)} %g_join.1.refs_0_, bf16[1024,3072]{1,0:T(8,128)(2,1)} %all-gather.3.cloned.1.call-done.refs_0_.refs_1_, bf16[1024,3072]{1,0:T(8,128)(2,1)} %all-gather.5.cloned.1.call-done.refs_2_.refs_0_, f32[512,1024]{1,0:T(8,128)} %get-tuple-element.62.refs_3_.refs_1_), custom_call_target="tpu_custom_call" | custom-call | flops 1000 | bytes 1000 | tf_op jit(solution)/shard_map/rows_term/pallas_call | solution.py:47
  294.4 9.9 %collective-permute-done.23.refs_6_.refs_5_ = bf16[512,768]{1,0:T(8,128)(2,1)S(1)} collective-permute-done((bf16[512,768]{1,0:T(8,128)(2,1)}, bf16[512,768]{1,0:T(8,128)(2,1)S(1)}, u32[]{:S(2)}, u32[]{:S(2)}) %collective-permute-start.23) | collective-permute-done | bytes 786464 | tf_op jit(solution)/shard_map/ppermute | solution.py:26
  304.4 6.4 %collective-permute-done.20.refs_2_ = bf16[512,1024]{1,0:T(8,128)(2,1)S(1)} collective-permute-done((bf16[512,1024]{1,0:T(8,128)(2,1)}, bf16[512,1024]{1,0:T(8,128)(2,1)S(1)}, u32[]{:S(2)}, u32[]{:S(2)}) %collective-permute-start.20) | collective-permute-done | bytes 1048608 | tf_op jit(solution)/shard_map/ppermute | solution.py:30
  310.8 8.4 %collective-permute-done.21.refs_4_.refs_1_ = bf16[128,3072]{1,0:T(8,128)(2,1)S(1)} collective-permute-done((bf16[128,3072]{1,0:T(8,128)(2,1)}, bf16[128,3072]{1,0:T(8,128)(2,1)S(1)}, u32[]{:S(2)}, u32[]{:S(2)}) %collective-permute-start.21) | collective-permute-done | bytes 786464 | tf_op jit(solution)/shard_map/ppermute | solution.py:263
  320.1 3.0 settle.3
  323.1 2.3 add_terms.1
  325.3 2.0 collective-permute-start.24
  327.4 2.2 collective-permute-start.25
  331.5 1.9 collective-permute-done.29.refs_2_
  333.8 4.5 %add_rows.1 = bf16[1024,768]{1,0:T(8,128)(2,1)} custom-call(s32[4]{0:T(128)} %pad_add_fusion.refs_0_, s32[8]{0:T(128)} %refs_1_.5, f32[1024,768]{1,0:T(8,128)} %rows_term.7.refs_3_.refs_2_, bf16[512,768]{1,0:T(8,128)(2,1)} %collective-permute-done.27.refs_3_, bf16[512,768]{1,0:T(8,128)(2,1)} %copy-done.6, bf16[512,768]{1,0:T(8,128)(2,1)} %copy-done.7, ...), custom_call_target="tpu_custom_call" | custom-call | flops 1000 | bytes 1000 | tf_op jit(solution)/shard_map/add_rows/pallas_call | solution.py:47
  338.3 4.0 %collective-permute-done.30.refs_3_ = bf16[128,768]{1,0:T(8,128)(2,1)S(1)} collective-permute-done((bf16[128,768]{1,0:T(8,128)(2,1)}, bf16[128,768]{1,0:T(8,128)(2,1)S(1)}, u32[]{:S(2)}, u32[]{:S(2)}) %collective-permute-start.30) | collective-permute-done | bytes 196640 | tf_op jit(solution)/shard_map/ppermute | solution.py:26
  342.3 2.0 collective-permute-done.31.refs_4_
  345.0 2.5 join_term.1
  349.0 3.3 join_out.1
  (119 shorter events, 25.2 us)
Async XLA Ops:
  7.2 132.6 %all-gather.3.cloned.1.call-start = ((), (), s32[]{:S(2)}) async-start(), calls=%async_computation.2 | async-start | bytes 7077888 | tf_op jit(solution)/shard_map/all_gather | solution.py:138
  11.9 21.1 %collective-permute-start = (bf16[128,2816]{1,0:T(8,128)(2,1)}, bf16[128,2816]{1,0:T(8,128)(2,1)S(1)}, u32[]{:S(2)}, u32[]{:S(2)}) collective-permute-start(bf16[128,2816]{1,0:T(8,128)(2,1)} %get-tuple-element.39), channel_id=1, source_target_pairs={{0,2},{1,3},{2,4},{3,5},{4,6},{5,7},{6,0},{7,1},{8,10},{9,11},{10,... | collective-permute-start | bytes 2162696 | tf_op jit(solution)/shard_map/ppermute | solution.py:26
  13.9 35.1 %collective-permute-start.1 = (bf16[128,2816]{1,0:T(8,128)(2,1)}, bf16[128,2816]{1,0:T(8,128)(2,1)S(1)}, u32[]{:S(2)}, u32[]{:S(2)}) collective-permute-start(bf16[128,2816]{1,0:T(8,128)(2,1)} %get-tuple-element.40), channel_id=1, source_target_pairs={{0,4},{1,5},{2,6},{3,7},{4,0},{5,1},{6,2},{7,3},{8,12},{9,13},{10,... | collective-permute-start | bytes 2162696 | tf_op jit(solution)/shard_map/ppermute | solution.py:26
  17.5 31.5 %collective-permute-start.2 = (bf16[128,2816]{1,0:T(8,128)(2,1)}, bf16[128,2816]{1,0:T(8,128)(2,1)S(1)}, u32[]{:S(2)}, u32[]{:S(2)}) collective-permute-start(bf16[128,2816]{1,0:T(8,128)(2,1)} %get-tuple-element.41), channel_id=1, source_target_pairs={{0,6},{1,7},{2,0},{3,1},{4,2},{5,3},{6,4},{7,5},{8,14},{9,15},{10,... | collective-permute-start | bytes 2162696 | tf_op jit(solution)/shard_map/ppermute | solution.py:26
  18.5 14.5 %collective-permute-start.3 = (bf16[128,2048]{1,0:T(8,128)(2,1)}, bf16[128,2048]{1,0:T(8,128)(2,1)S(1)}, u32[]{:S(2)}, u32[]{:S(2)}) collective-permute-start(bf16[128,2048]{1,0:T(8,128)(2,1)} %get-tuple-element.43.refs_5_), channel_id=1, source_target_pairs={{0,1},{1,0},{2,3},{3,2},{4,5},{5,4},{6,7},{7,6},{8,9},{9,8},{10,11... | collective-permute-start | bytes 1572872 | tf_op jit(solution)/shard_map/ppermute | solution.py:30
  33.0 16.0 %copy-start.9 = (bf16[128,2048]{1,0:T(8,128)(2,1)}, bf16[128,2048]{1,0:T(8,128)(2,1)S(1)}, u32[]{:S(2)}) copy-start(bf16[128,2048]{1,0:T(8,128)(2,1)S(1)} %collective-permute-done.3.refs_5_.refs_1_) | copy-start | bytes 1572868
  33.0 16.0 %copy-start.22 = (bf16[128,2816]{1,0:T(8,128)(2,1)}, bf16[128,2816]{1,0:T(8,128)(2,1)S(1)}, u32[]{:S(2)}) copy-start(bf16[128,2816]{1,0:T(8,128)(2,1)S(1)} %collective-permute-done.refs_1_) | copy-start | bytes 2162692
  53.3 150.9 %all-gather.5.cloned.1.call-start = ((), (), s32[]{:S(2)}) async-start(), calls=%async_computation.3 | async-start | bytes 7077888 | tf_op jit(solution)/shard_map/all_gather | solution.py:138
  53.4 18.9 %collective-permute-start.7 = (bf16[512,768]{1,0:T(8,128)(2,1)S(1)}, bf16[512,768]{1,0:T(8,128)(2,1)S(1)}, u32[]{:S(2)}, u32[]{:S(2)}) collective-permute-start(bf16[512,768]{1,0:T(8,128)(2,1)S(1)} %copy-done.3), channel_id=1, source_target_pairs={{0,6},{1,7},{2,0},{3,1},{4,2},{5,3},{6,4},{7,5},{8,14},{9,15},{10,... | collective-permute-start | bytes 2359304 | tf_op jit(solution)/shard_map/ppermute | solution.py:26
  55.3 20.4 %collective-permute-start.4 = (bf16[512,768]{1,0:T(8,128)(2,1)S(1)}, bf16[512,768]{1,0:T(8,128)(2,1)S(1)}, u32[]{:S(2)}, u32[]{:S(2)}) collective-permute-start(bf16[512,768]{1,0:T(8,128)(2,1)S(1)} %copy-done), channel_id=1, source_target_pairs={{0,2},{1,3},{2,4},{3,5},{4,6},{5,7},{6,0},{7,1},{8,10},{9,11},{10,... | collective-permute-start | bytes 2359304 | tf_op jit(solution)/shard_map/ppermute | solution.py:26
  55.5 44.1 %collective-permute-start.17 = (bf16[128,3072]{1,0:T(8,128)(2,1)}, bf16[128,3072]{1,0:T(8,128)(2,1)S(1)}, u32[]{:S(2)}, u32[]{:S(2)}) collective-permute-start(bf16[128,3072]{1,0:T(8,128)(2,1)} %get-tuple-element.44), channel_id=1, source_target_pairs={{0,64},{8,72},{16,80},{24,88},{32,96},{40,104},{48,112},{56,120},{... | collective-permute-start | bytes 2359304 | tf_op jit(solution)/shard_map/ppermute | solution.py:133
  57.0 32.8 %collective-permute-start.11 = (bf16[128,2048]{1,0:T(8,128)(2,1)}, bf16[128,2048]{1,0:T(8,128)(2,1)S(1)}, u32[]{:S(2)}, u32[]{:S(2)}) collective-permute-start(bf16[128,2048]{1,0:T(8,128)(2,1)} %get-tuple-element.48.refs_6_), channel_id=1, source_target_pairs={{0,1},{1,0},{2,3},{3,2},{4,5},{5,4},{6,7},{7,6},{8,9},{9,8},{10,11... | collective-permute-start | bytes 1572872 | tf_op jit(solution)/shard_map/ppermute | solution.py:30
  59.9 39.6 %collective-permute-start.13 = (bf16[128,2048]{1,0:T(8,128)(2,1)}, bf16[128,2048]{1,0:T(8,128)(2,1)S(1)}, u32[]{:S(2)}, u32[]{:S(2)}) collective-permute-start(bf16[128,2048]{1,0:T(8,128)(2,1)} %get-tuple-element.50.refs_8_), channel_id=1, source_target_pairs={{0,1},{1,0},{2,3},{3,2},{4,5},{5,4},{6,7},{7,6},{8,9},{9,8},{10,11... | collective-permute-start | bytes 1572872 | tf_op jit(solution)/shard_map/ppermute | solution.py:30
  72.2 27.3 %copy-start.1 = (bf16[512,768]{1,0:T(8,128)(2,1)}, bf16[512,768]{1,0:T(8,128)(2,1)S(1)}, u32[]{:S(2)}) copy-start(bf16[512,768]{1,0:T(8,128)(2,1)S(1)} %collective-permute-done.7.refs_8_.refs_2_) | copy-start | bytes 2359300
  75.7 23.9 %copy-start.2 = (bf16[512,768]{1,0:T(8,128)(2,1)}, bf16[512,768]{1,0:T(8,128)(2,1)S(1)}, u32[]{:S(2)}) copy-start(bf16[512,768]{1,0:T(8,128)(2,1)S(1)} %collective-permute-done.4.refs_3_.refs_1_) | copy-start | bytes 2359300
  89.8 9.8 %copy-start.10 = (bf16[128,2048]{1,0:T(8,128)(2,1)}, bf16[128,2048]{1,0:T(8,128)(2,1)S(1)}, u32[]{:S(2)}) copy-start(bf16[128,2048]{1,0:T(8,128)(2,1)S(1)} %collective-permute-done.11.refs_2_.refs_3_) | copy-start | bytes 1572868
  103.4 180.3 %reduce-scatter.3.cloned.1.call-start = ((), (), s32[]{:S(2)}) async-start(), calls=%async_computation.4 | async-start | bytes 7077888 | tf_op jit(solution)/shard_map/reduce_scatter | solution.py:215
  103.4 23.9 %collective-permute-start.5 = (bf16[512,768]{1,0:T(8,128)(2,1)S(1)}, bf16[512,768]{1,0:T(8,128)(2,1)S(1)}, u32[]{:S(2)}, u32[]{:S(2)}) collective-permute-start(bf16[512,768]{1,0:T(8,128)(2,1)S(1)} %copy-done.3), channel_id=1, source_target_pairs={{0,2},{1,3},{2,4},{3,5},{4,6},{5,7},{6,0},{7,1},{8,10},{9,11},{10,... | collective-permute-start | bytes 2359304 | tf_op jit(solution)/shard_map/ppermute | solution.py:26
  103.8 23.5 %collective-permute-start.9 = (bf16[512,768]{1,0:T(8,128)(2,1)S(1)}, bf16[512,768]{1,0:T(8,128)(2,1)S(1)}, u32[]{:S(2)}, u32[]{:S(2)}) collective-permute-start(bf16[512,768]{1,0:T(8,128)(2,1)S(1)} %copy-done), channel_id=1, source_target_pairs={{0,6},{1,7},{2,0},{3,1},{4,2},{5,3},{6,4},{7,5},{8,14},{9,15},{10,... | collective-permute-start | bytes 2359304 | tf_op jit(solution)/shard_map/ppermute | solution.py:26
  106.8 32.3 %collective-permute-start.8 = (bf16[512,768]{1,0:T(8,128)(2,1)}, bf16[512,768]{1,0:T(8,128)(2,1)}, u32[]{:S(2)}, u32[]{:S(2)}) collective-permute-start(bf16[512,768]{1,0:T(8,128)(2,1)} %copy-done.1), channel_id=1, source_target_pairs={{0,6},{1,7},{2,0},{3,1},{4,2},{5,3},{6,4},{7,5},{8,14},{9,15},{10,... | collective-permute-start | bytes 2359304 | tf_op jit(solution)/shard_map/ppermute | solution.py:26
  108.5 31.3 %collective-permute-start.6 = (bf16[512,768]{1,0:T(8,128)(2,1)}, bf16[512,768]{1,0:T(8,128)(2,1)}, u32[]{:S(2)}, u32[]{:S(2)}) collective-permute-start(bf16[512,768]{1,0:T(8,128)(2,1)} %copy-done.2), channel_id=1, source_target_pairs={{0,2},{1,3},{2,4},{3,5},{4,6},{5,7},{6,0},{7,1},{8,10},{9,11},{10,... | collective-permute-start | bytes 2359304 | tf_op jit(solution)/shard_map/ppermute | solution.py:26
  108.8 13.1 %collective-permute-start.12 = (bf16[128,2048]{1,0:T(8,128)(2,1)}, bf16[128,2048]{1,0:T(8,128)(2,1)S(1)}, u32[]{:S(2)}, u32[]{:S(2)}) collective-permute-start(bf16[128,2048]{1,0:T(8,128)(2,1)} %get-tuple-element.49.refs_7_), channel_id=1, source_target_pairs={{0,1},{1,0},{2,3},{3,2},{4,5},{5,4},{6,7},{7,6},{8,9},{9,8},{10,11... | collective-permute-start | bytes 1572872 | tf_op jit(solution)/shard_map/ppermute | solution.py:30
  127.3 12.5 %copy-start.4 = (bf16[512,768]{1,0:T(8,128)(2,1)}, bf16[512,768]{1,0:T(8,128)(2,1)S(1)}, u32[]{:S(2)}) copy-start(bf16[512,768]{1,0:T(8,128)(2,1)S(1)} %collective-permute-done.5.refs_4_) | copy-start | bytes 2359300
  127.3 12.5 %copy-start.5 = (bf16[512,768]{1,0:T(8,128)(2,1)}, bf16[512,768]{1,0:T(8,128)(2,1)S(1)}, u32[]{:S(2)}) copy-start(bf16[512,768]{1,0:T(8,128)(2,1)S(1)} %collective-permute-done.9.refs_7_) | copy-start | bytes 2359300
  163.1 159.9 %reduce-scatter.5.cloned.1.call-start = ((), (), s32[]{:S(2)}) async-start(), calls=%async_computation.5 | async-start | bytes 7077888 | tf_op jit(solution)/shard_map/reduce_scatter | solution.py:215
  175.9 24.3 %collective-permute-start.10 = (bf16[512,1024]{1,0:T(8,128)(2,1)S(1)}, bf16[512,1024]{1,0:T(8,128)(2,1)S(1)}, u32[]{:S(2)}, u32[]{:S(2)}) collective-permute-start(bf16[512,1024]{1,0:T(8,128)(2,1)S(1)} %copy-done.16), channel_id=1, source_target_pairs={{0,1},{1,0},{2,3},{3,2},{4,5},{5,4},{6,7},{7,6},{8,9},{9,8},{10,11... | collective-permute-start | bytes 3145736 | tf_op jit(solution)/shard_map/ppermute | solution.py:30
  204.2 9.9 %copy-start.34 = (bf16[128,1024]{1,0:T(8,128)(2,1)S(1)}, bf16[128,1024]{1,0:T(8,128)(2,1)}, u32[]{:S(2)}) copy-start(bf16[128,1024]{1,0:T(8,128)(2,1)} %get-tuple-element.52) | copy-start | bytes 786436
  211.3 55.3 %collective-permute-start.19 = (bf16[512,768]{1,0:T(8,128)(2,1)}, bf16[512,768]{1,0:T(8,128)(2,1)S(1)}, u32[]{:S(2)}, u32[]{:S(2)}) collective-permute-start(bf16[512,768]{1,0:T(8,128)(2,1)} %get-tuple-element.59), channel_id=1, source_target_pairs={{0,6},{1,7},{2,0},{3,1},{4,2},{5,3},{6,4},{7,5},{8,14},{9,15},{10,... | collective-permute-start | bytes 2359304 | tf_op jit(solution)/shard_map/ppermute | solution.py:26
  214.1 52.6 %collective-permute-start.18 = (bf16[512,768]{1,0:T(8,128)(2,1)}, bf16[512,768]{1,0:T(8,128)(2,1)S(1)}, u32[]{:S(2)}, u32[]{:S(2)}) collective-permute-start(bf16[512,768]{1,0:T(8,128)(2,1)} %get-tuple-element.55.refs_3_), channel_id=1, source_target_pairs={{0,2},{1,3},{2,4},{3,5},{4,6},{5,7},{6,0},{7,1},{8,10},{9,11},{10,... | collective-permute-start | bytes 2359304 | tf_op jit(solution)/shard_map/ppermute | solution.py:26
  214.1 27.5 %copy-start.32 = (bf16[128,1024]{1,0:T(8,128)(2,1)S(1)}, bf16[128,1024]{1,0:T(8,128)(2,1)}, u32[]{:S(2)}) copy-start(bf16[128,1024]{1,0:T(8,128)(2,1)} %get-tuple-element.54) | copy-start | bytes 786436
  214.1 27.5 %collective-permute-start.14 = (bf16[128,1024]{1,0:T(8,128)(2,1)S(1)}, bf16[128,1024]{1,0:T(8,128)(2,1)S(1)}, u32[]{:S(2)}, u32[]{:S(2)}) collective-permute-start(bf16[128,1024]{1,0:T(8,128)(2,1)S(1)} %copy-done.34), channel_id=1, source_target_pairs={{0,2},{1,3},{2,4},{3,5},{4,6},{5,7},{6,0},{7,1},{8,10},{9,11},{10,... | collective-permute-start | bytes 786440 | tf_op jit(solution)/shard_map/ppermute | solution.py:26
  222.0 64.4 %collective-permute-start.22 = (bf16[512,768]{1,0:T(8,128)(2,1)}, bf16[512,768]{1,0:T(8,128)(2,1)S(1)}, u32[]{:S(2)}, u32[]{:S(2)}) collective-permute-start(bf16[512,768]{1,0:T(8,128)(2,1)} %get-tuple-element.57.refs_3_), channel_id=1, source_target_pairs={{0,2},{1,3},{2,4},{3,5},{4,6},{5,7},{6,0},{7,1},{8,10},{9,11},{10,... | collective-permute-start | bytes 2359304 | tf_op jit(solution)/shard_map/ppermute | solution.py:26
  223.5 34.5 %collective-permute-start.15 = (bf16[128,1024]{1,0:T(8,128)(2,1)S(1)}, bf16[128,1024]{1,0:T(8,128)(2,1)S(1)}, u32[]{:S(2)}, u32[]{:S(2)}) collective-permute-start(bf16[128,1024]{1,0:T(8,128)(2,1)S(1)} %copy-done.33), channel_id=1, source_target_pairs={{0,4},{1,5},{2,6},{3,7},{4,0},{5,1},{6,2},{7,3},{8,12},{9,13},{10,... | collective-permute-start | bytes 786440 | tf_op jit(solution)/shard_map/ppermute | solution.py:26
  241.6 16.4 %copy-start.12 = (bf16[128,1024]{1,0:T(8,128)(2,1)}, bf16[128,1024]{1,0:T(8,128)(2,1)S(1)}, u32[]{:S(2)}) copy-start(bf16[128,1024]{1,0:T(8,128)(2,1)S(1)} %collective-permute-done.14.refs_4_.refs_2_) | copy-start | bytes 786436
  241.6 16.4 %collective-permute-start.16 = (bf16[128,1024]{1,0:T(8,128)(2,1)S(1)}, bf16[128,1024]{1,0:T(8,128)(2,1)S(1)}, u32[]{:S(2)}, u32[]{:S(2)}) collective-permute-start(bf16[128,1024]{1,0:T(8,128)(2,1)S(1)} %copy-done.32), channel_id=1, source_target_pairs={{0,6},{1,7},{2,0},{3,1},{4,2},{5,3},{6,4},{7,5},{8,14},{9,15},{10,... | collective-permute-start | bytes 786440 | tf_op jit(solution)/shard_map/ppermute | solution.py:26
  271.4 15.0 %copy-start.18 = (bf16[512,768]{1,0:T(8,128)(2,1)S(1)}, bf16[512,768]{1,0:T(8,128)(2,1)}, u32[]{:S(2)}) copy-start(bf16[512,768]{1,0:T(8,128)(2,1)} %get-tuple-element.61.refs_9_) | copy-start | bytes 2359300
  283.0 27.8 %collective-permute-start.20 = (bf16[512,1024]{1,0:T(8,128)(2,1)}, bf16[512,1024]{1,0:T(8,128)(2,1)S(1)}, u32[]{:S(2)}, u32[]{:S(2)}) collective-permute-start(bf16[512,1024]{1,0:T(8,128)(2,1)} %get-tuple-element.63), channel_id=1, source_target_pairs={{0,1},{1,0},{2,3},{3,2},{4,5},{5,4},{6,7},{7,6},{8,9},{9,8},{10,11... | collective-permute-start | bytes 3145736 | tf_op jit(solution)/shard_map/ppermute | solution.py:30
  283.7 20.7 %collective-permute-start.23 = (bf16[512,768]{1,0:T(8,128)(2,1)}, bf16[512,768]{1,0:T(8,128)(2,1)S(1)}, u32[]{:S(2)}, u32[]{:S(2)}) collective-permute-start(bf16[512,768]{1,0:T(8,128)(2,1)} %get-tuple-element.60.refs_4_), channel_id=1, source_target_pairs={{0,6},{1,7},{2,0},{3,1},{4,2},{5,3},{6,4},{7,5},{8,14},{9,15},{10,... | collective-permute-start | bytes 2359304 | tf_op jit(solution)/shard_map/ppermute | solution.py:26
  283.7 35.5 %collective-permute-start.21 = (bf16[128,3072]{1,0:T(8,128)(2,1)}, bf16[128,3072]{1,0:T(8,128)(2,1)S(1)}, u32[]{:S(2)}, u32[]{:S(2)}) collective-permute-start(bf16[128,3072]{1,0:T(8,128)(2,1)} %reduce-scatter.3.cloned.1.call-done), channel_id=1, source_target_pairs={{0,64},{8,72},{16,80},{24,88},{32,96},{40,104},{48,112},{56,120},{... | collective-permute-start | bytes 2359304 | tf_op jit(solution)/shard_map/ppermute | solution.py:263
  284.0 45.6 %collective-permute-start.28 = (bf16[512,768]{1,0:T(8,128)(2,1)}, bf16[512,768]{1,0:T(8,128)(2,1)}, u32[]{:S(2)}, u32[]{:S(2)}) collective-permute-start(bf16[512,768]{1,0:T(8,128)(2,1)} %get-tuple-element.68), channel_id=1, source_target_pairs={{0,6},{1,7},{2,0},{3,1},{4,2},{5,3},{6,4},{7,5},{8,14},{9,15},{10,... | collective-permute-start | bytes 2359304 | tf_op jit(solution)/shard_map/ppermute | solution.py:26
  286.4 43.7 %collective-permute-start.27 = (bf16[512,768]{1,0:T(8,128)(2,1)S(1)}, bf16[512,768]{1,0:T(8,128)(2,1)}, u32[]{:S(2)}, u32[]{:S(2)}) collective-permute-start(bf16[512,768]{1,0:T(8,128)(2,1)S(1)} %copy-done.18), channel_id=1, source_target_pairs={{0,2},{1,3},{2,4},{3,5},{4,6},{5,7},{6,0},{7,1},{8,10},{9,11},{10,... | collective-permute-start | bytes 2359304 | tf_op jit(solution)/shard_map/ppermute | solution.py:26
  304.4 14.8 %copy-start.7 = (bf16[512,768]{1,0:T(8,128)(2,1)}, bf16[512,768]{1,0:T(8,128)(2,1)S(1)}, u32[]{:S(2)}) copy-start(bf16[512,768]{1,0:T(8,128)(2,1)S(1)} %collective-permute-done.23.refs_6_.refs_5_) | copy-start | bytes 2359300
  325.3 8.0 %collective-permute-start.29 = (bf16[128,768]{1,0:T(8,128)(2,1)}, bf16[128,768]{1,0:T(8,128)(2,1)S(1)}, u32[]{:S(2)}, u32[]{:S(2)}) collective-permute-start(bf16[128,768]{1,0:T(8,128)(2,1)} %get-tuple-element.70), channel_id=1, source_target_pairs={{0,6},{1,7},{2,0},{3,1},{4,2},{5,3},{6,4},{7,5},{8,14},{9,15},{10,... | collective-permute-start | bytes 589832 | tf_op jit(solution)/shard_map/ppermute | solution.py:26
  325.3 22.1 %collective-permute-start.24 = (bf16[128,1024]{1,0:T(8,128)(2,1)}, bf16[128,1024]{1,0:T(8,128)(2,1)S(1)}, u32[]{:S(2)}, u32[]{:S(2)}) collective-permute-start(bf16[128,1024]{1,0:T(8,128)(2,1)} %get-tuple-element.65), channel_id=1, source_target_pairs={{0,2},{1,3},{2,4},{3,5},{4,6},{5,7},{6,0},{7,1},{8,10},{9,11},{10,... | collective-permute-start | bytes 786440 | tf_op jit(solution)/shard_map/ppermute | solution.py:26
  327.4 20.1 %collective-permute-start.25 = (bf16[128,1024]{1,0:T(8,128)(2,1)}, bf16[128,1024]{1,0:T(8,128)(2,1)S(1)}, u32[]{:S(2)}, u32[]{:S(2)}) collective-permute-start(bf16[128,1024]{1,0:T(8,128)(2,1)} %get-tuple-element.66), channel_id=1, source_target_pairs={{0,4},{1,5},{2,6},{3,7},{4,0},{5,1},{6,2},{7,3},{8,12},{9,13},{10,... | collective-permute-start | bytes 786440 | tf_op jit(solution)/shard_map/ppermute | solution.py:26
  329.6 18.0 %collective-permute-start.26 = (bf16[128,1024]{1,0:T(8,128)(2,1)}, bf16[128,1024]{1,0:T(8,128)(2,1)S(1)}, u32[]{:S(2)}, u32[]{:S(2)}) collective-permute-start(bf16[128,1024]{1,0:T(8,128)(2,1)} %get-tuple-element.67), channel_id=1, source_target_pairs={{0,6},{1,7},{2,0},{3,1},{4,2},{5,3},{6,4},{7,5},{8,14},{9,15},{10,... | collective-permute-start | bytes 786440 | tf_op jit(solution)/shard_map/ppermute | solution.py:26
  330.2 12.2 %collective-permute-start.30 = (bf16[128,768]{1,0:T(8,128)(2,1)}, bf16[128,768]{1,0:T(8,128)(2,1)S(1)}, u32[]{:S(2)}, u32[]{:S(2)}) collective-permute-start(bf16[128,768]{1,0:T(8,128)(2,1)} %get-tuple-element.71), channel_id=1, source_target_pairs={{0,4},{1,5},{2,6},{3,7},{4,0},{5,1},{6,2},{7,3},{8,12},{9,13},{10,... | collective-permute-start | bytes 589832 | tf_op jit(solution)/shard_map/ppermute | solution.py:26
  333.4 10.9 %collective-permute-start.31 = (bf16[128,768]{1,0:T(8,128)(2,1)}, bf16[128,768]{1,0:T(8,128)(2,1)S(1)}, u32[]{:S(2)}, u32[]{:S(2)}) collective-permute-start(bf16[128,768]{1,0:T(8,128)(2,1)} %get-tuple-element.72), channel_id=1, source_target_pairs={{0,2},{1,3},{2,4},{3,5},{4,6},{5,7},{6,0},{7,1},{8,10},{9,11},{10,... | collective-permute-start | bytes 589832 | tf_op jit(solution)/shard_map/ppermute | solution.py:26
  (23 other events, 55.0 us)
Sparse Core Ops, SparseCore 0:
  53.4 41.2 all-gather.2
  103.5 39.5 all-gather.4
  163.2 41.2 reduce-scatter.2
  206.8 42.1 reduce-scatter.4

commit v6 on v4

--- a/solution.py
+++ b/solution.py
@@ -220,14 +220,28 @@
 
     term_pair = term_of(1, ())
     term_own = term_of(0, (term_pair,))
-    sent0, kept0 = project(0, (term_own,))
-    got0 = swap(sent0)
+    def settle(place_ref, kept_ref, got_ref, *outs):
+        for k in range(NZ):
+            row = block(own_rows, (place_ref[0] + k) % NZ)
+            outs[k][...] = (kept_ref[row, :] + got_ref[row, :].astype(jnp.float32)).astype(
+                jnp.bfloat16
+            )
+
+    def spread(kept, got, after):
+        outs = run(
+            settle, [of((own_rows, feats))] * NZ, (place, kept, got), [SMEM, VMEM, VMEM],
+            after=after, out_specs=[VMEM] * NZ, name="settle",
+        )
+        return [outs[0]] + [shift(outs[k], k) for k in range(1, NZ)], outs[0]
+
     bf16, f32 = jnp.bfloat16, jnp.float32
-    far = rows_term(2, (bf16, bf16), (sent0,))
+    far = rows_term(2, (bf16, bf16), (term_own,))
     up = shift(far[0], 1)
     down = shift(far[1], -1)
-    right_top, right_bottom = rows_term(3, (f32, bf16), (far[0],))
-    left_top, left_bottom = rows_term(1, (bf16, f32), (right_bottom,))
+    sent0, kept0 = project(0, (far[0],))
+    got0 = swap(sent0)
+    right_top, right_bottom = rows_term(3, (f32, bf16), (sent0,))
+    left_top, left_bottom = rows_term(1, (bf16, f32), (right_bottom, up, down))
     from_left_bottom = shift(right_bottom, 1)
     from_right_top = shift(left_top, -1)
 
@@ -243,27 +257,14 @@
     from_right = [from_right_top, shift(left_bottom, -1)]
     sent1, kept1 = project(1, (right_top,))
     got1 = swap(sent1)
-    stay = rows_term(0, (f32,), (kept1,))[0]
-    term_pair = scatter(term_pair)
+    quarters0, last = spread(kept0, got0, (sent1, from_left_bottom, from_right_top))
+    stay = rows_term(0, (f32,), (last,))[0]
+    quarters1, last = spread(kept1, got1, (stay, *quarters0[1:]))
+    term_pair = run(
+        move, of((piece, lanes)), (scatter(term_pair),), [VMEM], after=(stay,), name="move"
+    )
+    term_pair = lax.ppermute(term_pair, "dp", pair)
     term_own = scatter(term_own)
-
-    def settle(place_ref, kept_ref, got_ref, *outs):
-        for k in range(NZ):
-            row = block(own_rows, (place_ref[0] + k) % NZ)
-            outs[k][...] = (kept_ref[row, :] + got_ref[row, :].astype(jnp.float32)).astype(
-                jnp.bfloat16
-            )
-
-    def spread(kept, got, after):
-        outs = run(
-            settle, [of((own_rows, feats))] * NZ, (place, kept, got), [SMEM, VMEM, VMEM],
-            after=after, out_specs=[VMEM] * NZ, name="settle",
-        )
-        return [outs[0]] + [shift(outs[k], k) for k in range(1, NZ)], outs[0]
-
-    quarters0, last = spread(kept0, got0, (stay, term_pair, from_left_bottom, from_right_top))
-    term_pair = lax.ppermute(term_pair, "dp", pair)
-    quarters1, last = spread(kept1, got1, (term_pair, *quarters0[1:]))
 
     def add_rows(place_ref, counts_ref, stay_ref, *refs):
         slot = lax.broadcasted_iota(jnp.int32, (1, width), 1) // HD
@@ -311,7 +312,7 @@
 
     parts = run(
         add_terms, [of((piece, width))] * NZ, (term_own, term_pair), [VMEM] * 2,
-        after=(last,), out_specs=[VMEM] * NZ, name="add_terms",
+        after=(last, grad_rows), out_specs=[VMEM] * NZ, name="add_terms",
     )
     parts = [parts[0]] + [shift(parts[k], -k) for k in range(1, NZ)]
 

time: 288 us -> 283 us (0.983)
  waiting for transfers between devices: 89.9 us -> 82.5 us
    ppermute x6, waiting for transfers between devices: 36.8 us -> 26.8 us  [swap(): return lax.ppermute(value, 'tensor', SWAP)]
    ppermute x27, waiting for transfers between devices: 51.8 us -> 55.6 us  [shift(): return lax.ppermute(value, 'tensor', ring(step))]
    pallas_call x21 -> x22, Pallas kernels: 116 us -> 118 us  [run(): pl.pallas_call(kernel, out_shape=out, grid=grid, in_specs=list(specs) + [...]
    unnamed x76 -> x80, local copies, waits for them, and re-layouts: 10.3 us -> 12.1 us
  transfers between devices with their start and end apart: 39 -> 39, of which waited for: 16 -> 11; matrix products, arithmetic and copies ran while one was open for 0% -> 0% of each run, Pallas kernels for 38% -> 39%
where the time goes in v6:
time: 283 us
  Pallas kernels  118 us (42%)
  waiting for transfers between devices  82.5 us (29%)
  starting transfers between devices  56 us (20%)
  between operations  14.1 us (5%)
  local copies, waits for them, and re-layouts  12.1 us (4%)
    pallas_call x22, Pallas kernels, run(): pl.pallas_call(kernel, out_shape=out, grid=grid, in_specs=list(specs) + [...  118 us
    ppermute x27, waiting for transfers between devices, shift(): return lax.ppermute(value, 'tensor', ring(step))  55.6 us
    ppermute x27, starting transfers between devices, shift(): return lax.ppermute(value, 'tensor', ring(step))  38.5 us
    ppermute x6, waiting for transfers between devices, swap(): return lax.ppermute(value, 'tensor', SWAP)  26.8 us
    ppermute x6, starting transfers between devices, swap(): return lax.ppermute(value, 'tensor', SWAP)  14.1 us
    unnamed x80, local copies, waits for them, and re-layouts  12.1 us
  transfers between devices with their start and end apart: 39, of which 11 were waited for; matrix products, arithmetic and copies ran while one was open for 0% of the time, Pallas kernels for 39%

profile of v6, /device:TPU:0, one launch (start us, length us, event | category | flops | bytes accessed | tf_op | source)
XLA Modules:
  0.0 283.0 jit_solution(5274252983665942196)
XLA Ops:
  7.8 2.1 w_split.1
  9.9 2.0 collective-permute-start
  11.9 3.6 %collective-permute-start.1 = (bf16[128,768]{1,0:T(8,128)(2,1)}, bf16[128,768]{1,0:T(8,128)(2,1)S(1)}, u32[]{:S(2)}, u32[]{:S(2)}) collective-permute-start(bf16[128,768]{1,0:T(8,128)(2,1)} %get-tuple-element.39), channel_id=1, source_target_pairs={{0,4},{1,5},{2,6},{3,7},{4,0},{5,1},{6,2},{7,3},{8,12},{9,13},{10,... | collective-permute-start | bytes 589832 | tf_op jit(solution)/shard_map/ppermute | solution.py:26
  16.5 3.5 %g_split.1 = (bf16[128,2048]{1,0:T(8,128)(2,1)}, bf16[128,2048]{1,0:T(8,128)(2,1)}, bf16[128,2048]{1,0:T(8,128)(2,1)}, bf16[128,2048]{1,0:T(8,128)(2,1)}) custom-call(s32[4]{0:T(128)} %pad_add_fusion.refs_0_, bf16[128,8192]{1,0:T(8,128)(2,1)} %bitcast.9, bf16[128,768]{1,0:T(8,128)(2,1)} %get-tuple-element.37.refs_2_.refs_0_), custom_call_target="tpu_custom_call" | custom-call | flops 1000 | bytes 1000 | tf_op jit(solution)/shard_map/g_split/pallas_call | solution.py:47
  20.0 2.7 mask.1
  22.8 1.7 collective-permute-done.1.refs_2_
  25.3 2.1 w_join.1
  28.6 2.4 collective-permute-start.12
  33.1 1.6 collective-permute-start.16
  34.6 20.2 %collective-permute-done.10.refs_6_.refs_3_ = bf16[128,2048]{1,0:T(8,128)(2,1)S(1)} collective-permute-done((bf16[128,2048]{1,0:T(8,128)(2,1)}, bf16[128,2048]{1,0:T(8,128)(2,1)S(1)}, u32[]{:S(2)}, u32[]{:S(2)}) %collective-permute-start.10) | collective-permute-done | bytes 524320 | tf_op jit(solution)/shard_map/ppermute | solution.py:26
  55.3 3.2 %collective-permute-start.9 = (bf16[128,2048]{1,0:T(8,128)(2,1)S(1)}, bf16[128,2048]{1,0:T(8,128)(2,1)S(1)}, u32[]{:S(2)}, u32[]{:S(2)}) collective-permute-start(bf16[128,2048]{1,0:T(8,128)(2,1)S(1)} %copy-done.16), channel_id=1, source_target_pairs={{0,1},{1,0},{2,3},{3,2},{4,5},{5,4},{6,7},{7,6},{8,9},{9,8},{10,11... | collective-permute-start | bytes 1572872 | tf_op jit(solution)/shard_map/ppermute | solution.py:30
  58.5 12.0 %collective-permute-done.14.refs_8_.refs_5_ = bf16[128,2048]{1,0:T(8,128)(2,1)S(1)} collective-permute-done((bf16[128,2048]{1,0:T(8,128)(2,1)S(1)}, bf16[128,2048]{1,0:T(8,128)(2,1)S(1)}, u32[]{:S(2)}, u32[]{:S(2)}) %collective-permute-start.14) | collective-permute-done | bytes 524320 | tf_op jit(solution)/shard_map/ppermute | solution.py:26
  72.9 2.1 w_move.1
  75.0 3.3 %collective-permute-start.11 = (bf16[128,2048]{1,0:T(8,128)(2,1)}, bf16[128,2048]{1,0:T(8,128)(2,1)S(1)}, u32[]{:S(2)}, u32[]{:S(2)}) collective-permute-start(bf16[128,2048]{1,0:T(8,128)(2,1)} %copy-done.12), channel_id=1, source_target_pairs={{0,1},{1,0},{2,3},{3,2},{4,5},{5,4},{6,7},{7,6},{8,9},{9,8},{10,11... | collective-permute-start | bytes 1572872 | tf_op jit(solution)/shard_map/ppermute | solution.py:30
  79.9 2.0 collective-permute-start.8
  81.9 1.4 collective-permute-start.7
  83.3 8.4 %collective-permute-done.11.refs_2_ = bf16[128,2048]{1,0:T(8,128)(2,1)S(1)} collective-permute-done((bf16[128,2048]{1,0:T(8,128)(2,1)}, bf16[128,2048]{1,0:T(8,128)(2,1)S(1)}, u32[]{:S(2)}, u32[]{:S(2)}) %collective-permute-start.11) | collective-permute-done | bytes 524320 | tf_op jit(solution)/shard_map/ppermute | solution.py:30
  92.8 8.0 %collective-permute-done.13.refs_3_ = bf16[128,2048]{1,0:T(8,128)(2,1)S(1)} collective-permute-done((bf16[128,2048]{1,0:T(8,128)(2,1)}, bf16[128,2048]{1,0:T(8,128)(2,1)S(1)}, u32[]{:S(2)}, u32[]{:S(2)}) %collective-permute-start.13) | collective-permute-done | bytes 524320 | tf_op jit(solution)/shard_map/ppermute | solution.py:30
  100.8 3.2 %collective-permute-start.15 = (bf16[128,2048]{1,0:T(8,128)(2,1)}, bf16[128,2048]{1,0:T(8,128)(2,1)S(1)}, u32[]{:S(2)}, u32[]{:S(2)}) collective-permute-start(bf16[128,2048]{1,0:T(8,128)(2,1)} %copy-done.14), channel_id=1, source_target_pairs={{0,1},{1,0},{2,3},{3,2},{4,5},{5,4},{6,7},{7,6},{8,9},{9,8},{10,11... | collective-permute-start | bytes 1572872 | tf_op jit(solution)/shard_map/ppermute | solution.py:30
  104.0 10.4 %collective-permute-done.15.refs_4_ = bf16[128,2048]{1,0:T(8,128)(2,1)S(1)} collective-permute-done((bf16[128,2048]{1,0:T(8,128)(2,1)}, bf16[128,2048]{1,0:T(8,128)(2,1)S(1)}, u32[]{:S(2)}, u32[]{:S(2)}) %collective-permute-start.15) | collective-permute-done | bytes 524320 | tf_op jit(solution)/shard_map/ppermute | solution.py:30
  115.3 4.5 %g_join.1.refs_0_ = bf16[1024,2048]{1,0:T(8,128)(2,1)} custom-call(s32[4]{0:T(128)} %pad_add_fusion.refs_0_, bf16[128,2048]{1,0:T(8,128)(2,1)} %copy-done.15, bf16[128,2048]{1,0:T(8,128)(2,1)} %copy-done.25, bf16[128,2048]{1,0:T(8,128)(2,1)} %copy-done.26, bf16[128,2048]{1,0:T(8,128)(2,1)} %copy-done.27, ...), custom_call_target="tpu_custom_call" | custom-call | flops 1000 | bytes 1000 | tf_op jit(solution)/shard_map/g_join/pallas_call | solution.py:47
  122.0 11.6 %term.2.refs_9_ = bf16[1024,3072]{1,0:T(8,128)(2,1)} custom-call(bf16[1024,2048]{1,0:T(8,128)(2,1)} %g_join.1.refs_0_, bf16[512,768]{1,0:T(8,128)(2,1)} %get-tuple-element.42.refs_4_.refs_1_, bf16[512,768]{1,0:T(8,128)(2,1)} %get-tuple-element.43.refs_2_, bf16[512,768]{1,0:T(8,128)(2,1)} %copy-done.1, bf16[512,768]{1,0:T(8,128)(2,1)} %copy-done.4, ...), custom_call_target="tpu_custom_call" | custom-call | flops 1000 | bytes 1000 | tf_op jit(solution)/shard_map/term/pallas_call | solution.py:47
  133.6 11.6 %term.3.refs_3_ = bf16[1024,3072]{1,0:T(8,128)(2,1)} custom-call(bf16[1024,2048]{1,0:T(8,128)(2,1)} %g_join.1.refs_0_, bf16[512,768]{1,0:T(8,128)(2,1)} %get-tuple-element.42.refs_4_.refs_1_, bf16[512,768]{1,0:T(8,128)(2,1)} %get-tuple-element.43.refs_2_, bf16[512,768]{1,0:T(8,128)(2,1)} %copy-done.1, bf16[512,768]{1,0:T(8,128)(2,1)} %copy-done.4, ...), custom_call_target="tpu_custom_call" | custom-call | flops 1000 | bytes 1000 | tf_op jit(solution)/shard_map/term/pallas_call | solution.py:47
  145.3 7.3 %rows_term.4 = (bf16[512,768]{1,0:T(8,128)(2,1)}, bf16[512,768]{1,0:T(8,128)(2,1)}) custom-call(bf16[1024,2048]{1,0:T(8,128)(2,1)} %g_join.1.refs_0_, bf16[1024,3072]{1,0:T(8,128)(2,1)} %all-gather.3.cloned.1.call-done.refs_1_.refs_0_, bf16[1024,3072]{1,0:T(8,128)(2,1)} %all-gather.5.cloned.1.call-done.refs_2_.refs_0_, bf16[1024,3072]{1,0:T(8,128)(2,1)} %term.3.refs_3_), custom_call_target="tpu_custom_call" | custom-call | flops 1000 | bytes 1000 | tf_op jit(solution)/shard_map/rows_term/pallas_call | solution.py:47
  152.6 4.6 %collective-permute-start.19 = (bf16[512,768]{1,0:T(8,128)(2,1)}, bf16[512,768]{1,0:T(8,128)(2,1)S(1)}, u32[]{:S(2)}, u32[]{:S(2)}) collective-permute-start(bf16[512,768]{1,0:T(8,128)(2,1)} %get-tuple-element.52), channel_id=1, source_target_pairs={{0,6},{1,7},{2,0},{3,1},{4,2},{5,3},{6,4},{7,5},{8,14},{9,15},{10,... | collective-permute-start | bytes 2359304 | tf_op jit(solution)/shard_map/ppermute | solution.py:26
  157.2 11.7 %project.2 = (bf16[512,1024]{1,0:T(8,128)(2,1)}, f32[512,1024]{1,0:T(8,128)}) custom-call(bf16[1024,3072]{1,0:T(8,128)(2,1)} %all-gather.3.cloned.1.call-done.refs_1_.refs_0_, bf16[512,768]{1,0:T(8,128)(2,1)} %get-tuple-element.42.refs_4_.refs_1_, bf16[512,768]{1,0:T(8,128)(2,1)} %get-tuple-element.43.refs_2_, bf16[512,768]{1,0:T(8,128)(2,1)} %copy-done.1, ...), custom_call_target="tpu_custom_call" | custom-call | flops 1000 | bytes 1000 | tf_op jit(solution)/shard_map/project/pallas_call | solution.py:47
  168.9 3.3 %collective-permute-start.17 = (bf16[512,1024]{1,0:T(8,128)(2,1)}, bf16[512,1024]{1,0:T(8,128)(2,1)S(1)}, u32[]{:S(2)}, u32[]{:S(2)}) collective-permute-start(bf16[512,1024]{1,0:T(8,128)(2,1)} %get-tuple-element.49.refs_3_), channel_id=1, source_target_pairs={{0,1},{1,0},{2,3},{3,2},{4,5},{5,4},{6,7},{7,6},{8,9},{9,8},{10,11... | collective-permute-start | bytes 3145736 | tf_op jit(solution)/shard_map/ppermute | solution.py:30
  172.1 7.3 %rows_term.5 = (f32[512,768]{1,0:T(8,128)}, bf16[512,768]{1,0:T(8,128)(2,1)}) custom-call(bf16[1024,2048]{1,0:T(8,128)(2,1)} %g_join.1.refs_0_, bf16[1024,3072]{1,0:T(8,128)(2,1)} %all-gather.3.cloned.1.call-done.refs_1_.refs_0_, bf16[1024,3072]{1,0:T(8,128)(2,1)} %all-gather.5.cloned.1.call-done.refs_2_.refs_0_, bf16[512,1024]{1,0:T(8,128)(2,1)} %get-tuple-element.49.refs_3_), custom_call_target="tpu_custom_call" | custom-call | flops 1000 | bytes 1000 | tf_op jit(solution)/shard_map/rows_term/pallas_call | solution.py:47
  181.9 7.2 %rows_term.6 = (bf16[512,768]{1,0:T(8,128)(2,1)}, f32[512,768]{1,0:T(8,128)}) custom-call(bf16[1024,2048]{1,0:T(8,128)(2,1)} %g_join.1.refs_0_, bf16[1024,3072]{1,0:T(8,128)(2,1)} %all-gather.3.cloned.1.call-done.refs_1_.refs_0_, bf16[1024,3072]{1,0:T(8,128)(2,1)} %all-gather.5.cloned.1.call-done.refs_2_.refs_0_, ...), custom_call_target="tpu_custom_call" | custom-call | flops 1000 | bytes 1000 | tf_op jit(solution)/shard_map/rows_term/pallas_call | solution.py:47
  189.1 2.6 collective-permute-start.21
  191.7 3.6 %add_far.1 = (bf16[512,768]{1,0:T(8,128)(2,1)}, bf16[512,768]{1,0:T(8,128)(2,1)}) custom-call(f32[512,768]{1,0:T(8,128)} %get-tuple-element.50.refs_0_, bf16[512,768]{1,0:T(8,128)(2,1)} %copy-done.9, f32[512,768]{1,0:T(8,128)} %get-tuple-element.53.refs_2_, bf16[512,768]{1,0:T(8,128)(2,1)} %copy-done.8, bf16[512,768]{1,0:T(8,128)(2,1)} %get-tuple-element.54.refs_4_), custom_call_target="tpu_custom_call" | custom-call | flops 1000 | bytes 1000 | tf_op jit(solution)/shard_map/add_far/pallas_call | solution.py:47
  195.4 11.7 %project.3 = (bf16[512,1024]{1,0:T(8,128)(2,1)}, f32[512,1024]{1,0:T(8,128)}) custom-call(bf16[1024,3072]{1,0:T(8,128)(2,1)} %all-gather.5.cloned.1.call-done.refs_2_.refs_0_, bf16[512,768]{1,0:T(8,128)(2,1)} %get-tuple-element.42.refs_4_.refs_1_, bf16[512,768]{1,0:T(8,128)(2,1)} %get-tuple-element.43.refs_2_, bf16[512,768]{1,0:T(8,128)(2,1)} %copy-done.1, ...), custom_call_target="tpu_custom_call" | custom-call | flops 1000 | bytes 1000 | tf_op jit(solution)/shard_map/project/pallas_call | solution.py:47
  209.4 3.1 %settle.2 = (bf16[128,1024]{1,0:T(8,128)(2,1)}, bf16[128,1024]{1,0:T(8,128)(2,1)}, bf16[128,1024]{1,0:T(8,128)(2,1)}, bf16[128,1024]{1,0:T(8,128)(2,1)}) custom-call(s32[4]{0:T(128)} %pad_add_fusion.refs_0_, f32[512,1024]{1,0:T(8,128)} %get-tuple-element.48.refs_1_, bf16[512,1024]{1,0:T(8,128)(2,1)} %copy-done.21, ...), custom_call_target="tpu_custom_call" | custom-call | flops 1000 | bytes 1000 | tf_op jit(solution)/shard_map/settle/pallas_call | solution.py:47
  212.6 3.2 %collective-permute-start.30 = (bf16[512,768]{1,0:T(8,128)(2,1)}, bf16[512,768]{1,0:T(8,128)(2,1)S(1)}, u32[]{:S(2)}, u32[]{:S(2)}) collective-permute-start(bf16[512,768]{1,0:T(8,128)(2,1)} %get-tuple-element.66), channel_id=1, source_target_pairs={{0,6},{1,7},{2,0},{3,1},{4,2},{5,3},{6,4},{7,5},{8,14},{9,15},{10,... | collective-permute-start | bytes 2359304 | tf_op jit(solution)/shard_map/ppermute | solution.py:26
  215.8 2.1 collective-permute-start.23
  217.9 7.7 %rows_term.7.refs_3_.refs_2_.refs_1_ = f32[1024,768]{1,0:T(8,128)} custom-call(bf16[1024,2048]{1,0:T(8,128)(2,1)} %g_join.1.refs_0_, bf16[1024,3072]{1,0:T(8,128)(2,1)} %all-gather.3.cloned.1.call-done.refs_1_.refs_0_, bf16[1024,3072]{1,0:T(8,128)(2,1)} %all-gather.5.cloned.1.call-done.refs_2_.refs_0_, bf16[128,1024]{1,0:T(8,128)(2,1)} %get-tuple-element.57.refs_3_.refs_1_), custom_call_target="tpu_custom_call" | custom-call | flops 1000 | bytes 1000 | tf_op jit(solution)/shard_map/rows_term/pallas_call | solution.py:47
  225.6 2.1 move.1
  227.7 1.7 collective-permute-start.31
  229.4 12.4 %collective-permute-done.23.refs_5_.refs_3_ = bf16[128,1024]{1,0:T(8,128)(2,1)S(1)} collective-permute-done((bf16[128,1024]{1,0:T(8,128)(2,1)}, bf16[128,1024]{1,0:T(8,128)(2,1)S(1)}, u32[]{:S(2)}, u32[]{:S(2)}) %collective-permute-start.23) | collective-permute-done | bytes 262176 | tf_op jit(solution)/shard_map/ppermute | solution.py:26
  241.8 6.4 %collective-permute-done.24.refs_6_.refs_4_ = bf16[128,1024]{1,0:T(8,128)(2,1)S(1)} collective-permute-done((bf16[128,1024]{1,0:T(8,128)(2,1)S(1)}, bf16[128,1024]{1,0:T(8,128)(2,1)S(1)}, u32[]{:S(2)}, u32[]{:S(2)}) %collective-permute-start.24) | collective-permute-done | bytes 262176 | tf_op jit(solution)/shard_map/ppermute | solution.py:26
  249.2 3.0 %settle.3 = (bf16[128,1024]{1,0:T(8,128)(2,1)}, bf16[128,1024]{1,0:T(8,128)(2,1)}, bf16[128,1024]{1,0:T(8,128)(2,1)}, bf16[128,1024]{1,0:T(8,128)(2,1)}) custom-call(s32[4]{0:T(128)} %pad_add_fusion.refs_0_, f32[512,1024]{1,0:T(8,128)} %get-tuple-element.61.refs_1_, bf16[512,1024]{1,0:T(8,128)(2,1)} %copy-done.20, ...), custom_call_target="tpu_custom_call" | custom-call | flops 1000 | bytes 1000 | tf_op jit(solution)/shard_map/settle/pallas_call | solution.py:47
  252.2 2.7 collective-permute-start.27
  255.8 4.5 %add_rows.1.refs_3_ = bf16[1024,768]{1,0:T(8,128)(2,1)} custom-call(s32[4]{0:T(128)} %pad_add_fusion.refs_0_, s32[8]{0:T(128)} %refs_1_.5, f32[1024,768]{1,0:T(8,128)} %rows_term.7.refs_3_.refs_2_.refs_1_, bf16[512,768]{1,0:T(8,128)(2,1)} %collective-permute-done.29.refs_3_, bf16[512,768]{1,0:T(8,128)(2,1)} %copy-done.10, bf16[512,768]{1,0:T(8,128)(2,1)} %copy-done.11, ...), custom_call_target="tpu_custom_call" | custom-call | flops 1000 | bytes 1000 | tf_op jit(solution)/shard_map/add_rows/pallas_call | solution.py:47
  260.3 2.4 add_terms.1
  263.2 2.9 %collective-permute-start.33 = (bf16[128,768]{1,0:T(8,128)(2,1)}, bf16[128,768]{1,0:T(8,128)(2,1)S(1)}, u32[]{:S(2)}, u32[]{:S(2)}) collective-permute-start(bf16[128,768]{1,0:T(8,128)(2,1)} %get-tuple-element.69), channel_id=1, source_target_pairs={{0,4},{1,5},{2,6},{3,7},{4,0},{5,1},{6,2},{7,3},{8,12},{9,13},{10,... | collective-permute-start | bytes 589832 | tf_op jit(solution)/shard_map/ppermute | solution.py:26
  268.2 3.3 %join_out.1 = bf16[128,8192]{1,0:T(8,128)(2,1)} custom-call(s32[4]{0:T(128)} %pad_add_fusion.refs_0_, bf16[128,1024]{1,0:T(8,128)(2,1)} %get-tuple-element.57.refs_3_.refs_1_, bf16[128,1024]{1,0:T(8,128)(2,1)} %copy-done.17, bf16[128,1024]{1,0:T(8,128)(2,1)} %copy-done.18, bf16[128,1024]{1,0:T(8,128)(2,1)} %copy-done.19, ...), custom_call_target="tpu_custom_call" | custom-call | flops 1000 | bytes 1000 | tf_op jit(solution)/shard_map/join_out/pallas_call | solution.py:47
  271.5 1.7 collective-permute-done.34.refs_4_
  273.9 2.5 join_term.1
  (137 shorter events, 24.3 us)
Async XLA Ops:
  7.2 138.1 %all-gather.3.cloned.1.call-start = ((), (), s32[]{:S(2)}) async-start(), calls=%async_computation.2 | async-start | bytes 7077888 | tf_op jit(solution)/shard_map/all_gather | solution.py:140
  9.9 12.9 %collective-permute-start = (bf16[128,768]{1,0:T(8,128)(2,1)}, bf16[128,768]{1,0:T(8,128)(2,1)S(1)}, u32[]{:S(2)}, u32[]{:S(2)}) collective-permute-start(bf16[128,768]{1,0:T(8,128)(2,1)} %get-tuple-element.38), channel_id=1, source_target_pairs={{0,2},{1,3},{2,4},{3,5},{4,6},{5,7},{6,0},{7,1},{8,10},{9,11},{10,... | collective-permute-start | bytes 589832 | tf_op jit(solution)/shard_map/ppermute | solution.py:26
  11.9 12.6 %collective-permute-start.1 = (bf16[128,768]{1,0:T(8,128)(2,1)}, bf16[128,768]{1,0:T(8,128)(2,1)S(1)}, u32[]{:S(2)}, u32[]{:S(2)}) collective-permute-start(bf16[128,768]{1,0:T(8,128)(2,1)} %get-tuple-element.39), channel_id=1, source_target_pairs={{0,4},{1,5},{2,6},{3,7},{4,0},{5,1},{6,2},{7,3},{8,12},{9,13},{10,... | collective-permute-start | bytes 589832 | tf_op jit(solution)/shard_map/ppermute | solution.py:26
  15.5 9.0 %collective-permute-start.2 = (bf16[128,768]{1,0:T(8,128)(2,1)}, bf16[128,768]{1,0:T(8,128)(2,1)S(1)}, u32[]{:S(2)}, u32[]{:S(2)}) collective-permute-start(bf16[128,768]{1,0:T(8,128)(2,1)} %get-tuple-element.40), channel_id=1, source_target_pairs={{0,6},{1,7},{2,0},{3,1},{4,2},{5,3},{6,4},{7,5},{8,14},{9,15},{10,... | collective-permute-start | bytes 589832 | tf_op jit(solution)/shard_map/ppermute | solution.py:26
  22.7 9.6 %copy-start.2 = (bf16[512,768]{1,0:T(8,128)(2,1)S(1)}, bf16[512,768]{1,0:T(8,128)(2,1)}, u32[]{:S(2)}) copy-start(bf16[512,768]{1,0:T(8,128)(2,1)} %get-tuple-element.42.refs_4_.refs_1_) | copy-start | bytes 2359300
  22.7 32.1 %copy-start.37 = (bf16[128,2048]{1,0:T(8,128)(2,1)S(1)}, bf16[128,2048]{1,0:T(8,128)(2,1)}, u32[]{:S(2)}) copy-start(bf16[128,2048]{1,0:T(8,128)(2,1)} %get-tuple-element.46) | copy-start | bytes 1572868
  22.8 32.5 %copy-start.16 = (bf16[128,2048]{1,0:T(8,128)(2,1)S(1)}, bf16[128,2048]{1,0:T(8,128)(2,1)}, u32[]{:S(2)}) copy-start(bf16[128,2048]{1,0:T(8,128)(2,1)} %get-tuple-element.41.refs_3_.refs_5_) | copy-start | bytes 1572868
  27.4 117.8 %all-gather.5.cloned.1.call-start = ((), (), s32[]{:S(2)}) async-start(), calls=%async_computation.3 | async-start | bytes 7077888 | tf_op jit(solution)/shard_map/all_gather | solution.py:140
  27.5 27.4 %collective-permute-start.10 = (bf16[128,2048]{1,0:T(8,128)(2,1)}, bf16[128,2048]{1,0:T(8,128)(2,1)S(1)}, u32[]{:S(2)}, u32[]{:S(2)}) collective-permute-start(bf16[128,2048]{1,0:T(8,128)(2,1)} %get-tuple-element.44), channel_id=1, source_target_pairs={{0,2},{1,3},{2,4},{3,5},{4,6},{5,7},{6,0},{7,1},{8,10},{9,11},{10,... | collective-permute-start | bytes 1572872 | tf_op jit(solution)/shard_map/ppermute | solution.py:26
  28.6 26.6 %collective-permute-start.12 = (bf16[128,2048]{1,0:T(8,128)(2,1)S(1)}, bf16[128,2048]{1,0:T(8,128)(2,1)S(1)}, u32[]{:S(2)}, u32[]{:S(2)}) collective-permute-start(bf16[128,2048]{1,0:T(8,128)(2,1)S(1)} %copy-done.38), channel_id=1, source_target_pairs={{0,4},{1,5},{2,6},{3,7},{4,0},{5,1},{6,2},{7,3},{8,12},{9,13},{10,... | collective-permute-start | bytes 1572872 | tf_op jit(solution)/shard_map/ppermute | solution.py:26
  31.0 39.4 %collective-permute-start.6 = (bf16[512,768]{1,0:T(8,128)(2,1)S(1)}, bf16[512,768]{1,0:T(8,128)(2,1)S(1)}, u32[]{:S(2)}, u32[]{:S(2)}) collective-permute-start(bf16[512,768]{1,0:T(8,128)(2,1)S(1)} %copy-done.3), channel_id=1, source_target_pairs={{0,6},{1,7},{2,0},{3,1},{4,2},{5,3},{6,4},{7,5},{8,14},{9,15},{10,... | collective-permute-start | bytes 2359304 | tf_op jit(solution)/shard_map/ppermute | solution.py:26
  32.4 38.1 %collective-permute-start.3 = (bf16[512,768]{1,0:T(8,128)(2,1)S(1)}, bf16[512,768]{1,0:T(8,128)(2,1)S(1)}, u32[]{:S(2)}, u32[]{:S(2)}) collective-permute-start(bf16[512,768]{1,0:T(8,128)(2,1)S(1)} %copy-done.2), channel_id=1, source_target_pairs={{0,2},{1,3},{2,4},{3,5},{4,6},{5,7},{6,0},{7,1},{8,10},{9,11},{10,... | collective-permute-start | bytes 2359304 | tf_op jit(solution)/shard_map/ppermute | solution.py:26
  33.1 37.4 %collective-permute-start.16 = (bf16[128,3072]{1,0:T(8,128)(2,1)}, bf16[128,3072]{1,0:T(8,128)(2,1)S(1)}, u32[]{:S(2)}, u32[]{:S(2)}) collective-permute-start(bf16[128,3072]{1,0:T(8,128)(2,1)} %w_join.1), channel_id=1, source_target_pairs={{0,64},{8,72},{16,80},{24,88},{32,96},{40,104},{48,112},{56,120},{... | collective-permute-start | bytes 2359304 | tf_op jit(solution)/shard_map/ppermute | solution.py:135
  54.9 15.6 %copy-start.12 = (bf16[128,2048]{1,0:T(8,128)(2,1)}, bf16[128,2048]{1,0:T(8,128)(2,1)S(1)}, u32[]{:S(2)}) copy-start(bf16[128,2048]{1,0:T(8,128)(2,1)S(1)} %collective-permute-done.10.refs_6_.refs_3_) | copy-start | bytes 1572868
  54.9 15.6 %collective-permute-start.14 = (bf16[128,2048]{1,0:T(8,128)(2,1)S(1)}, bf16[128,2048]{1,0:T(8,128)(2,1)S(1)}, u32[]{:S(2)}, u32[]{:S(2)}) collective-permute-start(bf16[128,2048]{1,0:T(8,128)(2,1)S(1)} %copy-done.37), channel_id=1, source_target_pairs={{0,6},{1,7},{2,0},{3,1},{4,2},{5,3},{6,4},{7,5},{8,14},{9,15},{10,... | collective-permute-start | bytes 1572872 | tf_op jit(solution)/shard_map/ppermute | solution.py:26
  55.3 15.2 %copy-start.13 = (bf16[128,2048]{1,0:T(8,128)(2,1)}, bf16[128,2048]{1,0:T(8,128)(2,1)S(1)}, u32[]{:S(2)}) copy-start(bf16[128,2048]{1,0:T(8,128)(2,1)S(1)} %collective-permute-done.12.refs_7_.refs_4_) | copy-start | bytes 1572868
  55.3 15.2 %collective-permute-start.9 = (bf16[128,2048]{1,0:T(8,128)(2,1)S(1)}, bf16[128,2048]{1,0:T(8,128)(2,1)S(1)}, u32[]{:S(2)}, u32[]{:S(2)}) collective-permute-start(bf16[128,2048]{1,0:T(8,128)(2,1)S(1)} %copy-done.16), channel_id=1, source_target_pairs={{0,1},{1,0},{2,3},{3,2},{4,5},{5,4},{6,7},{7,6},{8,9},{9,8},{10,11... | collective-permute-start | bytes 1572872 | tf_op jit(solution)/shard_map/ppermute | solution.py:30
  75.0 150.7 %reduce-scatter.5.cloned.1.call-start = ((), (), s32[]{:S(2)}) async-start(), calls=%async_computation.5 | async-start | bytes 7077888 | tf_op jit(solution)/shard_map/reduce_scatter | solution.py:217
  75.0 16.7 %collective-permute-start.11 = (bf16[128,2048]{1,0:T(8,128)(2,1)}, bf16[128,2048]{1,0:T(8,128)(2,1)S(1)}, u32[]{:S(2)}, u32[]{:S(2)}) collective-permute-start(bf16[128,2048]{1,0:T(8,128)(2,1)} %copy-done.12), channel_id=1, source_target_pairs={{0,1},{1,0},{2,3},{3,2},{4,5},{5,4},{6,7},{7,6},{8,9},{9,8},{10,11... | collective-permute-start | bytes 1572872 | tf_op jit(solution)/shard_map/ppermute | solution.py:30
  78.3 22.5 %collective-permute-start.13 = (bf16[128,2048]{1,0:T(8,128)(2,1)}, bf16[128,2048]{1,0:T(8,128)(2,1)S(1)}, u32[]{:S(2)}, u32[]{:S(2)}) collective-permute-start(bf16[128,2048]{1,0:T(8,128)(2,1)} %copy-done.13), channel_id=1, source_target_pairs={{0,1},{1,0},{2,3},{3,2},{4,5},{5,4},{6,7},{7,6},{8,9},{9,8},{10,11... | collective-permute-start | bytes 1572872 | tf_op jit(solution)/shard_map/ppermute | solution.py:30
  78.6 41.1 %collective-permute-start.4 = (bf16[512,768]{1,0:T(8,128)(2,1)S(1)}, bf16[512,768]{1,0:T(8,128)(2,1)S(1)}, u32[]{:S(2)}, u32[]{:S(2)}) collective-permute-start(bf16[512,768]{1,0:T(8,128)(2,1)S(1)} %copy-done.3), channel_id=1, source_target_pairs={{0,2},{1,3},{2,4},{3,5},{4,6},{5,7},{6,0},{7,1},{8,10},{9,11},{10,... | collective-permute-start | bytes 2359304 | tf_op jit(solution)/shard_map/ppermute | solution.py:26
  79.9 39.9 %collective-permute-start.8 = (bf16[512,768]{1,0:T(8,128)(2,1)S(1)}, bf16[512,768]{1,0:T(8,128)(2,1)S(1)}, u32[]{:S(2)}, u32[]{:S(2)}) collective-permute-start(bf16[512,768]{1,0:T(8,128)(2,1)S(1)} %copy-done.2), channel_id=1, source_target_pairs={{0,6},{1,7},{2,0},{3,1},{4,2},{5,3},{6,4},{7,5},{8,14},{9,15},{10,... | collective-permute-start | bytes 2359304 | tf_op jit(solution)/shard_map/ppermute | solution.py:26
  81.9 37.9 %collective-permute-start.7 = (bf16[512,768]{1,0:T(8,128)(2,1)}, bf16[512,768]{1,0:T(8,128)(2,1)S(1)}, u32[]{:S(2)}, u32[]{:S(2)}) collective-permute-start(bf16[512,768]{1,0:T(8,128)(2,1)} %copy-done), channel_id=1, source_target_pairs={{0,6},{1,7},{2,0},{3,1},{4,2},{5,3},{6,4},{7,5},{8,14},{9,15},{10,... | collective-permute-start | bytes 2359304 | tf_op jit(solution)/shard_map/ppermute | solution.py:26
  91.7 22.8 %copy-start.25 = (bf16[128,2048]{1,0:T(8,128)(2,1)}, bf16[128,2048]{1,0:T(8,128)(2,1)S(1)}, u32[]{:S(2)}) copy-start(bf16[128,2048]{1,0:T(8,128)(2,1)S(1)} %collective-permute-done.11.refs_2_) | copy-start | bytes 1572868
  91.7 28.1 %collective-permute-start.5 = (bf16[512,768]{1,0:T(8,128)(2,1)}, bf16[512,768]{1,0:T(8,128)(2,1)S(1)}, u32[]{:S(2)}, u32[]{:S(2)}) collective-permute-start(bf16[512,768]{1,0:T(8,128)(2,1)} %copy-done.1), channel_id=1, source_target_pairs={{0,2},{1,3},{2,4},{3,5},{4,6},{5,7},{6,0},{7,1},{8,10},{9,11},{10,... | collective-permute-start | bytes 2359304 | tf_op jit(solution)/shard_map/ppermute | solution.py:26
  100.8 13.6 %copy-start.26 = (bf16[128,2048]{1,0:T(8,128)(2,1)}, bf16[128,2048]{1,0:T(8,128)(2,1)S(1)}, u32[]{:S(2)}) copy-start(bf16[128,2048]{1,0:T(8,128)(2,1)S(1)} %collective-permute-done.13.refs_3_) | copy-start | bytes 1572868
  100.8 13.6 %collective-permute-start.15 = (bf16[128,2048]{1,0:T(8,128)(2,1)}, bf16[128,2048]{1,0:T(8,128)(2,1)S(1)}, u32[]{:S(2)}, u32[]{:S(2)}) collective-permute-start(bf16[128,2048]{1,0:T(8,128)(2,1)} %copy-done.14), channel_id=1, source_target_pairs={{0,1},{1,0},{2,3},{3,2},{4,5},{5,4},{6,7},{7,6},{8,9},{9,8},{10,11... | collective-permute-start | bytes 1572872 | tf_op jit(solution)/shard_map/ppermute | solution.py:30
  133.6 126.7 %reduce-scatter.3.cloned.1.call-start = ((), (), s32[]{:S(2)}) async-start(), calls=%async_computation.4 | async-start | bytes 7077888 | tf_op jit(solution)/shard_map/reduce_scatter | solution.py:217
  152.6 27.5 %collective-permute-start.19 = (bf16[512,768]{1,0:T(8,128)(2,1)}, bf16[512,768]{1,0:T(8,128)(2,1)S(1)}, u32[]{:S(2)}, u32[]{:S(2)}) collective-permute-start(bf16[512,768]{1,0:T(8,128)(2,1)} %get-tuple-element.52), channel_id=1, source_target_pairs={{0,6},{1,7},{2,0},{3,1},{4,2},{5,3},{6,4},{7,5},{8,14},{9,15},{10,... | collective-permute-start | bytes 2359304 | tf_op jit(solution)/shard_map/ppermute | solution.py:26
  157.2 22.9 %collective-permute-start.18 = (bf16[512,768]{1,0:T(8,128)(2,1)}, bf16[512,768]{1,0:T(8,128)(2,1)S(1)}, u32[]{:S(2)}, u32[]{:S(2)}) collective-permute-start(bf16[512,768]{1,0:T(8,128)(2,1)} %get-tuple-element.47.refs_9_), channel_id=1, source_target_pairs={{0,2},{1,3},{2,4},{3,5},{4,6},{5,7},{6,0},{7,1},{8,10},{9,11},{10,... | collective-permute-start | bytes 2359304 | tf_op jit(solution)/shard_map/ppermute | solution.py:26
  168.9 39.0 %collective-permute-start.17 = (bf16[512,1024]{1,0:T(8,128)(2,1)}, bf16[512,1024]{1,0:T(8,128)(2,1)S(1)}, u32[]{:S(2)}, u32[]{:S(2)}) collective-permute-start(bf16[512,1024]{1,0:T(8,128)(2,1)} %get-tuple-element.49.refs_3_), channel_id=1, source_target_pairs={{0,1},{1,0},{2,3},{3,2},{4,5},{5,4},{6,7},{7,6},{8,9},{9,8},{10,11... | collective-permute-start | bytes 3145736 | tf_op jit(solution)/shard_map/ppermute | solution.py:30
  179.4 28.4 %collective-permute-start.20 = (bf16[512,768]{1,0:T(8,128)(2,1)}, bf16[512,768]{1,0:T(8,128)(2,1)S(1)}, u32[]{:S(2)}, u32[]{:S(2)}) collective-permute-start(bf16[512,768]{1,0:T(8,128)(2,1)} %get-tuple-element.51.refs_3_), channel_id=1, source_target_pairs={{0,2},{1,3},{2,4},{3,5},{4,6},{5,7},{6,0},{7,1},{8,10},{9,11},{10,... | collective-permute-start | bytes 2359304 | tf_op jit(solution)/shard_map/ppermute | solution.py:26
  189.1 18.7 %collective-permute-start.21 = (bf16[512,768]{1,0:T(8,128)(2,1)}, bf16[512,768]{1,0:T(8,128)(2,1)S(1)}, u32[]{:S(2)}, u32[]{:S(2)}) collective-permute-start(bf16[512,768]{1,0:T(8,128)(2,1)} %get-tuple-element.54.refs_4_), channel_id=1, source_target_pairs={{0,6},{1,7},{2,0},{3,1},{4,2},{5,3},{6,4},{7,5},{8,14},{9,15},{10,... | collective-permute-start | bytes 2359304 | tf_op jit(solution)/shard_map/ppermute | solution.py:26
  207.1 41.1 %collective-permute-start.25 = (bf16[512,1024]{1,0:T(8,128)(2,1)}, bf16[512,1024]{1,0:T(8,128)(2,1)S(1)}, u32[]{:S(2)}, u32[]{:S(2)}) collective-permute-start(bf16[512,1024]{1,0:T(8,128)(2,1)} %get-tuple-element.56.refs_3_), channel_id=1, source_target_pairs={{0,1},{1,0},{2,3},{3,2},{4,5},{5,4},{6,7},{7,6},{8,9},{9,8},{10,11... | collective-permute-start | bytes 3145736 | tf_op jit(solution)/shard_map/ppermute | solution.py:30
  212.5 15.2 %collective-permute-start.22 = (bf16[128,1024]{1,0:T(8,128)(2,1)}, bf16[128,1024]{1,0:T(8,128)(2,1)S(1)}, u32[]{:S(2)}, u32[]{:S(2)}) collective-permute-start(bf16[128,1024]{1,0:T(8,128)(2,1)} %get-tuple-element.58), channel_id=1, source_target_pairs={{0,2},{1,3},{2,4},{3,5},{4,6},{5,7},{6,0},{7,1},{8,10},{9,11},{10,... | collective-permute-start | bytes 786440 | tf_op jit(solution)/shard_map/ppermute | solution.py:26
  212.6 42.3 %collective-permute-start.30 = (bf16[512,768]{1,0:T(8,128)(2,1)}, bf16[512,768]{1,0:T(8,128)(2,1)S(1)}, u32[]{:S(2)}, u32[]{:S(2)}) collective-permute-start(bf16[512,768]{1,0:T(8,128)(2,1)} %get-tuple-element.66), channel_id=1, source_target_pairs={{0,6},{1,7},{2,0},{3,1},{4,2},{5,3},{6,4},{7,5},{8,14},{9,15},{10,... | collective-permute-start | bytes 2359304 | tf_op jit(solution)/shard_map/ppermute | solution.py:26
  215.8 39.8 %collective-permute-start.29 = (bf16[512,768]{1,0:T(8,128)(2,1)S(1)}, bf16[512,768]{1,0:T(8,128)(2,1)}, u32[]{:S(2)}, u32[]{:S(2)}) collective-permute-start(bf16[512,768]{1,0:T(8,128)(2,1)S(1)} %copy-done.22), channel_id=1, source_target_pairs={{0,2},{1,3},{2,4},{3,5},{4,6},{5,7},{6,0},{7,1},{8,10},{9,11},{10,... | collective-permute-start | bytes 2359304 | tf_op jit(solution)/shard_map/ppermute | solution.py:26
  215.8 26.0 %collective-permute-start.23 = (bf16[128,1024]{1,0:T(8,128)(2,1)}, bf16[128,1024]{1,0:T(8,128)(2,1)S(1)}, u32[]{:S(2)}, u32[]{:S(2)}) collective-permute-start(bf16[128,1024]{1,0:T(8,128)(2,1)} %get-tuple-element.59), channel_id=1, source_target_pairs={{0,4},{1,5},{2,6},{3,7},{4,0},{5,1},{6,2},{7,3},{8,12},{9,13},{10,... | collective-permute-start | bytes 786440 | tf_op jit(solution)/shard_map/ppermute | solution.py:26
  225.6 16.2 %copy-start.39 = (bf16[128,1024]{1,0:T(8,128)(2,1)S(1)}, bf16[128,1024]{1,0:T(8,128)(2,1)}, u32[]{:S(2)}) copy-start(bf16[128,1024]{1,0:T(8,128)(2,1)} %get-tuple-element.60) | copy-start | bytes 786436
  227.7 20.5 %copy-start.17 = (bf16[128,1024]{1,0:T(8,128)(2,1)}, bf16[128,1024]{1,0:T(8,128)(2,1)S(1)}, u32[]{:S(2)}) copy-start(bf16[128,1024]{1,0:T(8,128)(2,1)S(1)} %collective-permute-done.22.refs_4_.refs_2_) | copy-start | bytes 786436
  227.7 32.5 %collective-permute-start.31 = (bf16[128,3072]{1,0:T(8,128)(2,1)}, bf16[128,3072]{1,0:T(8,128)(2,1)}, u32[]{:S(2)}, u32[]{:S(2)}) collective-permute-start(bf16[128,3072]{1,0:T(8,128)(2,1)} %move.1), channel_id=1, source_target_pairs={{0,64},{8,72},{16,80},{24,88},{32,96},{40,104},{48,112},{56,120},{... | collective-permute-start | bytes 2359304 | tf_op jit(solution)/shard_map/ppermute | solution.py:266
  241.8 6.4 %collective-permute-start.24 = (bf16[128,1024]{1,0:T(8,128)(2,1)S(1)}, bf16[128,1024]{1,0:T(8,128)(2,1)S(1)}, u32[]{:S(2)}, u32[]{:S(2)}) collective-permute-start(bf16[128,1024]{1,0:T(8,128)(2,1)S(1)} %copy-done.39), channel_id=1, source_target_pairs={{0,6},{1,7},{2,0},{3,1},{4,2},{5,3},{6,4},{7,5},{8,14},{9,15},{10,... | collective-permute-start | bytes 786440 | tf_op jit(solution)/shard_map/ppermute | solution.py:26
  252.2 14.0 %collective-permute-start.26 = (bf16[128,1024]{1,0:T(8,128)(2,1)}, bf16[128,1024]{1,0:T(8,128)(2,1)S(1)}, u32[]{:S(2)}, u32[]{:S(2)}) collective-permute-start(bf16[128,1024]{1,0:T(8,128)(2,1)} %get-tuple-element.63), channel_id=1, source_target_pairs={{0,2},{1,3},{2,4},{3,5},{4,6},{5,7},{6,0},{7,1},{8,10},{9,11},{10,... | collective-permute-start | bytes 786440 | tf_op jit(solution)/shard_map/ppermute | solution.py:26
  252.2 14.5 %collective-permute-start.27 = (bf16[128,1024]{1,0:T(8,128)(2,1)}, bf16[128,1024]{1,0:T(8,128)(2,1)S(1)}, u32[]{:S(2)}, u32[]{:S(2)}) collective-permute-start(bf16[128,1024]{1,0:T(8,128)(2,1)} %get-tuple-element.64), channel_id=1, source_target_pairs={{0,4},{1,5},{2,6},{3,7},{4,0},{5,1},{6,2},{7,3},{8,12},{9,13},{10,... | collective-permute-start | bytes 786440 | tf_op jit(solution)/shard_map/ppermute | solution.py:26
  254.9 12.6 %collective-permute-start.28 = (bf16[128,1024]{1,0:T(8,128)(2,1)}, bf16[128,1024]{1,0:T(8,128)(2,1)S(1)}, u32[]{:S(2)}, u32[]{:S(2)}) collective-permute-start(bf16[128,1024]{1,0:T(8,128)(2,1)} %get-tuple-element.65), channel_id=1, source_target_pairs={{0,6},{1,7},{2,0},{3,1},{4,2},{5,3},{6,4},{7,5},{8,14},{9,15},{10,... | collective-permute-start | bytes 786440 | tf_op jit(solution)/shard_map/ppermute | solution.py:26
  262.7 8.8 %collective-permute-start.32 = (bf16[128,768]{1,0:T(8,128)(2,1)}, bf16[128,768]{1,0:T(8,128)(2,1)S(1)}, u32[]{:S(2)}, u32[]{:S(2)}) collective-permute-start(bf16[128,768]{1,0:T(8,128)(2,1)} %get-tuple-element.68), channel_id=1, source_target_pairs={{0,6},{1,7},{2,0},{3,1},{4,2},{5,3},{6,4},{7,5},{8,14},{9,15},{10,... | collective-permute-start | bytes 589832 | tf_op jit(solution)/shard_map/ppermute | solution.py:26
  263.2 8.3 %collective-permute-start.33 = (bf16[128,768]{1,0:T(8,128)(2,1)}, bf16[128,768]{1,0:T(8,128)(2,1)S(1)}, u32[]{:S(2)}, u32[]{:S(2)}) collective-permute-start(bf16[128,768]{1,0:T(8,128)(2,1)} %get-tuple-element.69), channel_id=1, source_target_pairs={{0,4},{1,5},{2,6},{3,7},{4,0},{5,1},{6,2},{7,3},{8,12},{9,13},{10,... | collective-permute-start | bytes 589832 | tf_op jit(solution)/shard_map/ppermute | solution.py:26
  266.2 7.1 %collective-permute-start.34 = (bf16[128,768]{1,0:T(8,128)(2,1)}, bf16[128,768]{1,0:T(8,128)(2,1)S(1)}, u32[]{:S(2)}, u32[]{:S(2)}) collective-permute-start(bf16[128,768]{1,0:T(8,128)(2,1)} %get-tuple-element.70), channel_id=1, source_target_pairs={{0,2},{1,3},{2,4},{3,5},{4,6},{5,7},{6,0},{7,1},{8,10},{9,11},{10,... | collective-permute-start | bytes 589832 | tf_op jit(solution)/shard_map/ppermute | solution.py:26
  (31 other events, 55.7 us)
Sparse Core Ops, SparseCore 0:
  27.6 41.3 all-gather.2
  75.1 41.8 all-gather.4
  133.7 45.5 reduce-scatter.4
  181.6 42.1 reduce-scatter.2

commit v7 on v6

--- a/solution.py
+++ b/solution.py
@@ -176,19 +176,25 @@
             name="term", limit=BIG,
         )
 
-    def project(i, after):
+    def project(i, cuts, after):
+        part = half // cuts
+
         def body(w_ref, *refs):
             for q in range(2):
                 total = 0.0
                 for k in range(NZ):
                     w = w_ref[:, k * width : (k + 1) * width]
                     total += dot(refs[2 * k + q][...], w, ((1,), (1,)))
-                refs[8 + q][...] = total.astype(refs[8 + q].dtype)
+                if q:
+                    refs[8 + cuts][...] = total
+                else:
+                    for p in range(cuts):
+                        refs[8 + p][...] = total[p * part : (p + 1) * part].astype(jnp.bfloat16)
 
         return run(
-            body, [of((half, feats)), of((half, feats), jnp.float32)], (w_all[i], *acts),
+            body, [of((part, feats))] * cuts + [of((half, feats), jnp.float32)], (w_all[i], *acts),
             [pl.BlockSpec((tile, lanes), lambda j: (j, 0))] + [VMEM] * 8,
-            after=after, grid=(steps,), out_specs=[pl.BlockSpec((half, tile), lambda j: (0, j))] * 2,
+            after=after, grid=(steps,), out_specs=[pl.BlockSpec((r, tile), lambda j: (0, j)) for r in [part] * cuts + [half]],
             name="project", limit=BIG,
         )
 
@@ -218,32 +224,37 @@
             x, "dp", scatter_dimension=0, tiled=True, axis_index_groups=groups
         )
 
-    term_pair = term_of(1, ())
-    term_own = term_of(0, (term_pair,))
-    def settle(place_ref, kept_ref, got_ref, *outs):
-        for k in range(NZ):
-            row = block(own_rows, (place_ref[0] + k) % NZ)
-            outs[k][...] = (kept_ref[row, :] + got_ref[row, :].astype(jnp.float32)).astype(
-                jnp.bfloat16
-            )
+    def settle(place_ref, kept_ref, *refs):
+        got, outs = refs[:-NZ], refs[-NZ:]
+        near = NZ // len(got)
+        for k in range(NZ):
+            zk = (place_ref[0] + k) % NZ
+            row = block(own_rows, zk % near)
+            total = got[0][row, :].astype(jnp.float32)
+            if len(got) == 2:
+                total = jnp.where(zk < near, total, got[1][row, :].astype(jnp.float32))
+            outs[k][...] = (kept_ref[block(own_rows, zk), :] + total).astype(jnp.bfloat16)
 
     def spread(kept, got, after):
         outs = run(
-            settle, [of((own_rows, feats))] * NZ, (place, kept, got), [SMEM, VMEM, VMEM],
+            settle, [of((own_rows, feats))] * NZ, (place, kept, *got), [SMEM] + [VMEM] * (1 + len(got)),
             after=after, out_specs=[VMEM] * NZ, name="settle",
         )
         return [outs[0]] + [shift(outs[k], k) for k in range(1, NZ)], outs[0]
 
     bf16, f32 = jnp.bfloat16, jnp.float32
-    far = rows_term(2, (bf16, bf16), (term_own,))
+    *sent0, kept0 = project(0, 1, ())
+    got0 = [swap(x) for x in sent0]
+    term_pair = term_of(1, (kept0,))
+    far = rows_term(2, (bf16, bf16), (term_pair,))
     up = shift(far[0], 1)
     down = shift(far[1], -1)
-    sent0, kept0 = project(0, (far[0],))
-    got0 = swap(sent0)
-    right_top, right_bottom = rows_term(3, (f32, bf16), (sent0,))
-    left_top, left_bottom = rows_term(1, (bf16, f32), (right_bottom, up, down))
+    right_top, right_bottom = rows_term(3, (f32, bf16), (far[0],))
+    left_top, left_bottom = rows_term(1, (bf16, f32), (right_bottom,))
     from_left_bottom = shift(right_bottom, 1)
     from_right_top = shift(left_top, -1)
+    stay = rows_term(0, (f32,), (left_top,))[0]
+    term_own = term_of(0, (stay, *got0, up, down))
 
     def add_far(a_ref, up_ref, b_ref, down_ref, *outs):
         outs[0][...] = (a_ref[...] + up_ref[...].astype(jnp.float32)).astype(jnp.bfloat16)
@@ -251,19 +262,14 @@
 
     right_top, left_bottom = run(
         add_far, [of((half, width))] * 2, (right_top, up, left_bottom, down), [VMEM] * 4,
-        after=(left_top,), out_specs=[VMEM] * 2, name="add_far",
+        after=(term_own,), out_specs=[VMEM] * 2, name="add_far",
     )
     from_left = [shift(right_top, 1), from_left_bottom]
     from_right = [from_right_top, shift(left_bottom, -1)]
-    sent1, kept1 = project(1, (right_top,))
-    got1 = swap(sent1)
-    quarters0, last = spread(kept0, got0, (sent1, from_left_bottom, from_right_top))
-    stay = rows_term(0, (f32,), (last,))[0]
-    quarters1, last = spread(kept1, got1, (stay, *quarters0[1:]))
-    term_pair = run(
-        move, of((piece, lanes)), (scatter(term_pair),), [VMEM], after=(stay,), name="move"
-    )
-    term_pair = lax.ppermute(term_pair, "dp", pair)
+    quarters0, last = spread(kept0, got0, (right_top,))
+    *sent1, kept1 = project(1, 2, (last,))
+    got1 = [swap(x) for x in sent1]
+    term_pair = lax.ppermute(scatter(term_pair), "dp", pair)
     term_own = scatter(term_own)
 
     def add_rows(place_ref, counts_ref, stay_ref, *refs):
@@ -284,8 +290,9 @@
 
     grad_rows = run(
         add_rows, of((s, width)), (place, counts, stay, *from_left, *from_right), [SMEM] * 2 + [VMEM] * 5,
-        after=(last,), name="add_rows",
-    )
+        name="add_rows",
+    )
+    quarters1, last = spread(kept1, got1, (grad_rows,))
 
     def join_out(place_ref, *refs):
         out_ref = refs[-1]
@@ -312,7 +319,7 @@
 
     parts = run(
         add_terms, [of((piece, width))] * NZ, (term_own, term_pair), [VMEM] * 2,
-        after=(last, grad_rows), out_specs=[VMEM] * NZ, name="add_terms",
+        after=(last, *quarters0[1:]), out_specs=[VMEM] * NZ, name="add_terms",
     )
     parts = [parts[0]] + [shift(parts[k], -k) for k in range(1, NZ)]
 

time: 283 us -> 297 us (1.049)
  waiting for transfers between devices: 82.5 us -> 93.1 us
  starting transfers between devices: 56 us -> 60.1 us
    ppermute x6 -> x7, waiting for transfers between devices: 26.8 us -> 53.7 us  [swap(): return lax.ppermute(value, 'tensor', SWAP)]
    ppermute x27, waiting for transfers between devices: 55.6 us -> 39.2 us  [shift(): return lax.ppermute(value, 'tensor', ring(step))]
    ppermute x6 -> x7, starting transfers between devices: 14.1 us -> 16.6 us  [swap(): return lax.ppermute(value, 'tensor', SWAP)]
    pallas_call x22 -> x21, Pallas kernels: 118 us -> 116 us  [run(): pl.pallas_call(kernel, out_shape=out, grid=grid, in_specs=list(specs) + [...]
  transfers between devices with their start and end apart: 39 -> 40, of which waited for: 11 -> 12; matrix products, arithmetic and copies ran while one was open for 0% -> 0% of each run, Pallas kernels for 39% -> 37%
where the time goes in v7:
time: 297 us; the launch traced here: 296 us
  Pallas kernels  116 us (39%)
  waiting for transfers between devices  93.1 us (31%)
  starting transfers between devices  60.1 us (20%)
  between operations  14.1 us (5%)
  local copies, waits for them, and re-layouts  12.7 us (4%)
    pallas_call x21, Pallas kernels, run(): pl.pallas_call(kernel, out_shape=out, grid=grid, in_specs=list(specs) + [...  116 us
    ppermute x7, waiting for transfers between devices, swap(): return lax.ppermute(value, 'tensor', SWAP)  53.7 us
    ppermute x27, starting transfers between devices, shift(): return lax.ppermute(value, 'tensor', ring(step))  40.5 us
    ppermute x27, waiting for transfers between devices, shift(): return lax.ppermute(value, 'tensor', ring(step))  39.2 us
    ppermute x7, starting transfers between devices, swap(): return lax.ppermute(value, 'tensor', SWAP)  16.6 us
    unnamed x80, local copies, waits for them, and re-layouts  12.7 us
  transfers between devices with their start and end apart: 40, of which 12 were waited for; matrix products, arithmetic and copies ran while one was open for 0% of the time, Pallas kernels for 37%

profile of v7, /device:TPU:0, one launch (start us, length us, event | category | flops | bytes accessed | tf_op | source)
XLA Modules:
  0.0 296.1 jit_solution(14070372952295551902)
XLA Ops:
  7.8 2.1 w_split.1
  9.9 2.0 collective-permute-start
  11.9 3.6 %collective-permute-start.1 = (bf16[128,768]{1,0:T(8,128)(2,1)}, bf16[128,768]{1,0:T(8,128)(2,1)S(1)}, u32[]{:S(2)}, u32[]{:S(2)}) collective-permute-start(bf16[128,768]{1,0:T(8,128)(2,1)} %get-tuple-element.40), channel_id=1, source_target_pairs={{0,4},{1,5},{2,6},{3,7},{4,0},{5,1},{6,2},{7,3},{8,12},{9,13},{10,... | collective-permute-start | bytes 589832 | tf_op jit(solution)/shard_map/ppermute | solution.py:26
  16.5 3.5 %g_split.1 = (bf16[128,2048]{1,0:T(8,128)(2,1)}, bf16[128,2048]{1,0:T(8,128)(2,1)}, bf16[128,2048]{1,0:T(8,128)(2,1)}, bf16[128,2048]{1,0:T(8,128)(2,1)}) custom-call(s32[4]{0:T(128)} %pad_add_fusion.refs_0_, bf16[128,8192]{1,0:T(8,128)(2,1)} %bitcast.9, bf16[128,768]{1,0:T(8,128)(2,1)} %get-tuple-element.38.refs_2_.refs_0_), custom_call_target="tpu_custom_call" | custom-call | flops 1000 | bytes 1000 | tf_op jit(solution)/shard_map/g_split/pallas_call | solution.py:47
  20.0 2.8 mask.1
  22.8 1.7 collective-permute-done.1.refs_2_
  25.3 2.1 w_join.1
  28.7 2.4 collective-permute-start.13
  31.0 1.3 collective-permute-start.6
  33.1 1.6 collective-permute-start.17
  34.7 20.3 %collective-permute-done.11.refs_6_.refs_3_ = bf16[128,2048]{1,0:T(8,128)(2,1)S(1)} collective-permute-done((bf16[128,2048]{1,0:T(8,128)(2,1)}, bf16[128,2048]{1,0:T(8,128)(2,1)S(1)}, u32[]{:S(2)}, u32[]{:S(2)}) %collective-permute-start.11) | collective-permute-done | bytes 524320 | tf_op jit(solution)/shard_map/ppermute | solution.py:26
  55.3 3.2 %collective-permute-start.10 = (bf16[128,2048]{1,0:T(8,128)(2,1)S(1)}, bf16[128,2048]{1,0:T(8,128)(2,1)S(1)}, u32[]{:S(2)}, u32[]{:S(2)}) collective-permute-start(bf16[128,2048]{1,0:T(8,128)(2,1)S(1)} %copy-done.13), channel_id=1, source_target_pairs={{0,1},{1,0},{2,3},{3,2},{4,5},{5,4},{6,7},{7,6},{8,9},{9,8},{10,11... | collective-permute-start | bytes 1572872 | tf_op jit(solution)/shard_map/ppermute | solution.py:30
  58.5 12.0 %collective-permute-done.15.refs_8_.refs_5_ = bf16[128,2048]{1,0:T(8,128)(2,1)S(1)} collective-permute-done((bf16[128,2048]{1,0:T(8,128)(2,1)S(1)}, bf16[128,2048]{1,0:T(8,128)(2,1)S(1)}, u32[]{:S(2)}, u32[]{:S(2)}) %collective-permute-start.15) | collective-permute-done | bytes 524320 | tf_op jit(solution)/shard_map/ppermute | solution.py:26
  72.9 2.1 w_move.1
  75.1 3.3 %collective-permute-start.12 = (bf16[128,2048]{1,0:T(8,128)(2,1)}, bf16[128,2048]{1,0:T(8,128)(2,1)S(1)}, u32[]{:S(2)}, u32[]{:S(2)}) collective-permute-start(bf16[128,2048]{1,0:T(8,128)(2,1)} %copy-done.9), channel_id=1, source_target_pairs={{0,1},{1,0},{2,3},{3,2},{4,5},{5,4},{6,7},{7,6},{8,9},{9,8},{10,11... | collective-permute-start | bytes 1572872 | tf_op jit(solution)/shard_map/ppermute | solution.py:30
  79.9 2.0 collective-permute-start.8
  81.9 1.4 collective-permute-start.7
  83.3 8.4 %collective-permute-done.12.refs_2_ = bf16[128,2048]{1,0:T(8,128)(2,1)S(1)} collective-permute-done((bf16[128,2048]{1,0:T(8,128)(2,1)}, bf16[128,2048]{1,0:T(8,128)(2,1)S(1)}, u32[]{:S(2)}, u32[]{:S(2)}) %collective-permute-start.12) | collective-permute-done | bytes 524320 | tf_op jit(solution)/shard_map/ppermute | solution.py:30
  92.9 8.0 %collective-permute-done.14.refs_3_ = bf16[128,2048]{1,0:T(8,128)(2,1)S(1)} collective-permute-done((bf16[128,2048]{1,0:T(8,128)(2,1)}, bf16[128,2048]{1,0:T(8,128)(2,1)S(1)}, u32[]{:S(2)}, u32[]{:S(2)}) %collective-permute-start.14) | collective-permute-done | bytes 524320 | tf_op jit(solution)/shard_map/ppermute | solution.py:30
  100.9 3.2 %collective-permute-start.16 = (bf16[128,2048]{1,0:T(8,128)(2,1)}, bf16[128,2048]{1,0:T(8,128)(2,1)S(1)}, u32[]{:S(2)}, u32[]{:S(2)}) collective-permute-start(bf16[128,2048]{1,0:T(8,128)(2,1)} %copy-done.11), channel_id=1, source_target_pairs={{0,1},{1,0},{2,3},{3,2},{4,5},{5,4},{6,7},{7,6},{8,9},{9,8},{10,11... | collective-permute-start | bytes 1572872 | tf_op jit(solution)/shard_map/ppermute | solution.py:30
  104.1 10.4 %collective-permute-done.16.refs_4_ = bf16[128,2048]{1,0:T(8,128)(2,1)S(1)} collective-permute-done((bf16[128,2048]{1,0:T(8,128)(2,1)}, bf16[128,2048]{1,0:T(8,128)(2,1)S(1)}, u32[]{:S(2)}, u32[]{:S(2)}) %collective-permute-start.16) | collective-permute-done | bytes 524320 | tf_op jit(solution)/shard_map/ppermute | solution.py:30
  115.3 4.5 %g_join.1.refs_0_ = bf16[1024,2048]{1,0:T(8,128)(2,1)} custom-call(s32[4]{0:T(128)} %pad_add_fusion.refs_0_, bf16[128,2048]{1,0:T(8,128)(2,1)} %copy-done.12, bf16[128,2048]{1,0:T(8,128)(2,1)} %copy-done.24, bf16[128,2048]{1,0:T(8,128)(2,1)} %copy-done.25, bf16[128,2048]{1,0:T(8,128)(2,1)} %copy-done.26, ...), custom_call_target="tpu_custom_call" | custom-call | flops 1000 | bytes 1000 | tf_op jit(solution)/shard_map/g_join/pallas_call | solution.py:47
  121.0 11.5 %project.2 = (bf16[512,1024]{1,0:T(8,128)(2,1)}, f32[512,1024]{1,0:T(8,128)}) custom-call(bf16[1024,3072]{1,0:T(8,128)(2,1)} %all-gather.3.cloned.1.call-done.refs_0_.refs_1_, bf16[512,768]{1,0:T(8,128)(2,1)} %get-tuple-element.43.refs_4_.refs_1_, bf16[512,768]{1,0:T(8,128)(2,1)} %get-tuple-element.44.refs_2_, bf16[512,768]{1,0:T(8,128)(2,1)} %copy-done.1, ...), custom_call_target="tpu_custom_call" | custom-call | flops 1000 | bytes 1000 | tf_op jit(solution)/shard_map/project/pallas_call | solution.py:47
  132.4 11.6 %term.2.refs_3_ = bf16[1024,3072]{1,0:T(8,128)(2,1)} custom-call(bf16[1024,2048]{1,0:T(8,128)(2,1)} %g_join.1.refs_0_, bf16[512,768]{1,0:T(8,128)(2,1)} %get-tuple-element.43.refs_4_.refs_1_, bf16[512,768]{1,0:T(8,128)(2,1)} %get-tuple-element.44.refs_2_, bf16[512,768]{1,0:T(8,128)(2,1)} %copy-done.1, bf16[512,768]{1,0:T(8,128)(2,1)} %copy-done.4, ...), custom_call_target="tpu_custom_call" | custom-call | flops 1000 | bytes 1000 | tf_op jit(solution)/shard_map/term/pallas_call | solution.py:47
  145.2 3.3 %collective-permute-start.9 = (bf16[512,1024]{1,0:T(8,128)(2,1)S(1)}, bf16[512,1024]{1,0:T(8,128)(2,1)S(1)}, u32[]{:S(2)}, u32[]{:S(2)}) collective-permute-start(bf16[512,1024]{1,0:T(8,128)(2,1)S(1)} %copy-done.36), channel_id=1, source_target_pairs={{0,1},{1,0},{2,3},{3,2},{4,5},{5,4},{6,7},{7,6},{8,9},{9,8},{10,11... | collective-permute-start | bytes 3145736 | tf_op jit(solution)/shard_map/ppermute | solution.py:30
  148.5 7.1 %rows_term.4 = (bf16[512,768]{1,0:T(8,128)(2,1)}, bf16[512,768]{1,0:T(8,128)(2,1)}) custom-call(bf16[1024,2048]{1,0:T(8,128)(2,1)} %g_join.1.refs_0_, bf16[1024,3072]{1,0:T(8,128)(2,1)} %all-gather.3.cloned.1.call-done.refs_0_.refs_1_, bf16[1024,3072]{1,0:T(8,128)(2,1)} %all-gather.5.cloned.1.call-done.refs_2_.refs_0_, bf16[1024,3072]{1,0:T(8,128)(2,1)} %term.2.refs_3_), custom_call_target="tpu_custom_call" | custom-call | flops 1000 | bytes 1000 | tf_op jit(solution)/shard_map/rows_term/pallas_call | solution.py:47
  155.6 4.8 %collective-permute-start.19 = (bf16[512,768]{1,0:T(8,128)(2,1)}, bf16[512,768]{1,0:T(8,128)(2,1)S(1)}, u32[]{:S(2)}, u32[]{:S(2)}) collective-permute-start(bf16[512,768]{1,0:T(8,128)(2,1)} %get-tuple-element.54), channel_id=1, source_target_pairs={{0,6},{1,7},{2,0},{3,1},{4,2},{5,3},{6,4},{7,5},{8,14},{9,15},{10,... | collective-permute-start | bytes 2359304 | tf_op jit(solution)/shard_map/ppermute | solution.py:26
  160.4 7.3 %rows_term.5 = (f32[512,768]{1,0:T(8,128)}, bf16[512,768]{1,0:T(8,128)(2,1)}) custom-call(bf16[1024,2048]{1,0:T(8,128)(2,1)} %g_join.1.refs_0_, bf16[1024,3072]{1,0:T(8,128)(2,1)} %all-gather.3.cloned.1.call-done.refs_0_.refs_1_, bf16[1024,3072]{1,0:T(8,128)(2,1)} %all-gather.5.cloned.1.call-done.refs_2_.refs_0_, bf16[512,768]{1,0:T(8,128)(2,1)} %get-tuple-element.50.refs_3_), custom_call_target="tpu_custom_call" | custom-call | flops 1000 | bytes 1000 | tf_op jit(solution)/shard_map/rows_term/pallas_call | solution.py:47
  167.7 7.4 %rows_term.6 = (bf16[512,768]{1,0:T(8,128)(2,1)}, f32[512,768]{1,0:T(8,128)}) custom-call(bf16[1024,2048]{1,0:T(8,128)(2,1)} %g_join.1.refs_0_, bf16[1024,3072]{1,0:T(8,128)(2,1)} %all-gather.3.cloned.1.call-done.refs_0_.refs_1_, bf16[1024,3072]{1,0:T(8,128)(2,1)} %all-gather.5.cloned.1.call-done.refs_2_.refs_0_, bf16[512,768]{1,0:T(8,128)(2,1)} %get-tuple-element.52.refs_3_), custom_call_target="tpu_custom_call" | custom-call | flops 1000 | bytes 1000 | tf_op jit(solution)/shard_map/rows_term/pallas_call | solution.py:47
  175.1 7.9 %rows_term.7.refs_9_.refs_2_ = f32[1024,768]{1,0:T(8,128)} custom-call(bf16[1024,2048]{1,0:T(8,128)(2,1)} %g_join.1.refs_0_, bf16[1024,3072]{1,0:T(8,128)(2,1)} %all-gather.3.cloned.1.call-done.refs_0_.refs_1_, bf16[1024,3072]{1,0:T(8,128)(2,1)} %all-gather.5.cloned.1.call-done.refs_2_.refs_0_, bf16[512,768]{1,0:T(8,128)(2,1)} %get-tuple-element.55.refs_3_), custom_call_target="tpu_custom_call" | custom-call | flops 1000 | bytes 1000 | tf_op jit(solution)/shard_map/rows_term/pallas_call | solution.py:47
  185.1 11.7 %term.3.refs_4_ = bf16[1024,3072]{1,0:T(8,128)(2,1)} custom-call(bf16[1024,2048]{1,0:T(8,128)(2,1)} %g_join.1.refs_0_, bf16[512,768]{1,0:T(8,128)(2,1)} %get-tuple-element.43.refs_4_.refs_1_, bf16[512,768]{1,0:T(8,128)(2,1)} %get-tuple-element.44.refs_2_, bf16[512,768]{1,0:T(8,128)(2,1)} %copy-done.1, bf16[512,768]{1,0:T(8,128)(2,1)} %copy-done.4, ...), custom_call_target="tpu_custom_call" | custom-call | flops 1000 | bytes 1000 | tf_op jit(solution)/shard_map/term/pallas_call | solution.py:47
  198.4 3.0 %collective-permute-start.27 = (bf16[512,768]{1,0:T(8,128)(2,1)S(1)}, bf16[512,768]{1,0:T(8,128)(2,1)S(1)}, u32[]{:S(2)}, u32[]{:S(2)}) collective-permute-start(bf16[512,768]{1,0:T(8,128)(2,1)S(1)} %copy-done.17), channel_id=1, source_target_pairs={{0,6},{1,7},{2,0},{3,1},{4,2},{5,3},{6,4},{7,5},{8,14},{9,15},{10,... | collective-permute-start | bytes 2359304 | tf_op jit(solution)/shard_map/ppermute | solution.py:26
  201.4 3.6 %add_far.1 = (bf16[512,768]{1,0:T(8,128)(2,1)}, bf16[512,768]{1,0:T(8,128)(2,1)}) custom-call(f32[512,768]{1,0:T(8,128)} %get-tuple-element.51.refs_0_, bf16[512,768]{1,0:T(8,128)(2,1)} %copy-done.8, f32[512,768]{1,0:T(8,128)} %get-tuple-element.53.refs_2_, bf16[512,768]{1,0:T(8,128)(2,1)} %copy-done.7, bf16[1024,3072]{1,0:T(8,128)(2,1)} %term.3.refs_4_), custom_call_target="tpu_custom_call" | custom-call | flops 1000 | bytes 1000 | tf_op jit(solution)/shard_map/add_far/pallas_call | solution.py:47
  205.1 1.8 collective-permute-start.28
  207.1 3.0 %settle.2 = (bf16[128,1024]{1,0:T(8,128)(2,1)}, bf16[128,1024]{1,0:T(8,128)(2,1)}, bf16[128,1024]{1,0:T(8,128)(2,1)}, bf16[128,1024]{1,0:T(8,128)(2,1)}) custom-call(s32[4]{0:T(128)} %pad_add_fusion.refs_0_, f32[512,1024]{1,0:T(8,128)} %get-tuple-element.45.refs_9_.refs_1_, bf16[512,1024]{1,0:T(8,128)(2,1)} %copy-done.6, ...), custom_call_target="tpu_custom_call" | custom-call | flops 1000 | bytes 1000 | tf_op jit(solution)/shard_map/settle/pallas_call | solution.py:47
  210.1 11.7 %project.3 = (bf16[256,1024]{1,0:T(8,128)(2,1)}, bf16[256,1024]{1,0:T(8,128)(2,1)}, f32[512,1024]{1,0:T(8,128)}) custom-call(bf16[1024,3072]{1,0:T(8,128)(2,1)} %all-gather.5.cloned.1.call-done.refs_2_.refs_0_, bf16[512,768]{1,0:T(8,128)(2,1)} %get-tuple-element.43.refs_4_.refs_1_, bf16[512,768]{1,0:T(8,128)(2,1)} %get-tuple-element.44.refs_2_, ...), custom_call_target="tpu_custom_call" | custom-call | flops 1000 | bytes 1000 | tf_op jit(solution)/shard_map/project/pallas_call | solution.py:47
  223.6 2.8 collective-permute-start.24
  226.4 12.1 %collective-permute-done.23.refs_2_ = bf16[256,1024]{1,0:T(8,128)(2,1)} collective-permute-done((bf16[256,1024]{1,0:T(8,128)(2,1)}, bf16[256,1024]{1,0:T(8,128)(2,1)}, u32[]{:S(2)}, u32[]{:S(2)}) %collective-permute-start.23) | collective-permute-done | bytes 524320 | tf_op jit(solution)/shard_map/ppermute | solution.py:30
  238.5 4.5 %collective-permute-start.21 = (bf16[128,1024]{1,0:T(8,128)(2,1)}, bf16[128,1024]{1,0:T(8,128)(2,1)S(1)}, u32[]{:S(2)}, u32[]{:S(2)}) collective-permute-start(bf16[128,1024]{1,0:T(8,128)(2,1)} %get-tuple-element.59), channel_id=1, source_target_pairs={{0,4},{1,5},{2,6},{3,7},{4,0},{5,1},{6,2},{7,3},{8,12},{9,13},{10,... | collective-permute-start | bytes 786440 | tf_op jit(solution)/shard_map/ppermute | solution.py:26
  243.0 4.5 %add_rows.1.refs_4_ = bf16[1024,768]{1,0:T(8,128)(2,1)} custom-call(s32[4]{0:T(128)} %pad_add_fusion.refs_0_, s32[8]{0:T(128)} %refs_1_.5, f32[1024,768]{1,0:T(8,128)} %rows_term.7.refs_9_.refs_2_, bf16[512,768]{1,0:T(8,128)(2,1)} %collective-permute-done.25.refs_3_, bf16[512,768]{1,0:T(8,128)(2,1)} %copy-done.19, bf16[512,768]{1,0:T(8,128)(2,1)} %copy-done.20, ...), custom_call_target="tpu_custom_call" | custom-call | flops 1000 | bytes 1000 | tf_op jit(solution)/shard_map/add_rows/pallas_call | solution.py:47
  247.5 14.8 %collective-permute-done.24.refs_3_ = bf16[256,1024]{1,0:T(8,128)(2,1)S(1)} collective-permute-done((bf16[256,1024]{1,0:T(8,128)(2,1)}, bf16[256,1024]{1,0:T(8,128)(2,1)S(1)}, u32[]{:S(2)}, u32[]{:S(2)}) %collective-permute-start.24) | collective-permute-done | bytes 524320 | tf_op jit(solution)/shard_map/ppermute | solution.py:30
  263.1 3.1 %settle.3 = (bf16[128,1024]{1,0:T(8,128)(2,1)}, bf16[128,1024]{1,0:T(8,128)(2,1)}, bf16[128,1024]{1,0:T(8,128)(2,1)}, bf16[128,1024]{1,0:T(8,128)(2,1)}) custom-call(s32[4]{0:T(128)} %pad_add_fusion.refs_0_, f32[512,1024]{1,0:T(8,128)} %get-tuple-element.61.refs_1_, bf16[256,1024]{1,0:T(8,128)(2,1)} %collective-permute-done.23.refs_2_, ...), custom_call_target="tpu_custom_call" | custom-call | flops 1000 | bytes 1000 | tf_op jit(solution)/shard_map/settle/pallas_call | solution.py:47
  266.2 3.8 %collective-permute-start.30 = (bf16[128,1024]{1,0:T(8,128)(2,1)}, bf16[128,1024]{1,0:T(8,128)(2,1)S(1)}, u32[]{:S(2)}, u32[]{:S(2)}) collective-permute-start(bf16[128,1024]{1,0:T(8,128)(2,1)} %get-tuple-element.67), channel_id=1, source_target_pairs={{0,4},{1,5},{2,6},{3,7},{4,0},{5,1},{6,2},{7,3},{8,12},{9,13},{10,... | collective-permute-start | bytes 786440 | tf_op jit(solution)/shard_map/ppermute | solution.py:26
  271.0 2.3 add_terms.1
  273.9 3.4 %collective-permute-start.34 = (bf16[128,768]{1,0:T(8,128)(2,1)}, bf16[128,768]{1,0:T(8,128)(2,1)S(1)}, u32[]{:S(2)}, u32[]{:S(2)}) collective-permute-start(bf16[128,768]{1,0:T(8,128)(2,1)} %get-tuple-element.71), channel_id=1, source_target_pairs={{0,4},{1,5},{2,6},{3,7},{4,0},{5,1},{6,2},{7,3},{8,12},{9,13},{10,... | collective-permute-start | bytes 589832 | tf_op jit(solution)/shard_map/ppermute | solution.py:26
  277.6 3.9 %collective-permute-done.30.refs_7_ = bf16[128,1024]{1,0:T(8,128)(2,1)S(1)} collective-permute-done((bf16[128,1024]{1,0:T(8,128)(2,1)}, bf16[128,1024]{1,0:T(8,128)(2,1)S(1)}, u32[]{:S(2)}, u32[]{:S(2)}) %collective-permute-start.30) | collective-permute-done | bytes 262176 | tf_op jit(solution)/shard_map/ppermute | solution.py:26
  282.9 3.3 %join_out.1 = bf16[128,8192]{1,0:T(8,128)(2,1)} custom-call(s32[4]{0:T(128)} %pad_add_fusion.refs_0_, bf16[128,1024]{1,0:T(8,128)(2,1)} %get-tuple-element.57.refs_9_.refs_1_, bf16[128,1024]{1,0:T(8,128)(2,1)} %copy-done.14, bf16[128,1024]{1,0:T(8,128)(2,1)} %copy-done.15, bf16[128,1024]{1,0:T(8,128)(2,1)} %copy-done.16, ...), custom_call_target="tpu_custom_call" | custom-call | flops 1000 | bytes 1000 | tf_op jit(solution)/shard_map/join_out/pallas_call | solution.py:47
  287.1 2.5 join_term.1
  (138 shorter events, 23.6 us)
Async XLA Ops:
  7.2 112.7 %all-gather.3.cloned.1.call-start = ((), (), s32[]{:S(2)}) async-start(), calls=%async_computation.2 | async-start | bytes 7077888 | tf_op jit(solution)/shard_map/all_gather | solution.py:140
  9.9 12.9 %collective-permute-start = (bf16[128,768]{1,0:T(8,128)(2,1)}, bf16[128,768]{1,0:T(8,128)(2,1)S(1)}, u32[]{:S(2)}, u32[]{:S(2)}) collective-permute-start(bf16[128,768]{1,0:T(8,128)(2,1)} %get-tuple-element.39), channel_id=1, source_target_pairs={{0,2},{1,3},{2,4},{3,5},{4,6},{5,7},{6,0},{7,1},{8,10},{9,11},{10,... | collective-permute-start | bytes 589832 | tf_op jit(solution)/shard_map/ppermute | solution.py:26
  11.9 12.6 %collective-permute-start.1 = (bf16[128,768]{1,0:T(8,128)(2,1)}, bf16[128,768]{1,0:T(8,128)(2,1)S(1)}, u32[]{:S(2)}, u32[]{:S(2)}) collective-permute-start(bf16[128,768]{1,0:T(8,128)(2,1)} %get-tuple-element.40), channel_id=1, source_target_pairs={{0,4},{1,5},{2,6},{3,7},{4,0},{5,1},{6,2},{7,3},{8,12},{9,13},{10,... | collective-permute-start | bytes 589832 | tf_op jit(solution)/shard_map/ppermute | solution.py:26
  15.5 9.0 %collective-permute-start.2 = (bf16[128,768]{1,0:T(8,128)(2,1)}, bf16[128,768]{1,0:T(8,128)(2,1)S(1)}, u32[]{:S(2)}, u32[]{:S(2)}) collective-permute-start(bf16[128,768]{1,0:T(8,128)(2,1)} %get-tuple-element.41), channel_id=1, source_target_pairs={{0,6},{1,7},{2,0},{3,1},{4,2},{5,3},{6,4},{7,5},{8,14},{9,15},{10,... | collective-permute-start | bytes 589832 | tf_op jit(solution)/shard_map/ppermute | solution.py:26
  22.8 32.1 %copy-start.37 = (bf16[128,2048]{1,0:T(8,128)(2,1)S(1)}, bf16[128,2048]{1,0:T(8,128)(2,1)}, u32[]{:S(2)}) copy-start(bf16[128,2048]{1,0:T(8,128)(2,1)} %get-tuple-element.49) | copy-start | bytes 1572868
  22.8 32.5 %copy-start.13 = (bf16[128,2048]{1,0:T(8,128)(2,1)S(1)}, bf16[128,2048]{1,0:T(8,128)(2,1)}, u32[]{:S(2)}) copy-start(bf16[128,2048]{1,0:T(8,128)(2,1)} %get-tuple-element.42.refs_3_.refs_5_) | copy-start | bytes 1572868
  27.5 121.0 %all-gather.5.cloned.1.call-start = ((), (), s32[]{:S(2)}) async-start(), calls=%async_computation.3 | async-start | bytes 7077888 | tf_op jit(solution)/shard_map/all_gather | solution.py:140
  27.5 27.4 %collective-permute-start.11 = (bf16[128,2048]{1,0:T(8,128)(2,1)}, bf16[128,2048]{1,0:T(8,128)(2,1)S(1)}, u32[]{:S(2)}, u32[]{:S(2)}) collective-permute-start(bf16[128,2048]{1,0:T(8,128)(2,1)} %get-tuple-element.47), channel_id=1, source_target_pairs={{0,2},{1,3},{2,4},{3,5},{4,6},{5,7},{6,0},{7,1},{8,10},{9,11},{10,... | collective-permute-start | bytes 1572872 | tf_op jit(solution)/shard_map/ppermute | solution.py:26
  28.7 26.6 %collective-permute-start.13 = (bf16[128,2048]{1,0:T(8,128)(2,1)S(1)}, bf16[128,2048]{1,0:T(8,128)(2,1)S(1)}, u32[]{:S(2)}, u32[]{:S(2)}) collective-permute-start(bf16[128,2048]{1,0:T(8,128)(2,1)S(1)} %copy-done.38), channel_id=1, source_target_pairs={{0,4},{1,5},{2,6},{3,7},{4,0},{5,1},{6,2},{7,3},{8,12},{9,13},{10,... | collective-permute-start | bytes 1572872 | tf_op jit(solution)/shard_map/ppermute | solution.py:26
  31.0 39.4 %collective-permute-start.6 = (bf16[512,768]{1,0:T(8,128)(2,1)S(1)}, bf16[512,768]{1,0:T(8,128)(2,1)S(1)}, u32[]{:S(2)}, u32[]{:S(2)}) collective-permute-start(bf16[512,768]{1,0:T(8,128)(2,1)S(1)} %copy-done.3), channel_id=1, source_target_pairs={{0,6},{1,7},{2,0},{3,1},{4,2},{5,3},{6,4},{7,5},{8,14},{9,15},{10,... | collective-permute-start | bytes 2359304 | tf_op jit(solution)/shard_map/ppermute | solution.py:26
  32.4 38.1 %collective-permute-start.3 = (bf16[512,768]{1,0:T(8,128)(2,1)S(1)}, bf16[512,768]{1,0:T(8,128)(2,1)S(1)}, u32[]{:S(2)}, u32[]{:S(2)}) collective-permute-start(bf16[512,768]{1,0:T(8,128)(2,1)S(1)} %copy-done.2), channel_id=1, source_target_pairs={{0,2},{1,3},{2,4},{3,5},{4,6},{5,7},{6,0},{7,1},{8,10},{9,11},{10,... | collective-permute-start | bytes 2359304 | tf_op jit(solution)/shard_map/ppermute | solution.py:26
  33.1 37.4 %collective-permute-start.17 = (bf16[128,3072]{1,0:T(8,128)(2,1)}, bf16[128,3072]{1,0:T(8,128)(2,1)S(1)}, u32[]{:S(2)}, u32[]{:S(2)}) collective-permute-start(bf16[128,3072]{1,0:T(8,128)(2,1)} %w_join.1), channel_id=1, source_target_pairs={{0,64},{8,72},{16,80},{24,88},{32,96},{40,104},{48,112},{56,120},{... | collective-permute-start | bytes 2359304 | tf_op jit(solution)/shard_map/ppermute | solution.py:135
  54.9 15.6 %copy-start.9 = (bf16[128,2048]{1,0:T(8,128)(2,1)}, bf16[128,2048]{1,0:T(8,128)(2,1)S(1)}, u32[]{:S(2)}) copy-start(bf16[128,2048]{1,0:T(8,128)(2,1)S(1)} %collective-permute-done.11.refs_6_.refs_3_) | copy-start | bytes 1572868
  54.9 15.5 %collective-permute-start.15 = (bf16[128,2048]{1,0:T(8,128)(2,1)S(1)}, bf16[128,2048]{1,0:T(8,128)(2,1)S(1)}, u32[]{:S(2)}, u32[]{:S(2)}) collective-permute-start(bf16[128,2048]{1,0:T(8,128)(2,1)S(1)} %copy-done.37), channel_id=1, source_target_pairs={{0,6},{1,7},{2,0},{3,1},{4,2},{5,3},{6,4},{7,5},{8,14},{9,15},{10,... | collective-permute-start | bytes 1572872 | tf_op jit(solution)/shard_map/ppermute | solution.py:26
  55.3 15.2 %copy-start.10 = (bf16[128,2048]{1,0:T(8,128)(2,1)}, bf16[128,2048]{1,0:T(8,128)(2,1)S(1)}, u32[]{:S(2)}) copy-start(bf16[128,2048]{1,0:T(8,128)(2,1)S(1)} %collective-permute-done.13.refs_7_.refs_4_) | copy-start | bytes 1572868
  55.3 15.2 %collective-permute-start.10 = (bf16[128,2048]{1,0:T(8,128)(2,1)S(1)}, bf16[128,2048]{1,0:T(8,128)(2,1)S(1)}, u32[]{:S(2)}, u32[]{:S(2)}) collective-permute-start(bf16[128,2048]{1,0:T(8,128)(2,1)S(1)} %copy-done.13), channel_id=1, source_target_pairs={{0,1},{1,0},{2,3},{3,2},{4,5},{5,4},{6,7},{7,6},{8,9},{9,8},{10,11... | collective-permute-start | bytes 1572872 | tf_op jit(solution)/shard_map/ppermute | solution.py:30
  75.0 147.4 %reduce-scatter.5.cloned.1.call-start = ((), (), s32[]{:S(2)}) async-start(), calls=%async_computation.5 | async-start | bytes 7077888 | tf_op jit(solution)/shard_map/reduce_scatter | solution.py:223
  75.1 16.7 %collective-permute-start.12 = (bf16[128,2048]{1,0:T(8,128)(2,1)}, bf16[128,2048]{1,0:T(8,128)(2,1)S(1)}, u32[]{:S(2)}, u32[]{:S(2)}) collective-permute-start(bf16[128,2048]{1,0:T(8,128)(2,1)} %copy-done.9), channel_id=1, source_target_pairs={{0,1},{1,0},{2,3},{3,2},{4,5},{5,4},{6,7},{7,6},{8,9},{9,8},{10,11... | collective-permute-start | bytes 1572872 | tf_op jit(solution)/shard_map/ppermute | solution.py:30
  78.3 22.5 %collective-permute-start.14 = (bf16[128,2048]{1,0:T(8,128)(2,1)}, bf16[128,2048]{1,0:T(8,128)(2,1)S(1)}, u32[]{:S(2)}, u32[]{:S(2)}) collective-permute-start(bf16[128,2048]{1,0:T(8,128)(2,1)} %copy-done.10), channel_id=1, source_target_pairs={{0,1},{1,0},{2,3},{3,2},{4,5},{5,4},{6,7},{7,6},{8,9},{9,8},{10,11... | collective-permute-start | bytes 1572872 | tf_op jit(solution)/shard_map/ppermute | solution.py:30
  78.7 41.1 %collective-permute-start.4 = (bf16[512,768]{1,0:T(8,128)(2,1)S(1)}, bf16[512,768]{1,0:T(8,128)(2,1)S(1)}, u32[]{:S(2)}, u32[]{:S(2)}) collective-permute-start(bf16[512,768]{1,0:T(8,128)(2,1)S(1)} %copy-done.3), channel_id=1, source_target_pairs={{0,2},{1,3},{2,4},{3,5},{4,6},{5,7},{6,0},{7,1},{8,10},{9,11},{10,... | collective-permute-start | bytes 2359304 | tf_op jit(solution)/shard_map/ppermute | solution.py:26
  79.9 39.9 %collective-permute-start.8 = (bf16[512,768]{1,0:T(8,128)(2,1)S(1)}, bf16[512,768]{1,0:T(8,128)(2,1)S(1)}, u32[]{:S(2)}, u32[]{:S(2)}) collective-permute-start(bf16[512,768]{1,0:T(8,128)(2,1)S(1)} %copy-done.2), channel_id=1, source_target_pairs={{0,6},{1,7},{2,0},{3,1},{4,2},{5,3},{6,4},{7,5},{8,14},{9,15},{10,... | collective-permute-start | bytes 2359304 | tf_op jit(solution)/shard_map/ppermute | solution.py:26
  81.9 37.9 %collective-permute-start.7 = (bf16[512,768]{1,0:T(8,128)(2,1)}, bf16[512,768]{1,0:T(8,128)(2,1)}, u32[]{:S(2)}, u32[]{:S(2)}) collective-permute-start(bf16[512,768]{1,0:T(8,128)(2,1)} %copy-done), channel_id=1, source_target_pairs={{0,6},{1,7},{2,0},{3,1},{4,2},{5,3},{6,4},{7,5},{8,14},{9,15},{10,... | collective-permute-start | bytes 2359304 | tf_op jit(solution)/shard_map/ppermute | solution.py:26
  91.7 22.8 %copy-start.24 = (bf16[128,2048]{1,0:T(8,128)(2,1)}, bf16[128,2048]{1,0:T(8,128)(2,1)S(1)}, u32[]{:S(2)}) copy-start(bf16[128,2048]{1,0:T(8,128)(2,1)S(1)} %collective-permute-done.12.refs_2_) | copy-start | bytes 1572868
  91.7 28.1 %collective-permute-start.5 = (bf16[512,768]{1,0:T(8,128)(2,1)}, bf16[512,768]{1,0:T(8,128)(2,1)}, u32[]{:S(2)}, u32[]{:S(2)}) collective-permute-start(bf16[512,768]{1,0:T(8,128)(2,1)} %copy-done.1), channel_id=1, source_target_pairs={{0,2},{1,3},{2,4},{3,5},{4,6},{5,7},{6,0},{7,1},{8,10},{9,11},{10,... | collective-permute-start | bytes 2359304 | tf_op jit(solution)/shard_map/ppermute | solution.py:26
  100.9 13.6 %collective-permute-start.16 = (bf16[128,2048]{1,0:T(8,128)(2,1)}, bf16[128,2048]{1,0:T(8,128)(2,1)S(1)}, u32[]{:S(2)}, u32[]{:S(2)}) collective-permute-start(bf16[128,2048]{1,0:T(8,128)(2,1)} %copy-done.11), channel_id=1, source_target_pairs={{0,1},{1,0},{2,3},{3,2},{4,5},{5,4},{6,7},{7,6},{8,9},{9,8},{10,11... | collective-permute-start | bytes 1572872 | tf_op jit(solution)/shard_map/ppermute | solution.py:30
  144.0 126.0 %reduce-scatter.3.cloned.1.call-start = ((), (), s32[]{:S(2)}) async-start(), calls=%async_computation.4 | async-start | bytes 7077888 | tf_op jit(solution)/shard_map/reduce_scatter | solution.py:223
  145.2 37.7 %collective-permute-start.9 = (bf16[512,1024]{1,0:T(8,128)(2,1)S(1)}, bf16[512,1024]{1,0:T(8,128)(2,1)S(1)}, u32[]{:S(2)}, u32[]{:S(2)}) collective-permute-start(bf16[512,1024]{1,0:T(8,128)(2,1)S(1)} %copy-done.36), channel_id=1, source_target_pairs={{0,1},{1,0},{2,3},{3,2},{4,5},{5,4},{6,7},{7,6},{8,9},{9,8},{10,11... | collective-permute-start | bytes 3145736 | tf_op jit(solution)/shard_map/ppermute | solution.py:30
  155.6 27.3 %collective-permute-start.19 = (bf16[512,768]{1,0:T(8,128)(2,1)}, bf16[512,768]{1,0:T(8,128)(2,1)S(1)}, u32[]{:S(2)}, u32[]{:S(2)}) collective-permute-start(bf16[512,768]{1,0:T(8,128)(2,1)} %get-tuple-element.54), channel_id=1, source_target_pairs={{0,6},{1,7},{2,0},{3,1},{4,2},{5,3},{6,4},{7,5},{8,14},{9,15},{10,... | collective-permute-start | bytes 2359304 | tf_op jit(solution)/shard_map/ppermute | solution.py:26
  160.4 22.6 %collective-permute-start.18 = (bf16[512,768]{1,0:T(8,128)(2,1)}, bf16[512,768]{1,0:T(8,128)(2,1)S(1)}, u32[]{:S(2)}, u32[]{:S(2)}) collective-permute-start(bf16[512,768]{1,0:T(8,128)(2,1)} %get-tuple-element.50.refs_3_), channel_id=1, source_target_pairs={{0,2},{1,3},{2,4},{3,5},{4,6},{5,7},{6,0},{7,1},{8,10},{9,11},{10,... | collective-permute-start | bytes 2359304 | tf_op jit(solution)/shard_map/ppermute | solution.py:26
  197.9 24.5 %collective-permute-start.26 = (bf16[512,768]{1,0:T(8,128)(2,1)S(1)}, bf16[512,768]{1,0:T(8,128)(2,1)S(1)}, u32[]{:S(2)}, u32[]{:S(2)}) collective-permute-start(bf16[512,768]{1,0:T(8,128)(2,1)S(1)} %copy-done.18), channel_id=1, source_target_pairs={{0,2},{1,3},{2,4},{3,5},{4,6},{5,7},{6,0},{7,1},{8,10},{9,11},{10,... | collective-permute-start | bytes 2359304 | tf_op jit(solution)/shard_map/ppermute | solution.py:26
  198.4 25.2 %collective-permute-start.27 = (bf16[512,768]{1,0:T(8,128)(2,1)S(1)}, bf16[512,768]{1,0:T(8,128)(2,1)S(1)}, u32[]{:S(2)}, u32[]{:S(2)}) collective-permute-start(bf16[512,768]{1,0:T(8,128)(2,1)S(1)} %copy-done.17), channel_id=1, source_target_pairs={{0,6},{1,7},{2,0},{3,1},{4,2},{5,3},{6,4},{7,5},{8,14},{9,15},{10,... | collective-permute-start | bytes 2359304 | tf_op jit(solution)/shard_map/ppermute | solution.py:26
  205.1 33.4 %collective-permute-start.28 = (bf16[512,768]{1,0:T(8,128)(2,1)}, bf16[512,768]{1,0:T(8,128)(2,1)}, u32[]{:S(2)}, u32[]{:S(2)}) collective-permute-start(bf16[512,768]{1,0:T(8,128)(2,1)} %get-tuple-element.64), channel_id=1, source_target_pairs={{0,6},{1,7},{2,0},{3,1},{4,2},{5,3},{6,4},{7,5},{8,14},{9,15},{10,... | collective-permute-start | bytes 2359304 | tf_op jit(solution)/shard_map/ppermute | solution.py:26
  206.9 36.1 %collective-permute-start.25 = (bf16[512,768]{1,0:T(8,128)(2,1)}, bf16[512,768]{1,0:T(8,128)(2,1)}, u32[]{:S(2)}, u32[]{:S(2)}) collective-permute-start(bf16[512,768]{1,0:T(8,128)(2,1)} %get-tuple-element.56.refs_3_), channel_id=1, source_target_pairs={{0,2},{1,3},{2,4},{3,5},{4,6},{5,7},{6,0},{7,1},{8,10},{9,11},{10,... | collective-permute-start | bytes 2359304 | tf_op jit(solution)/shard_map/ppermute | solution.py:26
  210.1 32.8 %copy-start.39 = (bf16[128,1024]{1,0:T(8,128)(2,1)S(1)}, bf16[128,1024]{1,0:T(8,128)(2,1)}, u32[]{:S(2)}) copy-start(bf16[128,1024]{1,0:T(8,128)(2,1)} %get-tuple-element.60) | copy-start | bytes 786436
  221.8 16.7 %collective-permute-start.23 = (bf16[256,1024]{1,0:T(8,128)(2,1)}, bf16[256,1024]{1,0:T(8,128)(2,1)}, u32[]{:S(2)}, u32[]{:S(2)}) collective-permute-start(bf16[256,1024]{1,0:T(8,128)(2,1)} %get-tuple-element.62), channel_id=1, source_target_pairs={{0,1},{1,0},{2,3},{3,2},{4,5},{5,4},{6,7},{7,6},{8,9},{9,8},{10,11... | collective-permute-start | bytes 1572872 | tf_op jit(solution)/shard_map/ppermute | solution.py:30
  222.4 20.5 %copy-start.19 = (bf16[512,768]{1,0:T(8,128)(2,1)}, bf16[512,768]{1,0:T(8,128)(2,1)S(1)}, u32[]{:S(2)}) copy-start(bf16[512,768]{1,0:T(8,128)(2,1)S(1)} %collective-permute-done.26.refs_4_) | copy-start | bytes 2359300
  222.4 47.6 %collective-permute-start.32 = (bf16[128,3072]{1,0:T(8,128)(2,1)}, bf16[128,3072]{1,0:T(8,128)(2,1)S(1)}, u32[]{:S(2)}, u32[]{:S(2)}) collective-permute-start(bf16[128,3072]{1,0:T(8,128)(2,1)} %reduce-scatter.5.cloned.1.call-done), channel_id=1, source_target_pairs={{0,64},{8,72},{16,80},{24,88},{32,96},{40,104},{48,112},{56,120},{... | collective-permute-start | bytes 2359304 | tf_op jit(solution)/shard_map/ppermute | solution.py:272
  223.6 19.4 %copy-start.20 = (bf16[512,768]{1,0:T(8,128)(2,1)}, bf16[512,768]{1,0:T(8,128)(2,1)S(1)}, u32[]{:S(2)}) copy-start(bf16[512,768]{1,0:T(8,128)(2,1)S(1)} %collective-permute-done.27.refs_5_) | copy-start | bytes 2359300
  223.6 38.7 %collective-permute-start.24 = (bf16[256,1024]{1,0:T(8,128)(2,1)}, bf16[256,1024]{1,0:T(8,128)(2,1)S(1)}, u32[]{:S(2)}, u32[]{:S(2)}) collective-permute-start(bf16[256,1024]{1,0:T(8,128)(2,1)} %get-tuple-element.63), channel_id=1, source_target_pairs={{0,1},{1,0},{2,3},{3,2},{4,5},{5,4},{6,7},{7,6},{8,9},{9,8},{10,11... | collective-permute-start | bytes 1572872 | tf_op jit(solution)/shard_map/ppermute | solution.py:30
  238.5 27.7 %collective-permute-start.20 = (bf16[128,1024]{1,0:T(8,128)(2,1)}, bf16[128,1024]{1,0:T(8,128)(2,1)S(1)}, u32[]{:S(2)}, u32[]{:S(2)}) collective-permute-start(bf16[128,1024]{1,0:T(8,128)(2,1)} %get-tuple-element.58), channel_id=1, source_target_pairs={{0,2},{1,3},{2,4},{3,5},{4,6},{5,7},{6,0},{7,1},{8,10},{9,11},{10,... | collective-permute-start | bytes 786440 | tf_op jit(solution)/shard_map/ppermute | solution.py:26
  238.5 31.5 %collective-permute-start.21 = (bf16[128,1024]{1,0:T(8,128)(2,1)}, bf16[128,1024]{1,0:T(8,128)(2,1)S(1)}, u32[]{:S(2)}, u32[]{:S(2)}) collective-permute-start(bf16[128,1024]{1,0:T(8,128)(2,1)} %get-tuple-element.59), channel_id=1, source_target_pairs={{0,4},{1,5},{2,6},{3,7},{4,0},{5,1},{6,2},{7,3},{8,12},{9,13},{10,... | collective-permute-start | bytes 786440 | tf_op jit(solution)/shard_map/ppermute | solution.py:26
  242.9 27.0 %collective-permute-start.22 = (bf16[128,1024]{1,0:T(8,128)(2,1)S(1)}, bf16[128,1024]{1,0:T(8,128)(2,1)S(1)}, u32[]{:S(2)}, u32[]{:S(2)}) collective-permute-start(bf16[128,1024]{1,0:T(8,128)(2,1)S(1)} %copy-done.39), channel_id=1, source_target_pairs={{0,6},{1,7},{2,0},{3,1},{4,2},{5,3},{6,4},{7,5},{8,14},{9,15},{10,... | collective-permute-start | bytes 786440 | tf_op jit(solution)/shard_map/ppermute | solution.py:26
  266.1 11.5 %collective-permute-start.29 = (bf16[128,1024]{1,0:T(8,128)(2,1)}, bf16[128,1024]{1,0:T(8,128)(2,1)S(1)}, u32[]{:S(2)}, u32[]{:S(2)}) collective-permute-start(bf16[128,1024]{1,0:T(8,128)(2,1)} %get-tuple-element.66), channel_id=1, source_target_pairs={{0,2},{1,3},{2,4},{3,5},{4,6},{5,7},{6,0},{7,1},{8,10},{9,11},{10,... | collective-permute-start | bytes 786440 | tf_op jit(solution)/shard_map/ppermute | solution.py:26
  266.2 15.4 %collective-permute-start.30 = (bf16[128,1024]{1,0:T(8,128)(2,1)}, bf16[128,1024]{1,0:T(8,128)(2,1)S(1)}, u32[]{:S(2)}, u32[]{:S(2)}) collective-permute-start(bf16[128,1024]{1,0:T(8,128)(2,1)} %get-tuple-element.67), channel_id=1, source_target_pairs={{0,4},{1,5},{2,6},{3,7},{4,0},{5,1},{6,2},{7,3},{8,12},{9,13},{10,... | collective-permute-start | bytes 786440 | tf_op jit(solution)/shard_map/ppermute | solution.py:26
  269.9 12.2 %collective-permute-start.31 = (bf16[128,1024]{1,0:T(8,128)(2,1)}, bf16[128,1024]{1,0:T(8,128)(2,1)S(1)}, u32[]{:S(2)}, u32[]{:S(2)}) collective-permute-start(bf16[128,1024]{1,0:T(8,128)(2,1)} %get-tuple-element.68), channel_id=1, source_target_pairs={{0,6},{1,7},{2,0},{3,1},{4,2},{5,3},{6,4},{7,5},{8,14},{9,15},{10,... | collective-permute-start | bytes 786440 | tf_op jit(solution)/shard_map/ppermute | solution.py:26
  273.3 12.9 %collective-permute-start.33 = (bf16[128,768]{1,0:T(8,128)(2,1)}, bf16[128,768]{1,0:T(8,128)(2,1)S(1)}, u32[]{:S(2)}, u32[]{:S(2)}) collective-permute-start(bf16[128,768]{1,0:T(8,128)(2,1)} %get-tuple-element.70), channel_id=1, source_target_pairs={{0,6},{1,7},{2,0},{3,1},{4,2},{5,3},{6,4},{7,5},{8,14},{9,15},{10,... | collective-permute-start | bytes 589832 | tf_op jit(solution)/shard_map/ppermute | solution.py:26
  273.9 12.4 %collective-permute-start.34 = (bf16[128,768]{1,0:T(8,128)(2,1)}, bf16[128,768]{1,0:T(8,128)(2,1)S(1)}, u32[]{:S(2)}, u32[]{:S(2)}) collective-permute-start(bf16[128,768]{1,0:T(8,128)(2,1)} %get-tuple-element.71), channel_id=1, source_target_pairs={{0,4},{1,5},{2,6},{3,7},{4,0},{5,1},{6,2},{7,3},{8,12},{9,13},{10,... | collective-permute-start | bytes 589832 | tf_op jit(solution)/shard_map/ppermute | solution.py:26
  277.6 8.6 %collective-permute-start.35 = (bf16[128,768]{1,0:T(8,128)(2,1)}, bf16[128,768]{1,0:T(8,128)(2,1)S(1)}, u32[]{:S(2)}, u32[]{:S(2)}) collective-permute-start(bf16[128,768]{1,0:T(8,128)(2,1)} %get-tuple-element.72), channel_id=1, source_target_pairs={{0,2},{1,3},{2,4},{3,5},{4,6},{5,7},{6,0},{7,1},{8,10},{9,11},{10,... | collective-permute-start | bytes 589832 | tf_op jit(solution)/shard_map/ppermute | solution.py:26
  (32 other events, 71.3 us)
Sparse Core Ops, SparseCore 0:
  27.6 41.3 all-gather.2
  75.1 41.8 all-gather.4
  144.2 45.6 reduce-scatter.4
  196.9 42.2 reduce-scatter.2

commit v8 on v7

--- a/solution.py
+++ b/solution.py
@@ -200,13 +200,18 @@
 
     cols = width // 3 if width % 384 == 0 else width
 
-    def rows_term(k, dtypes, after):
+    def rows_term(k, dtypes, after, more=(), q=0):
         def body(g_ref, w_ref, v_ref, *refs):
             total = dot(g_ref[:, :feats], w_ref[...], ((1,), (0,)))
             total += dot(g_ref[:, feats:], v_ref[...], ((1,), (0,)))
             if len(dtypes) == 2:
                 refs[0][...] = total[:half].astype(dtypes[0])
                 refs[1][...] = total[half:].astype(dtypes[1])
+            elif more:
+                parts = [total[:half], total[half:]]
+                parts[q] += refs[0][...].astype(jnp.float32)
+                refs[1][:half, :] = parts[0].astype(dtypes[0])
+                refs[1][half:, :] = parts[1].astype(dtypes[0])
             else:
                 refs[0][...] = total.astype(dtypes[0])
 
@@ -214,7 +219,9 @@
         outs = [of((s // len(dtypes), width), dtype) for dtype in dtypes]
         column = pl.BlockSpec((feats, cols), lambda j: (0, k * n + j))
         return run(
-            body, outs, [cot, w_all[0], w_all[1]], [VMEM, column, column], after=after, grid=(n,),
+            body, outs, [cot, w_all[0], w_all[1], *more],
+            [VMEM, column, column] + [pl.BlockSpec((half, cols), lambda j: (0, j))] * len(more),
+            after=after, grid=(n,),
             out_specs=[pl.BlockSpec((o.shape[0], cols), lambda j: (0, j)) for o in outs],
             name="rows_term", limit=BIG,
         )
@@ -243,33 +250,25 @@
         return [outs[0]] + [shift(outs[k], k) for k in range(1, NZ)], outs[0]
 
     bf16, f32 = jnp.bfloat16, jnp.float32
-    *sent0, kept0 = project(0, 1, ())
-    got0 = [swap(x) for x in sent0]
-    term_pair = term_of(1, (kept0,))
-    far = rows_term(2, (bf16, bf16), (term_pair,))
+    term_pair = term_of(1, ())
+    term_own = term_of(0, (term_pair,))
+    far = rows_term(2, (bf16, bf16), (term_own,))
     up = shift(far[0], 1)
     down = shift(far[1], -1)
-    right_top, right_bottom = rows_term(3, (f32, bf16), (far[0],))
-    left_top, left_bottom = rows_term(1, (bf16, f32), (right_bottom,))
-    from_left_bottom = shift(right_bottom, 1)
-    from_right_top = shift(left_top, -1)
-    stay = rows_term(0, (f32,), (left_top,))[0]
-    term_own = term_of(0, (stay, *got0, up, down))
-
-    def add_far(a_ref, up_ref, b_ref, down_ref, *outs):
-        outs[0][...] = (a_ref[...] + up_ref[...].astype(jnp.float32)).astype(jnp.bfloat16)
-        outs[1][...] = (b_ref[...] + down_ref[...].astype(jnp.float32)).astype(jnp.bfloat16)
-
-    right_top, left_bottom = run(
-        add_far, [of((half, width))] * 2, (right_top, up, left_bottom, down), [VMEM] * 4,
-        after=(term_own,), out_specs=[VMEM] * 2, name="add_far",
-    )
-    from_left = [shift(right_top, 1), from_left_bottom]
-    from_right = [from_right_top, shift(left_bottom, -1)]
-    quarters0, last = spread(kept0, got0, (right_top,))
-    *sent1, kept1 = project(1, 2, (last,))
+    *sent0, kept0 = project(0, 1, (far[0],))
+    got0 = [swap(x) for x in sent0]
+    to_right = rows_term(3, (bf16,), (kept0,), (up,), 0)[0]
+    to_left = rows_term(1, (bf16,), (to_right,), (down,), 1)[0]
+    from_left = shift(to_right, 1)
+    from_right = shift(to_left, -1)
+    stay = rows_term(0, (f32,), (to_left,))[0]
+    term_pair = run(
+        move, of((piece, lanes)), (scatter(term_pair),), [VMEM], after=(stay,), name="move"
+    )
+    *sent1, kept1 = project(1, 1, (stay, term_pair, *got0))
     got1 = [swap(x) for x in sent1]
-    term_pair = lax.ppermute(scatter(term_pair), "dp", pair)
+    quarters0, last = spread(kept0, got0, (kept1,))
+    term_pair = lax.ppermute(term_pair, "dp", pair)
     term_own = scatter(term_own)
 
     def add_rows(place_ref, counts_ref, stay_ref, *refs):
@@ -278,18 +277,19 @@
         for q in range(2):
             parity = (place_ref[1] + 1 + q) % NH
             for a in range(NZ):
-                rows = slice(a * own_rows, (a + 1) * own_rows)
+                row = q * half + a * own_rows
+                rows = slice(row, row + own_rows)
                 total = (
-                    stay_ref[q * half + a * own_rows : q * half + (a + 1) * own_rows, :]
-                    + refs[q][rows, :].astype(jnp.float32)
-                    + refs[2 + q][rows, :].astype(jnp.float32)
+                    stay_ref[rows, :]
+                    + refs[0][rows, :].astype(jnp.float32)
+                    + refs[1][rows, :].astype(jnp.float32)
                 )
-                refs[4][block(own_rows, a * NH + parity), :] = (total * live).astype(
+                refs[2][block(own_rows, a * NH + parity), :] = (total * live).astype(
                     jnp.bfloat16
                 )
 
     grad_rows = run(
-        add_rows, of((s, width)), (place, counts, stay, *from_left, *from_right), [SMEM] * 2 + [VMEM] * 5,
+        add_rows, of((s, width)), (place, counts, stay, from_left, from_right), [SMEM] * 2 + [VMEM] * 3,
         name="add_rows",
     )
     quarters1, last = spread(kept1, got1, (grad_rows,))
@@ -331,7 +331,7 @@
 
     grad_w = run(
         join_term, of((NZ * piece, width), jnp.float32), (place, *parts),
-        [SMEM] + [VMEM] * NZ, name="join_term",
+        [SMEM] + [VMEM] * NZ, after=(projected,), name="join_term",
     )
     return (projected[None], grad_rows[None], grad_w)
 

time: 297 us -> 282 us (0.949)
  starting transfers between devices: 60.1 us -> 53.1 us
  waiting for transfers between devices: 93.1 us -> 87.5 us
    ppermute x7 -> x6, waiting for transfers between devices: 53.7 us -> 34.4 us  [swap(): return lax.ppermute(value, 'tensor', SWAP)]
    ppermute x27 -> x25, waiting for transfers between devices: 39.2 us -> 47.8 us  [shift(): return lax.ppermute(value, 'tensor', ring(step))]
    ppermute x27 -> x25, starting transfers between devices: 40.5 us -> 34.4 us  [shift(): return lax.ppermute(value, 'tensor', ring(step))]
    ppermute x1, waiting for transfers between devices: 0.01 us -> 5.14 us  [per_device(): term_pair = lax.ppermute(term_pair, 'dp', pair)]
    unnamed x80 -> x70, local copies, waits for them, and re-layouts: 12.7 us -> 11.3 us
    ppermute x7 -> x6, starting transfers between devices: 16.6 us -> 16.5 us  [swap(): return lax.ppermute(value, 'tensor', SWAP)]
  transfers between devices with their start and end apart: 40 -> 37, of which waited for: 12 -> 15; matrix products, arithmetic and copies ran while one was open for 0% -> 0% of each run, Pallas kernels for 37% -> 38%
where the time goes in v8:
time: 282 us; the launch traced here: 281 us
  Pallas kernels  114 us (40%)
  waiting for transfers between devices  87.5 us (31%)
  starting transfers between devices  53.1 us (19%)
  between operations  14.1 us (5%)
  local copies, waits for them, and re-layouts  11.3 us (4%)
    pallas_call x21, Pallas kernels, run(): pl.pallas_call(kernel, out_shape=out, grid=grid, in_specs=list(specs) + [...  114 us
    ppermute x25, waiting for transfers between devices, shift(): return lax.ppermute(value, 'tensor', ring(step))  47.8 us
    ppermute x25, starting transfers between devices, shift(): return lax.ppermute(value, 'tensor', ring(step))  34.4 us
    ppermute x6, waiting for transfers between devices, swap(): return lax.ppermute(value, 'tensor', SWAP)  34.4 us
    ppermute x6, starting transfers between devices, swap(): return lax.ppermute(value, 'tensor', SWAP)  16.5 us
    unnamed x70, local copies, waits for them, and re-layouts  11.3 us
  transfers between devices with their start and end apart: 37, of which 15 were waited for; matrix products, arithmetic and copies ran while one was open for 0% of the time, Pallas kernels for 38%

profile of v8, /device:TPU:0, one launch (start us, length us, event | category | flops | bytes accessed | tf_op | source)
XLA Modules:
  0.0 281.1 jit_solution(11316066922365094013)
XLA Ops:
  7.9 2.1 w_split.1
  10.0 2.0 collective-permute-start
  12.0 3.6 %collective-permute-start.1 = (bf16[128,768]{1,0:T(8,128)(2,1)}, bf16[128,768]{1,0:T(8,128)(2,1)S(1)}, u32[]{:S(2)}, u32[]{:S(2)}) collective-permute-start(bf16[128,768]{1,0:T(8,128)(2,1)} %get-tuple-element.33), channel_id=1, source_target_pairs={{0,4},{1,5},{2,6},{3,7},{4,0},{5,1},{6,2},{7,3},{8,12},{9,13},{10,... | collective-permute-start | bytes 589832 | tf_op jit(solution)/shard_map/ppermute | solution.py:26
  16.6 3.5 %g_split.1 = (bf16[128,2048]{1,0:T(8,128)(2,1)}, bf16[128,2048]{1,0:T(8,128)(2,1)}, bf16[128,2048]{1,0:T(8,128)(2,1)}, bf16[128,2048]{1,0:T(8,128)(2,1)}) custom-call(s32[4]{0:T(128)} %pad_add_fusion.refs_0_, bf16[128,8192]{1,0:T(8,128)(2,1)} %bitcast.10, bf16[128,768]{1,0:T(8,128)(2,1)} %get-tuple-element.31.refs_2_.refs_0_), custom_call_target="tpu_custom_call" | custom-call | flops 1000 | bytes 1000 | tf_op jit(solution)/shard_map/g_split/pallas_call | solution.py:47
  20.1 2.7 mask.1
  22.8 1.8 collective-permute-done.1.refs_2_
  25.3 2.1 w_join.1
  28.7 2.4 collective-permute-start.12
  33.1 1.6 collective-permute-start.16
  34.7 20.2 %collective-permute-done.10.refs_6_.refs_3_ = bf16[128,2048]{1,0:T(8,128)(2,1)S(1)} collective-permute-done((bf16[128,2048]{1,0:T(8,128)(2,1)}, bf16[128,2048]{1,0:T(8,128)(2,1)S(1)}, u32[]{:S(2)}, u32[]{:S(2)}) %collective-permute-start.10) | collective-permute-done | bytes 524320 | tf_op jit(solution)/shard_map/ppermute | solution.py:26
  55.4 3.2 %collective-permute-start.9 = (bf16[128,2048]{1,0:T(8,128)(2,1)S(1)}, bf16[128,2048]{1,0:T(8,128)(2,1)S(1)}, u32[]{:S(2)}, u32[]{:S(2)}) collective-permute-start(bf16[128,2048]{1,0:T(8,128)(2,1)S(1)} %copy-done.15), channel_id=1, source_target_pairs={{0,1},{1,0},{2,3},{3,2},{4,5},{5,4},{6,7},{7,6},{8,9},{9,8},{10,11... | collective-permute-start | bytes 1572872 | tf_op jit(solution)/shard_map/ppermute | solution.py:30
  58.6 12.2 %collective-permute-done.14.refs_8_.refs_5_ = bf16[128,2048]{1,0:T(8,128)(2,1)S(1)} collective-permute-done((bf16[128,2048]{1,0:T(8,128)(2,1)}, bf16[128,2048]{1,0:T(8,128)(2,1)S(1)}, u32[]{:S(2)}, u32[]{:S(2)}) %collective-permute-start.14) | collective-permute-done | bytes 524320 | tf_op jit(solution)/shard_map/ppermute | solution.py:26
  73.1 2.1 w_move.1
  75.3 3.3 %collective-permute-start.11 = (bf16[128,2048]{1,0:T(8,128)(2,1)}, bf16[128,2048]{1,0:T(8,128)(2,1)S(1)}, u32[]{:S(2)}, u32[]{:S(2)}) collective-permute-start(bf16[128,2048]{1,0:T(8,128)(2,1)} %copy-done.11), channel_id=1, source_target_pairs={{0,1},{1,0},{2,3},{3,2},{4,5},{5,4},{6,7},{7,6},{8,9},{9,8},{10,11... | collective-permute-start | bytes 1572872 | tf_op jit(solution)/shard_map/ppermute | solution.py:30
  80.1 2.0 collective-permute-start.8
  83.5 8.4 %collective-permute-done.11.refs_2_ = bf16[128,2048]{1,0:T(8,128)(2,1)S(1)} collective-permute-done((bf16[128,2048]{1,0:T(8,128)(2,1)}, bf16[128,2048]{1,0:T(8,128)(2,1)S(1)}, u32[]{:S(2)}, u32[]{:S(2)}) %collective-permute-start.11) | collective-permute-done | bytes 524320 | tf_op jit(solution)/shard_map/ppermute | solution.py:30
  93.1 8.1 %collective-permute-done.13.refs_3_ = bf16[128,2048]{1,0:T(8,128)(2,1)S(1)} collective-permute-done((bf16[128,2048]{1,0:T(8,128)(2,1)}, bf16[128,2048]{1,0:T(8,128)(2,1)S(1)}, u32[]{:S(2)}, u32[]{:S(2)}) %collective-permute-start.13) | collective-permute-done | bytes 524320 | tf_op jit(solution)/shard_map/ppermute | solution.py:30
  101.2 3.2 %collective-permute-start.15 = (bf16[128,2048]{1,0:T(8,128)(2,1)}, bf16[128,2048]{1,0:T(8,128)(2,1)S(1)}, u32[]{:S(2)}, u32[]{:S(2)}) collective-permute-start(bf16[128,2048]{1,0:T(8,128)(2,1)} %copy-done.13), channel_id=1, source_target_pairs={{0,1},{1,0},{2,3},{3,2},{4,5},{5,4},{6,7},{7,6},{8,9},{9,8},{10,11... | collective-permute-start | bytes 1572872 | tf_op jit(solution)/shard_map/ppermute | solution.py:30
  104.4 10.5 %collective-permute-done.15.refs_4_ = bf16[128,2048]{1,0:T(8,128)(2,1)S(1)} collective-permute-done((bf16[128,2048]{1,0:T(8,128)(2,1)}, bf16[128,2048]{1,0:T(8,128)(2,1)S(1)}, u32[]{:S(2)}, u32[]{:S(2)}) %collective-permute-start.15) | collective-permute-done | bytes 524320 | tf_op jit(solution)/shard_map/ppermute | solution.py:30
  115.7 4.6 %g_join.1.refs_0_ = bf16[1024,2048]{1,0:T(8,128)(2,1)} custom-call(s32[4]{0:T(128)} %pad_add_fusion.refs_0_, bf16[128,2048]{1,0:T(8,128)(2,1)} %copy-done.14, bf16[128,2048]{1,0:T(8,128)(2,1)} %copy-done.23, bf16[128,2048]{1,0:T(8,128)(2,1)} %copy-done.24, bf16[128,2048]{1,0:T(8,128)(2,1)} %copy-done.25, ...), custom_call_target="tpu_custom_call" | custom-call | flops 1000 | bytes 1000 | tf_op jit(solution)/shard_map/g_join/pallas_call | solution.py:47
  122.6 11.6 %term.2.refs_9_ = bf16[1024,3072]{1,0:T(8,128)(2,1)} custom-call(bf16[1024,2048]{1,0:T(8,128)(2,1)} %g_join.1.refs_0_, bf16[512,768]{1,0:T(8,128)(2,1)} %get-tuple-element.36.refs_4_.refs_1_, bf16[512,768]{1,0:T(8,128)(2,1)} %get-tuple-element.37.refs_2_, bf16[512,768]{1,0:T(8,128)(2,1)} %copy-done.1, bf16[512,768]{1,0:T(8,128)(2,1)} %copy-done.4, ...), custom_call_target="tpu_custom_call" | custom-call | flops 1000 | bytes 1000 | tf_op jit(solution)/shard_map/term/pallas_call | solution.py:47
  134.3 11.6 %term.3.refs_3_ = bf16[1024,3072]{1,0:T(8,128)(2,1)} custom-call(bf16[1024,2048]{1,0:T(8,128)(2,1)} %g_join.1.refs_0_, bf16[512,768]{1,0:T(8,128)(2,1)} %get-tuple-element.36.refs_4_.refs_1_, bf16[512,768]{1,0:T(8,128)(2,1)} %get-tuple-element.37.refs_2_, bf16[512,768]{1,0:T(8,128)(2,1)} %copy-done.1, bf16[512,768]{1,0:T(8,128)(2,1)} %copy-done.4, ...), custom_call_target="tpu_custom_call" | custom-call | flops 1000 | bytes 1000 | tf_op jit(solution)/shard_map/term/pallas_call | solution.py:47
  146.0 7.2 %rows_term.4 = (bf16[512,768]{1,0:T(8,128)(2,1)}, bf16[512,768]{1,0:T(8,128)(2,1)}) custom-call(bf16[1024,2048]{1,0:T(8,128)(2,1)} %g_join.1.refs_0_, bf16[1024,3072]{1,0:T(8,128)(2,1)} %all-gather.3.cloned.1.call-done.refs_1_.refs_0_, bf16[1024,3072]{1,0:T(8,128)(2,1)} %all-gather.5.cloned.1.call-done.refs_2_.refs_0_, bf16[1024,3072]{1,0:T(8,128)(2,1)} %term.3.refs_3_), custom_call_target="tpu_custom_call" | custom-call | flops 1000 | bytes 1000 | tf_op jit(solution)/shard_map/rows_term/pallas_call | solution.py:47
  153.2 3.1 %collective-permute-start.19 = (bf16[512,768]{1,0:T(8,128)(2,1)}, bf16[512,768]{1,0:T(8,128)(2,1)S(1)}, u32[]{:S(2)}, u32[]{:S(2)}) collective-permute-start(bf16[512,768]{1,0:T(8,128)(2,1)} %get-tuple-element.41.refs_9_), channel_id=1, source_target_pairs={{0,2},{1,3},{2,4},{3,5},{4,6},{5,7},{6,0},{7,1},{8,10},{9,11},{10,... | collective-permute-start | bytes 2359304 | tf_op jit(solution)/shard_map/ppermute | solution.py:26
  156.3 1.6 collective-permute-start.18
  157.9 11.7 %project.2 = (bf16[512,1024]{1,0:T(8,128)(2,1)}, f32[512,1024]{1,0:T(8,128)}) custom-call(bf16[1024,3072]{1,0:T(8,128)(2,1)} %all-gather.3.cloned.1.call-done.refs_1_.refs_0_, bf16[512,768]{1,0:T(8,128)(2,1)} %get-tuple-element.36.refs_4_.refs_1_, bf16[512,768]{1,0:T(8,128)(2,1)} %get-tuple-element.37.refs_2_, bf16[512,768]{1,0:T(8,128)(2,1)} %copy-done.1, ...), custom_call_target="tpu_custom_call" | custom-call | flops 1000 | bytes 1000 | tf_op jit(solution)/shard_map/project/pallas_call | solution.py:47
  169.6 3.3 %collective-permute-start.17 = (bf16[512,1024]{1,0:T(8,128)(2,1)}, bf16[512,1024]{1,0:T(8,128)(2,1)S(1)}, u32[]{:S(2)}, u32[]{:S(2)}) collective-permute-start(bf16[512,1024]{1,0:T(8,128)(2,1)} %get-tuple-element.43), channel_id=1, source_target_pairs={{0,1},{1,0},{2,3},{3,2},{4,5},{5,4},{6,7},{7,6},{8,9},{9,8},{10,11... | collective-permute-start | bytes 3145736 | tf_op jit(solution)/shard_map/ppermute | solution.py:30
  175.0 7.7 %rows_term.5.refs_4_ = bf16[1024,768]{1,0:T(8,128)(2,1)} custom-call(bf16[1024,2048]{1,0:T(8,128)(2,1)} %g_join.1.refs_0_, bf16[1024,3072]{1,0:T(8,128)(2,1)} %all-gather.3.cloned.1.call-done.refs_1_.refs_0_, bf16[1024,3072]{1,0:T(8,128)(2,1)} %all-gather.5.cloned.1.call-done.refs_2_.refs_0_, bf16[512,768]{1,0:T(8,128)(2,1)} %copy-done.22, ...), custom_call_target="tpu_custom_call" | custom-call | flops 1000 | bytes 1000 | tf_op jit(solution)/shard_map/rows_term/pallas_call | solution.py:47
  183.6 7.6 %rows_term.6.refs_3_ = bf16[1024,768]{1,0:T(8,128)(2,1)} custom-call(bf16[1024,2048]{1,0:T(8,128)(2,1)} %g_join.1.refs_0_, bf16[1024,3072]{1,0:T(8,128)(2,1)} %all-gather.3.cloned.1.call-done.refs_1_.refs_0_, bf16[1024,3072]{1,0:T(8,128)(2,1)} %all-gather.5.cloned.1.call-done.refs_2_.refs_0_, bf16[512,768]{1,0:T(8,128)(2,1)} %copy-done.20, ...), custom_call_target="tpu_custom_call" | custom-call | flops 1000 | bytes 1000 | tf_op jit(solution)/shard_map/rows_term/pallas_call | solution.py:47
  191.2 1.7 collective-permute-start.25
  193.3 7.7 %rows_term.7.refs_1_.refs_9_.refs_2_ = f32[1024,768]{1,0:T(8,128)} custom-call(bf16[1024,2048]{1,0:T(8,128)(2,1)} %g_join.1.refs_0_, bf16[1024,3072]{1,0:T(8,128)(2,1)} %all-gather.3.cloned.1.call-done.refs_1_.refs_0_, bf16[1024,3072]{1,0:T(8,128)(2,1)} %all-gather.5.cloned.1.call-done.refs_2_.refs_0_, bf16[1024,768]{1,0:T(8,128)(2,1)} %rows_term.6.refs_3_), custom_call_target="tpu_custom_call" | custom-call | flops 1000 | bytes 1000 | tf_op jit(solution)/shard_map/rows_term/pallas_call | solution.py:47
  200.9 2.1 move.1.refs_10_
  204.0 11.7 %project.3 = (bf16[512,1024]{1,0:T(8,128)(2,1)}, f32[512,1024]{1,0:T(8,128)}) custom-call(bf16[1024,3072]{1,0:T(8,128)(2,1)} %all-gather.5.cloned.1.call-done.refs_2_.refs_0_, bf16[512,768]{1,0:T(8,128)(2,1)} %get-tuple-element.36.refs_4_.refs_1_, bf16[512,768]{1,0:T(8,128)(2,1)} %get-tuple-element.37.refs_2_, bf16[512,768]{1,0:T(8,128)(2,1)} %copy-done.1, ...), custom_call_target="tpu_custom_call" | custom-call | flops 1000 | bytes 1000 | tf_op jit(solution)/shard_map/project/pallas_call | solution.py:47
  215.7 3.2 %collective-permute-start.23 = (bf16[512,1024]{1,0:T(8,128)(2,1)}, bf16[512,1024]{1,0:T(8,128)(2,1)S(1)}, u32[]{:S(2)}, u32[]{:S(2)}) collective-permute-start(bf16[512,1024]{1,0:T(8,128)(2,1)} %get-tuple-element.50), channel_id=1, source_target_pairs={{0,1},{1,0},{2,3},{3,2},{4,5},{5,4},{6,7},{7,6},{8,9},{9,8},{10,11... | collective-permute-start | bytes 3145736 | tf_op jit(solution)/shard_map/ppermute | solution.py:30
  219.4 3.0 %settle.2 = (bf16[128,1024]{1,0:T(8,128)(2,1)}, bf16[128,1024]{1,0:T(8,128)(2,1)}, bf16[128,1024]{1,0:T(8,128)(2,1)}, bf16[128,1024]{1,0:T(8,128)(2,1)}) custom-call(s32[4]{0:T(128)} %pad_add_fusion.refs_0_, f32[512,1024]{1,0:T(8,128)} %get-tuple-element.42.refs_4_.refs_1_, bf16[512,1024]{1,0:T(8,128)(2,1)} %copy-done.9, ...), custom_call_target="tpu_custom_call" | custom-call | flops 1000 | bytes 1000 | tf_op jit(solution)/shard_map/settle/pallas_call | solution.py:47
  222.7 3.1 %collective-permute-done.25.refs_4_ = bf16[1024,768]{1,0:T(8,128)(2,1)} collective-permute-done((bf16[1024,768]{1,0:T(8,128)(2,1)}, bf16[1024,768]{1,0:T(8,128)(2,1)}, u32[]{:S(2)}, u32[]{:S(2)}) %collective-permute-start.25) | collective-permute-done | bytes 1572896 | tf_op jit(solution)/shard_map/ppermute | solution.py:26
  227.1 4.5 %collective-permute-done.24.refs_3_ = bf16[1024,768]{1,0:T(8,128)(2,1)} collective-permute-done((bf16[1024,768]{1,0:T(8,128)(2,1)S(1)}, bf16[1024,768]{1,0:T(8,128)(2,1)}, u32[]{:S(2)}, u32[]{:S(2)}) %collective-permute-start.24) | collective-permute-done | bytes 1572896 | tf_op jit(solution)/shard_map/ppermute | solution.py:26
  231.6 4.5 %add_rows.1.refs_3_ = bf16[1024,768]{1,0:T(8,128)(2,1)} custom-call(s32[4]{0:T(128)} %pad_add_fusion.refs_0_, s32[8]{0:T(128)} %refs_1_.5, f32[1024,768]{1,0:T(8,128)} %rows_term.7.refs_1_.refs_9_.refs_2_, bf16[1024,768]{1,0:T(8,128)(2,1)} %collective-permute-done.24.refs_3_, bf16[1024,768]{1,0:T(8,128)(2,1)} %collective-permute-done.25.refs_4_), custom_call_target="tpu_custom_call" | custom-call | flops 1000 | bytes 1000 | tf_op jit(solution)/shard_map/add_rows/pallas_call | solution.py:47
  236.2 7.3 %collective-permute-done.23.refs_2_ = bf16[512,1024]{1,0:T(8,128)(2,1)S(1)} collective-permute-done((bf16[512,1024]{1,0:T(8,128)(2,1)}, bf16[512,1024]{1,0:T(8,128)(2,1)S(1)}, u32[]{:S(2)}, u32[]{:S(2)}) %collective-permute-start.23) | collective-permute-done | bytes 1048608 | tf_op jit(solution)/shard_map/ppermute | solution.py:30
  244.5 3.0 %settle.3 = (bf16[128,1024]{1,0:T(8,128)(2,1)}, bf16[128,1024]{1,0:T(8,128)(2,1)}, bf16[128,1024]{1,0:T(8,128)(2,1)}, bf16[128,1024]{1,0:T(8,128)(2,1)}) custom-call(s32[4]{0:T(128)} %pad_add_fusion.refs_0_, f32[512,1024]{1,0:T(8,128)} %get-tuple-element.45.refs_3_.refs_1_, bf16[512,1024]{1,0:T(8,128)(2,1)} %copy-done.16, bf16[1024,768]{1,0:T(8,128)(2,1)} %add_rows.1.refs_3_), custom_call_target="tpu_custom_call" | custom-call | flops 1000 | bytes 1000 | tf_op jit(solution)/shard_map/settle/pallas_call | solution.py:47
  247.8 4.1 %collective-permute-start.27 = (bf16[128,1024]{1,0:T(8,128)(2,1)}, bf16[128,1024]{1,0:T(8,128)(2,1)S(1)}, u32[]{:S(2)}, u32[]{:S(2)}) collective-permute-start(bf16[128,1024]{1,0:T(8,128)(2,1)} %get-tuple-element.53), channel_id=1, source_target_pairs={{0,4},{1,5},{2,6},{3,7},{4,0},{5,1},{6,2},{7,3},{8,12},{9,13},{10,... | collective-permute-start | bytes 786440 | tf_op jit(solution)/shard_map/ppermute | solution.py:26
  251.9 5.1 %collective-permute-done.29.refs_1_ = bf16[128,3072]{1,0:T(8,128)(2,1)} collective-permute-done((bf16[128,3072]{1,0:T(8,128)(2,1)S(1)}, bf16[128,3072]{1,0:T(8,128)(2,1)}, u32[]{:S(2)}, u32[]{:S(2)}) %collective-permute-start.29) | collective-permute-done | bytes 786464 | tf_op jit(solution)/shard_map/ppermute | solution.py:271
  257.0 2.3 add_terms.1
  259.4 2.8 collective-permute-start.30
  263.8 3.3 %join_out.1.refs_5_ = bf16[128,8192]{1,0:T(8,128)(2,1)} custom-call(s32[4]{0:T(128)} %pad_add_fusion.refs_0_, bf16[128,1024]{1,0:T(8,128)(2,1)} %get-tuple-element.46.refs_1_, bf16[128,1024]{1,0:T(8,128)(2,1)} %copy-done.17, bf16[128,1024]{1,0:T(8,128)(2,1)} %copy-done.18, bf16[128,1024]{1,0:T(8,128)(2,1)} %copy-done.19, ...), custom_call_target="tpu_custom_call" | custom-call | flops 1000 | bytes 1000 | tf_op jit(solution)/shard_map/join_out/pallas_call | solution.py:47
  267.8 1.8 collective-permute-done.31.refs_3_
  269.6 1.8 collective-permute-done.32.refs_4_
  272.1 2.5 join_term.1
  (122 shorter events, 26.5 us)
Async XLA Ops:
  7.2 138.8 %all-gather.3.cloned.1.call-start = ((), (), s32[]{:S(2)}) async-start(), calls=%async_computation.2 | async-start | bytes 7077888 | tf_op jit(solution)/shard_map/all_gather | solution.py:140
  10.0 12.8 %collective-permute-start = (bf16[128,768]{1,0:T(8,128)(2,1)}, bf16[128,768]{1,0:T(8,128)(2,1)S(1)}, u32[]{:S(2)}, u32[]{:S(2)}) collective-permute-start(bf16[128,768]{1,0:T(8,128)(2,1)} %get-tuple-element.32), channel_id=1, source_target_pairs={{0,2},{1,3},{2,4},{3,5},{4,6},{5,7},{6,0},{7,1},{8,10},{9,11},{10,... | collective-permute-start | bytes 589832 | tf_op jit(solution)/shard_map/ppermute | solution.py:26
  12.0 12.6 %collective-permute-start.1 = (bf16[128,768]{1,0:T(8,128)(2,1)}, bf16[128,768]{1,0:T(8,128)(2,1)S(1)}, u32[]{:S(2)}, u32[]{:S(2)}) collective-permute-start(bf16[128,768]{1,0:T(8,128)(2,1)} %get-tuple-element.33), channel_id=1, source_target_pairs={{0,4},{1,5},{2,6},{3,7},{4,0},{5,1},{6,2},{7,3},{8,12},{9,13},{10,... | collective-permute-start | bytes 589832 | tf_op jit(solution)/shard_map/ppermute | solution.py:26
  15.6 9.0 %collective-permute-start.2 = (bf16[128,768]{1,0:T(8,128)(2,1)}, bf16[128,768]{1,0:T(8,128)(2,1)S(1)}, u32[]{:S(2)}, u32[]{:S(2)}) collective-permute-start(bf16[128,768]{1,0:T(8,128)(2,1)} %get-tuple-element.34), channel_id=1, source_target_pairs={{0,6},{1,7},{2,0},{3,1},{4,2},{5,3},{6,4},{7,5},{8,14},{9,15},{10,... | collective-permute-start | bytes 589832 | tf_op jit(solution)/shard_map/ppermute | solution.py:26
  22.7 8.4 %copy-start.3 = (bf16[512,768]{1,0:T(8,128)(2,1)S(1)}, bf16[512,768]{1,0:T(8,128)(2,1)}, u32[]{:S(2)}) copy-start(bf16[512,768]{1,0:T(8,128)(2,1)} %get-tuple-element.37.refs_2_) | copy-start | bytes 2359300
  22.7 9.7 %copy-start.2 = (bf16[512,768]{1,0:T(8,128)(2,1)S(1)}, bf16[512,768]{1,0:T(8,128)(2,1)}, u32[]{:S(2)}) copy-start(bf16[512,768]{1,0:T(8,128)(2,1)} %get-tuple-element.36.refs_4_.refs_1_) | copy-start | bytes 2359300
  22.7 32.6 %copy-start.15 = (bf16[128,2048]{1,0:T(8,128)(2,1)S(1)}, bf16[128,2048]{1,0:T(8,128)(2,1)}, u32[]{:S(2)}) copy-start(bf16[128,2048]{1,0:T(8,128)(2,1)} %get-tuple-element.35.refs_3_.refs_5_) | copy-start | bytes 1572868
  27.5 118.5 %all-gather.5.cloned.1.call-start = ((), (), s32[]{:S(2)}) async-start(), calls=%async_computation.3 | async-start | bytes 7077888 | tf_op jit(solution)/shard_map/all_gather | solution.py:140
  27.6 27.4 %collective-permute-start.10 = (bf16[128,2048]{1,0:T(8,128)(2,1)}, bf16[128,2048]{1,0:T(8,128)(2,1)S(1)}, u32[]{:S(2)}, u32[]{:S(2)}) collective-permute-start(bf16[128,2048]{1,0:T(8,128)(2,1)} %get-tuple-element.38), channel_id=1, source_target_pairs={{0,2},{1,3},{2,4},{3,5},{4,6},{5,7},{6,0},{7,1},{8,10},{9,11},{10,... | collective-permute-start | bytes 1572872 | tf_op jit(solution)/shard_map/ppermute | solution.py:26
  28.7 26.6 %collective-permute-start.12 = (bf16[128,2048]{1,0:T(8,128)(2,1)}, bf16[128,2048]{1,0:T(8,128)(2,1)S(1)}, u32[]{:S(2)}, u32[]{:S(2)}) collective-permute-start(bf16[128,2048]{1,0:T(8,128)(2,1)} %get-tuple-element.39), channel_id=1, source_target_pairs={{0,4},{1,5},{2,6},{3,7},{4,0},{5,1},{6,2},{7,3},{8,12},{9,13},{10,... | collective-permute-start | bytes 1572872 | tf_op jit(solution)/shard_map/ppermute | solution.py:26
  31.1 39.6 %collective-permute-start.6 = (bf16[512,768]{1,0:T(8,128)(2,1)S(1)}, bf16[512,768]{1,0:T(8,128)(2,1)S(1)}, u32[]{:S(2)}, u32[]{:S(2)}) collective-permute-start(bf16[512,768]{1,0:T(8,128)(2,1)S(1)} %copy-done.3), channel_id=1, source_target_pairs={{0,6},{1,7},{2,0},{3,1},{4,2},{5,3},{6,4},{7,5},{8,14},{9,15},{10,... | collective-permute-start | bytes 2359304 | tf_op jit(solution)/shard_map/ppermute | solution.py:26
  32.5 38.3 %collective-permute-start.3 = (bf16[512,768]{1,0:T(8,128)(2,1)S(1)}, bf16[512,768]{1,0:T(8,128)(2,1)S(1)}, u32[]{:S(2)}, u32[]{:S(2)}) collective-permute-start(bf16[512,768]{1,0:T(8,128)(2,1)S(1)} %copy-done.2), channel_id=1, source_target_pairs={{0,2},{1,3},{2,4},{3,5},{4,6},{5,7},{6,0},{7,1},{8,10},{9,11},{10,... | collective-permute-start | bytes 2359304 | tf_op jit(solution)/shard_map/ppermute | solution.py:26
  33.1 37.6 %collective-permute-start.16 = (bf16[128,3072]{1,0:T(8,128)(2,1)}, bf16[128,3072]{1,0:T(8,128)(2,1)S(1)}, u32[]{:S(2)}, u32[]{:S(2)}) collective-permute-start(bf16[128,3072]{1,0:T(8,128)(2,1)} %w_join.1), channel_id=1, source_target_pairs={{0,64},{8,72},{16,80},{24,88},{32,96},{40,104},{48,112},{56,120},{... | collective-permute-start | bytes 2359304 | tf_op jit(solution)/shard_map/ppermute | solution.py:135
  54.9 15.8 %copy-start.11 = (bf16[128,2048]{1,0:T(8,128)(2,1)}, bf16[128,2048]{1,0:T(8,128)(2,1)S(1)}, u32[]{:S(2)}) copy-start(bf16[128,2048]{1,0:T(8,128)(2,1)S(1)} %collective-permute-done.10.refs_6_.refs_3_) | copy-start | bytes 1572868
  54.9 15.8 %collective-permute-start.14 = (bf16[128,2048]{1,0:T(8,128)(2,1)}, bf16[128,2048]{1,0:T(8,128)(2,1)S(1)}, u32[]{:S(2)}, u32[]{:S(2)}) collective-permute-start(bf16[128,2048]{1,0:T(8,128)(2,1)} %get-tuple-element.40), channel_id=1, source_target_pairs={{0,6},{1,7},{2,0},{3,1},{4,2},{5,3},{6,4},{7,5},{8,14},{9,15},{10,... | collective-permute-start | bytes 1572872 | tf_op jit(solution)/shard_map/ppermute | solution.py:26
  55.4 15.4 %copy-start.12 = (bf16[128,2048]{1,0:T(8,128)(2,1)}, bf16[128,2048]{1,0:T(8,128)(2,1)S(1)}, u32[]{:S(2)}) copy-start(bf16[128,2048]{1,0:T(8,128)(2,1)S(1)} %collective-permute-done.12.refs_7_.refs_4_) | copy-start | bytes 1572868
  55.4 15.4 %collective-permute-start.9 = (bf16[128,2048]{1,0:T(8,128)(2,1)S(1)}, bf16[128,2048]{1,0:T(8,128)(2,1)S(1)}, u32[]{:S(2)}, u32[]{:S(2)}) collective-permute-start(bf16[128,2048]{1,0:T(8,128)(2,1)S(1)} %copy-done.15), channel_id=1, source_target_pairs={{0,1},{1,0},{2,3},{3,2},{4,5},{5,4},{6,7},{7,6},{8,9},{9,8},{10,11... | collective-permute-start | bytes 1572872 | tf_op jit(solution)/shard_map/ppermute | solution.py:30
  75.2 125.7 %reduce-scatter.3.cloned.1.call-start = ((), (), s32[]{:S(2)}) async-start(), calls=%async_computation.4 | async-start | bytes 7077888 | tf_op jit(solution)/shard_map/reduce_scatter | solution.py:230
  75.3 16.7 %collective-permute-start.11 = (bf16[128,2048]{1,0:T(8,128)(2,1)}, bf16[128,2048]{1,0:T(8,128)(2,1)S(1)}, u32[]{:S(2)}, u32[]{:S(2)}) collective-permute-start(bf16[128,2048]{1,0:T(8,128)(2,1)} %copy-done.11), channel_id=1, source_target_pairs={{0,1},{1,0},{2,3},{3,2},{4,5},{5,4},{6,7},{7,6},{8,9},{9,8},{10,11... | collective-permute-start | bytes 1572872 | tf_op jit(solution)/shard_map/ppermute | solution.py:30
  78.5 22.6 %collective-permute-start.13 = (bf16[128,2048]{1,0:T(8,128)(2,1)}, bf16[128,2048]{1,0:T(8,128)(2,1)S(1)}, u32[]{:S(2)}, u32[]{:S(2)}) collective-permute-start(bf16[128,2048]{1,0:T(8,128)(2,1)} %copy-done.12), channel_id=1, source_target_pairs={{0,1},{1,0},{2,3},{3,2},{4,5},{5,4},{6,7},{7,6},{8,9},{9,8},{10,11... | collective-permute-start | bytes 1572872 | tf_op jit(solution)/shard_map/ppermute | solution.py:30
  78.9 41.5 %collective-permute-start.4 = (bf16[512,768]{1,0:T(8,128)(2,1)S(1)}, bf16[512,768]{1,0:T(8,128)(2,1)S(1)}, u32[]{:S(2)}, u32[]{:S(2)}) collective-permute-start(bf16[512,768]{1,0:T(8,128)(2,1)S(1)} %copy-done.3), channel_id=1, source_target_pairs={{0,2},{1,3},{2,4},{3,5},{4,6},{5,7},{6,0},{7,1},{8,10},{9,11},{10,... | collective-permute-start | bytes 2359304 | tf_op jit(solution)/shard_map/ppermute | solution.py:26
  80.1 40.2 %collective-permute-start.8 = (bf16[512,768]{1,0:T(8,128)(2,1)S(1)}, bf16[512,768]{1,0:T(8,128)(2,1)S(1)}, u32[]{:S(2)}, u32[]{:S(2)}) collective-permute-start(bf16[512,768]{1,0:T(8,128)(2,1)S(1)} %copy-done.2), channel_id=1, source_target_pairs={{0,6},{1,7},{2,0},{3,1},{4,2},{5,3},{6,4},{7,5},{8,14},{9,15},{10,... | collective-permute-start | bytes 2359304 | tf_op jit(solution)/shard_map/ppermute | solution.py:26
  82.1 38.2 %collective-permute-start.7 = (bf16[512,768]{1,0:T(8,128)(2,1)}, bf16[512,768]{1,0:T(8,128)(2,1)S(1)}, u32[]{:S(2)}, u32[]{:S(2)}) collective-permute-start(bf16[512,768]{1,0:T(8,128)(2,1)} %copy-done), channel_id=1, source_target_pairs={{0,6},{1,7},{2,0},{3,1},{4,2},{5,3},{6,4},{7,5},{8,14},{9,15},{10,... | collective-permute-start | bytes 2359304 | tf_op jit(solution)/shard_map/ppermute | solution.py:26
  91.9 23.0 %copy-start.23 = (bf16[128,2048]{1,0:T(8,128)(2,1)}, bf16[128,2048]{1,0:T(8,128)(2,1)S(1)}, u32[]{:S(2)}) copy-start(bf16[128,2048]{1,0:T(8,128)(2,1)S(1)} %collective-permute-done.11.refs_2_) | copy-start | bytes 1572868
  91.9 28.5 %collective-permute-start.5 = (bf16[512,768]{1,0:T(8,128)(2,1)}, bf16[512,768]{1,0:T(8,128)(2,1)S(1)}, u32[]{:S(2)}, u32[]{:S(2)}) collective-permute-start(bf16[512,768]{1,0:T(8,128)(2,1)} %copy-done.1), channel_id=1, source_target_pairs={{0,2},{1,3},{2,4},{3,5},{4,6},{5,7},{6,0},{7,1},{8,10},{9,11},{10,... | collective-permute-start | bytes 2359304 | tf_op jit(solution)/shard_map/ppermute | solution.py:26
  101.2 13.7 %copy-start.24 = (bf16[128,2048]{1,0:T(8,128)(2,1)}, bf16[128,2048]{1,0:T(8,128)(2,1)S(1)}, u32[]{:S(2)}) copy-start(bf16[128,2048]{1,0:T(8,128)(2,1)S(1)} %collective-permute-done.13.refs_3_) | copy-start | bytes 1572868
  101.2 13.7 %collective-permute-start.15 = (bf16[128,2048]{1,0:T(8,128)(2,1)}, bf16[128,2048]{1,0:T(8,128)(2,1)S(1)}, u32[]{:S(2)}, u32[]{:S(2)}) collective-permute-start(bf16[128,2048]{1,0:T(8,128)(2,1)} %copy-done.13), channel_id=1, source_target_pairs={{0,1},{1,0},{2,3},{3,2},{4,5},{5,4},{6,7},{7,6},{8,9},{9,8},{10,11... | collective-permute-start | bytes 1572872 | tf_op jit(solution)/shard_map/ppermute | solution.py:30
  134.3 117.6 %reduce-scatter.5.cloned.1.call-start = ((), (), s32[]{:S(2)}) async-start(), calls=%async_computation.5 | async-start | bytes 7077888 | tf_op jit(solution)/shard_map/reduce_scatter | solution.py:230
  153.2 21.0 %collective-permute-start.19 = (bf16[512,768]{1,0:T(8,128)(2,1)}, bf16[512,768]{1,0:T(8,128)(2,1)S(1)}, u32[]{:S(2)}, u32[]{:S(2)}) collective-permute-start(bf16[512,768]{1,0:T(8,128)(2,1)} %get-tuple-element.41.refs_9_), channel_id=1, source_target_pairs={{0,2},{1,3},{2,4},{3,5},{4,6},{5,7},{6,0},{7,1},{8,10},{9,11},{10,... | collective-permute-start | bytes 2359304 | tf_op jit(solution)/shard_map/ppermute | solution.py:26
  156.3 26.4 %collective-permute-start.18 = (bf16[512,768]{1,0:T(8,128)(2,1)}, bf16[512,768]{1,0:T(8,128)(2,1)S(1)}, u32[]{:S(2)}, u32[]{:S(2)}) collective-permute-start(bf16[512,768]{1,0:T(8,128)(2,1)} %get-tuple-element.44), channel_id=1, source_target_pairs={{0,6},{1,7},{2,0},{3,1},{4,2},{5,3},{6,4},{7,5},{8,14},{9,15},{10,... | collective-permute-start | bytes 2359304 | tf_op jit(solution)/shard_map/ppermute | solution.py:26
  169.6 33.4 %collective-permute-start.17 = (bf16[512,1024]{1,0:T(8,128)(2,1)}, bf16[512,1024]{1,0:T(8,128)(2,1)S(1)}, u32[]{:S(2)}, u32[]{:S(2)}) collective-permute-start(bf16[512,1024]{1,0:T(8,128)(2,1)} %get-tuple-element.43), channel_id=1, source_target_pairs={{0,1},{1,0},{2,3},{3,2},{4,5},{5,4},{6,7},{7,6},{8,9},{9,8},{10,11... | collective-permute-start | bytes 3145736 | tf_op jit(solution)/shard_map/ppermute | solution.py:30
  182.7 10.2 %copy-start.8 = (bf16[1024,768]{1,0:T(8,128)(2,1)S(1)}, bf16[1024,768]{1,0:T(8,128)(2,1)}, u32[]{:S(2)}) copy-start(bf16[1024,768]{1,0:T(8,128)(2,1)} %rows_term.5.refs_4_) | copy-start | bytes 4718596
  191.2 34.6 %collective-permute-start.25 = (bf16[1024,768]{1,0:T(8,128)(2,1)}, bf16[1024,768]{1,0:T(8,128)(2,1)}, u32[]{:S(2)}, u32[]{:S(2)}) collective-permute-start(bf16[1024,768]{1,0:T(8,128)(2,1)} %rows_term.6.refs_3_), channel_id=1, source_target_pairs={{0,6},{1,7},{2,0},{3,1},{4,2},{5,3},{6,4},{7,5},{8,14},{9,15},{10,... | collective-permute-start | bytes 4718600 | tf_op jit(solution)/shard_map/ppermute | solution.py:26
  193.0 38.6 %collective-permute-start.24 = (bf16[1024,768]{1,0:T(8,128)(2,1)S(1)}, bf16[1024,768]{1,0:T(8,128)(2,1)}, u32[]{:S(2)}, u32[]{:S(2)}) collective-permute-start(bf16[1024,768]{1,0:T(8,128)(2,1)S(1)} %copy-done.8), channel_id=1, source_target_pairs={{0,2},{1,3},{2,4},{3,5},{4,6},{5,7},{6,0},{7,1},{8,10},{9,11},{10,... | collective-permute-start | bytes 4718600 | tf_op jit(solution)/shard_map/ppermute | solution.py:26
  203.0 15.9 %copy-start.10 = (bf16[128,3072]{1,0:T(8,128)(2,1)S(1)}, bf16[128,3072]{1,0:T(8,128)(2,1)}, u32[]{:S(2)}) copy-start(bf16[128,3072]{1,0:T(8,128)(2,1)} %move.1.refs_10_) | copy-start | bytes 2359300
  215.7 27.8 %collective-permute-start.23 = (bf16[512,1024]{1,0:T(8,128)(2,1)}, bf16[512,1024]{1,0:T(8,128)(2,1)S(1)}, u32[]{:S(2)}, u32[]{:S(2)}) collective-permute-start(bf16[512,1024]{1,0:T(8,128)(2,1)} %get-tuple-element.50), channel_id=1, source_target_pairs={{0,1},{1,0},{2,3},{3,2},{4,5},{5,4},{6,7},{7,6},{8,9},{9,8},{10,11... | collective-permute-start | bytes 3145736 | tf_op jit(solution)/shard_map/ppermute | solution.py:30
  218.9 38.1 %collective-permute-start.29 = (bf16[128,3072]{1,0:T(8,128)(2,1)S(1)}, bf16[128,3072]{1,0:T(8,128)(2,1)}, u32[]{:S(2)}, u32[]{:S(2)}) collective-permute-start(bf16[128,3072]{1,0:T(8,128)(2,1)S(1)} %copy-done.10), channel_id=1, source_target_pairs={{0,64},{8,72},{16,80},{24,88},{32,96},{40,104},{48,112},{56,120},{... | collective-permute-start | bytes 2359304 | tf_op jit(solution)/shard_map/ppermute | solution.py:271
  222.3 25.4 %collective-permute-start.20 = (bf16[128,1024]{1,0:T(8,128)(2,1)}, bf16[128,1024]{1,0:T(8,128)(2,1)S(1)}, u32[]{:S(2)}, u32[]{:S(2)}) collective-permute-start(bf16[128,1024]{1,0:T(8,128)(2,1)} %get-tuple-element.47), channel_id=1, source_target_pairs={{0,2},{1,3},{2,4},{3,5},{4,6},{5,7},{6,0},{7,1},{8,10},{9,11},{10,... | collective-permute-start | bytes 786440 | tf_op jit(solution)/shard_map/ppermute | solution.py:26
  225.8 26.0 %collective-permute-start.21 = (bf16[128,1024]{1,0:T(8,128)(2,1)}, bf16[128,1024]{1,0:T(8,128)(2,1)S(1)}, u32[]{:S(2)}, u32[]{:S(2)}) collective-permute-start(bf16[128,1024]{1,0:T(8,128)(2,1)} %get-tuple-element.48), channel_id=1, source_target_pairs={{0,4},{1,5},{2,6},{3,7},{4,0},{5,1},{6,2},{7,3},{8,12},{9,13},{10,... | collective-permute-start | bytes 786440 | tf_op jit(solution)/shard_map/ppermute | solution.py:26
  231.6 20.3 %collective-permute-start.22 = (bf16[128,1024]{1,0:T(8,128)(2,1)}, bf16[128,1024]{1,0:T(8,128)(2,1)S(1)}, u32[]{:S(2)}, u32[]{:S(2)}) collective-permute-start(bf16[128,1024]{1,0:T(8,128)(2,1)} %get-tuple-element.49), channel_id=1, source_target_pairs={{0,6},{1,7},{2,0},{3,1},{4,2},{5,3},{6,4},{7,5},{8,14},{9,15},{10,... | collective-permute-start | bytes 786440 | tf_op jit(solution)/shard_map/ppermute | solution.py:26
  247.4 14.7 %collective-permute-start.26 = (bf16[128,1024]{1,0:T(8,128)(2,1)}, bf16[128,1024]{1,0:T(8,128)(2,1)S(1)}, u32[]{:S(2)}, u32[]{:S(2)}) collective-permute-start(bf16[128,1024]{1,0:T(8,128)(2,1)} %get-tuple-element.52), channel_id=1, source_target_pairs={{0,2},{1,3},{2,4},{3,5},{4,6},{5,7},{6,0},{7,1},{8,10},{9,11},{10,... | collective-permute-start | bytes 786440 | tf_op jit(solution)/shard_map/ppermute | solution.py:26
  247.8 9.3 %copy-start.17 = (bf16[128,1024]{1,0:T(8,128)(2,1)}, bf16[128,1024]{1,0:T(8,128)(2,1)S(1)}, u32[]{:S(2)}) copy-start(bf16[128,1024]{1,0:T(8,128)(2,1)S(1)} %collective-permute-done.20.refs_2_.refs_3_) | copy-start | bytes 786436
  247.8 15.2 %collective-permute-start.27 = (bf16[128,1024]{1,0:T(8,128)(2,1)}, bf16[128,1024]{1,0:T(8,128)(2,1)S(1)}, u32[]{:S(2)}, u32[]{:S(2)}) collective-permute-start(bf16[128,1024]{1,0:T(8,128)(2,1)} %get-tuple-element.53), channel_id=1, source_target_pairs={{0,4},{1,5},{2,6},{3,7},{4,0},{5,1},{6,2},{7,3},{8,12},{9,13},{10,... | collective-permute-start | bytes 786440 | tf_op jit(solution)/shard_map/ppermute | solution.py:26
  251.8 5.2 %copy-start.18 = (bf16[128,1024]{1,0:T(8,128)(2,1)}, bf16[128,1024]{1,0:T(8,128)(2,1)S(1)}, u32[]{:S(2)}) copy-start(bf16[128,1024]{1,0:T(8,128)(2,1)S(1)} %collective-permute-done.21.refs_3_.refs_4_) | copy-start | bytes 786436
  251.8 11.2 %collective-permute-start.28 = (bf16[128,1024]{1,0:T(8,128)(2,1)}, bf16[128,1024]{1,0:T(8,128)(2,1)S(1)}, u32[]{:S(2)}, u32[]{:S(2)}) collective-permute-start(bf16[128,1024]{1,0:T(8,128)(2,1)} %get-tuple-element.54), channel_id=1, source_target_pairs={{0,6},{1,7},{2,0},{3,1},{4,2},{5,3},{6,4},{7,5},{8,14},{9,15},{10,... | collective-permute-start | bytes 786440 | tf_op jit(solution)/shard_map/ppermute | solution.py:26
  259.4 8.4 %collective-permute-start.30 = (bf16[128,768]{1,0:T(8,128)(2,1)}, bf16[128,768]{1,0:T(8,128)(2,1)S(1)}, u32[]{:S(2)}, u32[]{:S(2)}) collective-permute-start(bf16[128,768]{1,0:T(8,128)(2,1)} %get-tuple-element.56), channel_id=1, source_target_pairs={{0,6},{1,7},{2,0},{3,1},{4,2},{5,3},{6,4},{7,5},{8,14},{9,15},{10,... | collective-permute-start | bytes 589832 | tf_op jit(solution)/shard_map/ppermute | solution.py:26
  262.1 7.5 %collective-permute-start.31 = (bf16[128,768]{1,0:T(8,128)(2,1)}, bf16[128,768]{1,0:T(8,128)(2,1)S(1)}, u32[]{:S(2)}, u32[]{:S(2)}) collective-permute-start(bf16[128,768]{1,0:T(8,128)(2,1)} %get-tuple-element.57), channel_id=1, source_target_pairs={{0,4},{1,5},{2,6},{3,7},{4,0},{5,1},{6,2},{7,3},{8,12},{9,13},{10,... | collective-permute-start | bytes 589832 | tf_op jit(solution)/shard_map/ppermute | solution.py:26
  262.2 9.3 %collective-permute-start.32 = (bf16[128,768]{1,0:T(8,128)(2,1)}, bf16[128,768]{1,0:T(8,128)(2,1)S(1)}, u32[]{:S(2)}, u32[]{:S(2)}) collective-permute-start(bf16[128,768]{1,0:T(8,128)(2,1)} %get-tuple-element.58), channel_id=1, source_target_pairs={{0,2},{1,3},{2,4},{3,5},{4,6},{5,7},{6,0},{7,1},{8,10},{9,11},{10,... | collective-permute-start | bytes 589832 | tf_op jit(solution)/shard_map/ppermute | solution.py:26
  (24 other events, 31.2 us)
Sparse Core Ops, SparseCore 0:
  27.6 41.3 all-gather.2
  75.3 41.8 all-gather.4
  134.4 45.3 reduce-scatter.2
  182.1 42.5 reduce-scatter.4

commit v9 on v8

--- a/solution.py
+++ b/solution.py
@@ -13,7 +13,7 @@
 SMEM = pl.BlockSpec(memory_space=pltpu.SMEM)
 VMEM = pl.BlockSpec(memory_space=pltpu.VMEM)
 BIG = 56 << 20
-SMALL = 56 << 20
+SMALL = 32 << 20
 
 
 def ring(step):
@@ -38,7 +38,7 @@
     return jax.ShapeDtypeStruct(shape, dtype)
 
 
-def run(body, out, args, specs, after=(), grid=(), out_specs=VMEM, name=None, limit=SMALL):
+def run(body, out, args, specs, after=(), grid=(), out_specs=VMEM, name=None, limit=BIG):
     n, m = len(args), len(after)
 
     def kernel(*refs):
@@ -82,7 +82,7 @@
 
     w_out4 = run(
         split_w, [of((piece, width))] * NZ, (place, w_out), [SMEM, VMEM],
-        out_specs=[VMEM] * NZ, name="w_split",
+        out_specs=[VMEM] * NZ, name="w_split", limit=SMALL,
     )
     w_near = [w_out4[0]] + [shift(w_out4[k], k) for k in range(1, NZ)]
 
@@ -98,7 +98,7 @@
 
     g_out4 = run(
         split_g, [of((own_rows, 2 * feats))] * NZ, (place, grad_out[0]), [SMEM, VMEM],
-        after=(w_out4[0],), out_specs=[VMEM] * NZ, name="g_split",
+        after=(w_out4[0],), out_specs=[VMEM] * NZ, name="g_split", limit=SMALL,
     )
     g_near = [g_out4[0]] + [shift(g_out4[k], k) for k in range(1, NZ)]
 
@@ -114,7 +114,7 @@
 
     act = run(
         mask_body, [of((half, width))] * 2, (place, counts, attn[0]), [SMEM, SMEM, VMEM],
-        after=(g_out4[0],), out_specs=[VMEM] * 2, name="mask",
+        after=(g_out4[0],), out_specs=[VMEM] * 2, name="mask", limit=SMALL,
     )
     left = [shift(act[0], 1), None]
     right = [None, shift(act[1], -1)]
@@ -125,7 +125,7 @@
             out_ref[:, k * width : (k + 1) * width] = ref[...]
 
     w_own = run(
-        join_w, of((piece, lanes)), w_near, [VMEM] * NZ, after=(act[0],), name="w_join"
+        join_w, of((piece, lanes)), w_near, [VMEM] * NZ, after=(act[0],), name="w_join", limit=SMALL
     )
 
     def move(a_ref, out_ref):
@@ -258,17 +258,17 @@
     *sent0, kept0 = project(0, 1, (far[0],))
     got0 = [swap(x) for x in sent0]
     to_right = rows_term(3, (bf16,), (kept0,), (up,), 0)[0]
-    to_left = rows_term(1, (bf16,), (to_right,), (down,), 1)[0]
+    term_pair = run(
+        move, of((piece, lanes)), (scatter(term_pair),), [VMEM], after=(to_right,), name="move"
+    )
+    to_left = rows_term(1, (bf16,), (to_right, term_pair), (down,), 1)[0]
+    term_pair = lax.ppermute(term_pair, "dp", pair)
     from_left = shift(to_right, 1)
     from_right = shift(to_left, -1)
-    stay = rows_term(0, (f32,), (to_left,))[0]
-    term_pair = run(
-        move, of((piece, lanes)), (scatter(term_pair),), [VMEM], after=(stay,), name="move"
-    )
-    *sent1, kept1 = project(1, 1, (stay, term_pair, *got0))
+    *sent1, kept1 = project(1, 1, (to_left, *got0))
     got1 = [swap(x) for x in sent1]
-    quarters0, last = spread(kept0, got0, (kept1,))
-    term_pair = lax.ppermute(term_pair, "dp", pair)
+    stay = rows_term(0, (f32,), (kept1,))[0]
+    quarters0, last = spread(kept0, got0, (stay,))
     term_own = scatter(term_own)
 
     def add_rows(place_ref, counts_ref, stay_ref, *refs):
@@ -290,7 +290,7 @@
 
     grad_rows = run(
         add_rows, of((s, width)), (place, counts, stay, from_left, from_right), [SMEM] * 2 + [VMEM] * 3,
-        name="add_rows",
+        name="add_rows", limit=SMALL,
     )
     quarters1, last = spread(kept1, got1, (grad_rows,))
 
@@ -307,7 +307,7 @@
 
     projected = run(
         join_out, of((own_rows, d)), (place, *quarters0, *quarters1),
-        [SMEM] + [VMEM] * (2 * NZ), name="join_out",
+        [SMEM] + [VMEM] * (2 * NZ), name="join_out", limit=SMALL,
     )
 
     def add_terms(a_ref, b_ref, *outs):
@@ -319,7 +319,7 @@
 
     parts = run(
         add_terms, [of((piece, width))] * NZ, (term_own, term_pair), [VMEM] * 2,
-        after=(last, *quarters0[1:]), out_specs=[VMEM] * NZ, name="add_terms",
+        after=(last, *quarters0[1:]), out_specs=[VMEM] * NZ, name="add_terms", limit=SMALL,
     )
     parts = [parts[0]] + [shift(parts[k], -k) for k in range(1, NZ)]
 
@@ -331,7 +331,7 @@
 
     grad_w = run(
         join_term, of((NZ * piece, width), jnp.float32), (place, *parts),
-        [SMEM] + [VMEM] * NZ, after=(projected,), name="join_term",
+        [SMEM] + [VMEM] * NZ, after=(projected,), name="join_term", limit=SMALL,
     )
     return (projected[None], grad_rows[None], grad_w)
 

time: 282 us -> 274 us (0.972)
  Pallas kernels: 114 us -> 102 us
    pallas_call x21, Pallas kernels: 114 us -> 102 us  [run(): pl.pallas_call(kernel, out_shape=out, grid=grid, in_specs=list(specs) + [...]
    ppermute x25, waiting for transfers between devices: 47.8 us -> 58.8 us  [shift(): return lax.ppermute(value, 'tensor', ring(step))]
    ppermute x6, waiting for transfers between devices: 34.4 us -> 26.8 us  [swap(): return lax.ppermute(value, 'tensor', SWAP)]
    unnamed x70 -> x66, local copies, waits for them, and re-layouts: 11.3 us -> 13.9 us
  transfers between devices with their start and end apart: 37 -> 37, of which waited for: 15 -> 12; matrix products, arithmetic and copies ran while one was open for 0% -> 0% of each run, Pallas kernels for 38% -> 36%
where the time goes in v9:
time: 274 us; the launch traced here: 273 us
  Pallas kernels  102 us (37%)
  waiting for transfers between devices  88.4 us (32%)
  starting transfers between devices  54.8 us (20%)
  between operations  14.1 us (5%)
  local copies, waits for them, and re-layouts  13.9 us (5%)
    pallas_call x21, Pallas kernels, run(): pl.pallas_call(kernel, out_shape=out, grid=grid, in_specs=list(specs) + [...  102 us
    ppermute x25, waiting for transfers between devices, shift(): return lax.ppermute(value, 'tensor', ring(step))  58.8 us
    ppermute x25, starting transfers between devices, shift(): return lax.ppermute(value, 'tensor', ring(step))  36.1 us
    ppermute x6, waiting for transfers between devices, swap(): return lax.ppermute(value, 'tensor', SWAP)  26.8 us
    ppermute x6, starting transfers between devices, swap(): return lax.ppermute(value, 'tensor', SWAP)  16.7 us
    unnamed x66, local copies, waits for them, and re-layouts  13.9 us
  transfers between devices with their start and end apart: 37, of which 12 were waited for; matrix products, arithmetic and copies ran while one was open for 0% of the time, Pallas kernels for 36%

profile of v9, /device:TPU:0, one launch (start us, length us, event | category | flops | bytes accessed | tf_op | source)
XLA Modules:
  0.0 273.2 jit_solution(3728148659046400789)
XLA Ops:
  9.1 2.1 collective-permute-start
  11.1 3.6 %collective-permute-start.1 = (bf16[128,768]{1,0:T(8,128)(2,1)S(1)}, bf16[128,768]{1,0:T(8,128)(2,1)S(1)}, u32[]{:S(2)}, u32[]{:S(2)}) collective-permute-start(bf16[128,768]{1,0:T(8,128)(2,1)S(1)} %get-tuple-element.33), channel_id=1, source_target_pairs={{0,4},{1,5},{2,6},{3,7},{4,0},{5,1},{6,2},{7,3},{8,12},{9,13},{10,... | collective-permute-start | bytes 589832 | tf_op jit(solution)/shard_map/ppermute | solution.py:26
  15.7 1.6 copy-done.4
  19.4 4.1 %collective-permute-done.1.refs_2_ = bf16[128,768]{1,0:T(8,128)(2,1)S(1)} collective-permute-done((bf16[128,768]{1,0:T(8,128)(2,1)S(1)}, bf16[128,768]{1,0:T(8,128)(2,1)S(1)}, u32[]{:S(2)}, u32[]{:S(2)}) %collective-permute-start.1) | collective-permute-done | bytes 196640 | tf_op jit(solution)/shard_map/ppermute | solution.py:26
  24.6 1.3 collective-permute-start.10
  25.9 2.4 collective-permute-start.12
  30.3 1.6 collective-permute-start.16
  31.9 19.9 %collective-permute-done.10.refs_6_.refs_3_ = bf16[128,2048]{1,0:T(8,128)(2,1)S(1)} collective-permute-done((bf16[128,2048]{1,0:T(8,128)(2,1)}, bf16[128,2048]{1,0:T(8,128)(2,1)S(1)}, u32[]{:S(2)}, u32[]{:S(2)}) %collective-permute-start.10) | collective-permute-done | bytes 524320 | tf_op jit(solution)/shard_map/ppermute | solution.py:26
  52.5 3.2 %collective-permute-start.9 = (bf16[128,2048]{1,0:T(8,128)(2,1)S(1)}, bf16[128,2048]{1,0:T(8,128)(2,1)S(1)}, u32[]{:S(2)}, u32[]{:S(2)}) collective-permute-start(bf16[128,2048]{1,0:T(8,128)(2,1)S(1)} %get-tuple-element.35.refs_3_.refs_5_), channel_id=1, source_target_pairs={{0,1},{1,0},{2,3},{3,2},{4,5},{5,4},{6,7},{7,6},{8,9},{9,8},{10,11... | collective-permute-start | bytes 1572872 | tf_op jit(solution)/shard_map/ppermute | solution.py:30
  55.7 12.0 %collective-permute-done.14.refs_8_.refs_5_ = bf16[128,2048]{1,0:T(8,128)(2,1)S(1)} collective-permute-done((bf16[128,2048]{1,0:T(8,128)(2,1)S(1)}, bf16[128,2048]{1,0:T(8,128)(2,1)S(1)}, u32[]{:S(2)}, u32[]{:S(2)}) %collective-permute-start.14) | collective-permute-done | bytes 524320 | tf_op jit(solution)/shard_map/ppermute | solution.py:26
  70.0 2.1 w_move.1
  72.2 3.3 %collective-permute-start.11 = (bf16[128,2048]{1,0:T(8,128)(2,1)}, bf16[128,2048]{1,0:T(8,128)(2,1)S(1)}, u32[]{:S(2)}, u32[]{:S(2)}) collective-permute-start(bf16[128,2048]{1,0:T(8,128)(2,1)} %copy-done.24), channel_id=1, source_target_pairs={{0,1},{1,0},{2,3},{3,2},{4,5},{5,4},{6,7},{7,6},{8,9},{9,8},{10,11... | collective-permute-start | bytes 1572872 | tf_op jit(solution)/shard_map/ppermute | solution.py:30
  77.1 1.9 collective-permute-start.8
  79.0 1.4 collective-permute-start.7
  80.5 8.4 %collective-permute-done.11.refs_2_ = bf16[128,2048]{1,0:T(8,128)(2,1)S(1)} collective-permute-done((bf16[128,2048]{1,0:T(8,128)(2,1)}, bf16[128,2048]{1,0:T(8,128)(2,1)S(1)}, u32[]{:S(2)}, u32[]{:S(2)}) %collective-permute-start.11) | collective-permute-done | bytes 524320 | tf_op jit(solution)/shard_map/ppermute | solution.py:30
  90.1 7.9 %collective-permute-done.13.refs_3_ = bf16[128,2048]{1,0:T(8,128)(2,1)S(1)} collective-permute-done((bf16[128,2048]{1,0:T(8,128)(2,1)}, bf16[128,2048]{1,0:T(8,128)(2,1)S(1)}, u32[]{:S(2)}, u32[]{:S(2)}) %collective-permute-start.13) | collective-permute-done | bytes 524320 | tf_op jit(solution)/shard_map/ppermute | solution.py:30
  98.0 3.2 %collective-permute-start.15 = (bf16[128,2048]{1,0:T(8,128)(2,1)}, bf16[128,2048]{1,0:T(8,128)(2,1)S(1)}, u32[]{:S(2)}, u32[]{:S(2)}) collective-permute-start(bf16[128,2048]{1,0:T(8,128)(2,1)} %copy-done.26), channel_id=1, source_target_pairs={{0,1},{1,0},{2,3},{3,2},{4,5},{5,4},{6,7},{7,6},{8,9},{9,8},{10,11... | collective-permute-start | bytes 1572872 | tf_op jit(solution)/shard_map/ppermute | solution.py:30
  101.2 10.4 %collective-permute-done.15.refs_4_ = bf16[128,2048]{1,0:T(8,128)(2,1)S(1)} collective-permute-done((bf16[128,2048]{1,0:T(8,128)(2,1)}, bf16[128,2048]{1,0:T(8,128)(2,1)S(1)}, u32[]{:S(2)}, u32[]{:S(2)}) %collective-permute-start.15) | collective-permute-done | bytes 524320 | tf_op jit(solution)/shard_map/ppermute | solution.py:30
  112.4 4.5 %g_join.1.refs_0_ = bf16[1024,2048]{1,0:T(8,128)(2,1)} custom-call(s32[4]{0:T(128)} %copy-done.12, bf16[128,2048]{1,0:T(8,128)(2,1)} %copy-done.27, bf16[128,2048]{1,0:T(8,128)(2,1)} %copy-done.30, bf16[128,2048]{1,0:T(8,128)(2,1)} %copy-done.31, bf16[128,2048]{1,0:T(8,128)(2,1)} %copy-done.32, bf16[128,2048]{1,0:T(8,128)(2,1)} %copy-done.5, ...), custom_call_target="tpu_custom_call" | custom-call | flops 1000 | bytes 1000 | tf_op jit(solution)/shard_map/g_join/pallas_call | solution.py:47
  119.2 11.5 %term.2.refs_9_ = bf16[1024,3072]{1,0:T(8,128)(2,1)} custom-call(bf16[1024,2048]{1,0:T(8,128)(2,1)} %g_join.1.refs_0_, bf16[512,768]{1,0:T(8,128)(2,1)} %copy-done.1, bf16[512,768]{1,0:T(8,128)(2,1)} %copy-done.2, bf16[512,768]{1,0:T(8,128)(2,1)} %copy-done.18, bf16[512,768]{1,0:T(8,128)(2,1)} %copy-done.19, bf16[512,768]{1,0:T(8,128)(2,1)} %copy-done.22, ...), custom_call_target="tpu_custom_call" | custom-call | flops 1000 | bytes 1000 | tf_op jit(solution)/shard_map/term/pallas_call | solution.py:47
  130.9 11.5 %term.3.refs_3_ = bf16[1024,3072]{1,0:T(8,128)(2,1)} custom-call(bf16[1024,2048]{1,0:T(8,128)(2,1)} %g_join.1.refs_0_, bf16[512,768]{1,0:T(8,128)(2,1)} %copy-done.1, bf16[512,768]{1,0:T(8,128)(2,1)} %copy-done.2, bf16[512,768]{1,0:T(8,128)(2,1)} %copy-done.18, bf16[512,768]{1,0:T(8,128)(2,1)} %copy-done.19, bf16[512,768]{1,0:T(8,128)(2,1)} %copy-done.22, ...), custom_call_target="tpu_custom_call" | custom-call | flops 1000 | bytes 1000 | tf_op jit(solution)/shard_map/term/pallas_call | solution.py:47
  142.5 7.3 %rows_term.4 = (bf16[512,768]{1,0:T(8,128)(2,1)}, bf16[512,768]{1,0:T(8,128)(2,1)}) custom-call(bf16[1024,2048]{1,0:T(8,128)(2,1)} %g_join.1.refs_0_, bf16[1024,3072]{1,0:T(8,128)(2,1)} %all-gather.3.cloned.1.call-done.refs_1_.refs_0_, bf16[1024,3072]{1,0:T(8,128)(2,1)} %all-gather.5.cloned.1.call-done.refs_2_.refs_0_, bf16[1024,3072]{1,0:T(8,128)(2,1)} %term.3.refs_3_), custom_call_target="tpu_custom_call" | custom-call | flops 1000 | bytes 1000 | tf_op jit(solution)/shard_map/rows_term/pallas_call | solution.py:47
  149.8 3.3 %collective-permute-start.19 = (bf16[512,768]{1,0:T(8,128)(2,1)}, bf16[512,768]{1,0:T(8,128)(2,1)S(1)}, u32[]{:S(2)}, u32[]{:S(2)}) collective-permute-start(bf16[512,768]{1,0:T(8,128)(2,1)} %get-tuple-element.41.refs_9_), channel_id=1, source_target_pairs={{0,2},{1,3},{2,4},{3,5},{4,6},{5,7},{6,0},{7,1},{8,10},{9,11},{10,... | collective-permute-start | bytes 2359304 | tf_op jit(solution)/shard_map/ppermute | solution.py:26
  153.0 1.5 collective-permute-start.18
  154.6 11.7 %project.2 = (bf16[512,1024]{1,0:T(8,128)(2,1)}, f32[512,1024]{1,0:T(8,128)}) custom-call(bf16[1024,3072]{1,0:T(8,128)(2,1)} %all-gather.3.cloned.1.call-done.refs_1_.refs_0_, bf16[512,768]{1,0:T(8,128)(2,1)} %copy-done.1, bf16[512,768]{1,0:T(8,128)(2,1)} %copy-done.2, bf16[512,768]{1,0:T(8,128)(2,1)} %copy-done.18, bf16[512,768]{1,0:T(8,128)(2,1)} %copy-done.19, ...), custom_call_target="tpu_custom_call" | custom-call | flops 1000 | bytes 1000 | tf_op jit(solution)/shard_map/project/pallas_call | solution.py:47
  166.3 3.3 %collective-permute-start.17 = (bf16[512,1024]{1,0:T(8,128)(2,1)}, bf16[512,1024]{1,0:T(8,128)(2,1)S(1)}, u32[]{:S(2)}, u32[]{:S(2)}) collective-permute-start(bf16[512,1024]{1,0:T(8,128)(2,1)} %get-tuple-element.43), channel_id=1, source_target_pairs={{0,1},{1,0},{2,3},{3,2},{4,5},{5,4},{6,7},{7,6},{8,9},{9,8},{10,11... | collective-permute-start | bytes 3145736 | tf_op jit(solution)/shard_map/ppermute | solution.py:30
  169.5 1.3 collective-permute-done.19.refs_3_
  171.7 7.7 %rows_term.5.refs_1_.refs_4_ = bf16[1024,768]{1,0:T(8,128)(2,1)} custom-call(bf16[1024,2048]{1,0:T(8,128)(2,1)} %g_join.1.refs_0_, bf16[1024,3072]{1,0:T(8,128)(2,1)} %all-gather.3.cloned.1.call-done.refs_1_.refs_0_, bf16[1024,3072]{1,0:T(8,128)(2,1)} %all-gather.5.cloned.1.call-done.refs_2_.refs_0_, bf16[512,768]{1,0:T(8,128)(2,1)} %copy-done.29, ...), custom_call_target="tpu_custom_call" | custom-call | flops 1000 | bytes 1000 | tf_op jit(solution)/shard_map/rows_term/pallas_call | solution.py:47
  179.8 2.1 move.1.refs_5_
  181.9 7.8 %rows_term.6.refs_9_ = bf16[1024,768]{1,0:T(8,128)(2,1)} custom-call(bf16[1024,2048]{1,0:T(8,128)(2,1)} %g_join.1.refs_0_, bf16[1024,3072]{1,0:T(8,128)(2,1)} %all-gather.3.cloned.1.call-done.refs_1_.refs_0_, bf16[1024,3072]{1,0:T(8,128)(2,1)} %all-gather.5.cloned.1.call-done.refs_2_.refs_0_, bf16[512,768]{1,0:T(8,128)(2,1)} %collective-permute-done.18.refs_3_, ...), custom_call_target="tpu_custom_call" | custom-call | flops 1000 | bytes 1000 | tf_op jit(solution)/shard_map/rows_term/pallas_call | solution.py:47
  189.6 2.7 collective-permute-start.25
  193.3 11.8 %project.3 = (bf16[512,1024]{1,0:T(8,128)(2,1)}, f32[512,1024]{1,0:T(8,128)}) custom-call(bf16[1024,3072]{1,0:T(8,128)(2,1)} %all-gather.5.cloned.1.call-done.refs_2_.refs_0_, bf16[512,768]{1,0:T(8,128)(2,1)} %copy-done.1, bf16[512,768]{1,0:T(8,128)(2,1)} %copy-done.2, bf16[512,768]{1,0:T(8,128)(2,1)} %copy-done.18, bf16[512,768]{1,0:T(8,128)(2,1)} %copy-done.19, ...), custom_call_target="tpu_custom_call" | custom-call | flops 1000 | bytes 1000 | tf_op jit(solution)/shard_map/project/pallas_call | solution.py:47
  205.1 3.4 %collective-permute-start.23 = (bf16[512,1024]{1,0:T(8,128)(2,1)}, bf16[512,1024]{1,0:T(8,128)(2,1)}, u32[]{:S(2)}, u32[]{:S(2)}) collective-permute-start(bf16[512,1024]{1,0:T(8,128)(2,1)} %get-tuple-element.50), channel_id=1, source_target_pairs={{0,1},{1,0},{2,3},{3,2},{4,5},{5,4},{6,7},{7,6},{8,9},{9,8},{10,11... | collective-permute-start | bytes 3145736 | tf_op jit(solution)/shard_map/ppermute | solution.py:30
  208.8 7.8 %rows_term.7.refs_3_.refs_2_ = f32[1024,768]{1,0:T(8,128)} custom-call(bf16[1024,2048]{1,0:T(8,128)(2,1)} %g_join.1.refs_0_, bf16[1024,3072]{1,0:T(8,128)(2,1)} %all-gather.3.cloned.1.call-done.refs_1_.refs_0_, bf16[1024,3072]{1,0:T(8,128)(2,1)} %all-gather.5.cloned.1.call-done.refs_2_.refs_0_, f32[512,1024]{1,0:T(8,128)} %get-tuple-element.45.refs_3_.refs_1_), custom_call_target="tpu_custom_call" | custom-call | flops 1000 | bytes 1000 | tf_op jit(solution)/shard_map/rows_term/pallas_call | solution.py:47
  216.6 3.2 %settle.2 = (bf16[128,1024]{1,0:T(8,128)(2,1)}, bf16[128,1024]{1,0:T(8,128)(2,1)}, bf16[128,1024]{1,0:T(8,128)(2,1)}, bf16[128,1024]{1,0:T(8,128)(2,1)}) custom-call(s32[4]{0:T(128)} %copy-done.12, f32[512,1024]{1,0:T(8,128)} %get-tuple-element.42.refs_4_.refs_1_, bf16[512,1024]{1,0:T(8,128)(2,1)} %copy-done.23, f32[1024,768]{1,0:T(8,128)} %rows_term.7.refs_3_.refs_2_), custom_call_target="tpu_custom_call" | custom-call | flops 1000 | bytes 1000 | tf_op jit(solution)/shard_map/settle/pallas_call | solution.py:47
  219.9 1.9 collective-permute-start.21
  221.8 9.3 %collective-permute-done.25.refs_4_ = bf16[1024,768]{1,0:T(8,128)(2,1)S(1)} collective-permute-done((bf16[1024,768]{1,0:T(8,128)(2,1)}, bf16[1024,768]{1,0:T(8,128)(2,1)S(1)}, u32[]{:S(2)}, u32[]{:S(2)}) %collective-permute-start.25) | collective-permute-done | bytes 1572896 | tf_op jit(solution)/shard_map/ppermute | solution.py:26
  231.0 3.7 %collective-permute-start.22 = (bf16[128,1024]{1,0:T(8,128)(2,1)}, bf16[128,1024]{1,0:T(8,128)(2,1)S(1)}, u32[]{:S(2)}, u32[]{:S(2)}) collective-permute-start(bf16[128,1024]{1,0:T(8,128)(2,1)} %get-tuple-element.49), channel_id=1, source_target_pairs={{0,6},{1,7},{2,0},{3,1},{4,2},{5,3},{6,4},{7,5},{8,14},{9,15},{10,... | collective-permute-start | bytes 786440 | tf_op jit(solution)/shard_map/ppermute | solution.py:26
  234.8 2.2 add_rows.1.refs_3_
  237.0 3.0 %settle.3 = (bf16[128,1024]{1,0:T(8,128)(2,1)}, bf16[128,1024]{1,0:T(8,128)(2,1)}, bf16[128,1024]{1,0:T(8,128)(2,1)}, bf16[128,1024]{1,0:T(8,128)(2,1)}) custom-call(s32[4]{0:T(128)} %copy-done.12, f32[512,1024]{1,0:T(8,128)} %get-tuple-element.45.refs_3_.refs_1_, bf16[512,1024]{1,0:T(8,128)(2,1)} %collective-permute-done.23.refs_2_, ...), custom_call_target="tpu_custom_call" | custom-call | flops 1000 | bytes 1000 | tf_op jit(solution)/shard_map/settle/pallas_call | solution.py:47
  240.0 1.5 collective-permute-start.27
  241.5 1.8 collective-permute-start.28
  243.4 2.8 %collective-permute-done.29.refs_1_ = bf16[128,3072]{1,0:T(8,128)(2,1)S(1)} collective-permute-done((bf16[128,3072]{1,0:T(8,128)(2,1)}, bf16[128,3072]{1,0:T(8,128)(2,1)S(1)}, u32[]{:S(2)}, u32[]{:S(2)}) %collective-permute-start.29) | collective-permute-done | bytes 786464 | tf_op jit(solution)/shard_map/ppermute | solution.py:265
  249.5 6.9 %collective-permute-done.26.refs_6_ = bf16[128,1024]{1,0:T(8,128)(2,1)S(1)} collective-permute-done((bf16[128,1024]{1,0:T(8,128)(2,1)}, bf16[128,1024]{1,0:T(8,128)(2,1)S(1)}, u32[]{:S(2)}, u32[]{:S(2)}) %collective-permute-start.26) | collective-permute-done | bytes 262176 | tf_op jit(solution)/shard_map/ppermute | solution.py:26
  256.4 2.4 join_out.1.refs_5_
  258.8 4.5 %collective-permute-done.32.refs_4_ = bf16[128,768]{1,0:T(8,128)(2,1)S(1)} collective-permute-done((bf16[128,768]{1,0:T(8,128)(2,1)S(1)}, bf16[128,768]{1,0:T(8,128)(2,1)S(1)}, u32[]{:S(2)}, u32[]{:S(2)}) %collective-permute-start.32) | collective-permute-done | bytes 196640 | tf_op jit(solution)/shard_map/ppermute | solution.py:26
  263.3 1.6 copy-done.3
  264.9 1.8 join_term.1
  (118 shorter events, 23.0 us)
Async XLA Ops:
  7.2 135.3 %all-gather.3.cloned.1.call-start = ((), (), s32[]{:S(2)}) async-start(), calls=%async_computation.2 | async-start | bytes 7077888 | tf_op jit(solution)/shard_map/all_gather | solution.py:140
  9.1 10.4 %collective-permute-start = (bf16[128,768]{1,0:T(8,128)(2,1)S(1)}, bf16[128,768]{1,0:T(8,128)(2,1)S(1)}, u32[]{:S(2)}, u32[]{:S(2)}) collective-permute-start(bf16[128,768]{1,0:T(8,128)(2,1)S(1)} %get-tuple-element.32), channel_id=1, source_target_pairs={{0,2},{1,3},{2,4},{3,5},{4,6},{5,7},{6,0},{7,1},{8,10},{9,11},{10,... | collective-permute-start | bytes 589832 | tf_op jit(solution)/shard_map/ppermute | solution.py:26
  11.1 12.4 %collective-permute-start.1 = (bf16[128,768]{1,0:T(8,128)(2,1)S(1)}, bf16[128,768]{1,0:T(8,128)(2,1)S(1)}, u32[]{:S(2)}, u32[]{:S(2)}) collective-permute-start(bf16[128,768]{1,0:T(8,128)(2,1)S(1)} %get-tuple-element.33), channel_id=1, source_target_pairs={{0,4},{1,5},{2,6},{3,7},{4,0},{5,1},{6,2},{7,3},{8,12},{9,13},{10,... | collective-permute-start | bytes 589832 | tf_op jit(solution)/shard_map/ppermute | solution.py:26
  14.7 8.8 %collective-permute-start.2 = (bf16[128,768]{1,0:T(8,128)(2,1)S(1)}, bf16[128,768]{1,0:T(8,128)(2,1)S(1)}, u32[]{:S(2)}, u32[]{:S(2)}) collective-permute-start(bf16[128,768]{1,0:T(8,128)(2,1)S(1)} %get-tuple-element.34), channel_id=1, source_target_pairs={{0,6},{1,7},{2,0},{3,1},{4,2},{5,3},{6,4},{7,5},{8,14},{9,15},{10,... | collective-permute-start | bytes 589832 | tf_op jit(solution)/shard_map/ppermute | solution.py:26
  18.4 34.1 %copy-start.5 = (bf16[128,2048]{1,0:T(8,128)(2,1)}, bf16[128,2048]{1,0:T(8,128)(2,1)S(1)}, u32[]{:S(2)}) copy-start(bf16[128,2048]{1,0:T(8,128)(2,1)S(1)} %get-tuple-element.35.refs_3_.refs_5_) | copy-start | bytes 1572868
  19.4 56.4 %copy-start.2 = (bf16[512,768]{1,0:T(8,128)(2,1)}, bf16[512,768]{1,0:T(8,128)(2,1)S(1)}, u32[]{:S(2)}) copy-start(bf16[512,768]{1,0:T(8,128)(2,1)S(1)} %get-tuple-element.37.refs_2_) | copy-start | bytes 2359300
  19.4 57.7 %copy-start.1 = (bf16[512,768]{1,0:T(8,128)(2,1)}, bf16[512,768]{1,0:T(8,128)(2,1)S(1)}, u32[]{:S(2)}) copy-start(bf16[512,768]{1,0:T(8,128)(2,1)S(1)} %get-tuple-element.36.refs_4_.refs_1_) | copy-start | bytes 2359300
  24.5 118.0 %all-gather.5.cloned.1.call-start = ((), (), s32[]{:S(2)}) async-start(), calls=%async_computation.3 | async-start | bytes 7077888 | tf_op jit(solution)/shard_map/all_gather | solution.py:140
  24.6 27.2 %collective-permute-start.10 = (bf16[128,2048]{1,0:T(8,128)(2,1)}, bf16[128,2048]{1,0:T(8,128)(2,1)S(1)}, u32[]{:S(2)}, u32[]{:S(2)}) collective-permute-start(bf16[128,2048]{1,0:T(8,128)(2,1)} %copy-done.16), channel_id=1, source_target_pairs={{0,2},{1,3},{2,4},{3,5},{4,6},{5,7},{6,0},{7,1},{8,10},{9,11},{10,... | collective-permute-start | bytes 1572872 | tf_op jit(solution)/shard_map/ppermute | solution.py:26
  25.9 26.6 %collective-permute-start.12 = (bf16[128,2048]{1,0:T(8,128)(2,1)S(1)}, bf16[128,2048]{1,0:T(8,128)(2,1)S(1)}, u32[]{:S(2)}, u32[]{:S(2)}) collective-permute-start(bf16[128,2048]{1,0:T(8,128)(2,1)S(1)} %get-tuple-element.39), channel_id=1, source_target_pairs={{0,4},{1,5},{2,6},{3,7},{4,0},{5,1},{6,2},{7,3},{8,12},{9,13},{10,... | collective-permute-start | bytes 1572872 | tf_op jit(solution)/shard_map/ppermute | solution.py:26
  28.3 39.4 %collective-permute-start.6 = (bf16[512,768]{1,0:T(8,128)(2,1)S(1)}, bf16[512,768]{1,0:T(8,128)(2,1)S(1)}, u32[]{:S(2)}, u32[]{:S(2)}) collective-permute-start(bf16[512,768]{1,0:T(8,128)(2,1)S(1)} %get-tuple-element.37.refs_2_), channel_id=1, source_target_pairs={{0,6},{1,7},{2,0},{3,1},{4,2},{5,3},{6,4},{7,5},{8,14},{9,15},{10,... | collective-permute-start | bytes 2359304 | tf_op jit(solution)/shard_map/ppermute | solution.py:26
  29.5 38.2 %collective-permute-start.3 = (bf16[512,768]{1,0:T(8,128)(2,1)S(1)}, bf16[512,768]{1,0:T(8,128)(2,1)S(1)}, u32[]{:S(2)}, u32[]{:S(2)}) collective-permute-start(bf16[512,768]{1,0:T(8,128)(2,1)S(1)} %get-tuple-element.36.refs_4_.refs_1_), channel_id=1, source_target_pairs={{0,2},{1,3},{2,4},{3,5},{4,6},{5,7},{6,0},{7,1},{8,10},{9,11},{10,... | collective-permute-start | bytes 2359304 | tf_op jit(solution)/shard_map/ppermute | solution.py:26
  30.3 37.5 %collective-permute-start.16 = (bf16[128,3072]{1,0:T(8,128)(2,1)}, bf16[128,3072]{1,0:T(8,128)(2,1)S(1)}, u32[]{:S(2)}, u32[]{:S(2)}) collective-permute-start(bf16[128,3072]{1,0:T(8,128)(2,1)} %w_join.1), channel_id=1, source_target_pairs={{0,64},{8,72},{16,80},{24,88},{32,96},{40,104},{48,112},{56,120},{... | collective-permute-start | bytes 2359304 | tf_op jit(solution)/shard_map/ppermute | solution.py:135
  51.8 16.0 %copy-start.24 = (bf16[128,2048]{1,0:T(8,128)(2,1)}, bf16[128,2048]{1,0:T(8,128)(2,1)S(1)}, u32[]{:S(2)}) copy-start(bf16[128,2048]{1,0:T(8,128)(2,1)S(1)} %collective-permute-done.10.refs_6_.refs_3_) | copy-start | bytes 1572868
  51.8 15.9 %collective-permute-start.14 = (bf16[128,2048]{1,0:T(8,128)(2,1)S(1)}, bf16[128,2048]{1,0:T(8,128)(2,1)S(1)}, u32[]{:S(2)}, u32[]{:S(2)}) collective-permute-start(bf16[128,2048]{1,0:T(8,128)(2,1)S(1)} %get-tuple-element.40), channel_id=1, source_target_pairs={{0,6},{1,7},{2,0},{3,1},{4,2},{5,3},{6,4},{7,5},{8,14},{9,15},{10,... | collective-permute-start | bytes 1572872 | tf_op jit(solution)/shard_map/ppermute | solution.py:26
  52.5 15.2 %copy-start.25 = (bf16[128,2048]{1,0:T(8,128)(2,1)}, bf16[128,2048]{1,0:T(8,128)(2,1)S(1)}, u32[]{:S(2)}) copy-start(bf16[128,2048]{1,0:T(8,128)(2,1)S(1)} %collective-permute-done.12.refs_7_.refs_4_) | copy-start | bytes 1572868
  52.5 15.2 %collective-permute-start.9 = (bf16[128,2048]{1,0:T(8,128)(2,1)S(1)}, bf16[128,2048]{1,0:T(8,128)(2,1)S(1)}, u32[]{:S(2)}, u32[]{:S(2)}) collective-permute-start(bf16[128,2048]{1,0:T(8,128)(2,1)S(1)} %get-tuple-element.35.refs_3_.refs_5_), channel_id=1, source_target_pairs={{0,1},{1,0},{2,3},{3,2},{4,5},{5,4},{6,7},{7,6},{8,9},{9,8},{10,11... | collective-permute-start | bytes 1572872 | tf_op jit(solution)/shard_map/ppermute | solution.py:30
  72.1 107.7 %reduce-scatter.3.cloned.1.call-start = ((), (), s32[]{:S(2)}) async-start(), calls=%async_computation.4 | async-start | bytes 7077888 | tf_op jit(solution)/shard_map/reduce_scatter | solution.py:230
  72.2 16.7 %collective-permute-start.11 = (bf16[128,2048]{1,0:T(8,128)(2,1)}, bf16[128,2048]{1,0:T(8,128)(2,1)S(1)}, u32[]{:S(2)}, u32[]{:S(2)}) collective-permute-start(bf16[128,2048]{1,0:T(8,128)(2,1)} %copy-done.24), channel_id=1, source_target_pairs={{0,1},{1,0},{2,3},{3,2},{4,5},{5,4},{6,7},{7,6},{8,9},{9,8},{10,11... | collective-permute-start | bytes 1572872 | tf_op jit(solution)/shard_map/ppermute | solution.py:30
  75.5 22.5 %collective-permute-start.13 = (bf16[128,2048]{1,0:T(8,128)(2,1)}, bf16[128,2048]{1,0:T(8,128)(2,1)S(1)}, u32[]{:S(2)}, u32[]{:S(2)}) collective-permute-start(bf16[128,2048]{1,0:T(8,128)(2,1)} %copy-done.25), channel_id=1, source_target_pairs={{0,1},{1,0},{2,3},{3,2},{4,5},{5,4},{6,7},{7,6},{8,9},{9,8},{10,11... | collective-permute-start | bytes 1572872 | tf_op jit(solution)/shard_map/ppermute | solution.py:30
  75.8 41.1 %collective-permute-start.4 = (bf16[512,768]{1,0:T(8,128)(2,1)S(1)}, bf16[512,768]{1,0:T(8,128)(2,1)S(1)}, u32[]{:S(2)}, u32[]{:S(2)}) collective-permute-start(bf16[512,768]{1,0:T(8,128)(2,1)S(1)} %get-tuple-element.37.refs_2_), channel_id=1, source_target_pairs={{0,2},{1,3},{2,4},{3,5},{4,6},{5,7},{6,0},{7,1},{8,10},{9,11},{10,... | collective-permute-start | bytes 2359304 | tf_op jit(solution)/shard_map/ppermute | solution.py:26
  77.1 39.8 %collective-permute-start.8 = (bf16[512,768]{1,0:T(8,128)(2,1)S(1)}, bf16[512,768]{1,0:T(8,128)(2,1)S(1)}, u32[]{:S(2)}, u32[]{:S(2)}) collective-permute-start(bf16[512,768]{1,0:T(8,128)(2,1)S(1)} %get-tuple-element.36.refs_4_.refs_1_), channel_id=1, source_target_pairs={{0,6},{1,7},{2,0},{3,1},{4,2},{5,3},{6,4},{7,5},{8,14},{9,15},{10,... | collective-permute-start | bytes 2359304 | tf_op jit(solution)/shard_map/ppermute | solution.py:26
  79.0 37.9 %collective-permute-start.7 = (bf16[512,768]{1,0:T(8,128)(2,1)}, bf16[512,768]{1,0:T(8,128)(2,1)S(1)}, u32[]{:S(2)}, u32[]{:S(2)}) collective-permute-start(bf16[512,768]{1,0:T(8,128)(2,1)} %copy-done.17), channel_id=1, source_target_pairs={{0,6},{1,7},{2,0},{3,1},{4,2},{5,3},{6,4},{7,5},{8,14},{9,15},{10,... | collective-permute-start | bytes 2359304 | tf_op jit(solution)/shard_map/ppermute | solution.py:26
  88.8 22.8 %copy-start.30 = (bf16[128,2048]{1,0:T(8,128)(2,1)}, bf16[128,2048]{1,0:T(8,128)(2,1)S(1)}, u32[]{:S(2)}) copy-start(bf16[128,2048]{1,0:T(8,128)(2,1)S(1)} %collective-permute-done.11.refs_2_) | copy-start | bytes 1572868
  88.8 28.1 %collective-permute-start.5 = (bf16[512,768]{1,0:T(8,128)(2,1)}, bf16[512,768]{1,0:T(8,128)(2,1)S(1)}, u32[]{:S(2)}, u32[]{:S(2)}) collective-permute-start(bf16[512,768]{1,0:T(8,128)(2,1)} %copy-done.18), channel_id=1, source_target_pairs={{0,2},{1,3},{2,4},{3,5},{4,6},{5,7},{6,0},{7,1},{8,10},{9,11},{10,... | collective-permute-start | bytes 2359304 | tf_op jit(solution)/shard_map/ppermute | solution.py:26
  98.0 13.6 %copy-start.31 = (bf16[128,2048]{1,0:T(8,128)(2,1)}, bf16[128,2048]{1,0:T(8,128)(2,1)S(1)}, u32[]{:S(2)}) copy-start(bf16[128,2048]{1,0:T(8,128)(2,1)S(1)} %collective-permute-done.13.refs_3_) | copy-start | bytes 1572868
  98.0 13.6 %collective-permute-start.15 = (bf16[128,2048]{1,0:T(8,128)(2,1)}, bf16[128,2048]{1,0:T(8,128)(2,1)S(1)}, u32[]{:S(2)}, u32[]{:S(2)}) collective-permute-start(bf16[128,2048]{1,0:T(8,128)(2,1)} %copy-done.26), channel_id=1, source_target_pairs={{0,1},{1,0},{2,3},{3,2},{4,5},{5,4},{6,7},{7,6},{8,9},{9,8},{10,11... | collective-permute-start | bytes 1572872 | tf_op jit(solution)/shard_map/ppermute | solution.py:30
  130.8 112.5 %reduce-scatter.5.cloned.1.call-start = ((), (), s32[]{:S(2)}) async-start(), calls=%async_computation.5 | async-start | bytes 7077888 | tf_op jit(solution)/shard_map/reduce_scatter | solution.py:230
  149.8 21.1 %collective-permute-start.19 = (bf16[512,768]{1,0:T(8,128)(2,1)}, bf16[512,768]{1,0:T(8,128)(2,1)S(1)}, u32[]{:S(2)}, u32[]{:S(2)}) collective-permute-start(bf16[512,768]{1,0:T(8,128)(2,1)} %get-tuple-element.41.refs_9_), channel_id=1, source_target_pairs={{0,2},{1,3},{2,4},{3,5},{4,6},{5,7},{6,0},{7,1},{8,10},{9,11},{10,... | collective-permute-start | bytes 2359304 | tf_op jit(solution)/shard_map/ppermute | solution.py:26
  153.0 28.8 %collective-permute-start.18 = (bf16[512,768]{1,0:T(8,128)(2,1)}, bf16[512,768]{1,0:T(8,128)(2,1)}, u32[]{:S(2)}, u32[]{:S(2)}) collective-permute-start(bf16[512,768]{1,0:T(8,128)(2,1)} %get-tuple-element.44), channel_id=1, source_target_pairs={{0,6},{1,7},{2,0},{3,1},{4,2},{5,3},{6,4},{7,5},{8,14},{9,15},{10,... | collective-permute-start | bytes 2359304 | tf_op jit(solution)/shard_map/ppermute | solution.py:26
  166.3 26.1 %collective-permute-start.17 = (bf16[512,1024]{1,0:T(8,128)(2,1)}, bf16[512,1024]{1,0:T(8,128)(2,1)S(1)}, u32[]{:S(2)}, u32[]{:S(2)}) collective-permute-start(bf16[512,1024]{1,0:T(8,128)(2,1)} %get-tuple-element.43), channel_id=1, source_target_pairs={{0,1},{1,0},{2,3},{3,2},{4,5},{5,4},{6,7},{7,6},{8,9},{9,8},{10,11... | collective-permute-start | bytes 3145736 | tf_op jit(solution)/shard_map/ppermute | solution.py:30
  179.4 40.4 %collective-permute-start.24 = (bf16[1024,768]{1,0:T(8,128)(2,1)}, bf16[1024,768]{1,0:T(8,128)(2,1)S(1)}, u32[]{:S(2)}, u32[]{:S(2)}) collective-permute-start(bf16[1024,768]{1,0:T(8,128)(2,1)} %rows_term.5.refs_1_.refs_4_), channel_id=1, source_target_pairs={{0,2},{1,3},{2,4},{3,5},{4,6},{5,7},{6,0},{7,1},{8,10},{9,11},{10,... | collective-permute-start | bytes 4718600 | tf_op jit(solution)/shard_map/ppermute | solution.py:26
  189.6 41.4 %collective-permute-start.25 = (bf16[1024,768]{1,0:T(8,128)(2,1)}, bf16[1024,768]{1,0:T(8,128)(2,1)S(1)}, u32[]{:S(2)}, u32[]{:S(2)}) collective-permute-start(bf16[1024,768]{1,0:T(8,128)(2,1)} %rows_term.6.refs_9_), channel_id=1, source_target_pairs={{0,6},{1,7},{2,0},{3,1},{4,2},{5,3},{6,4},{7,5},{8,14},{9,15},{10,... | collective-permute-start | bytes 4718600 | tf_op jit(solution)/shard_map/ppermute | solution.py:26
  205.1 31.9 %collective-permute-start.23 = (bf16[512,1024]{1,0:T(8,128)(2,1)}, bf16[512,1024]{1,0:T(8,128)(2,1)}, u32[]{:S(2)}, u32[]{:S(2)}) collective-permute-start(bf16[512,1024]{1,0:T(8,128)(2,1)} %get-tuple-element.50), channel_id=1, source_target_pairs={{0,1},{1,0},{2,3},{3,2},{4,5},{5,4},{6,7},{7,6},{8,9},{9,8},{10,11... | collective-permute-start | bytes 3145736 | tf_op jit(solution)/shard_map/ppermute | solution.py:30
  208.5 37.6 %collective-permute-start.29 = (bf16[128,3072]{1,0:T(8,128)(2,1)}, bf16[128,3072]{1,0:T(8,128)(2,1)S(1)}, u32[]{:S(2)}, u32[]{:S(2)}) collective-permute-start(bf16[128,3072]{1,0:T(8,128)(2,1)} %move.1.refs_5_), channel_id=1, source_target_pairs={{0,64},{8,72},{16,80},{24,88},{32,96},{40,104},{48,112},{56,120},{... | collective-permute-start | bytes 2359304 | tf_op jit(solution)/shard_map/ppermute | solution.py:265
  216.6 18.1 %copy-start = (f32[1024,768]{1,0:T(8,128)S(1)}, f32[1024,768]{1,0:T(8,128)}, u32[]{:S(2)}) copy-start(f32[1024,768]{1,0:T(8,128)} %rows_term.7.refs_3_.refs_2_) | copy-start | bytes 9437188
  216.6 18.1 %copy-start.13 = (s32[4]{0:T(128)S(1)}, s32[4]{0:T(128)}, u32[]{:S(2)}) copy-start(s32[4]{0:T(128)} %copy-done.12) | copy-start | bytes 52
  219.9 20.2 %collective-permute-start.20 = (bf16[128,1024]{1,0:T(8,128)(2,1)}, bf16[128,1024]{1,0:T(8,128)(2,1)S(1)}, u32[]{:S(2)}, u32[]{:S(2)}) collective-permute-start(bf16[128,1024]{1,0:T(8,128)(2,1)} %get-tuple-element.47), channel_id=1, source_target_pairs={{0,2},{1,3},{2,4},{3,5},{4,6},{5,7},{6,0},{7,1},{8,10},{9,11},{10,... | collective-permute-start | bytes 786440 | tf_op jit(solution)/shard_map/ppermute | solution.py:26
  219.9 21.6 %collective-permute-start.21 = (bf16[128,1024]{1,0:T(8,128)(2,1)}, bf16[128,1024]{1,0:T(8,128)(2,1)S(1)}, u32[]{:S(2)}, u32[]{:S(2)}) collective-permute-start(bf16[128,1024]{1,0:T(8,128)(2,1)} %get-tuple-element.48), channel_id=1, source_target_pairs={{0,4},{1,5},{2,6},{3,7},{4,0},{5,1},{6,2},{7,3},{8,12},{9,13},{10,... | collective-permute-start | bytes 786440 | tf_op jit(solution)/shard_map/ppermute | solution.py:26
  231.0 12.3 %collective-permute-start.22 = (bf16[128,1024]{1,0:T(8,128)(2,1)}, bf16[128,1024]{1,0:T(8,128)(2,1)S(1)}, u32[]{:S(2)}, u32[]{:S(2)}) collective-permute-start(bf16[128,1024]{1,0:T(8,128)(2,1)} %get-tuple-element.49), channel_id=1, source_target_pairs={{0,6},{1,7},{2,0},{3,1},{4,2},{5,3},{6,4},{7,5},{8,14},{9,15},{10,... | collective-permute-start | bytes 786440 | tf_op jit(solution)/shard_map/ppermute | solution.py:26
  237.0 19.4 %copy-start.11 = (bf16[128,1024]{1,0:T(8,128)(2,1)S(1)}, bf16[128,1024]{1,0:T(8,128)(2,1)}, u32[]{:S(2)}) copy-start(bf16[128,1024]{1,0:T(8,128)(2,1)} %get-tuple-element.46.refs_1_) | copy-start | bytes 786436
  240.0 16.4 %copy-start.14 = (s32[4]{0:T(128)S(1)}, s32[4]{0:T(128)}, u32[]{:S(2)}) copy-start(s32[4]{0:T(128)} %copy-done.12) | copy-start | bytes 52
  240.0 16.4 %collective-permute-start.26 = (bf16[128,1024]{1,0:T(8,128)(2,1)}, bf16[128,1024]{1,0:T(8,128)(2,1)S(1)}, u32[]{:S(2)}, u32[]{:S(2)}) collective-permute-start(bf16[128,1024]{1,0:T(8,128)(2,1)} %get-tuple-element.52), channel_id=1, source_target_pairs={{0,2},{1,3},{2,4},{3,5},{4,6},{5,7},{6,0},{7,1},{8,10},{9,11},{10,... | collective-permute-start | bytes 786440 | tf_op jit(solution)/shard_map/ppermute | solution.py:26
  240.0 16.4 %collective-permute-start.27 = (bf16[128,1024]{1,0:T(8,128)(2,1)}, bf16[128,1024]{1,0:T(8,128)(2,1)S(1)}, u32[]{:S(2)}, u32[]{:S(2)}) collective-permute-start(bf16[128,1024]{1,0:T(8,128)(2,1)} %get-tuple-element.53), channel_id=1, source_target_pairs={{0,4},{1,5},{2,6},{3,7},{4,0},{5,1},{6,2},{7,3},{8,12},{9,13},{10,... | collective-permute-start | bytes 786440 | tf_op jit(solution)/shard_map/ppermute | solution.py:26
  241.5 14.9 %collective-permute-start.28 = (bf16[128,1024]{1,0:T(8,128)(2,1)}, bf16[128,1024]{1,0:T(8,128)(2,1)S(1)}, u32[]{:S(2)}, u32[]{:S(2)}) collective-permute-start(bf16[128,1024]{1,0:T(8,128)(2,1)} %get-tuple-element.54), channel_id=1, source_target_pairs={{0,6},{1,7},{2,0},{3,1},{4,2},{5,3},{6,4},{7,5},{8,14},{9,15},{10,... | collective-permute-start | bytes 786440 | tf_op jit(solution)/shard_map/ppermute | solution.py:26
  248.4 10.4 %collective-permute-start.30 = (bf16[128,768]{1,0:T(8,128)(2,1)S(1)}, bf16[128,768]{1,0:T(8,128)(2,1)S(1)}, u32[]{:S(2)}, u32[]{:S(2)}) collective-permute-start(bf16[128,768]{1,0:T(8,128)(2,1)S(1)} %get-tuple-element.56), channel_id=1, source_target_pairs={{0,6},{1,7},{2,0},{3,1},{4,2},{5,3},{6,4},{7,5},{8,14},{9,15},{10,... | collective-permute-start | bytes 589832 | tf_op jit(solution)/shard_map/ppermute | solution.py:26
  248.7 10.1 %collective-permute-start.31 = (bf16[128,768]{1,0:T(8,128)(2,1)S(1)}, bf16[128,768]{1,0:T(8,128)(2,1)S(1)}, u32[]{:S(2)}, u32[]{:S(2)}) collective-permute-start(bf16[128,768]{1,0:T(8,128)(2,1)S(1)} %get-tuple-element.57), channel_id=1, source_target_pairs={{0,4},{1,5},{2,6},{3,7},{4,0},{5,1},{6,2},{7,3},{8,12},{9,13},{10,... | collective-permute-start | bytes 589832 | tf_op jit(solution)/shard_map/ppermute | solution.py:26
  256.4 6.9 %collective-permute-start.32 = (bf16[128,768]{1,0:T(8,128)(2,1)S(1)}, bf16[128,768]{1,0:T(8,128)(2,1)S(1)}, u32[]{:S(2)}, u32[]{:S(2)}) collective-permute-start(bf16[128,768]{1,0:T(8,128)(2,1)S(1)} %get-tuple-element.58), channel_id=1, source_target_pairs={{0,2},{1,3},{2,4},{3,5},{4,6},{5,7},{6,0},{7,1},{8,10},{9,11},{10,... | collective-permute-start | bytes 589832 | tf_op jit(solution)/shard_map/ppermute | solution.py:26
  (22 other events, 55.7 us)
Sparse Core Ops, SparseCore 0:
  24.6 41.4 all-gather.2
  72.2 41.8 all-gather.4
  130.9 45.5 reduce-scatter.2
  178.8 42.4 reduce-scatter.4

commit v10 on v9

--- a/solution.py
+++ b/solution.py
@@ -146,35 +146,8 @@
     across = [shift(left[0], 1), shift(right[1], -1)]
     acts = [*act, *left, *across, *right]
 
-    def join_g(place_ref, *refs):
-        for q in range(2):
-            for k in range(NZ):
-                row = q * NZ + (place_ref[0] + NZ - k) % NZ
-                refs[-1][block(own_rows, row), :] = refs[q * NZ + k][...]
-
-    cot = run(
-        join_g, of((s, 2 * feats)), (place, *g_far, *g_near), [SMEM] + [VMEM] * (2 * NZ),
-        name="g_join",
-    )
-
     tile = min(256, feats)
     steps = feats // tile
-
-    def term_of(i, after):
-        def body(g_ref, *refs):
-            top, bottom, out_ref = g_ref[:half, :], g_ref[half:, :], refs[-1]
-            for k in range(NZ):
-                out_ref[:, k * width : (k + 1) * width] = (
-                    dot(top, refs[2 * k][...], ((0,), (0,)))
-                    + dot(bottom, refs[2 * k + 1][...], ((0,), (0,)))
-                ).astype(jnp.bfloat16)
-
-        return run(
-            body, of((feats, lanes)), (cot, *acts),
-            [pl.BlockSpec((s, tile), lambda j: (0, i * steps + j))] + [VMEM] * 8,
-            after=after, grid=(steps,), out_specs=pl.BlockSpec((tile, lanes), lambda j: (j, 0)),
-            name="term", limit=BIG,
-        )
 
     def project(i, cuts, after):
         part = half // cuts
@@ -196,6 +169,36 @@
             [pl.BlockSpec((tile, lanes), lambda j: (j, 0))] + [VMEM] * 8,
             after=after, grid=(steps,), out_specs=[pl.BlockSpec((r, tile), lambda j: (0, j)) for r in [part] * cuts + [half]],
             name="project", limit=BIG,
+        )
+
+    *sent0, kept0 = project(0, 1, ())
+    got0 = [swap(x) for x in sent0]
+
+    def join_g(place_ref, *refs):
+        for q in range(2):
+            for k in range(NZ):
+                row = q * NZ + (place_ref[0] + NZ - k) % NZ
+                refs[-1][block(own_rows, row), :] = refs[q * NZ + k][...]
+
+    cot = run(
+        join_g, of((s, 2 * feats)), (place, *g_far, *g_near), [SMEM] + [VMEM] * (2 * NZ),
+        after=(kept0,), name="g_join",
+    )
+
+    def term_of(i, after):
+        def body(g_ref, *refs):
+            top, bottom, out_ref = g_ref[:half, :], g_ref[half:, :], refs[-1]
+            for k in range(NZ):
+                out_ref[:, k * width : (k + 1) * width] = (
+                    dot(top, refs[2 * k][...], ((0,), (0,)))
+                    + dot(bottom, refs[2 * k + 1][...], ((0,), (0,)))
+                ).astype(jnp.bfloat16)
+
+        return run(
+            body, of((feats, lanes)), (cot, *acts),
+            [pl.BlockSpec((s, tile), lambda j: (0, i * steps + j))] + [VMEM] * 8,
+            after=after, grid=(steps,), out_specs=pl.BlockSpec((tile, lanes), lambda j: (j, 0)),
+            name="term", limit=BIG,
         )
 
     cols = width // 3 if width % 384 == 0 else width
@@ -255,9 +258,9 @@
     far = rows_term(2, (bf16, bf16), (term_own,))
     up = shift(far[0], 1)
     down = shift(far[1], -1)
-    *sent0, kept0 = project(0, 1, (far[0],))
-    got0 = [swap(x) for x in sent0]
-    to_right = rows_term(3, (bf16,), (kept0,), (up,), 0)[0]
+    *sent1, kept1 = project(1, 1, (far[0],))
+    got1 = [swap(x) for x in sent1]
+    to_right = rows_term(3, (bf16,), (kept1, *got0), (up,), 0)[0]
     term_pair = run(
         move, of((piece, lanes)), (scatter(term_pair),), [VMEM], after=(to_right,), name="move"
     )
@@ -265,9 +268,7 @@
     term_pair = lax.ppermute(term_pair, "dp", pair)
     from_left = shift(to_right, 1)
     from_right = shift(to_left, -1)
-    *sent1, kept1 = project(1, 1, (to_left, *got0))
-    got1 = [swap(x) for x in sent1]
-    stay = rows_term(0, (f32,), (kept1,))[0]
+    stay = rows_term(0, (f32,), (to_left,))[0]
     quarters0, last = spread(kept0, got0, (stay,))
     term_own = scatter(term_own)
 

time: 274 us -> 280 us (1.022)
  waiting for transfers between devices: 88.4 us -> 99.5 us
  starting transfers between devices: 54.8 us -> 51.5 us
    ppermute x25, waiting for transfers between devices: 58.8 us -> 99.3 us  [shift(): return lax.ppermute(value, 'tensor', ring(step))]
    ppermute x6, waiting for transfers between devices: 26.8 us -> 0.04 us  [swap(): return lax.ppermute(value, 'tensor', SWAP)]
    ppermute x6, starting transfers between devices: 16.7 us -> 13.1 us  [swap(): return lax.ppermute(value, 'tensor', SWAP)]
    unnamed x66 -> x62, local copies, waits for them, and re-layouts: 13.9 us -> 12.1 us
  transfers between devices with their start and end apart: 37 -> 37, of which waited for: 12 -> 14; matrix products, arithmetic and copies ran while one was open for 0% -> 0% of each run, Pallas kernels for 36% -> 35%
where the time goes in v10:
time: 280 us; the launch traced here: 279 us
  Pallas kernels  102 us (36%)
  waiting for transfers between devices  99.5 us (36%)
  starting transfers between devices  51.5 us (18%)
  between operations  14.1 us (5%)
  local copies, waits for them, and re-layouts  12.1 us (4%)
    pallas_call x21, Pallas kernels, run(): pl.pallas_call(kernel, out_shape=out, grid=grid, in_specs=list(specs) + [...  102 us
    ppermute x25, waiting for transfers between devices, shift(): return lax.ppermute(value, 'tensor', ring(step))  99.3 us
    ppermute x25, starting transfers between devices, shift(): return lax.ppermute(value, 'tensor', ring(step))  35.2 us
    ppermute x6, starting transfers between devices, swap(): return lax.ppermute(value, 'tensor', SWAP)  13.1 us
    unnamed x62, local copies, waits for them, and re-layouts  12.1 us
  transfers between devices with their start and end apart: 37, of which 14 were waited for; matrix products, arithmetic and copies ran while one was open for 0% of the time, Pallas kernels for 35%

profile of v10, /device:TPU:0, one launch (start us, length us, event | category | flops | bytes accessed | tf_op | source)
XLA Modules:
  0.0 279.2 jit_solution(17150911499702607200)
XLA Ops:
  9.1 2.1 collective-permute-start
  11.1 3.6 %collective-permute-start.1 = (bf16[128,768]{1,0:T(8,128)(2,1)S(1)}, bf16[128,768]{1,0:T(8,128)(2,1)S(1)}, u32[]{:S(2)}, u32[]{:S(2)}) collective-permute-start(bf16[128,768]{1,0:T(8,128)(2,1)S(1)} %get-tuple-element.33), channel_id=1, source_target_pairs={{0,4},{1,5},{2,6},{3,7},{4,0},{5,1},{6,2},{7,3},{8,12},{9,13},{10,... | collective-permute-start | bytes 589832 | tf_op jit(solution)/shard_map/ppermute | solution.py:26
  15.7 1.6 copy-done.4
  19.4 4.1 %collective-permute-done.1.refs_2_ = bf16[128,768]{1,0:T(8,128)(2,1)S(1)} collective-permute-done((bf16[128,768]{1,0:T(8,128)(2,1)S(1)}, bf16[128,768]{1,0:T(8,128)(2,1)S(1)}, u32[]{:S(2)}, u32[]{:S(2)}) %collective-permute-start.1) | collective-permute-done | bytes 196640 | tf_op jit(solution)/shard_map/ppermute | solution.py:26
  24.6 1.3 collective-permute-start.11
  25.9 2.4 collective-permute-start.13
  30.3 1.6 collective-permute-start.17
  31.9 19.9 %collective-permute-done.11.refs_6_.refs_3_ = bf16[128,2048]{1,0:T(8,128)(2,1)S(1)} collective-permute-done((bf16[128,2048]{1,0:T(8,128)(2,1)}, bf16[128,2048]{1,0:T(8,128)(2,1)S(1)}, u32[]{:S(2)}, u32[]{:S(2)}) %collective-permute-start.11) | collective-permute-done | bytes 524320 | tf_op jit(solution)/shard_map/ppermute | solution.py:26
  52.5 3.2 %collective-permute-start.10 = (bf16[128,2048]{1,0:T(8,128)(2,1)S(1)}, bf16[128,2048]{1,0:T(8,128)(2,1)S(1)}, u32[]{:S(2)}, u32[]{:S(2)}) collective-permute-start(bf16[128,2048]{1,0:T(8,128)(2,1)S(1)} %get-tuple-element.35.refs_3_.refs_5_), channel_id=1, source_target_pairs={{0,1},{1,0},{2,3},{3,2},{4,5},{5,4},{6,7},{7,6},{8,9},{9,8},{10,11... | collective-permute-start | bytes 1572872 | tf_op jit(solution)/shard_map/ppermute | solution.py:30
  55.7 12.0 %collective-permute-done.15.refs_8_.refs_5_ = bf16[128,2048]{1,0:T(8,128)(2,1)S(1)} collective-permute-done((bf16[128,2048]{1,0:T(8,128)(2,1)S(1)}, bf16[128,2048]{1,0:T(8,128)(2,1)S(1)}, u32[]{:S(2)}, u32[]{:S(2)}) %collective-permute-start.15) | collective-permute-done | bytes 524320 | tf_op jit(solution)/shard_map/ppermute | solution.py:26
  70.1 2.1 w_move.1
  72.2 1.4 collective-permute-start.4
  73.6 1.9 collective-permute-start.8
  75.5 1.4 collective-permute-start.7
  77.6 3.2 %collective-permute-start.12 = (bf16[128,2048]{1,0:T(8,128)(2,1)}, bf16[128,2048]{1,0:T(8,128)(2,1)}, u32[]{:S(2)}, u32[]{:S(2)}) collective-permute-start(bf16[128,2048]{1,0:T(8,128)(2,1)} %copy-done.22), channel_id=1, source_target_pairs={{0,1},{1,0},{2,3},{3,2},{4,5},{5,4},{6,7},{7,6},{8,9},{9,8},{10,11... | collective-permute-start | bytes 1572872 | tf_op jit(solution)/shard_map/ppermute | solution.py:30
  80.8 13.2 %collective-permute-done.4.refs_4_ = bf16[512,768]{1,0:T(8,128)(2,1)S(1)} collective-permute-done((bf16[512,768]{1,0:T(8,128)(2,1)S(1)}, bf16[512,768]{1,0:T(8,128)(2,1)S(1)}, u32[]{:S(2)}, u32[]{:S(2)}) %collective-permute-start.4) | collective-permute-done | bytes 786464 | tf_op jit(solution)/shard_map/ppermute | solution.py:26
  94.0 3.2 %collective-permute-start.14 = (bf16[128,2048]{1,0:T(8,128)(2,1)}, bf16[128,2048]{1,0:T(8,128)(2,1)S(1)}, u32[]{:S(2)}, u32[]{:S(2)}) collective-permute-start(bf16[128,2048]{1,0:T(8,128)(2,1)} %copy-done.23), channel_id=1, source_target_pairs={{0,1},{1,0},{2,3},{3,2},{4,5},{5,4},{6,7},{7,6},{8,9},{9,8},{10,11... | collective-permute-start | bytes 1572872 | tf_op jit(solution)/shard_map/ppermute | solution.py:30
  97.5 12.2 %collective-permute-done.7.refs_6_ = bf16[512,768]{1,0:T(8,128)(2,1)} collective-permute-done((bf16[512,768]{1,0:T(8,128)(2,1)}, bf16[512,768]{1,0:T(8,128)(2,1)}, u32[]{:S(2)}, u32[]{:S(2)}) %collective-permute-start.7) | collective-permute-done | bytes 786464 | tf_op jit(solution)/shard_map/ppermute | solution.py:26
  109.8 11.6 %project.2 = (bf16[512,1024]{1,0:T(8,128)(2,1)}, f32[512,1024]{1,0:T(8,128)}) custom-call(bf16[1024,3072]{1,0:T(8,128)(2,1)} %all-gather.3.cloned.1.call-done.refs_0_.refs_1_, bf16[512,768]{1,0:T(8,128)(2,1)} %copy-done.1, bf16[512,768]{1,0:T(8,128)(2,1)} %copy-done.2, bf16[512,768]{1,0:T(8,128)(2,1)} %copy-done.18, bf16[512,768]{1,0:T(8,128)(2,1)} %copy-done.19, ...), custom_call_target="tpu_custom_call" | custom-call | flops 1000 | bytes 1000 | tf_op jit(solution)/shard_map/project/pallas_call | solution.py:47
  122.4 4.4 %g_join.1.refs_0_ = bf16[1024,2048]{1,0:T(8,128)(2,1)} custom-call(s32[4]{0:T(128)} %copy-done.12, bf16[128,2048]{1,0:T(8,128)(2,1)} %copy-done.25, bf16[128,2048]{1,0:T(8,128)(2,1)} %collective-permute-done.12.refs_2_, bf16[128,2048]{1,0:T(8,128)(2,1)} %copy-done.28, bf16[128,2048]{1,0:T(8,128)(2,1)} %copy-done.29, bf16[128,2048]{1,0:T(8,128)(2,1)} %copy-done.5, ...), custom_call_target="tpu_custom_call" | custom-call | flops 1000 | bytes 1000 | tf_op jit(solution)/shard_map/g_join/pallas_call | solution.py:47
  126.8 11.6 %term.2.refs_9_ = bf16[1024,3072]{1,0:T(8,128)(2,1)} custom-call(bf16[1024,2048]{1,0:T(8,128)(2,1)} %g_join.1.refs_0_, bf16[512,768]{1,0:T(8,128)(2,1)} %copy-done.1, bf16[512,768]{1,0:T(8,128)(2,1)} %copy-done.2, bf16[512,768]{1,0:T(8,128)(2,1)} %copy-done.18, bf16[512,768]{1,0:T(8,128)(2,1)} %copy-done.19, ...), custom_call_target="tpu_custom_call" | custom-call | flops 1000 | bytes 1000 | tf_op jit(solution)/shard_map/term/pallas_call | solution.py:47
  138.4 11.5 %term.3.refs_3_ = bf16[1024,3072]{1,0:T(8,128)(2,1)} custom-call(bf16[1024,2048]{1,0:T(8,128)(2,1)} %g_join.1.refs_0_, bf16[512,768]{1,0:T(8,128)(2,1)} %copy-done.1, bf16[512,768]{1,0:T(8,128)(2,1)} %copy-done.2, bf16[512,768]{1,0:T(8,128)(2,1)} %copy-done.18, bf16[512,768]{1,0:T(8,128)(2,1)} %copy-done.19, ...), custom_call_target="tpu_custom_call" | custom-call | flops 1000 | bytes 1000 | tf_op jit(solution)/shard_map/term/pallas_call | solution.py:47
  151.2 3.2 %collective-permute-start.9 = (bf16[512,1024]{1,0:T(8,128)(2,1)S(1)}, bf16[512,1024]{1,0:T(8,128)(2,1)S(1)}, u32[]{:S(2)}, u32[]{:S(2)}) collective-permute-start(bf16[512,1024]{1,0:T(8,128)(2,1)S(1)} %copy-done.30), channel_id=1, source_target_pairs={{0,1},{1,0},{2,3},{3,2},{4,5},{5,4},{6,7},{7,6},{8,9},{9,8},{10,11... | collective-permute-start | bytes 3145736 | tf_op jit(solution)/shard_map/ppermute | solution.py:30
  154.4 7.3 %rows_term.4 = (bf16[512,768]{1,0:T(8,128)(2,1)}, bf16[512,768]{1,0:T(8,128)(2,1)}) custom-call(bf16[1024,2048]{1,0:T(8,128)(2,1)} %g_join.1.refs_0_, bf16[1024,3072]{1,0:T(8,128)(2,1)} %all-gather.3.cloned.1.call-done.refs_0_.refs_1_, bf16[1024,3072]{1,0:T(8,128)(2,1)} %all-gather.5.cloned.1.call-done.refs_2_.refs_0_, bf16[1024,3072]{1,0:T(8,128)(2,1)} %term.3.refs_3_), custom_call_target="tpu_custom_call" | custom-call | flops 1000 | bytes 1000 | tf_op jit(solution)/shard_map/rows_term/pallas_call | solution.py:47
  162.7 2.2 collective-permute-start.18
  164.9 11.7 %project.3 = (bf16[512,1024]{1,0:T(8,128)(2,1)}, f32[512,1024]{1,0:T(8,128)}) custom-call(bf16[1024,3072]{1,0:T(8,128)(2,1)} %all-gather.5.cloned.1.call-done.refs_2_.refs_0_, bf16[512,768]{1,0:T(8,128)(2,1)} %copy-done.1, bf16[512,768]{1,0:T(8,128)(2,1)} %copy-done.2, bf16[512,768]{1,0:T(8,128)(2,1)} %copy-done.18, bf16[512,768]{1,0:T(8,128)(2,1)} %copy-done.19, ...), custom_call_target="tpu_custom_call" | custom-call | flops 1000 | bytes 1000 | tf_op jit(solution)/shard_map/project/pallas_call | solution.py:47
  176.6 4.5 %collective-permute-done.19.refs_3_ = bf16[512,768]{1,0:T(8,128)(2,1)S(1)} collective-permute-done((bf16[512,768]{1,0:T(8,128)(2,1)}, bf16[512,768]{1,0:T(8,128)(2,1)S(1)}, u32[]{:S(2)}, u32[]{:S(2)}) %collective-permute-start.19) | collective-permute-done | bytes 786464 | tf_op jit(solution)/shard_map/ppermute | solution.py:26
  182.0 7.6 %rows_term.5.refs_1_.refs_4_ = bf16[1024,768]{1,0:T(8,128)(2,1)} custom-call(bf16[1024,2048]{1,0:T(8,128)(2,1)} %g_join.1.refs_0_, bf16[1024,3072]{1,0:T(8,128)(2,1)} %all-gather.3.cloned.1.call-done.refs_0_.refs_1_, bf16[1024,3072]{1,0:T(8,128)(2,1)} %all-gather.5.cloned.1.call-done.refs_2_.refs_0_, bf16[512,768]{1,0:T(8,128)(2,1)} %copy-done.26, ...), custom_call_target="tpu_custom_call" | custom-call | flops 1000 | bytes 1000 | tf_op jit(solution)/shard_map/rows_term/pallas_call | solution.py:47
  189.9 2.1 move.1.refs_5_
  192.0 8.1 %rows_term.6.refs_3_ = bf16[1024,768]{1,0:T(8,128)(2,1)} custom-call(bf16[1024,2048]{1,0:T(8,128)(2,1)} %g_join.1.refs_0_, bf16[1024,3072]{1,0:T(8,128)(2,1)} %all-gather.3.cloned.1.call-done.refs_0_.refs_1_, bf16[1024,3072]{1,0:T(8,128)(2,1)} %all-gather.5.cloned.1.call-done.refs_2_.refs_0_, bf16[512,768]{1,0:T(8,128)(2,1)} %collective-permute-done.18.refs_3_, ...), custom_call_target="tpu_custom_call" | custom-call | flops 1000 | bytes 1000 | tf_op jit(solution)/shard_map/rows_term/pallas_call | solution.py:47
  200.1 3.0 %collective-permute-start.25 = (bf16[1024,768]{1,0:T(8,128)(2,1)}, bf16[1024,768]{1,0:T(8,128)(2,1)S(1)}, u32[]{:S(2)}, u32[]{:S(2)}) collective-permute-start(bf16[1024,768]{1,0:T(8,128)(2,1)} %rows_term.6.refs_3_), channel_id=1, source_target_pairs={{0,6},{1,7},{2,0},{3,1},{4,2},{5,3},{6,4},{7,5},{8,14},{9,15},{10,... | collective-permute-start | bytes 4718600 | tf_op jit(solution)/shard_map/ppermute | solution.py:26
  203.1 1.5 collective-permute-start.29
  204.6 7.8 %rows_term.7.refs_3_.refs_2_ = f32[1024,768]{1,0:T(8,128)} custom-call(bf16[1024,2048]{1,0:T(8,128)(2,1)} %g_join.1.refs_0_, bf16[1024,3072]{1,0:T(8,128)(2,1)} %all-gather.3.cloned.1.call-done.refs_0_.refs_1_, bf16[1024,3072]{1,0:T(8,128)(2,1)} %all-gather.5.cloned.1.call-done.refs_2_.refs_0_, bf16[1024,768]{1,0:T(8,128)(2,1)} %rows_term.6.refs_3_), custom_call_target="tpu_custom_call" | custom-call | flops 1000 | bytes 1000 | tf_op jit(solution)/shard_map/rows_term/pallas_call | solution.py:47
  212.5 3.2 %settle.2 = (bf16[128,1024]{1,0:T(8,128)(2,1)}, bf16[128,1024]{1,0:T(8,128)(2,1)}, bf16[128,1024]{1,0:T(8,128)(2,1)}, bf16[128,1024]{1,0:T(8,128)(2,1)}) custom-call(s32[4]{0:T(128)} %copy-done.12, f32[512,1024]{1,0:T(8,128)} %get-tuple-element.38.refs_9_.refs_1_, bf16[512,1024]{1,0:T(8,128)(2,1)} %copy-done.21, f32[1024,768]{1,0:T(8,128)} %rows_term.7.refs_3_.refs_2_), custom_call_target="tpu_custom_call" | custom-call | flops 1000 | bytes 1000 | tf_op jit(solution)/shard_map/settle/pallas_call | solution.py:47
  215.7 13.4 %collective-permute-done.24.refs_3_ = bf16[1024,768]{1,0:T(8,128)(2,1)S(1)} collective-permute-done((bf16[1024,768]{1,0:T(8,128)(2,1)}, bf16[1024,768]{1,0:T(8,128)(2,1)S(1)}, u32[]{:S(2)}, u32[]{:S(2)}) %collective-permute-start.24) | collective-permute-done | bytes 1572896 | tf_op jit(solution)/shard_map/ppermute | solution.py:26
  229.1 11.3 %collective-permute-done.25.refs_4_ = bf16[1024,768]{1,0:T(8,128)(2,1)S(1)} collective-permute-done((bf16[1024,768]{1,0:T(8,128)(2,1)}, bf16[1024,768]{1,0:T(8,128)(2,1)S(1)}, u32[]{:S(2)}, u32[]{:S(2)}) %collective-permute-start.25) | collective-permute-done | bytes 1572896 | tf_op jit(solution)/shard_map/ppermute | solution.py:26
  240.4 4.0 %collective-permute-start.22 = (bf16[128,1024]{1,0:T(8,128)(2,1)}, bf16[128,1024]{1,0:T(8,128)(2,1)S(1)}, u32[]{:S(2)}, u32[]{:S(2)}) collective-permute-start(bf16[128,1024]{1,0:T(8,128)(2,1)} %get-tuple-element.49), channel_id=1, source_target_pairs={{0,6},{1,7},{2,0},{3,1},{4,2},{5,3},{6,4},{7,5},{8,14},{9,15},{10,... | collective-permute-start | bytes 786440 | tf_op jit(solution)/shard_map/ppermute | solution.py:26
  244.4 2.2 add_rows.1.refs_3_
  246.7 3.0 %settle.3 = (bf16[128,1024]{1,0:T(8,128)(2,1)}, bf16[128,1024]{1,0:T(8,128)(2,1)}, bf16[128,1024]{1,0:T(8,128)(2,1)}, bf16[128,1024]{1,0:T(8,128)(2,1)}) custom-call(s32[4]{0:T(128)} %copy-done.12, f32[512,1024]{1,0:T(8,128)} %get-tuple-element.45.refs_4_.refs_1_, bf16[512,1024]{1,0:T(8,128)(2,1)} %collective-permute-done.23.refs_2_, ...), custom_call_target="tpu_custom_call" | custom-call | flops 1000 | bytes 1000 | tf_op jit(solution)/shard_map/settle/pallas_call | solution.py:47
  249.7 1.5 collective-permute-start.27
  251.2 1.8 collective-permute-start.28
  255.4 3.7 %collective-permute-start.30 = (bf16[128,768]{1,0:T(8,128)(2,1)S(1)}, bf16[128,768]{1,0:T(8,128)(2,1)S(1)}, u32[]{:S(2)}, u32[]{:S(2)}) collective-permute-start(bf16[128,768]{1,0:T(8,128)(2,1)S(1)} %get-tuple-element.56), channel_id=1, source_target_pairs={{0,6},{1,7},{2,0},{3,1},{4,2},{5,3},{6,4},{7,5},{8,14},{9,15},{10,... | collective-permute-start | bytes 589832 | tf_op jit(solution)/shard_map/ppermute | solution.py:26
  259.1 3.3 %collective-permute-done.26.refs_6_ = bf16[128,1024]{1,0:T(8,128)(2,1)S(1)} collective-permute-done((bf16[128,1024]{1,0:T(8,128)(2,1)}, bf16[128,1024]{1,0:T(8,128)(2,1)S(1)}, u32[]{:S(2)}, u32[]{:S(2)}) %collective-permute-start.26) | collective-permute-done | bytes 262176 | tf_op jit(solution)/shard_map/ppermute | solution.py:26
  262.5 2.4 join_out.1.refs_5_
  264.9 1.4 collective-permute-done.31.refs_3_
  266.3 3.0 %collective-permute-done.32.refs_4_ = bf16[128,768]{1,0:T(8,128)(2,1)S(1)} collective-permute-done((bf16[128,768]{1,0:T(8,128)(2,1)S(1)}, bf16[128,768]{1,0:T(8,128)(2,1)S(1)}, u32[]{:S(2)}, u32[]{:S(2)}) %collective-permute-start.32) | collective-permute-done | bytes 196640 | tf_op jit(solution)/shard_map/ppermute | solution.py:26
  269.2 1.6 copy-done.3
  270.8 1.8 join_term.1
  (114 shorter events, 19.1 us)
Async XLA Ops:
  7.2 102.6 %all-gather.3.cloned.1.call-start = ((), (), s32[]{:S(2)}) async-start(), calls=%async_computation.2 | async-start | bytes 7077888 | tf_op jit(solution)/shard_map/all_gather | solution.py:140
  9.1 10.4 %collective-permute-start = (bf16[128,768]{1,0:T(8,128)(2,1)S(1)}, bf16[128,768]{1,0:T(8,128)(2,1)S(1)}, u32[]{:S(2)}, u32[]{:S(2)}) collective-permute-start(bf16[128,768]{1,0:T(8,128)(2,1)S(1)} %get-tuple-element.32), channel_id=1, source_target_pairs={{0,2},{1,3},{2,4},{3,5},{4,6},{5,7},{6,0},{7,1},{8,10},{9,11},{10,... | collective-permute-start | bytes 589832 | tf_op jit(solution)/shard_map/ppermute | solution.py:26
  11.1 12.4 %collective-permute-start.1 = (bf16[128,768]{1,0:T(8,128)(2,1)S(1)}, bf16[128,768]{1,0:T(8,128)(2,1)S(1)}, u32[]{:S(2)}, u32[]{:S(2)}) collective-permute-start(bf16[128,768]{1,0:T(8,128)(2,1)S(1)} %get-tuple-element.33), channel_id=1, source_target_pairs={{0,4},{1,5},{2,6},{3,7},{4,0},{5,1},{6,2},{7,3},{8,12},{9,13},{10,... | collective-permute-start | bytes 589832 | tf_op jit(solution)/shard_map/ppermute | solution.py:26
  14.7 8.8 %collective-permute-start.2 = (bf16[128,768]{1,0:T(8,128)(2,1)S(1)}, bf16[128,768]{1,0:T(8,128)(2,1)S(1)}, u32[]{:S(2)}, u32[]{:S(2)}) collective-permute-start(bf16[128,768]{1,0:T(8,128)(2,1)S(1)} %get-tuple-element.34), channel_id=1, source_target_pairs={{0,6},{1,7},{2,0},{3,1},{4,2},{5,3},{6,4},{7,5},{8,14},{9,15},{10,... | collective-permute-start | bytes 589832 | tf_op jit(solution)/shard_map/ppermute | solution.py:26
  18.4 34.1 %copy-start.5 = (bf16[128,2048]{1,0:T(8,128)(2,1)}, bf16[128,2048]{1,0:T(8,128)(2,1)S(1)}, u32[]{:S(2)}) copy-start(bf16[128,2048]{1,0:T(8,128)(2,1)S(1)} %get-tuple-element.35.refs_3_.refs_5_) | copy-start | bytes 1572868
  19.4 52.8 %copy-start.2 = (bf16[512,768]{1,0:T(8,128)(2,1)}, bf16[512,768]{1,0:T(8,128)(2,1)S(1)}, u32[]{:S(2)}) copy-start(bf16[512,768]{1,0:T(8,128)(2,1)S(1)} %get-tuple-element.37.refs_2_) | copy-start | bytes 2359300
  19.4 54.2 %copy-start.1 = (bf16[512,768]{1,0:T(8,128)(2,1)}, bf16[512,768]{1,0:T(8,128)(2,1)S(1)}, u32[]{:S(2)}) copy-start(bf16[512,768]{1,0:T(8,128)(2,1)S(1)} %get-tuple-element.36.refs_4_.refs_1_) | copy-start | bytes 2359300
  24.5 129.8 %all-gather.5.cloned.1.call-start = ((), (), s32[]{:S(2)}) async-start(), calls=%async_computation.3 | async-start | bytes 7077888 | tf_op jit(solution)/shard_map/all_gather | solution.py:140
  24.6 27.2 %collective-permute-start.11 = (bf16[128,2048]{1,0:T(8,128)(2,1)}, bf16[128,2048]{1,0:T(8,128)(2,1)S(1)}, u32[]{:S(2)}, u32[]{:S(2)}) collective-permute-start(bf16[128,2048]{1,0:T(8,128)(2,1)} %copy-done.16), channel_id=1, source_target_pairs={{0,2},{1,3},{2,4},{3,5},{4,6},{5,7},{6,0},{7,1},{8,10},{9,11},{10,... | collective-permute-start | bytes 1572872 | tf_op jit(solution)/shard_map/ppermute | solution.py:26
  25.9 26.6 %collective-permute-start.13 = (bf16[128,2048]{1,0:T(8,128)(2,1)S(1)}, bf16[128,2048]{1,0:T(8,128)(2,1)S(1)}, u32[]{:S(2)}, u32[]{:S(2)}) collective-permute-start(bf16[128,2048]{1,0:T(8,128)(2,1)S(1)} %get-tuple-element.41), channel_id=1, source_target_pairs={{0,4},{1,5},{2,6},{3,7},{4,0},{5,1},{6,2},{7,3},{8,12},{9,13},{10,... | collective-permute-start | bytes 1572872 | tf_op jit(solution)/shard_map/ppermute | solution.py:26
  28.3 39.4 %collective-permute-start.6 = (bf16[512,768]{1,0:T(8,128)(2,1)S(1)}, bf16[512,768]{1,0:T(8,128)(2,1)S(1)}, u32[]{:S(2)}, u32[]{:S(2)}) collective-permute-start(bf16[512,768]{1,0:T(8,128)(2,1)S(1)} %get-tuple-element.37.refs_2_), channel_id=1, source_target_pairs={{0,6},{1,7},{2,0},{3,1},{4,2},{5,3},{6,4},{7,5},{8,14},{9,15},{10,... | collective-permute-start | bytes 2359304 | tf_op jit(solution)/shard_map/ppermute | solution.py:26
  29.5 38.2 %collective-permute-start.3 = (bf16[512,768]{1,0:T(8,128)(2,1)S(1)}, bf16[512,768]{1,0:T(8,128)(2,1)S(1)}, u32[]{:S(2)}, u32[]{:S(2)}) collective-permute-start(bf16[512,768]{1,0:T(8,128)(2,1)S(1)} %get-tuple-element.36.refs_4_.refs_1_), channel_id=1, source_target_pairs={{0,2},{1,3},{2,4},{3,5},{4,6},{5,7},{6,0},{7,1},{8,10},{9,11},{10,... | collective-permute-start | bytes 2359304 | tf_op jit(solution)/shard_map/ppermute | solution.py:26
  30.3 37.5 %collective-permute-start.17 = (bf16[128,3072]{1,0:T(8,128)(2,1)}, bf16[128,3072]{1,0:T(8,128)(2,1)S(1)}, u32[]{:S(2)}, u32[]{:S(2)}) collective-permute-start(bf16[128,3072]{1,0:T(8,128)(2,1)} %w_join.1), channel_id=1, source_target_pairs={{0,64},{8,72},{16,80},{24,88},{32,96},{40,104},{48,112},{56,120},{... | collective-permute-start | bytes 2359304 | tf_op jit(solution)/shard_map/ppermute | solution.py:135
  51.8 16.0 %copy-start.22 = (bf16[128,2048]{1,0:T(8,128)(2,1)}, bf16[128,2048]{1,0:T(8,128)(2,1)S(1)}, u32[]{:S(2)}) copy-start(bf16[128,2048]{1,0:T(8,128)(2,1)S(1)} %collective-permute-done.11.refs_6_.refs_3_) | copy-start | bytes 1572868
  51.8 15.9 %collective-permute-start.15 = (bf16[128,2048]{1,0:T(8,128)(2,1)S(1)}, bf16[128,2048]{1,0:T(8,128)(2,1)S(1)}, u32[]{:S(2)}, u32[]{:S(2)}) collective-permute-start(bf16[128,2048]{1,0:T(8,128)(2,1)S(1)} %get-tuple-element.42), channel_id=1, source_target_pairs={{0,6},{1,7},{2,0},{3,1},{4,2},{5,3},{6,4},{7,5},{8,14},{9,15},{10,... | collective-permute-start | bytes 1572872 | tf_op jit(solution)/shard_map/ppermute | solution.py:26
  52.5 15.2 %copy-start.23 = (bf16[128,2048]{1,0:T(8,128)(2,1)}, bf16[128,2048]{1,0:T(8,128)(2,1)S(1)}, u32[]{:S(2)}) copy-start(bf16[128,2048]{1,0:T(8,128)(2,1)S(1)} %collective-permute-done.13.refs_7_.refs_4_) | copy-start | bytes 1572868
  52.5 15.2 %collective-permute-start.10 = (bf16[128,2048]{1,0:T(8,128)(2,1)S(1)}, bf16[128,2048]{1,0:T(8,128)(2,1)S(1)}, u32[]{:S(2)}, u32[]{:S(2)}) collective-permute-start(bf16[128,2048]{1,0:T(8,128)(2,1)S(1)} %get-tuple-element.35.refs_3_.refs_5_), channel_id=1, source_target_pairs={{0,1},{1,0},{2,3},{3,2},{4,5},{5,4},{6,7},{7,6},{8,9},{9,8},{10,11... | collective-permute-start | bytes 1572872 | tf_op jit(solution)/shard_map/ppermute | solution.py:30
  72.2 117.7 %reduce-scatter.3.cloned.1.call-start = ((), (), s32[]{:S(2)}) async-start(), calls=%async_computation.4 | async-start | bytes 7077888 | tf_op jit(solution)/shard_map/reduce_scatter | solution.py:233
  72.2 21.7 %collective-permute-start.4 = (bf16[512,768]{1,0:T(8,128)(2,1)S(1)}, bf16[512,768]{1,0:T(8,128)(2,1)S(1)}, u32[]{:S(2)}, u32[]{:S(2)}) collective-permute-start(bf16[512,768]{1,0:T(8,128)(2,1)S(1)} %get-tuple-element.37.refs_2_), channel_id=1, source_target_pairs={{0,2},{1,3},{2,4},{3,5},{4,6},{5,7},{6,0},{7,1},{8,10},{9,11},{10,... | collective-permute-start | bytes 2359304 | tf_op jit(solution)/shard_map/ppermute | solution.py:26
  73.6 23.6 %collective-permute-start.8 = (bf16[512,768]{1,0:T(8,128)(2,1)S(1)}, bf16[512,768]{1,0:T(8,128)(2,1)S(1)}, u32[]{:S(2)}, u32[]{:S(2)}) collective-permute-start(bf16[512,768]{1,0:T(8,128)(2,1)S(1)} %get-tuple-element.36.refs_4_.refs_1_), channel_id=1, source_target_pairs={{0,6},{1,7},{2,0},{3,1},{4,2},{5,3},{6,4},{7,5},{8,14},{9,15},{10,... | collective-permute-start | bytes 2359304 | tf_op jit(solution)/shard_map/ppermute | solution.py:26
  75.5 34.2 %collective-permute-start.7 = (bf16[512,768]{1,0:T(8,128)(2,1)}, bf16[512,768]{1,0:T(8,128)(2,1)}, u32[]{:S(2)}, u32[]{:S(2)}) collective-permute-start(bf16[512,768]{1,0:T(8,128)(2,1)} %copy-done.17), channel_id=1, source_target_pairs={{0,6},{1,7},{2,0},{3,1},{4,2},{5,3},{6,4},{7,5},{8,14},{9,15},{10,... | collective-permute-start | bytes 2359304 | tf_op jit(solution)/shard_map/ppermute | solution.py:26
  77.0 32.8 %collective-permute-start.5 = (bf16[512,768]{1,0:T(8,128)(2,1)}, bf16[512,768]{1,0:T(8,128)(2,1)}, u32[]{:S(2)}, u32[]{:S(2)}) collective-permute-start(bf16[512,768]{1,0:T(8,128)(2,1)} %copy-done.18), channel_id=1, source_target_pairs={{0,2},{1,3},{2,4},{3,5},{4,6},{5,7},{6,0},{7,1},{8,10},{9,11},{10,... | collective-permute-start | bytes 2359304 | tf_op jit(solution)/shard_map/ppermute | solution.py:26
  77.6 43.8 %collective-permute-start.12 = (bf16[128,2048]{1,0:T(8,128)(2,1)}, bf16[128,2048]{1,0:T(8,128)(2,1)}, u32[]{:S(2)}, u32[]{:S(2)}) collective-permute-start(bf16[128,2048]{1,0:T(8,128)(2,1)} %copy-done.22), channel_id=1, source_target_pairs={{0,1},{1,0},{2,3},{3,2},{4,5},{5,4},{6,7},{7,6},{8,9},{9,8},{10,11... | collective-permute-start | bytes 1572872 | tf_op jit(solution)/shard_map/ppermute | solution.py:30
  94.0 15.8 %copy-start.19 = (bf16[512,768]{1,0:T(8,128)(2,1)}, bf16[512,768]{1,0:T(8,128)(2,1)S(1)}, u32[]{:S(2)}) copy-start(bf16[512,768]{1,0:T(8,128)(2,1)S(1)} %collective-permute-done.4.refs_4_) | copy-start | bytes 2359300
  94.0 27.4 %collective-permute-start.14 = (bf16[128,2048]{1,0:T(8,128)(2,1)}, bf16[128,2048]{1,0:T(8,128)(2,1)S(1)}, u32[]{:S(2)}, u32[]{:S(2)}) collective-permute-start(bf16[128,2048]{1,0:T(8,128)(2,1)} %copy-done.23), channel_id=1, source_target_pairs={{0,1},{1,0},{2,3},{3,2},{4,5},{5,4},{6,7},{7,6},{8,9},{9,8},{10,11... | collective-permute-start | bytes 1572872 | tf_op jit(solution)/shard_map/ppermute | solution.py:30
  97.2 12.6 %copy-start.20 = (bf16[512,768]{1,0:T(8,128)(2,1)}, bf16[512,768]{1,0:T(8,128)(2,1)S(1)}, u32[]{:S(2)}) copy-start(bf16[512,768]{1,0:T(8,128)(2,1)S(1)} %collective-permute-done.8.refs_7_) | copy-start | bytes 2359300
  97.2 24.2 %collective-permute-start.16 = (bf16[128,2048]{1,0:T(8,128)(2,1)}, bf16[128,2048]{1,0:T(8,128)(2,1)S(1)}, u32[]{:S(2)}, u32[]{:S(2)}) collective-permute-start(bf16[128,2048]{1,0:T(8,128)(2,1)} %copy-done.24), channel_id=1, source_target_pairs={{0,1},{1,0},{2,3},{3,2},{4,5},{5,4},{6,7},{7,6},{8,9},{9,8},{10,11... | collective-permute-start | bytes 1572872 | tf_op jit(solution)/shard_map/ppermute | solution.py:30
  138.4 114.6 %reduce-scatter.5.cloned.1.call-start = ((), (), s32[]{:S(2)}) async-start(), calls=%async_computation.5 | async-start | bytes 7077888 | tf_op jit(solution)/shard_map/reduce_scatter | solution.py:233
  151.2 25.5 %collective-permute-start.9 = (bf16[512,1024]{1,0:T(8,128)(2,1)S(1)}, bf16[512,1024]{1,0:T(8,128)(2,1)S(1)}, u32[]{:S(2)}, u32[]{:S(2)}) collective-permute-start(bf16[512,1024]{1,0:T(8,128)(2,1)S(1)} %copy-done.30), channel_id=1, source_target_pairs={{0,1},{1,0},{2,3},{3,2},{4,5},{5,4},{6,7},{7,6},{8,9},{9,8},{10,11... | collective-permute-start | bytes 3145736 | tf_op jit(solution)/shard_map/ppermute | solution.py:30
  161.6 19.5 %collective-permute-start.19 = (bf16[512,768]{1,0:T(8,128)(2,1)}, bf16[512,768]{1,0:T(8,128)(2,1)S(1)}, u32[]{:S(2)}, u32[]{:S(2)}) collective-permute-start(bf16[512,768]{1,0:T(8,128)(2,1)} %get-tuple-element.44.refs_9_), channel_id=1, source_target_pairs={{0,2},{1,3},{2,4},{3,5},{4,6},{5,7},{6,0},{7,1},{8,10},{9,11},{10,... | collective-permute-start | bytes 2359304 | tf_op jit(solution)/shard_map/ppermute | solution.py:26
  162.7 29.4 %collective-permute-start.18 = (bf16[512,768]{1,0:T(8,128)(2,1)}, bf16[512,768]{1,0:T(8,128)(2,1)}, u32[]{:S(2)}, u32[]{:S(2)}) collective-permute-start(bf16[512,768]{1,0:T(8,128)(2,1)} %get-tuple-element.43), channel_id=1, source_target_pairs={{0,6},{1,7},{2,0},{3,1},{4,2},{5,3},{6,4},{7,5},{8,14},{9,15},{10,... | collective-permute-start | bytes 2359304 | tf_op jit(solution)/shard_map/ppermute | solution.py:26
  189.6 39.5 %collective-permute-start.24 = (bf16[1024,768]{1,0:T(8,128)(2,1)}, bf16[1024,768]{1,0:T(8,128)(2,1)S(1)}, u32[]{:S(2)}, u32[]{:S(2)}) collective-permute-start(bf16[1024,768]{1,0:T(8,128)(2,1)} %rows_term.5.refs_1_.refs_4_), channel_id=1, source_target_pairs={{0,2},{1,3},{2,4},{3,5},{4,6},{5,7},{6,0},{7,1},{8,10},{9,11},{10,... | collective-permute-start | bytes 4718600 | tf_op jit(solution)/shard_map/ppermute | solution.py:26
  200.1 40.3 %collective-permute-start.25 = (bf16[1024,768]{1,0:T(8,128)(2,1)}, bf16[1024,768]{1,0:T(8,128)(2,1)S(1)}, u32[]{:S(2)}, u32[]{:S(2)}) collective-permute-start(bf16[1024,768]{1,0:T(8,128)(2,1)} %rows_term.6.refs_3_), channel_id=1, source_target_pairs={{0,6},{1,7},{2,0},{3,1},{4,2},{5,3},{6,4},{7,5},{8,14},{9,15},{10,... | collective-permute-start | bytes 4718600 | tf_op jit(solution)/shard_map/ppermute | solution.py:26
  203.1 43.5 %collective-permute-start.23 = (bf16[512,1024]{1,0:T(8,128)(2,1)}, bf16[512,1024]{1,0:T(8,128)(2,1)}, u32[]{:S(2)}, u32[]{:S(2)}) collective-permute-start(bf16[512,1024]{1,0:T(8,128)(2,1)} %get-tuple-element.50), channel_id=1, source_target_pairs={{0,1},{1,0},{2,3},{3,2},{4,5},{5,4},{6,7},{7,6},{8,9},{9,8},{10,11... | collective-permute-start | bytes 3145736 | tf_op jit(solution)/shard_map/ppermute | solution.py:30
  203.1 50.0 %collective-permute-start.29 = (bf16[128,3072]{1,0:T(8,128)(2,1)}, bf16[128,3072]{1,0:T(8,128)(2,1)S(1)}, u32[]{:S(2)}, u32[]{:S(2)}) collective-permute-start(bf16[128,3072]{1,0:T(8,128)(2,1)} %move.1.refs_5_), channel_id=1, source_target_pairs={{0,64},{8,72},{16,80},{24,88},{32,96},{40,104},{48,112},{56,120},{... | collective-permute-start | bytes 2359304 | tf_op jit(solution)/shard_map/ppermute | solution.py:268
  212.5 31.9 %copy-start = (f32[1024,768]{1,0:T(8,128)S(1)}, f32[1024,768]{1,0:T(8,128)}, u32[]{:S(2)}) copy-start(f32[1024,768]{1,0:T(8,128)} %rows_term.7.refs_3_.refs_2_) | copy-start | bytes 9437188
  212.5 31.9 %copy-start.13 = (s32[4]{0:T(128)S(1)}, s32[4]{0:T(128)}, u32[]{:S(2)}) copy-start(s32[4]{0:T(128)} %copy-done.12) | copy-start | bytes 52
  215.7 34.0 %collective-permute-start.20 = (bf16[128,1024]{1,0:T(8,128)(2,1)}, bf16[128,1024]{1,0:T(8,128)(2,1)S(1)}, u32[]{:S(2)}, u32[]{:S(2)}) collective-permute-start(bf16[128,1024]{1,0:T(8,128)(2,1)} %get-tuple-element.47), channel_id=1, source_target_pairs={{0,2},{1,3},{2,4},{3,5},{4,6},{5,7},{6,0},{7,1},{8,10},{9,11},{10,... | collective-permute-start | bytes 786440 | tf_op jit(solution)/shard_map/ppermute | solution.py:26
  229.1 22.1 %collective-permute-start.21 = (bf16[128,1024]{1,0:T(8,128)(2,1)}, bf16[128,1024]{1,0:T(8,128)(2,1)S(1)}, u32[]{:S(2)}, u32[]{:S(2)}) collective-permute-start(bf16[128,1024]{1,0:T(8,128)(2,1)} %get-tuple-element.48), channel_id=1, source_target_pairs={{0,4},{1,5},{2,6},{3,7},{4,0},{5,1},{6,2},{7,3},{8,12},{9,13},{10,... | collective-permute-start | bytes 786440 | tf_op jit(solution)/shard_map/ppermute | solution.py:26
  240.4 12.8 %collective-permute-start.22 = (bf16[128,1024]{1,0:T(8,128)(2,1)}, bf16[128,1024]{1,0:T(8,128)(2,1)S(1)}, u32[]{:S(2)}, u32[]{:S(2)}) collective-permute-start(bf16[128,1024]{1,0:T(8,128)(2,1)} %get-tuple-element.49), channel_id=1, source_target_pairs={{0,6},{1,7},{2,0},{3,1},{4,2},{5,3},{6,4},{7,5},{8,14},{9,15},{10,... | collective-permute-start | bytes 786440 | tf_op jit(solution)/shard_map/ppermute | solution.py:26
  246.7 15.8 %copy-start.11 = (bf16[128,1024]{1,0:T(8,128)(2,1)S(1)}, bf16[128,1024]{1,0:T(8,128)(2,1)}, u32[]{:S(2)}) copy-start(bf16[128,1024]{1,0:T(8,128)(2,1)} %get-tuple-element.46.refs_1_) | copy-start | bytes 786436
  249.7 12.8 %copy-start.14 = (s32[4]{0:T(128)S(1)}, s32[4]{0:T(128)}, u32[]{:S(2)}) copy-start(s32[4]{0:T(128)} %copy-done.12) | copy-start | bytes 52
  249.7 12.7 %collective-permute-start.26 = (bf16[128,1024]{1,0:T(8,128)(2,1)}, bf16[128,1024]{1,0:T(8,128)(2,1)S(1)}, u32[]{:S(2)}, u32[]{:S(2)}) collective-permute-start(bf16[128,1024]{1,0:T(8,128)(2,1)} %get-tuple-element.52), channel_id=1, source_target_pairs={{0,2},{1,3},{2,4},{3,5},{4,6},{5,7},{6,0},{7,1},{8,10},{9,11},{10,... | collective-permute-start | bytes 786440 | tf_op jit(solution)/shard_map/ppermute | solution.py:26
  249.7 12.7 %collective-permute-start.27 = (bf16[128,1024]{1,0:T(8,128)(2,1)}, bf16[128,1024]{1,0:T(8,128)(2,1)S(1)}, u32[]{:S(2)}, u32[]{:S(2)}) collective-permute-start(bf16[128,1024]{1,0:T(8,128)(2,1)} %get-tuple-element.53), channel_id=1, source_target_pairs={{0,4},{1,5},{2,6},{3,7},{4,0},{5,1},{6,2},{7,3},{8,12},{9,13},{10,... | collective-permute-start | bytes 786440 | tf_op jit(solution)/shard_map/ppermute | solution.py:26
  251.2 11.3 %collective-permute-start.28 = (bf16[128,1024]{1,0:T(8,128)(2,1)}, bf16[128,1024]{1,0:T(8,128)(2,1)S(1)}, u32[]{:S(2)}, u32[]{:S(2)}) collective-permute-start(bf16[128,1024]{1,0:T(8,128)(2,1)} %get-tuple-element.54), channel_id=1, source_target_pairs={{0,6},{1,7},{2,0},{3,1},{4,2},{5,3},{6,4},{7,5},{8,14},{9,15},{10,... | collective-permute-start | bytes 786440 | tf_op jit(solution)/shard_map/ppermute | solution.py:26
  255.4 9.4 %collective-permute-start.30 = (bf16[128,768]{1,0:T(8,128)(2,1)S(1)}, bf16[128,768]{1,0:T(8,128)(2,1)S(1)}, u32[]{:S(2)}, u32[]{:S(2)}) collective-permute-start(bf16[128,768]{1,0:T(8,128)(2,1)S(1)} %get-tuple-element.56), channel_id=1, source_target_pairs={{0,6},{1,7},{2,0},{3,1},{4,2},{5,3},{6,4},{7,5},{8,14},{9,15},{10,... | collective-permute-start | bytes 589832 | tf_op jit(solution)/shard_map/ppermute | solution.py:26
  259.1 7.2 %collective-permute-start.31 = (bf16[128,768]{1,0:T(8,128)(2,1)S(1)}, bf16[128,768]{1,0:T(8,128)(2,1)S(1)}, u32[]{:S(2)}, u32[]{:S(2)}) collective-permute-start(bf16[128,768]{1,0:T(8,128)(2,1)S(1)} %get-tuple-element.57), channel_id=1, source_target_pairs={{0,4},{1,5},{2,6},{3,7},{4,0},{5,1},{6,2},{7,3},{8,12},{9,13},{10,... | collective-permute-start | bytes 589832 | tf_op jit(solution)/shard_map/ppermute | solution.py:26
  262.4 6.9 %collective-permute-start.32 = (bf16[128,768]{1,0:T(8,128)(2,1)S(1)}, bf16[128,768]{1,0:T(8,128)(2,1)S(1)}, u32[]{:S(2)}, u32[]{:S(2)}) collective-permute-start(bf16[128,768]{1,0:T(8,128)(2,1)S(1)} %get-tuple-element.58), channel_id=1, source_target_pairs={{0,2},{1,3},{2,4},{3,5},{4,6},{5,7},{6,0},{7,1},{8,10},{9,11},{10,... | collective-permute-start | bytes 589832 | tf_op jit(solution)/shard_map/ppermute | solution.py:26
  (20 other events, 56.2 us)
Sparse Core Ops, SparseCore 0:
  24.6 41.4 all-gather.2
  72.3 41.8 all-gather.4
  138.5 43.8 reduce-scatter.2
  184.6 42.3 reduce-scatter.4

commit v11 on v9

--- a/solution.py
+++ b/solution.py
@@ -251,13 +251,14 @@
 
     bf16, f32 = jnp.bfloat16, jnp.float32
     term_pair = term_of(1, ())
-    term_own = term_of(0, (term_pair,))
-    far = rows_term(2, (bf16, bf16), (term_own,))
+    far = rows_term(2, (bf16, bf16), (term_pair,))
     up = shift(far[0], 1)
     down = shift(far[1], -1)
     *sent0, kept0 = project(0, 1, (far[0],))
     got0 = [swap(x) for x in sent0]
-    to_right = rows_term(3, (bf16,), (kept0,), (up,), 0)[0]
+    stay = rows_term(0, (f32,), (kept0,))[0]
+    term_own = term_of(0, (stay, up, down))
+    to_right = rows_term(3, (bf16,), (term_own,), (up,), 0)[0]
     term_pair = run(
         move, of((piece, lanes)), (scatter(term_pair),), [VMEM], after=(to_right,), name="move"
     )
@@ -267,8 +268,7 @@
     from_right = shift(to_left, -1)
     *sent1, kept1 = project(1, 1, (to_left, *got0))
     got1 = [swap(x) for x in sent1]
-    stay = rows_term(0, (f32,), (kept1,))[0]
-    quarters0, last = spread(kept0, got0, (stay,))
+    quarters0, last = spread(kept0, got0, (kept1,))
     term_own = scatter(term_own)
 
     def add_rows(place_ref, counts_ref, stay_ref, *refs):

time: 274 us -> 280 us (1.022)
  starting transfers between devices: 54.8 us -> 58 us
    ppermute x25, starting transfers between devices: 36.1 us -> 39.3 us  [shift(): return lax.ppermute(value, 'tensor', ring(step))]
    ppermute x1, waiting for transfers between devices: 2.78 us -> 5.93 us  [per_device(): term_pair = lax.ppermute(term_pair, 'dp', pair)]
    unnamed x66 -> x68, local copies, waits for them, and re-layouts: 13.9 us -> 14.9 us
  transfers between devices with their start and end apart: 37 -> 37, of which waited for: 12 -> 14; matrix products, arithmetic and copies ran while one was open for 0% -> 0% of each run, Pallas kernels for 36% -> 35%
where the time goes in v11:
time: 280 us; the launch traced here: 279 us
  Pallas kernels  102 us (36%)
  waiting for transfers between devices  90.6 us (32%)
  starting transfers between devices  58 us (21%)
  local copies, waits for them, and re-layouts  14.9 us (5%)
  between operations  14.1 us (5%)
    pallas_call x21, Pallas kernels, run(): pl.pallas_call(kernel, out_shape=out, grid=grid, in_specs=list(specs) + [...  102 us
    ppermute x25, waiting for transfers between devices, shift(): return lax.ppermute(value, 'tensor', ring(step))  56.4 us
    ppermute x25, starting transfers between devices, shift(): return lax.ppermute(value, 'tensor', ring(step))  39.3 us
    ppermute x6, waiting for transfers between devices, swap(): return lax.ppermute(value, 'tensor', SWAP)  28.2 us
    ppermute x6, starting transfers between devices, swap(): return lax.ppermute(value, 'tensor', SWAP)  16.6 us
    unnamed x68, local copies, waits for them, and re-layouts  14.9 us
    ppermute x1, waiting for transfers between devices, per_device(): term_pair = lax.ppermute(term_pair, 'dp', pair)  5.93 us
  transfers between devices with their start and end apart: 37, of which 14 were waited for; matrix products, arithmetic and copies ran while one was open for 0% of the time, Pallas kernels for 35%

profile of v11, /device:TPU:0, one launch (start us, length us, event | category | flops | bytes accessed | tf_op | source)
XLA Modules:
  0.0 279.5 jit_solution(827541784728293171)
XLA Ops:
  9.1 2.1 collective-permute-start
  11.1 3.6 %collective-permute-start.1 = (bf16[128,768]{1,0:T(8,128)(2,1)S(1)}, bf16[128,768]{1,0:T(8,128)(2,1)S(1)}, u32[]{:S(2)}, u32[]{:S(2)}) collective-permute-start(bf16[128,768]{1,0:T(8,128)(2,1)S(1)} %get-tuple-element.33), channel_id=1, source_target_pairs={{0,4},{1,5},{2,6},{3,7},{4,0},{5,1},{6,2},{7,3},{8,12},{9,13},{10,... | collective-permute-start | bytes 589832 | tf_op jit(solution)/shard_map/ppermute | solution.py:26
  15.7 1.6 copy-done.4
  19.4 4.1 %collective-permute-done.1.refs_2_ = bf16[128,768]{1,0:T(8,128)(2,1)S(1)} collective-permute-done((bf16[128,768]{1,0:T(8,128)(2,1)S(1)}, bf16[128,768]{1,0:T(8,128)(2,1)S(1)}, u32[]{:S(2)}, u32[]{:S(2)}) %collective-permute-start.1) | collective-permute-done | bytes 196640 | tf_op jit(solution)/shard_map/ppermute | solution.py:26
  25.9 2.4 collective-permute-start.12
  30.3 1.6 collective-permute-start.16
  31.9 19.9 %collective-permute-done.10.refs_6_.refs_3_ = bf16[128,2048]{1,0:T(8,128)(2,1)S(1)} collective-permute-done((bf16[128,2048]{1,0:T(8,128)(2,1)}, bf16[128,2048]{1,0:T(8,128)(2,1)S(1)}, u32[]{:S(2)}, u32[]{:S(2)}) %collective-permute-start.10) | collective-permute-done | bytes 524320 | tf_op jit(solution)/shard_map/ppermute | solution.py:26
  52.5 3.2 %collective-permute-start.9 = (bf16[128,2048]{1,0:T(8,128)(2,1)S(1)}, bf16[128,2048]{1,0:T(8,128)(2,1)S(1)}, u32[]{:S(2)}, u32[]{:S(2)}) collective-permute-start(bf16[128,2048]{1,0:T(8,128)(2,1)S(1)} %get-tuple-element.35.refs_3_.refs_5_), channel_id=1, source_target_pairs={{0,1},{1,0},{2,3},{3,2},{4,5},{5,4},{6,7},{7,6},{8,9},{9,8},{10,11... | collective-permute-start | bytes 1572872 | tf_op jit(solution)/shard_map/ppermute | solution.py:30
  55.7 12.0 %collective-permute-done.14.refs_8_.refs_5_ = bf16[128,2048]{1,0:T(8,128)(2,1)S(1)} collective-permute-done((bf16[128,2048]{1,0:T(8,128)(2,1)S(1)}, bf16[128,2048]{1,0:T(8,128)(2,1)S(1)}, u32[]{:S(2)}, u32[]{:S(2)}) %collective-permute-start.14) | collective-permute-done | bytes 524320 | tf_op jit(solution)/shard_map/ppermute | solution.py:26
  70.1 2.1 w_move.1
  72.2 3.3 %collective-permute-start.11 = (bf16[128,2048]{1,0:T(8,128)(2,1)}, bf16[128,2048]{1,0:T(8,128)(2,1)S(1)}, u32[]{:S(2)}, u32[]{:S(2)}) collective-permute-start(bf16[128,2048]{1,0:T(8,128)(2,1)} %copy-done.26), channel_id=1, source_target_pairs={{0,1},{1,0},{2,3},{3,2},{4,5},{5,4},{6,7},{7,6},{8,9},{9,8},{10,11... | collective-permute-start | bytes 1572872 | tf_op jit(solution)/shard_map/ppermute | solution.py:30
  77.1 1.9 collective-permute-start.8
  79.1 1.4 collective-permute-start.7
  80.5 8.4 %collective-permute-done.11.refs_2_ = bf16[128,2048]{1,0:T(8,128)(2,1)S(1)} collective-permute-done((bf16[128,2048]{1,0:T(8,128)(2,1)}, bf16[128,2048]{1,0:T(8,128)(2,1)S(1)}, u32[]{:S(2)}, u32[]{:S(2)}) %collective-permute-start.11) | collective-permute-done | bytes 524320 | tf_op jit(solution)/shard_map/ppermute | solution.py:30
  90.1 7.9 %collective-permute-done.13.refs_3_ = bf16[128,2048]{1,0:T(8,128)(2,1)S(1)} collective-permute-done((bf16[128,2048]{1,0:T(8,128)(2,1)}, bf16[128,2048]{1,0:T(8,128)(2,1)S(1)}, u32[]{:S(2)}, u32[]{:S(2)}) %collective-permute-start.13) | collective-permute-done | bytes 524320 | tf_op jit(solution)/shard_map/ppermute | solution.py:30
  98.0 3.2 %collective-permute-start.15 = (bf16[128,2048]{1,0:T(8,128)(2,1)}, bf16[128,2048]{1,0:T(8,128)(2,1)S(1)}, u32[]{:S(2)}, u32[]{:S(2)}) collective-permute-start(bf16[128,2048]{1,0:T(8,128)(2,1)} %copy-done.28), channel_id=1, source_target_pairs={{0,1},{1,0},{2,3},{3,2},{4,5},{5,4},{6,7},{7,6},{8,9},{9,8},{10,11... | collective-permute-start | bytes 1572872 | tf_op jit(solution)/shard_map/ppermute | solution.py:30
  101.2 10.4 %collective-permute-done.15.refs_4_ = bf16[128,2048]{1,0:T(8,128)(2,1)S(1)} collective-permute-done((bf16[128,2048]{1,0:T(8,128)(2,1)}, bf16[128,2048]{1,0:T(8,128)(2,1)S(1)}, u32[]{:S(2)}, u32[]{:S(2)}) %collective-permute-start.15) | collective-permute-done | bytes 524320 | tf_op jit(solution)/shard_map/ppermute | solution.py:30
  112.5 4.6 %g_join.1.refs_0_ = bf16[1024,2048]{1,0:T(8,128)(2,1)} custom-call(s32[4]{0:T(128)} %copy-done.12, bf16[128,2048]{1,0:T(8,128)(2,1)} %copy-done.29, bf16[128,2048]{1,0:T(8,128)(2,1)} %copy-done.31, bf16[128,2048]{1,0:T(8,128)(2,1)} %copy-done.32, bf16[128,2048]{1,0:T(8,128)(2,1)} %copy-done.33, bf16[128,2048]{1,0:T(8,128)(2,1)} %copy-done.5, ...), custom_call_target="tpu_custom_call" | custom-call | flops 1000 | bytes 1000 | tf_op jit(solution)/shard_map/g_join/pallas_call | solution.py:47
  119.4 11.6 %term.2.refs_3_ = bf16[1024,3072]{1,0:T(8,128)(2,1)} custom-call(bf16[1024,2048]{1,0:T(8,128)(2,1)} %g_join.1.refs_0_, bf16[512,768]{1,0:T(8,128)(2,1)} %copy-done.1, bf16[512,768]{1,0:T(8,128)(2,1)} %copy-done.2, bf16[512,768]{1,0:T(8,128)(2,1)} %copy-done.18, bf16[512,768]{1,0:T(8,128)(2,1)} %copy-done.19, bf16[512,768]{1,0:T(8,128)(2,1)} %copy-done.22, ...), custom_call_target="tpu_custom_call" | custom-call | flops 1000 | bytes 1000 | tf_op jit(solution)/shard_map/term/pallas_call | solution.py:47
  131.2 7.1 %rows_term.4 = (bf16[512,768]{1,0:T(8,128)(2,1)}, bf16[512,768]{1,0:T(8,128)(2,1)}) custom-call(bf16[1024,2048]{1,0:T(8,128)(2,1)} %g_join.1.refs_0_, bf16[1024,3072]{1,0:T(8,128)(2,1)} %all-gather.3.cloned.1.call-done.refs_1_.refs_0_, bf16[1024,3072]{1,0:T(8,128)(2,1)} %all-gather.5.cloned.1.call-done.refs_2_.refs_0_, bf16[1024,3072]{1,0:T(8,128)(2,1)} %term.2.refs_3_), custom_call_target="tpu_custom_call" | custom-call | flops 1000 | bytes 1000 | tf_op jit(solution)/shard_map/rows_term/pallas_call | solution.py:47
  138.3 4.8 %collective-permute-start.18 = (bf16[512,768]{1,0:T(8,128)(2,1)}, bf16[512,768]{1,0:T(8,128)(2,1)S(1)}, u32[]{:S(2)}, u32[]{:S(2)}) collective-permute-start(bf16[512,768]{1,0:T(8,128)(2,1)} %get-tuple-element.44), channel_id=1, source_target_pairs={{0,6},{1,7},{2,0},{3,1},{4,2},{5,3},{6,4},{7,5},{8,14},{9,15},{10,... | collective-permute-start | bytes 2359304 | tf_op jit(solution)/shard_map/ppermute | solution.py:26
  143.1 11.6 %project.2 = (bf16[512,1024]{1,0:T(8,128)(2,1)}, f32[512,1024]{1,0:T(8,128)}) custom-call(bf16[1024,3072]{1,0:T(8,128)(2,1)} %all-gather.3.cloned.1.call-done.refs_1_.refs_0_, bf16[512,768]{1,0:T(8,128)(2,1)} %copy-done.1, bf16[512,768]{1,0:T(8,128)(2,1)} %copy-done.2, bf16[512,768]{1,0:T(8,128)(2,1)} %copy-done.18, bf16[512,768]{1,0:T(8,128)(2,1)} %copy-done.19, ...), custom_call_target="tpu_custom_call" | custom-call | flops 1000 | bytes 1000 | tf_op jit(solution)/shard_map/project/pallas_call | solution.py:47
  154.7 7.8 %rows_term.5.refs_9_.refs_2_ = f32[1024,768]{1,0:T(8,128)} custom-call(bf16[1024,2048]{1,0:T(8,128)(2,1)} %g_join.1.refs_0_, bf16[1024,3072]{1,0:T(8,128)(2,1)} %all-gather.3.cloned.1.call-done.refs_1_.refs_0_, bf16[1024,3072]{1,0:T(8,128)(2,1)} %all-gather.5.cloned.1.call-done.refs_2_.refs_0_, f32[512,1024]{1,0:T(8,128)} %get-tuple-element.42.refs_3_.refs_1_), custom_call_target="tpu_custom_call" | custom-call | flops 1000 | bytes 1000 | tf_op jit(solution)/shard_map/rows_term/pallas_call | solution.py:47
  164.3 11.7 %term.3.refs_4_ = bf16[1024,3072]{1,0:T(8,128)(2,1)} custom-call(bf16[1024,2048]{1,0:T(8,128)(2,1)} %g_join.1.refs_0_, bf16[512,768]{1,0:T(8,128)(2,1)} %copy-done.1, bf16[512,768]{1,0:T(8,128)(2,1)} %copy-done.2, bf16[512,768]{1,0:T(8,128)(2,1)} %copy-done.18, bf16[512,768]{1,0:T(8,128)(2,1)} %copy-done.19, bf16[512,768]{1,0:T(8,128)(2,1)} %copy-done.22, ...), custom_call_target="tpu_custom_call" | custom-call | flops 1000 | bytes 1000 | tf_op jit(solution)/shard_map/term/pallas_call | solution.py:47
  176.0 3.3 %collective-permute-start.17 = (bf16[512,1024]{1,0:T(8,128)(2,1)}, bf16[512,1024]{1,0:T(8,128)(2,1)S(1)}, u32[]{:S(2)}, u32[]{:S(2)}) collective-permute-start(bf16[512,1024]{1,0:T(8,128)(2,1)} %get-tuple-element.43), channel_id=1, source_target_pairs={{0,1},{1,0},{2,3},{3,2},{4,5},{5,4},{6,7},{7,6},{8,9},{9,8},{10,11... | collective-permute-start | bytes 3145736 | tf_op jit(solution)/shard_map/ppermute | solution.py:30
  179.3 7.8 %rows_term.6.refs_1_.refs_4_ = bf16[1024,768]{1,0:T(8,128)(2,1)} custom-call(bf16[1024,2048]{1,0:T(8,128)(2,1)} %g_join.1.refs_0_, bf16[1024,3072]{1,0:T(8,128)(2,1)} %all-gather.3.cloned.1.call-done.refs_1_.refs_0_, bf16[1024,3072]{1,0:T(8,128)(2,1)} %all-gather.5.cloned.1.call-done.refs_2_.refs_0_, bf16[512,768]{1,0:T(8,128)(2,1)} %copy-done.24, ...), custom_call_target="tpu_custom_call" | custom-call | flops 1000 | bytes 1000 | tf_op jit(solution)/shard_map/rows_term/pallas_call | solution.py:47
  188.1 2.1 move.1.refs_5_
  190.2 7.6 %rows_term.7.refs_9_ = bf16[1024,768]{1,0:T(8,128)(2,1)} custom-call(bf16[1024,2048]{1,0:T(8,128)(2,1)} %g_join.1.refs_0_, bf16[1024,3072]{1,0:T(8,128)(2,1)} %all-gather.3.cloned.1.call-done.refs_1_.refs_0_, bf16[1024,3072]{1,0:T(8,128)(2,1)} %all-gather.5.cloned.1.call-done.refs_2_.refs_0_, bf16[512,768]{1,0:T(8,128)(2,1)} %copy-done.25, ...), custom_call_target="tpu_custom_call" | custom-call | flops 1000 | bytes 1000 | tf_op jit(solution)/shard_map/rows_term/pallas_call | solution.py:47
  197.8 2.3 collective-permute-start.25
  200.1 1.4 collective-permute-done.17.refs_10_.refs_2_
  202.5 11.7 %project.3 = (bf16[512,1024]{1,0:T(8,128)(2,1)}, f32[512,1024]{1,0:T(8,128)}) custom-call(bf16[1024,3072]{1,0:T(8,128)(2,1)} %all-gather.5.cloned.1.call-done.refs_2_.refs_0_, bf16[512,768]{1,0:T(8,128)(2,1)} %copy-done.1, bf16[512,768]{1,0:T(8,128)(2,1)} %copy-done.2, bf16[512,768]{1,0:T(8,128)(2,1)} %copy-done.18, bf16[512,768]{1,0:T(8,128)(2,1)} %copy-done.19, ...), custom_call_target="tpu_custom_call" | custom-call | flops 1000 | bytes 1000 | tf_op jit(solution)/shard_map/project/pallas_call | solution.py:47
  214.2 3.3 %collective-permute-start.23 = (bf16[512,1024]{1,0:T(8,128)(2,1)}, bf16[512,1024]{1,0:T(8,128)(2,1)}, u32[]{:S(2)}, u32[]{:S(2)}) collective-permute-start(bf16[512,1024]{1,0:T(8,128)(2,1)} %get-tuple-element.50), channel_id=1, source_target_pairs={{0,1},{1,0},{2,3},{3,2},{4,5},{5,4},{6,7},{7,6},{8,9},{9,8},{10,11... | collective-permute-start | bytes 3145736 | tf_op jit(solution)/shard_map/ppermute | solution.py:30
  217.8 3.2 %settle.2 = (bf16[128,1024]{1,0:T(8,128)(2,1)}, bf16[128,1024]{1,0:T(8,128)(2,1)}, bf16[128,1024]{1,0:T(8,128)(2,1)}, bf16[128,1024]{1,0:T(8,128)(2,1)}) custom-call(s32[4]{0:T(128)} %copy-done.12, f32[512,1024]{1,0:T(8,128)} %get-tuple-element.42.refs_3_.refs_1_, bf16[512,1024]{1,0:T(8,128)(2,1)} %copy-done.23, f32[512,1024]{1,0:T(8,128)} %get-tuple-element.45.refs_3_.refs_1_), custom_call_target="tpu_custom_call" | custom-call | flops 1000 | bytes 1000 | tf_op jit(solution)/shard_map/settle/pallas_call | solution.py:47
  221.1 3.0 %collective-permute-done.24.refs_3_ = bf16[1024,768]{1,0:T(8,128)(2,1)S(1)} collective-permute-done((bf16[1024,768]{1,0:T(8,128)(2,1)}, bf16[1024,768]{1,0:T(8,128)(2,1)S(1)}, u32[]{:S(2)}, u32[]{:S(2)}) %collective-permute-start.24) | collective-permute-done | bytes 1572896 | tf_op jit(solution)/shard_map/ppermute | solution.py:26
  224.1 1.4 collective-permute-start.21
  225.5 10.9 %collective-permute-done.25.refs_4_ = bf16[1024,768]{1,0:T(8,128)(2,1)S(1)} collective-permute-done((bf16[1024,768]{1,0:T(8,128)(2,1)}, bf16[1024,768]{1,0:T(8,128)(2,1)S(1)}, u32[]{:S(2)}, u32[]{:S(2)}) %collective-permute-start.25) | collective-permute-done | bytes 1572896 | tf_op jit(solution)/shard_map/ppermute | solution.py:26
  236.4 4.1 %collective-permute-start.22 = (bf16[128,1024]{1,0:T(8,128)(2,1)}, bf16[128,1024]{1,0:T(8,128)(2,1)S(1)}, u32[]{:S(2)}, u32[]{:S(2)}) collective-permute-start(bf16[128,1024]{1,0:T(8,128)(2,1)} %get-tuple-element.49), channel_id=1, source_target_pairs={{0,6},{1,7},{2,0},{3,1},{4,2},{5,3},{6,4},{7,5},{8,14},{9,15},{10,... | collective-permute-start | bytes 786440 | tf_op jit(solution)/shard_map/ppermute | solution.py:26
  240.5 2.2 add_rows.1.refs_3_
  242.7 3.0 %settle.3 = (bf16[128,1024]{1,0:T(8,128)(2,1)}, bf16[128,1024]{1,0:T(8,128)(2,1)}, bf16[128,1024]{1,0:T(8,128)(2,1)}, bf16[128,1024]{1,0:T(8,128)(2,1)}) custom-call(s32[4]{0:T(128)} %copy-done.12, f32[512,1024]{1,0:T(8,128)} %get-tuple-element.45.refs_3_.refs_1_, bf16[512,1024]{1,0:T(8,128)(2,1)} %collective-permute-done.23.refs_2_, ...), custom_call_target="tpu_custom_call" | custom-call | flops 1000 | bytes 1000 | tf_op jit(solution)/shard_map/settle/pallas_call | solution.py:47
  245.8 3.8 %collective-permute-start.27 = (bf16[128,1024]{1,0:T(8,128)(2,1)}, bf16[128,1024]{1,0:T(8,128)(2,1)S(1)}, u32[]{:S(2)}, u32[]{:S(2)}) collective-permute-start(bf16[128,1024]{1,0:T(8,128)(2,1)} %get-tuple-element.53), channel_id=1, source_target_pairs={{0,4},{1,5},{2,6},{3,7},{4,0},{5,1},{6,2},{7,3},{8,12},{9,13},{10,... | collective-permute-start | bytes 786440 | tf_op jit(solution)/shard_map/ppermute | solution.py:26
  249.6 5.9 %collective-permute-done.29.refs_1_ = bf16[128,3072]{1,0:T(8,128)(2,1)S(1)} collective-permute-done((bf16[128,3072]{1,0:T(8,128)(2,1)}, bf16[128,3072]{1,0:T(8,128)(2,1)S(1)}, u32[]{:S(2)}, u32[]{:S(2)}) %collective-permute-start.29) | collective-permute-done | bytes 786464 | tf_op jit(solution)/shard_map/ppermute | solution.py:266
  257.8 2.8 collective-permute-start.30
  261.5 2.4 join_out.1.refs_5_
  263.9 2.0 collective-permute-done.30.refs_2_
  265.9 2.0 collective-permute-done.31.refs_3_
  267.8 1.7 collective-permute-done.32.refs_4_
  269.6 1.6 copy-done.3
  271.1 1.8 join_term.1
  (120 shorter events, 25.8 us)
Async XLA Ops:
  7.2 124.0 %all-gather.3.cloned.1.call-start = ((), (), s32[]{:S(2)}) async-start(), calls=%async_computation.2 | async-start | bytes 7077888 | tf_op jit(solution)/shard_map/all_gather | solution.py:140
  9.1 10.4 %collective-permute-start = (bf16[128,768]{1,0:T(8,128)(2,1)S(1)}, bf16[128,768]{1,0:T(8,128)(2,1)S(1)}, u32[]{:S(2)}, u32[]{:S(2)}) collective-permute-start(bf16[128,768]{1,0:T(8,128)(2,1)S(1)} %get-tuple-element.32), channel_id=1, source_target_pairs={{0,2},{1,3},{2,4},{3,5},{4,6},{5,7},{6,0},{7,1},{8,10},{9,11},{10,... | collective-permute-start | bytes 589832 | tf_op jit(solution)/shard_map/ppermute | solution.py:26
  11.1 12.4 %collective-permute-start.1 = (bf16[128,768]{1,0:T(8,128)(2,1)S(1)}, bf16[128,768]{1,0:T(8,128)(2,1)S(1)}, u32[]{:S(2)}, u32[]{:S(2)}) collective-permute-start(bf16[128,768]{1,0:T(8,128)(2,1)S(1)} %get-tuple-element.33), channel_id=1, source_target_pairs={{0,4},{1,5},{2,6},{3,7},{4,0},{5,1},{6,2},{7,3},{8,12},{9,13},{10,... | collective-permute-start | bytes 589832 | tf_op jit(solution)/shard_map/ppermute | solution.py:26
  14.7 8.8 %collective-permute-start.2 = (bf16[128,768]{1,0:T(8,128)(2,1)S(1)}, bf16[128,768]{1,0:T(8,128)(2,1)S(1)}, u32[]{:S(2)}, u32[]{:S(2)}) collective-permute-start(bf16[128,768]{1,0:T(8,128)(2,1)S(1)} %get-tuple-element.34), channel_id=1, source_target_pairs={{0,6},{1,7},{2,0},{3,1},{4,2},{5,3},{6,4},{7,5},{8,14},{9,15},{10,... | collective-permute-start | bytes 589832 | tf_op jit(solution)/shard_map/ppermute | solution.py:26
  18.4 34.1 %copy-start.5 = (bf16[128,2048]{1,0:T(8,128)(2,1)}, bf16[128,2048]{1,0:T(8,128)(2,1)S(1)}, u32[]{:S(2)}) copy-start(bf16[128,2048]{1,0:T(8,128)(2,1)S(1)} %get-tuple-element.35.refs_3_.refs_5_) | copy-start | bytes 1572868
  19.4 56.4 %copy-start.2 = (bf16[512,768]{1,0:T(8,128)(2,1)}, bf16[512,768]{1,0:T(8,128)(2,1)S(1)}, u32[]{:S(2)}) copy-start(bf16[512,768]{1,0:T(8,128)(2,1)S(1)} %get-tuple-element.37.refs_2_) | copy-start | bytes 2359300
  19.4 57.7 %copy-start.1 = (bf16[512,768]{1,0:T(8,128)(2,1)}, bf16[512,768]{1,0:T(8,128)(2,1)S(1)}, u32[]{:S(2)}) copy-start(bf16[512,768]{1,0:T(8,128)(2,1)S(1)} %get-tuple-element.36.refs_4_.refs_1_) | copy-start | bytes 2359300
  24.5 106.7 %all-gather.5.cloned.1.call-start = ((), (), s32[]{:S(2)}) async-start(), calls=%async_computation.3 | async-start | bytes 7077888 | tf_op jit(solution)/shard_map/all_gather | solution.py:140
  24.6 27.2 %collective-permute-start.10 = (bf16[128,2048]{1,0:T(8,128)(2,1)}, bf16[128,2048]{1,0:T(8,128)(2,1)S(1)}, u32[]{:S(2)}, u32[]{:S(2)}) collective-permute-start(bf16[128,2048]{1,0:T(8,128)(2,1)} %copy-done.16), channel_id=1, source_target_pairs={{0,2},{1,3},{2,4},{3,5},{4,6},{5,7},{6,0},{7,1},{8,10},{9,11},{10,... | collective-permute-start | bytes 1572872 | tf_op jit(solution)/shard_map/ppermute | solution.py:26
  25.9 26.6 %collective-permute-start.12 = (bf16[128,2048]{1,0:T(8,128)(2,1)S(1)}, bf16[128,2048]{1,0:T(8,128)(2,1)S(1)}, u32[]{:S(2)}, u32[]{:S(2)}) collective-permute-start(bf16[128,2048]{1,0:T(8,128)(2,1)S(1)} %get-tuple-element.39), channel_id=1, source_target_pairs={{0,4},{1,5},{2,6},{3,7},{4,0},{5,1},{6,2},{7,3},{8,12},{9,13},{10,... | collective-permute-start | bytes 1572872 | tf_op jit(solution)/shard_map/ppermute | solution.py:26
  28.3 39.4 %collective-permute-start.6 = (bf16[512,768]{1,0:T(8,128)(2,1)S(1)}, bf16[512,768]{1,0:T(8,128)(2,1)S(1)}, u32[]{:S(2)}, u32[]{:S(2)}) collective-permute-start(bf16[512,768]{1,0:T(8,128)(2,1)S(1)} %get-tuple-element.37.refs_2_), channel_id=1, source_target_pairs={{0,6},{1,7},{2,0},{3,1},{4,2},{5,3},{6,4},{7,5},{8,14},{9,15},{10,... | collective-permute-start | bytes 2359304 | tf_op jit(solution)/shard_map/ppermute | solution.py:26
  29.5 38.2 %collective-permute-start.3 = (bf16[512,768]{1,0:T(8,128)(2,1)S(1)}, bf16[512,768]{1,0:T(8,128)(2,1)S(1)}, u32[]{:S(2)}, u32[]{:S(2)}) collective-permute-start(bf16[512,768]{1,0:T(8,128)(2,1)S(1)} %get-tuple-element.36.refs_4_.refs_1_), channel_id=1, source_target_pairs={{0,2},{1,3},{2,4},{3,5},{4,6},{5,7},{6,0},{7,1},{8,10},{9,11},{10,... | collective-permute-start | bytes 2359304 | tf_op jit(solution)/shard_map/ppermute | solution.py:26
  30.3 37.5 %collective-permute-start.16 = (bf16[128,3072]{1,0:T(8,128)(2,1)}, bf16[128,3072]{1,0:T(8,128)(2,1)S(1)}, u32[]{:S(2)}, u32[]{:S(2)}) collective-permute-start(bf16[128,3072]{1,0:T(8,128)(2,1)} %w_join.1), channel_id=1, source_target_pairs={{0,64},{8,72},{16,80},{24,88},{32,96},{40,104},{48,112},{56,120},{... | collective-permute-start | bytes 2359304 | tf_op jit(solution)/shard_map/ppermute | solution.py:135
  51.8 16.0 %copy-start.26 = (bf16[128,2048]{1,0:T(8,128)(2,1)}, bf16[128,2048]{1,0:T(8,128)(2,1)S(1)}, u32[]{:S(2)}) copy-start(bf16[128,2048]{1,0:T(8,128)(2,1)S(1)} %collective-permute-done.10.refs_6_.refs_3_) | copy-start | bytes 1572868
  51.8 15.9 %collective-permute-start.14 = (bf16[128,2048]{1,0:T(8,128)(2,1)S(1)}, bf16[128,2048]{1,0:T(8,128)(2,1)S(1)}, u32[]{:S(2)}, u32[]{:S(2)}) collective-permute-start(bf16[128,2048]{1,0:T(8,128)(2,1)S(1)} %get-tuple-element.40), channel_id=1, source_target_pairs={{0,6},{1,7},{2,0},{3,1},{4,2},{5,3},{6,4},{7,5},{8,14},{9,15},{10,... | collective-permute-start | bytes 1572872 | tf_op jit(solution)/shard_map/ppermute | solution.py:26
  52.5 15.2 %copy-start.27 = (bf16[128,2048]{1,0:T(8,128)(2,1)}, bf16[128,2048]{1,0:T(8,128)(2,1)S(1)}, u32[]{:S(2)}) copy-start(bf16[128,2048]{1,0:T(8,128)(2,1)S(1)} %collective-permute-done.12.refs_7_.refs_4_) | copy-start | bytes 1572868
  52.5 15.2 %collective-permute-start.9 = (bf16[128,2048]{1,0:T(8,128)(2,1)S(1)}, bf16[128,2048]{1,0:T(8,128)(2,1)S(1)}, u32[]{:S(2)}, u32[]{:S(2)}) collective-permute-start(bf16[128,2048]{1,0:T(8,128)(2,1)S(1)} %get-tuple-element.35.refs_3_.refs_5_), channel_id=1, source_target_pairs={{0,1},{1,0},{2,3},{3,2},{4,5},{5,4},{6,7},{7,6},{8,9},{9,8},{10,11... | collective-permute-start | bytes 1572872 | tf_op jit(solution)/shard_map/ppermute | solution.py:30
  72.2 115.9 %reduce-scatter.3.cloned.1.call-start = ((), (), s32[]{:S(2)}) async-start(), calls=%async_computation.4 | async-start | bytes 7077888 | tf_op jit(solution)/shard_map/reduce_scatter | solution.py:230
  72.2 16.7 %collective-permute-start.11 = (bf16[128,2048]{1,0:T(8,128)(2,1)}, bf16[128,2048]{1,0:T(8,128)(2,1)S(1)}, u32[]{:S(2)}, u32[]{:S(2)}) collective-permute-start(bf16[128,2048]{1,0:T(8,128)(2,1)} %copy-done.26), channel_id=1, source_target_pairs={{0,1},{1,0},{2,3},{3,2},{4,5},{5,4},{6,7},{7,6},{8,9},{9,8},{10,11... | collective-permute-start | bytes 1572872 | tf_op jit(solution)/shard_map/ppermute | solution.py:30
  75.5 22.5 %collective-permute-start.13 = (bf16[128,2048]{1,0:T(8,128)(2,1)}, bf16[128,2048]{1,0:T(8,128)(2,1)S(1)}, u32[]{:S(2)}, u32[]{:S(2)}) collective-permute-start(bf16[128,2048]{1,0:T(8,128)(2,1)} %copy-done.27), channel_id=1, source_target_pairs={{0,1},{1,0},{2,3},{3,2},{4,5},{5,4},{6,7},{7,6},{8,9},{9,8},{10,11... | collective-permute-start | bytes 1572872 | tf_op jit(solution)/shard_map/ppermute | solution.py:30
  75.8 41.3 %collective-permute-start.4 = (bf16[512,768]{1,0:T(8,128)(2,1)S(1)}, bf16[512,768]{1,0:T(8,128)(2,1)S(1)}, u32[]{:S(2)}, u32[]{:S(2)}) collective-permute-start(bf16[512,768]{1,0:T(8,128)(2,1)S(1)} %get-tuple-element.37.refs_2_), channel_id=1, source_target_pairs={{0,2},{1,3},{2,4},{3,5},{4,6},{5,7},{6,0},{7,1},{8,10},{9,11},{10,... | collective-permute-start | bytes 2359304 | tf_op jit(solution)/shard_map/ppermute | solution.py:26
  77.1 40.0 %collective-permute-start.8 = (bf16[512,768]{1,0:T(8,128)(2,1)S(1)}, bf16[512,768]{1,0:T(8,128)(2,1)S(1)}, u32[]{:S(2)}, u32[]{:S(2)}) collective-permute-start(bf16[512,768]{1,0:T(8,128)(2,1)S(1)} %get-tuple-element.36.refs_4_.refs_1_), channel_id=1, source_target_pairs={{0,6},{1,7},{2,0},{3,1},{4,2},{5,3},{6,4},{7,5},{8,14},{9,15},{10,... | collective-permute-start | bytes 2359304 | tf_op jit(solution)/shard_map/ppermute | solution.py:26
  79.1 38.1 %collective-permute-start.7 = (bf16[512,768]{1,0:T(8,128)(2,1)}, bf16[512,768]{1,0:T(8,128)(2,1)S(1)}, u32[]{:S(2)}, u32[]{:S(2)}) collective-permute-start(bf16[512,768]{1,0:T(8,128)(2,1)} %copy-done.17), channel_id=1, source_target_pairs={{0,6},{1,7},{2,0},{3,1},{4,2},{5,3},{6,4},{7,5},{8,14},{9,15},{10,... | collective-permute-start | bytes 2359304 | tf_op jit(solution)/shard_map/ppermute | solution.py:26
  88.9 22.8 %copy-start.31 = (bf16[128,2048]{1,0:T(8,128)(2,1)}, bf16[128,2048]{1,0:T(8,128)(2,1)S(1)}, u32[]{:S(2)}) copy-start(bf16[128,2048]{1,0:T(8,128)(2,1)S(1)} %collective-permute-done.11.refs_2_) | copy-start | bytes 1572868
  88.9 28.3 %collective-permute-start.5 = (bf16[512,768]{1,0:T(8,128)(2,1)}, bf16[512,768]{1,0:T(8,128)(2,1)S(1)}, u32[]{:S(2)}, u32[]{:S(2)}) collective-permute-start(bf16[512,768]{1,0:T(8,128)(2,1)} %copy-done.18), channel_id=1, source_target_pairs={{0,2},{1,3},{2,4},{3,5},{4,6},{5,7},{6,0},{7,1},{8,10},{9,11},{10,... | collective-permute-start | bytes 2359304 | tf_op jit(solution)/shard_map/ppermute | solution.py:26
  98.0 13.6 %copy-start.32 = (bf16[128,2048]{1,0:T(8,128)(2,1)}, bf16[128,2048]{1,0:T(8,128)(2,1)S(1)}, u32[]{:S(2)}) copy-start(bf16[128,2048]{1,0:T(8,128)(2,1)S(1)} %collective-permute-done.13.refs_3_) | copy-start | bytes 1572868
  98.0 13.6 %collective-permute-start.15 = (bf16[128,2048]{1,0:T(8,128)(2,1)}, bf16[128,2048]{1,0:T(8,128)(2,1)S(1)}, u32[]{:S(2)}, u32[]{:S(2)}) collective-permute-start(bf16[128,2048]{1,0:T(8,128)(2,1)} %copy-done.28), channel_id=1, source_target_pairs={{0,1},{1,0},{2,3},{3,2},{4,5},{5,4},{6,7},{7,6},{8,9},{9,8},{10,11... | collective-permute-start | bytes 1572872 | tf_op jit(solution)/shard_map/ppermute | solution.py:30
  131.1 124.4 %reduce-scatter.5.cloned.1.call-start = ((), (), s32[]{:S(2)}) async-start(), calls=%async_computation.5 | async-start | bytes 7077888 | tf_op jit(solution)/shard_map/reduce_scatter | solution.py:230
  138.3 24.2 %collective-permute-start.18 = (bf16[512,768]{1,0:T(8,128)(2,1)}, bf16[512,768]{1,0:T(8,128)(2,1)S(1)}, u32[]{:S(2)}, u32[]{:S(2)}) collective-permute-start(bf16[512,768]{1,0:T(8,128)(2,1)} %get-tuple-element.44), channel_id=1, source_target_pairs={{0,6},{1,7},{2,0},{3,1},{4,2},{5,3},{6,4},{7,5},{8,14},{9,15},{10,... | collective-permute-start | bytes 2359304 | tf_op jit(solution)/shard_map/ppermute | solution.py:26
  143.1 19.5 %collective-permute-start.19 = (bf16[512,768]{1,0:T(8,128)(2,1)}, bf16[512,768]{1,0:T(8,128)(2,1)S(1)}, u32[]{:S(2)}, u32[]{:S(2)}) collective-permute-start(bf16[512,768]{1,0:T(8,128)(2,1)} %get-tuple-element.41.refs_9_), channel_id=1, source_target_pairs={{0,2},{1,3},{2,4},{3,5},{4,6},{5,7},{6,0},{7,1},{8,10},{9,11},{10,... | collective-permute-start | bytes 2359304 | tf_op jit(solution)/shard_map/ppermute | solution.py:26
  176.0 25.5 %collective-permute-start.17 = (bf16[512,1024]{1,0:T(8,128)(2,1)}, bf16[512,1024]{1,0:T(8,128)(2,1)S(1)}, u32[]{:S(2)}, u32[]{:S(2)}) collective-permute-start(bf16[512,1024]{1,0:T(8,128)(2,1)} %get-tuple-element.43), channel_id=1, source_target_pairs={{0,1},{1,0},{2,3},{3,2},{4,5},{5,4},{6,7},{7,6},{8,9},{9,8},{10,11... | collective-permute-start | bytes 3145736 | tf_op jit(solution)/shard_map/ppermute | solution.py:30
  187.1 37.0 %collective-permute-start.24 = (bf16[1024,768]{1,0:T(8,128)(2,1)}, bf16[1024,768]{1,0:T(8,128)(2,1)S(1)}, u32[]{:S(2)}, u32[]{:S(2)}) collective-permute-start(bf16[1024,768]{1,0:T(8,128)(2,1)} %rows_term.6.refs_1_.refs_4_), channel_id=1, source_target_pairs={{0,2},{1,3},{2,4},{3,5},{4,6},{5,7},{6,0},{7,1},{8,10},{9,11},{10,... | collective-permute-start | bytes 4718600 | tf_op jit(solution)/shard_map/ppermute | solution.py:26
  197.8 38.6 %collective-permute-start.25 = (bf16[1024,768]{1,0:T(8,128)(2,1)}, bf16[1024,768]{1,0:T(8,128)(2,1)S(1)}, u32[]{:S(2)}, u32[]{:S(2)}) collective-permute-start(bf16[1024,768]{1,0:T(8,128)(2,1)} %rows_term.7.refs_9_), channel_id=1, source_target_pairs={{0,6},{1,7},{2,0},{3,1},{4,2},{5,3},{6,4},{7,5},{8,14},{9,15},{10,... | collective-permute-start | bytes 4718600 | tf_op jit(solution)/shard_map/ppermute | solution.py:26
  214.2 28.5 %collective-permute-start.23 = (bf16[512,1024]{1,0:T(8,128)(2,1)}, bf16[512,1024]{1,0:T(8,128)(2,1)}, u32[]{:S(2)}, u32[]{:S(2)}) collective-permute-start(bf16[512,1024]{1,0:T(8,128)(2,1)} %get-tuple-element.50), channel_id=1, source_target_pairs={{0,1},{1,0},{2,3},{3,2},{4,5},{5,4},{6,7},{7,6},{8,9},{9,8},{10,11... | collective-permute-start | bytes 3145736 | tf_op jit(solution)/shard_map/ppermute | solution.py:30
  217.5 38.0 %collective-permute-start.29 = (bf16[128,3072]{1,0:T(8,128)(2,1)}, bf16[128,3072]{1,0:T(8,128)(2,1)S(1)}, u32[]{:S(2)}, u32[]{:S(2)}) collective-permute-start(bf16[128,3072]{1,0:T(8,128)(2,1)} %move.1.refs_5_), channel_id=1, source_target_pairs={{0,64},{8,72},{16,80},{24,88},{32,96},{40,104},{48,112},{56,120},{... | collective-permute-start | bytes 2359304 | tf_op jit(solution)/shard_map/ppermute | solution.py:266
  217.8 22.6 %copy-start = (f32[1024,768]{1,0:T(8,128)S(1)}, f32[1024,768]{1,0:T(8,128)}, u32[]{:S(2)}) copy-start(f32[1024,768]{1,0:T(8,128)} %rows_term.5.refs_9_.refs_2_) | copy-start | bytes 9437188
  217.8 22.6 %copy-start.13 = (s32[4]{0:T(128)S(1)}, s32[4]{0:T(128)}, u32[]{:S(2)}) copy-start(s32[4]{0:T(128)} %copy-done.12) | copy-start | bytes 52
  221.1 24.7 %collective-permute-start.20 = (bf16[128,1024]{1,0:T(8,128)(2,1)}, bf16[128,1024]{1,0:T(8,128)(2,1)S(1)}, u32[]{:S(2)}, u32[]{:S(2)}) collective-permute-start(bf16[128,1024]{1,0:T(8,128)(2,1)} %get-tuple-element.47), channel_id=1, source_target_pairs={{0,2},{1,3},{2,4},{3,5},{4,6},{5,7},{6,0},{7,1},{8,10},{9,11},{10,... | collective-permute-start | bytes 786440 | tf_op jit(solution)/shard_map/ppermute | solution.py:26
  224.1 25.5 %collective-permute-start.21 = (bf16[128,1024]{1,0:T(8,128)(2,1)}, bf16[128,1024]{1,0:T(8,128)(2,1)S(1)}, u32[]{:S(2)}, u32[]{:S(2)}) collective-permute-start(bf16[128,1024]{1,0:T(8,128)(2,1)} %get-tuple-element.48), channel_id=1, source_target_pairs={{0,4},{1,5},{2,6},{3,7},{4,0},{5,1},{6,2},{7,3},{8,12},{9,13},{10,... | collective-permute-start | bytes 786440 | tf_op jit(solution)/shard_map/ppermute | solution.py:26
  236.4 13.2 %collective-permute-start.22 = (bf16[128,1024]{1,0:T(8,128)(2,1)}, bf16[128,1024]{1,0:T(8,128)(2,1)S(1)}, u32[]{:S(2)}, u32[]{:S(2)}) collective-permute-start(bf16[128,1024]{1,0:T(8,128)(2,1)} %get-tuple-element.49), channel_id=1, source_target_pairs={{0,6},{1,7},{2,0},{3,1},{4,2},{5,3},{6,4},{7,5},{8,14},{9,15},{10,... | collective-permute-start | bytes 786440 | tf_op jit(solution)/shard_map/ppermute | solution.py:26
  242.7 18.8 %copy-start.11 = (bf16[128,1024]{1,0:T(8,128)(2,1)S(1)}, bf16[128,1024]{1,0:T(8,128)(2,1)}, u32[]{:S(2)}) copy-start(bf16[128,1024]{1,0:T(8,128)(2,1)} %get-tuple-element.46.refs_1_) | copy-start | bytes 786436
  245.7 15.8 %copy-start.14 = (s32[4]{0:T(128)S(1)}, s32[4]{0:T(128)}, u32[]{:S(2)}) copy-start(s32[4]{0:T(128)} %copy-done.12) | copy-start | bytes 52
  245.7 14.8 %collective-permute-start.26 = (bf16[128,1024]{1,0:T(8,128)(2,1)}, bf16[128,1024]{1,0:T(8,128)(2,1)S(1)}, u32[]{:S(2)}, u32[]{:S(2)}) collective-permute-start(bf16[128,1024]{1,0:T(8,128)(2,1)} %get-tuple-element.52), channel_id=1, source_target_pairs={{0,2},{1,3},{2,4},{3,5},{4,6},{5,7},{6,0},{7,1},{8,10},{9,11},{10,... | collective-permute-start | bytes 786440 | tf_op jit(solution)/shard_map/ppermute | solution.py:26
  245.8 15.8 %collective-permute-start.27 = (bf16[128,1024]{1,0:T(8,128)(2,1)}, bf16[128,1024]{1,0:T(8,128)(2,1)S(1)}, u32[]{:S(2)}, u32[]{:S(2)}) collective-permute-start(bf16[128,1024]{1,0:T(8,128)(2,1)} %get-tuple-element.53), channel_id=1, source_target_pairs={{0,4},{1,5},{2,6},{3,7},{4,0},{5,1},{6,2},{7,3},{8,12},{9,13},{10,... | collective-permute-start | bytes 786440 | tf_op jit(solution)/shard_map/ppermute | solution.py:26
  249.6 11.9 %collective-permute-start.28 = (bf16[128,1024]{1,0:T(8,128)(2,1)}, bf16[128,1024]{1,0:T(8,128)(2,1)S(1)}, u32[]{:S(2)}, u32[]{:S(2)}) collective-permute-start(bf16[128,1024]{1,0:T(8,128)(2,1)} %get-tuple-element.54), channel_id=1, source_target_pairs={{0,6},{1,7},{2,0},{3,1},{4,2},{5,3},{6,4},{7,5},{8,14},{9,15},{10,... | collective-permute-start | bytes 786440 | tf_op jit(solution)/shard_map/ppermute | solution.py:26
  257.8 8.1 %collective-permute-start.30 = (bf16[128,768]{1,0:T(8,128)(2,1)S(1)}, bf16[128,768]{1,0:T(8,128)(2,1)S(1)}, u32[]{:S(2)}, u32[]{:S(2)}) collective-permute-start(bf16[128,768]{1,0:T(8,128)(2,1)S(1)} %get-tuple-element.56), channel_id=1, source_target_pairs={{0,6},{1,7},{2,0},{3,1},{4,2},{5,3},{6,4},{7,5},{8,14},{9,15},{10,... | collective-permute-start | bytes 589832 | tf_op jit(solution)/shard_map/ppermute | solution.py:26
  260.6 7.3 %collective-permute-start.31 = (bf16[128,768]{1,0:T(8,128)(2,1)S(1)}, bf16[128,768]{1,0:T(8,128)(2,1)S(1)}, u32[]{:S(2)}, u32[]{:S(2)}) collective-permute-start(bf16[128,768]{1,0:T(8,128)(2,1)S(1)} %get-tuple-element.57), channel_id=1, source_target_pairs={{0,4},{1,5},{2,6},{3,7},{4,0},{5,1},{6,2},{7,3},{8,12},{9,13},{10,... | collective-permute-start | bytes 589832 | tf_op jit(solution)/shard_map/ppermute | solution.py:26
  260.6 9.0 %collective-permute-start.32 = (bf16[128,768]{1,0:T(8,128)(2,1)S(1)}, bf16[128,768]{1,0:T(8,128)(2,1)S(1)}, u32[]{:S(2)}, u32[]{:S(2)}) collective-permute-start(bf16[128,768]{1,0:T(8,128)(2,1)S(1)} %get-tuple-element.58), channel_id=1, source_target_pairs={{0,2},{1,3},{2,4},{3,5},{4,6},{5,7},{6,0},{7,1},{8,10},{9,11},{10,... | collective-permute-start | bytes 589832 | tf_op jit(solution)/shard_map/ppermute | solution.py:26
  (23 other events, 52.5 us)
Sparse Core Ops, SparseCore 0:
  24.6 41.4 all-gather.2
  72.3 41.8 all-gather.4
  131.2 45.5 reduce-scatter.2
  179.1 42.1 reduce-scatter.4
